TPU v7x, 32 devices: a whole 2x2x4 slice. The times are simulated.
32 devices in a mesh: ctx: 16 (over z, y, x), head: 2 (over core).
Axes of the slice: x: 2, y: 2, z: 4, core: 2. Of those that a mesh axis runs over, the one named last changes fastest.
Arguments:
- query_raw: bfloat16 [4096, 5120], P('ctx', 'head'), may hold values from -9 to 9
- key_raw: bfloat16 [4096, 5120], P('ctx', 'head'), may hold values from -9 to 9
- values: bfloat16 [4096, 5120], P('ctx', 'head'), may hold values from -6 to 6
- out_grad: bfloat16 [4096, 5120], P('ctx', 'head'), may hold values from -128 to 128
- query_gain: float32 [5120], P('head'), may hold values from 0.25 to 1.75
- key_gain: float32 [5120], P('head'), may hold values from 0.25 to 1.75
- key_tiles: int32 [32, 4], P('ctx'), may hold values from 0 to 31, as said below
- global_ids: int32 [32], P('ctx'), may hold values from 0 to 4095, as said below
- readers: int32 [16, 16], P('ctx'), may hold values from 0 to 1, as said below
Outputs:
- query_grad: bfloat16 [4096, 5120], P('ctx', 'head')
- key_grad: bfloat16 [4096, 5120], P('ctx', 'head')
- value_grad: bfloat16 [4096, 5120], P('ctx', 'head')
Inputs may be any that keep to these rules, and one draw needn't show every extreme that they name: `key_tiles`: row t lists, ascending, the 4 tiles of 4 consecutive tile-frames of 1 tiles; every listed tile lies on an index of ctx at most 1 away from tile t's, and in every draw some tile reads a tile exactly 1 below and some tile one exactly 1 above. `global_ids`: entries c * 2 to (c + 1) * 2 - 1 are distinct ascending tokens of index c of ctx. `readers`: each row has either one 1 or all 16 entries 1; at least one row has all.
All inputs are finite; a program needn't handle non-finite values.
Results may differ from a plain program's by a relative error of at most 0.02.
Values may be sent and summed in bfloat16 or wider, within the bound.
No kernel may reach another device: no remote copies, remote signals or barrier semaphores. Data moves between devices by JAX's collectives and lax.ppermute only.
A program may use at most 128 MiB of HBM per device.

v0:
```python
import jax
import jax.numpy as jnp
from jax import lax
from jax.sharding import PartitionSpec as P

HEAD_DIM = 128
D = 5120
TILE = 128
REACH = 1
G_DEV = 2


EPSILON = 1e-06


def passed_along(shard, axis, by):
    count = lax.axis_size(axis)
    return lax.ppermute(shard, axis, [(i, (i + by) % count) for i in range(count)])


def normalize(as_float, gain, squares):
    inverse = lax.rsqrt(squares[:, None] / D + EPSILON)
    return (inverse, (as_float * inverse * gain).astype(jnp.bfloat16))


def norm_grad(as_float, inverse, scaled, coeffs):
    return (inverse * scaled - as_float * inverse**3 * (coeffs[:, None] / D)).astype(jnp.bfloat16)


def body(
    query_raw, key_raw, values, out_grad, query_gain, key_gain, key_tiles, global_ids, readers
):
    tokens_here, width_here = query_raw.shape
    heads_here = width_here // HEAD_DIM
    tiles_here = tokens_here // TILE
    factor = HEAD_DIM ** (-0.5)
    device = lax.axis_index("ctx")
    query_rows = query_raw.astype(jnp.float32)
    key_rows = key_raw.astype(jnp.float32)
    query_sq, key_sq = lax.psum(
        (jnp.sum(query_rows * query_rows, axis=1), jnp.sum(key_rows * key_rows, axis=1)), "head"
    )
    query_inv, query_norm = normalize(query_rows, query_gain, query_sq)
    key_inv, key_norm = normalize(key_rows, key_gain, key_sq)
    own_rows = global_ids - device * tokens_here
    own_pair = jnp.stack([key_norm[own_rows], values[own_rows]])
    global_pair = lax.all_gather(own_pair, "ctx", axis=1, tiled=True)
    global_keys = global_pair[0].reshape(-1, heads_here, HEAD_DIM)
    global_vals = global_pair[1].reshape(-1, heads_here, HEAD_DIM)
    live_mask = jnp.repeat(readers[0] > 0, G_DEV)
    key_value = jnp.stack([key_norm, values])
    current = passed_along(key_value, "ctx", -REACH)
    pieces = [current]
    for hop_index in range(2 * REACH):
        current = passed_along(current, "ctx", 1)
        pieces.append(current)
    pieces = pieces[::-1]
    window_pair = jnp.concatenate(pieces, axis=1)
    first_tile = (device - REACH) * tiles_here
    local_tiles = key_tiles - first_tile
    window_rows = (
        local_tiles[:, :, None] * TILE + jnp.arange(TILE, dtype=jnp.int32)[None, None, :]
    ).reshape(tiles_here, -1)
    window_count = window_rows.shape[1]
    window_keys = window_pair[0][window_rows].reshape(
        tiles_here, window_count, heads_here, HEAD_DIM
    )
    window_vals = window_pair[1][window_rows].reshape(
        tiles_here, window_count, heads_here, HEAD_DIM
    )
    query_four = query_norm.reshape(tiles_here, TILE, heads_here, HEAD_DIM)
    grad_four = out_grad.reshape(tiles_here, TILE, heads_here, HEAD_DIM)

    def head_block(head_number):
        query_head = lax.dynamic_index_in_dim(query_four, head_number, 2, keepdims=False)
        grad_head = lax.dynamic_index_in_dim(grad_four, head_number, 2, keepdims=False)
        wkeys = lax.dynamic_index_in_dim(window_keys, head_number, 2, keepdims=False)
        wvals = lax.dynamic_index_in_dim(window_vals, head_number, 2, keepdims=False)
        gkeys = lax.dynamic_index_in_dim(global_keys, head_number, 1, keepdims=False)
        gvals = lax.dynamic_index_in_dim(global_vals, head_number, 1, keepdims=False)
        score_window = (
            jnp.einsum("tqd,tkd->tqk", query_head, wkeys, preferred_element_type=jnp.float32)
            * factor
        )
        score_global = (
            jnp.einsum("tqd,kd->tqk", query_head, gkeys, preferred_element_type=jnp.float32)
            * factor
        )
        score_global = jnp.where(live_mask, score_global, -jnp.inf)
        scores = jnp.concatenate([score_window, score_global], axis=2)
        largest = jnp.max(scores, axis=2, keepdims=True)
        log_total = largest + jnp.log(jnp.sum(jnp.exp(scores - largest), axis=2, keepdims=True))
        probs = jnp.exp(scores - log_total)
        probs_low = probs.astype(jnp.bfloat16)
        attended = jnp.einsum(
            "tqk,tkd->tqd", probs_low[..., :window_count], wvals, preferred_element_type=jnp.float32
        )
        attended = attended + jnp.einsum(
            "tqk,kd->tqd", probs_low[..., window_count:], gvals, preferred_element_type=jnp.float32
        )
        attended = lax.optimization_barrier(attended.astype(jnp.bfloat16))
        delta_rows = jnp.sum(grad_head.astype(jnp.float32) * attended.astype(jnp.float32), axis=2)
        dprob = jnp.concatenate(
            [
                jnp.einsum("tqd,tkd->tqk", grad_head, wvals, preferred_element_type=jnp.float32),
                jnp.einsum("tqd,kd->tqk", grad_head, gvals, preferred_element_type=jnp.float32),
            ],
            axis=2,
        )
        dscore = (probs * (dprob - delta_rows[..., None]) * factor).astype(jnp.bfloat16)
        grad_query = jnp.einsum(
            "tqk,tkd->tqd", dscore[..., :window_count], wkeys, preferred_element_type=jnp.float32
        )
        grad_query = grad_query + jnp.einsum(
            "tqk,kd->tqd", dscore[..., window_count:], gkeys, preferred_element_type=jnp.float32
        )
        window_dk = jnp.einsum(
            "tqk,tqd->tkd",
            dscore[..., :window_count],
            query_head,
            preferred_element_type=jnp.float32,
        )
        window_dv = jnp.einsum(
            "tqk,tqd->tkd",
            probs_low[..., :window_count],
            grad_head,
            preferred_element_type=jnp.float32,
        )
        global_dk = jnp.einsum(
            "tqk,tqd->kd",
            dscore[..., window_count:],
            query_head,
            preferred_element_type=jnp.float32,
        )
        global_dv = jnp.einsum(
            "tqk,tqd->kd",
            probs_low[..., window_count:],
            grad_head,
            preferred_element_type=jnp.float32,
        )
        return (grad_query, window_dk, window_dv, global_dk, global_dv)

    head_results = lax.map(head_block, jnp.arange(heads_here, dtype=jnp.int32))
    grad_query = jnp.moveaxis(head_results[0], 0, 2).reshape(tokens_here, width_here)
    window_dk = jnp.moveaxis(head_results[1], 0, 2).reshape(-1, width_here)
    window_dv = jnp.moveaxis(head_results[2], 0, 2).reshape(-1, width_here)
    global_dk = jnp.moveaxis(head_results[3], 0, 1).reshape(-1, width_here)
    global_dv = jnp.moveaxis(head_results[4], 0, 1).reshape(-1, width_here)
    window_grads = jnp.zeros((2, window_pair.shape[1], width_here), jnp.float32)
    window_grads = window_grads.at[:, window_rows.reshape(-1)].add(
        jnp.stack([window_dk, window_dv])
    )
    spread_grads = window_grads.reshape(2, 2 * REACH + 1, tokens_here, width_here)
    slots = [spread_grads[:, slot_index] for slot_index in range(2 * REACH + 1)]
    carried = slots[2 * REACH]
    for hop_index in range(2 * REACH):
        carried = (
            passed_along(carried.astype(jnp.bfloat16), "ctx", 1).astype(carried.dtype)
            + slots[2 * REACH - 1 - hop_index]
        )
    home_grads = passed_along(carried.astype(jnp.bfloat16), "ctx", -REACH).astype(carried.dtype)
    global_part = lax.psum_scatter(
        jnp.stack([global_dk, global_dv]), "ctx", scatter_dimension=1, tiled=True
    )
    home_grads = home_grads.at[:, own_rows].add(global_part)
    scaled_query = grad_query * query_gain
    scaled_key = home_grads[0] * key_gain
    query_dot, key_dot = lax.psum(
        (jnp.sum(scaled_query * query_rows, axis=1), jnp.sum(scaled_key * key_rows, axis=1)), "head"
    )
    query_grad = norm_grad(query_rows, query_inv, scaled_query, query_dot)
    key_grad = norm_grad(key_rows, key_inv, scaled_key, key_dot)
    return (query_grad, key_grad, home_grads[1].astype(jnp.bfloat16))


def solution(mesh):
    return jax.shard_map(
        body,
        mesh=mesh,
        in_specs=(
            P("ctx", "head"),
            P("ctx", "head"),
            P("ctx", "head"),
            P("ctx", "head"),
            P("head"),
            P("head"),
            P("ctx", None),
            P("ctx"),
            P("ctx", None),
        ),
        out_specs=(P("ctx", "head"), P("ctx", "head"), P("ctx", "head")),
        check_vma=False,
    )
```

profile of v0, /device:TPU:0, one launch (start us, length us, event | category | flops | bytes accessed | tf_op | source)
XLA Modules:
  0.0 1256.7 jit_solution(9374311525950108726)
XLA Ops:
  9.6 2.6 all-reduce.2
  13.8 6.9 collective-permute-start
  20.7 56.5 %collective-permute-done = bf16[2,256,2560]{2,1,0:T(8,128)(2,1)} collective-permute-done((bf16[2,256,2560]{2,1,0:T(8,128)(2,1)S(1)}, bf16[2,256,2560]{2,1,0:T(8,128)(2,1)}, u32[]{:S(2)}, u32[]{:S(2)}) %collective-permute-start) | collective-permute-done | bytes 2621472 | tf_op jit(solution)/shard_map/ppermute | solution.py:18
  78.7 61.3 %collective-permute-done.1 = bf16[2,256,2560]{2,1,0:T(8,128)(2,1)} collective-permute-done((bf16[2,256,2560]{2,1,0:T(8,128)(2,1)}, bf16[2,256,2560]{2,1,0:T(8,128)(2,1)}, u32[]{:S(2)}, u32[]{:S(2)}) %collective-permute-start.1) | collective-permute-done | bytes 2621472 | tf_op jit(solution)/shard_map/ppermute | solution.py:18
  140.0 2.1 gather_fusion.2
  142.1 2.1 gather_fusion.1
  145.9 3.5 reshape.219
  149.4 2.8 copy.70
  152.2 78.6 %all_gather.3 = bf16[2,32,2560]{2,0,1:T(2,128)(2,1)S(1)} all-gather(bf16[2,2,2560]{2,0,1:T(2,128)(2,1)S(1)} %copy.64), channel_id=1, replica_groups=mesh['ctx'=16,'head'=2] {'ctx'}, dimensions={1}, use_global_device_ids=true | all-gather | bytes 348160 | tf_op jit(solution)/shard_map/all_gather | solution.py:47
  238.1 3.5 slice_bitcast_fusion.2
  241.7 13.1 %gather_fusion = bf16[1024,2560]{1,0:T(8,128)(2,1)} fusion(bf16[768,2560]{1,0:T(8,128)(2,1)} %get-tuple-element.202, s32[1024]{0:T(1024)S(1)} %get-tuple-element.210), kind=kCustom, calls=%fused_computation | custom fusion | bytes 10489856 | tf_op jit(solution)/shard_map/gather | solution.py:65
  254.7 10.0 reshape.218
  264.7 6.4 copy.68
  271.1 13.1 %gather_fusion.3 = bf16[1024,2560]{1,0:T(8,128)(2,1)} fusion(bf16[768,2560]{1,0:T(8,128)(2,1)} %get-tuple-element.201, s32[1024]{0:T(1024)S(1)} %get-tuple-element.210), kind=kCustom, calls=%fused_computation.3 | custom fusion | bytes 10489856 | tf_op jit(solution)/shard_map/gather | solution.py:68
  284.1 10.0 reshape.220
  294.1 6.4 copy.71
  300.5 331.9 %while.19 = (s32[]{:T(128)}, f32[20,2,128,128]{3,2,1,0:T(8,128)}, f32[20,2,512,128]{3,2,1,0:T(8,128)}, f32[20,2,512,128]{3,2,1,0:T(8,128)}, f32[20,32,128]{2,1,0...) while((s32[]{:T(128)}, f32[20,2,128,128]{3,2,1,0:T(8,128)}, ...), condition=%wide.region_9.10_spmd.clone, body=%wide.region_4.9_spmd.clone.sunk | while | flops 216235520 | bytes 9030503 | solution.py:143
  312.0 1.9 fusion.155
  378.4 1.9 fusion.155
  395.0 2.0 fusion.155
  544.3 1.9 fusion.155
  560.9 1.9 fusion.155
  594.2 1.9 fusion.155
  632.4 16.1 %copy.74 = f32[2,512,20,128]{1,0,3,2:T(2,128)} copy(f32[2,512,20,128]{3,1,0,2:T(8,128)} %bitcast.206) | data formatting | bytes 20971520 | tf_op jit(solution)/shard_map/transpose | solution.py:145
  648.5 14.4 %stack_reshape.12 = f32[1,1024,2560]{1,2,0:T(8,128)} reshape(f32[2,512,20,128]{1,0,3,2:T(2,128)} %copy.74) | data formatting | bytes 20971520 | tf_op jit(solution)/shard_map/stack;reshape | solution.py:151
  662.9 16.1 %copy.75 = f32[2,512,20,128]{1,0,3,2:T(2,128)} copy(f32[2,512,20,128]{3,1,0,2:T(8,128)} %bitcast.207) | data formatting | bytes 20971520 | tf_op jit(solution)/shard_map/transpose | solution.py:146
  678.9 14.4 %stack_reshape.13 = f32[1,1024,2560]{1,2,0:T(8,128)} reshape(f32[2,512,20,128]{1,0,3,2:T(2,128)} %copy.75) | data formatting | bytes 20971520 | tf_op jit(solution)/shard_map/stack;reshape | solution.py:151
  693.3 16.5 %maximum_bitcast_fusion = f32[1024,2,2560]{0,2,1:T(8,128)} fusion(f32[1,1024,2560]{1,2,0:T(8,128)} %stack_reshape.13, f32[1,1024,2560]{1,2,0:T(8,128)} %stack_reshape.12), kind=kLoop, calls=%fused_computation.84 | loop fusion | flops 5242880 | bytes 41943040 | tf_op jit(solution)/shard_map/stack | solution.py:151
  709.8 31.4 %copy.76 = f32[1024,2,2560]{2,1,0:T(2,128)} copy(f32[1024,2,2560]{0,2,1:T(8,128)} %maximum_bitcast_fusion) | data formatting | bytes 41943040 | tf_op jit(solution)/shard_map/stack | solution.py:151
  741.2 5.8 broadcast_in_dim.59
  747.0 170.0 %scatter_fusion = f32[2,768,2560]{2,0,1:T(2,128)} fusion(f32[2,768,2560]{2,0,1:T(2,128)} %broadcast_in_dim.59, s32[1024]{0:T(1024)S(1)} %bitcast.215, f32[1024,2,2560]{2,1,0:T(2,128)} %copy.76), kind=kCustom, calls=%fused_computation.4 | custom fusion | flops 5242880 | bytes 62918656 | tf_op jit(solution)/shard_map/scatter-add | solution.py:150
  916.9 4.3 fusion.82
  921.2 2.4 collective-permute-start.3
  923.6 51.9 %collective-permute-done.3 = bf16[2,256,2560]{2,0,1:T(2,128)(2,1)S(1)} collective-permute-done((bf16[2,256,2560]{2,0,1:T(2,128)(2,1)S(1)}, bf16[2,256,2560]{2,0,1:T(2,128)(2,1)S(1)}, u32[]{:S(2)}, u32[]{:S(2)}) %collective-permute-start.3) | collective-permute-done | bytes 2621472 | tf_op jit(solution)/shard_map/ppermute | solution.py:18
  975.5 5.2 fusion.67
  980.7 103.6 %collective-permute-done.4 = bf16[2,256,2560]{2,0,1:T(2,128)(2,1)S(1)} collective-permute-done((bf16[2,256,2560]{2,0,1:T(2,128)(2,1)S(1)}, bf16[2,256,2560]{2,0,1:T(2,128)(2,1)S(1)}, u32[]{:S(2)}, u32[]{:S(2)}) %collective-permute-start.4) | collective-permute-done | bytes 2621472 | tf_op jit(solution)/shard_map/ppermute | solution.py:18
  1084.4 6.7 fusion.65
  1093.7 5.4 copy.73
  1099.1 2.2 fusion.74
  1101.3 117.1 %all-reduce.5.cloned.1.call-done = f32[2,32,2560]{2,1,0:T(8,128)} async-done(((f32[2,32,2560]{2,1,0:T(8,128)}), f32[2,32,2560]{2,1,0:T(8,128)}) %all-reduce.5.cloned.1.call-update) | async-done | bytes 655376
  1219.4 5.8 convert_element_type.66
  1225.2 2.0 scatter_fusion.1
  1227.2 4.4 slice.77
  1231.6 4.2 slice.113
  1236.3 2.5 all-reduce.1
  1238.8 3.4 fusion.73
  1242.2 2.4 copy.81
  1244.6 3.1 copy.120
  (546 shorter events, 300.1 us)
Async XLA Ops:
  7.2 2.1 copy-start
  7.2 5.6 copy-start.6
  7.2 1211.2 %all-reduce.5.cloned.1.call-start = ((), (), s32[]{:S(2)}) async-start(), calls=%async_computation | async-start | bytes 1310720
  12.2 1.3 copy-start.5
  12.8 64.5 %copy-start.9 = (f32[256]{0:T(256)}, f32[256]{0:T(256)S(1)}, u32[]{:S(2)}) copy-start(f32[256]{0:T(256)S(1)} %get-tuple-element.204) | copy-start | bytes 3076
  12.8 131.4 %copy-start.11 = (f32[256]{0:T(256)}, f32[256]{0:T(256)S(1)}, u32[]{:S(2)}) copy-start(f32[256]{0:T(256)S(1)} %get-tuple-element.207) | copy-start | bytes 3076
  13.5 63.6 %copy-start.15 = (s32[2,4]{1,0:T(2,128)S(1)}, s32[2,4]{1,0:T(2,128)}, u32[]{:S(2)}) copy-start(s32[2,4]{1,0:T(2,128)} %param.17) | copy-start | bytes 100
  13.5 63.7 %copy-start.16 = (s32[2]{0:T(128)S(1)}, s32[2]{0:T(128)}, u32[]{:S(2)}) copy-start(s32[2]{0:T(128)} %param.18) | copy-start | bytes 28
  13.8 130.5 %copy-start.8 = (f32[2560]{0:T(1024)S(1)}, f32[2560]{0:T(1024)}, u32[]{:S(2)}) copy-start(f32[2560]{0:T(1024)} %param.15) | copy-start | bytes 30724
  13.8 63.3 %collective-permute-start = (bf16[2,256,2560]{2,1,0:T(8,128)(2,1)S(1)}, bf16[2,256,2560]{2,1,0:T(8,128)(2,1)}, u32[]{:S(2)}, u32[]{:S(2)}) collective-permute-start(bf16[2,256,2560]{2,1,0:T(8,128)(2,1)S(1)} %pad_maximum_fusion.1), channel_id=1, source_target_pairs={{0,30},{2,0},{4,2},{6,4},{8,6},{10,8},{12,10},{14,12},{16,14},{18,... | collective-permute-start | bytes 7864328 | tf_op jit(solution)/shard_map/ppermute | solution.py:18
  77.1 62.9 %collective-permute-start.1 = (bf16[2,256,2560]{2,1,0:T(8,128)(2,1)}, bf16[2,256,2560]{2,1,0:T(8,128)(2,1)}, u32[]{:S(2)}, u32[]{:S(2)}) collective-permute-start(bf16[2,256,2560]{2,1,0:T(8,128)(2,1)} %collective-permute-done), channel_id=1, source_target_pairs={{0,2},{2,4},{4,6},{6,8},{8,10},{10,12},{12,14},{14,16},{16,18},{18... | collective-permute-start | bytes 7864328 | tf_op jit(solution)/shard_map/ppermute | solution.py:18
  140.0 92.4 %collective-permute-start.2 = (bf16[2,256,2560]{2,1,0:T(8,128)(2,1)}, bf16[2,256,2560]{2,1,0:T(8,128)(2,1)}, u32[]{:S(2)}, u32[]{:S(2)}) collective-permute-start(bf16[2,256,2560]{2,1,0:T(8,128)(2,1)} %collective-permute-done.1), channel_id=1, source_target_pairs={{0,2},{2,4},{4,6},{6,8},{8,10},{10,12},{12,14},{14,16},{16,18},{18... | collective-permute-start | bytes 7864328 | tf_op jit(solution)/shard_map/ppermute | solution.py:18
  149.4 82.8 %copy-start.17 = (s32[1,16]{1,0:T(1,128)S(1)}, s32[1,16]{1,0:T(1,128)}, u32[]{:S(2)}) copy-start(s32[1,16]{1,0:T(1,128)} %param.19) | copy-start | bytes 196
  921.2 54.2 %collective-permute-start.3 = (bf16[2,256,2560]{2,0,1:T(2,128)(2,1)S(1)}, bf16[2,256,2560]{2,0,1:T(2,128)(2,1)S(1)}, u32[]{:S(2)}, u32[]{:S(2)}) collective-permute-start(bf16[2,256,2560]{2,0,1:T(2,128)(2,1)S(1)} %fusion.82), channel_id=1, source_target_pairs={{0,2},{2,4},{4,6},{6,8},{8,10},{10,12},{12,14},{14,16},{16,18},{18... | collective-permute-start | bytes 7864328 | tf_op jit(solution)/shard_map/ppermute | solution.py:18
  980.7 103.7 %collective-permute-start.4 = (bf16[2,256,2560]{2,0,1:T(2,128)(2,1)S(1)}, bf16[2,256,2560]{2,0,1:T(2,128)(2,1)S(1)}, u32[]{:S(2)}, u32[]{:S(2)}) collective-permute-start(bf16[2,256,2560]{2,0,1:T(2,128)(2,1)S(1)} %fusion.67), channel_id=1, source_target_pairs={{0,2},{2,4},{4,6},{6,8},{8,10},{10,12},{12,14},{14,16},{16,18},{18... | collective-permute-start | bytes 7864328 | tf_op jit(solution)/shard_map/ppermute | solution.py:18
  1091.0 1.4 copy-start.18
  1091.0 128.3 %collective-permute-start.5 = (bf16[2,256,2560]{2,0,1:T(2,128)(2,1)}, bf16[2,256,2560]{2,0,1:T(2,128)(2,1)}, u32[]{:S(2)}, u32[]{:S(2)}) collective-permute-start(bf16[2,256,2560]{2,0,1:T(2,128)(2,1)} %fusion.65), channel_id=1, source_target_pairs={{0,30},{2,0},{4,2},{6,4},{8,6},{10,8},{12,10},{14,12},{16,14},{18,... | collective-permute-start | bytes 7864328 | tf_op jit(solution)/shard_map/ppermute | solution.py:18
  1227.2 4.4 copy-start.4
  1231.6 4.3 copy-start.2
  1231.6 4.3 copy-start.1
  1231.6 4.2 copy-start.7
  1235.9 2.9 copy-start.12
  1235.9 2.9 copy-start.14
  1244.6 3.1 copy-start.3
  1244.6 3.1 copy-start.10
  1244.6 3.1 copy-start.13
Sparse Core Ops, SparseCore 0:
  1092.6 125.7 all-reduce.4
where the time goes:
time: 1270 us; the launch traced here: 1260 us
  waiting for transfers between devices  390 us (31%)
  other arithmetic  251 us (20%)
  local copies, waits for them, and re-layouts  244 us (19%)
  matrix products  223 us (18%)
  blocking collectives  83.7 us (7%)
  loops' own time  39.9 us (3%)
  between operations  15.5 us (1%)
    ppermute x6, waiting for transfers between devices, passed_along(): lax.ppermute(shard, axis, [(i, (i + by) % count) for i in range(count)])  273 us
    scatter-add x1, other arithmetic, body(): window_grads.at[:, window_rows.reshape(-1)]  170 us
    unnamed x2, waiting for transfers between devices  117 us
    all_gather x1, blocking collectives, body(): global_pair = lax.all_gather(own_pair, 'ctx', axis=1, tiled=True)  78.6 us
    another operation x3, local copies, waits for them, and re-layouts, body(): jnp.stack([window_dk, window_dv])  60.1 us
    another operation x1, loops' own time, body(): head_results = lax.map(head_block, jnp.arange(heads_here, dtype=jnp.int32))  39.9 us
    dot_general x20, matrix products, head_block(): jnp.einsum('tqk,tqd->tkd', probs_low[..., :window_count], grad_head, pref...  38.5 us
    dot_general x20, matrix products, head_block(): jnp.einsum('tqk,tkd->tqd', dscore[..., :window_count], wkeys, preferred_e...  36.5 us
  transfers between devices with their start and end apart: 7, of which 5 were waited for; matrix products, arithmetic and copies ran while one was open for 2% of the time, Pallas kernels for 0%

commit v1 on v0

--- a/solution.py
+++ b/solution.py
@@ -1,6 +1,10 @@
+import functools
+
 import jax
 import jax.numpy as jnp
 from jax import lax
+from jax.experimental import pallas as pl
+from jax.experimental.pallas import tpu as pltpu
 from jax.sharding import PartitionSpec as P
 
 HEAD_DIM = 128
@@ -8,9 +12,513 @@
 TILE = 128
 REACH = 1
 G_DEV = 2
+GROUP = 4
+CHUNKS = (2, 2, 1)
 
 
 EPSILON = 1e-06
+FACTOR = HEAD_DIM ** (-0.5)
+F32 = jnp.float32
+BF16 = jnp.bfloat16
+VMEM_LIMIT = 48 * 1024 * 1024
+
+
+def swapped(shard, bit):
+    count = lax.axis_size("ctx")
+    return lax.ppermute(shard, "ctx", [(i, i ^ bit) for i in range(count)])
+
+
+def params():
+    return pltpu.CompilerParams(vmem_limit_bytes=VMEM_LIMIT)
+
+
+def cost(flops, read):
+    return pl.CostEstimate(flops=int(flops), bytes_accessed=int(read), transcendentals=0)
+
+
+def contract(a, b, dims, precision=None):
+    return lax.dot_general(
+        a, b, (dims, ((), ())), precision=precision, preferred_element_type=F32
+    )
+
+
+def lane_pair(first, second, rows):
+    lane = lax.broadcasted_iota(jnp.int32, (rows, HEAD_DIM), 1)
+    return jnp.where(lane < HEAD_DIM // 2, first, second)
+
+
+def squares_kernel(query_ref, key_ref, out_ref):
+    step = pl.program_id(0)
+    query = query_ref[...].astype(F32)
+    key = key_ref[...].astype(F32)
+    part = lane_pair(
+        jnp.sum(query * query, axis=1, keepdims=True),
+        jnp.sum(key * key, axis=1, keepdims=True),
+        query.shape[0],
+    )
+
+    @pl.when(step == 0)
+    def _():
+        out_ref[...] = part
+
+    @pl.when(step > 0)
+    def _():
+        out_ref[...] += part
+
+
+def squares(query_raw, key_raw):
+    rows, width = query_raw.shape
+    block = width // 4
+    return pl.pallas_call(
+        squares_kernel,
+        out_shape=jax.ShapeDtypeStruct((rows, HEAD_DIM), F32),
+        grid=(4,),
+        in_specs=[pl.BlockSpec((rows, block), lambda i: (0, i))] * 2,
+        out_specs=pl.BlockSpec((rows, HEAD_DIM), lambda i: (0, 0)),
+        compiler_params=params(),
+        cost_estimate=cost(4 * rows * width, 4 * rows * width),
+        name="squares",
+    )(query_raw, key_raw)
+
+
+def inverses(own, other):
+    both = lax.rsqrt((own + other) / D + EPSILON)
+    return both[:, :1], both[:, HEAD_DIM // 2 : HEAD_DIM // 2 + 1]
+
+
+def pack_kernel(place_ref, tiles_ref, ids_ref, readers_ref, own_ref, other_ref, *refs):
+    per = 6
+    me, plane = place_ref[0], place_ref[1]
+    query_inv, key_inv = inverses(own_ref[...], other_ref[...])
+    rows = own_ref.shape[0]
+    row = lax.broadcasted_iota(jnp.int32, (16, HEAD_DIM), 0)
+    lane = lax.broadcasted_iota(jnp.int32, (16, HEAD_DIM), 1)
+    facts = jnp.full((16, HEAD_DIM), -1, jnp.int32)
+    device = plane * GROUP + me
+    for r in range(G_DEV):
+        facts = jnp.where(row == me * G_DEV + r, ids_ref[r] - device * rows, facts)
+    for tile in range(rows // TILE):
+        start = tiles_ref[tile, 0] - (plane * GROUP - 1) * (rows // TILE)
+        facts = jnp.where(row == 9 + tile, start, facts)
+    for e in range(GROUP):
+        for j in range(GROUP):
+            live = readers_ref[0, (plane ^ e) * GROUP + j]
+            chosen = (row == 8) & (lane // G_DEV == GROUP * e + j)
+            facts = jnp.where(chosen, live, facts)
+    facts = facts.astype(F32).astype(BF16)
+    for d in range(GROUP):
+        key, value, query, grad, key_gain, query_gain = refs[per * d : per * d + per]
+        out = refs[per * GROUP + d]
+        out[0:rows] = (key[...].astype(F32) * key_inv * key_gain[...]).astype(BF16)
+        out[rows : 2 * rows] = value[...]
+        out[2 * rows : 3 * rows] = (
+            query[...].astype(F32) * query_inv * query_gain[...]
+        ).astype(BF16)
+        out[3 * rows : 4 * rows] = grad[...]
+        out[4 * rows :] = facts
+
+
+def pack(place, tiles, ids, readers, own, other, arrays, gains, first, count):
+    query_raw, key_raw, values, out_grad = arrays
+    query_gain, key_gain = gains
+    rows, width = query_raw.shape
+    each = width // HEAD_DIM // GROUP
+    smem = pl.BlockSpec(memory_space=pltpu.SMEM)
+    whole = pl.BlockSpec((rows, HEAD_DIM), lambda h, place: (0, 0))
+    specs, operands = [], []
+    for d in range(GROUP):
+        at = lambda h, place, d=d: (0, (place[0] ^ d) * each + first + h)
+        specs += [pl.BlockSpec((rows, HEAD_DIM), at)] * 4 + [pl.BlockSpec((1, HEAD_DIM), at)] * 2
+        operands += [key_raw, values, query_raw, out_grad, key_gain, query_gain]
+    out_rows = 4 * rows + 16
+    return pl.pallas_call(
+        pack_kernel,
+        out_shape=[jax.ShapeDtypeStruct((out_rows, count * HEAD_DIM), BF16)] * GROUP,
+        grid_spec=pltpu.PrefetchScalarGridSpec(
+            num_scalar_prefetch=1,
+            grid=(count,),
+            in_specs=[smem, smem, smem, whole, whole] + specs,
+            out_specs=[pl.BlockSpec((out_rows, HEAD_DIM), lambda h, place: (0, h))] * GROUP,
+        ),
+        compiler_params=params(),
+        cost_estimate=cost(1, 4 * out_rows * count * HEAD_DIM * 4),
+        name="pack",
+    )(place, tiles, ids, readers, own, other, *operands)
+
+
+def edges_kernel(place_ref, b0, b1, b2, b3, near_ref, far_ref, own_ref):
+    me, plane = place_ref[0], place_ref[1]
+    rows = (b0.shape[0] - 16) // 4
+    total = jnp.zeros((16, HEAD_DIM), F32)
+    lane = lax.broadcasted_iota(jnp.int32, (8, HEAD_DIM), 1)
+    for block in (b0, b1, b2, b3):
+        facts = block[4 * rows :].astype(F32)[:8].astype(jnp.int32)
+        hot = jnp.concatenate([facts == lane, facts == lane + HEAD_DIM], axis=1)
+        hot = hot.astype(F32).astype(BF16)
+        total = total + jnp.concatenate(
+            [
+                contract(hot, block[0:rows], ((1,), (0,))),
+                contract(hot, block[rows : 2 * rows], ((1,), (0,))),
+            ],
+            axis=0,
+        )
+    total = total.astype(BF16)
+    own_ref[...] = total
+    near_ref[2 * rows :] = total
+    far_ref[2 * rows :] = total
+    even = plane % 2 == 0
+    last, first = me ^ (GROUP - 1), me
+    for d, block in enumerate((b0, b1, b2, b3)):
+
+        @pl.when(jnp.where(even, last, first) == d)
+        def _(block=block):
+            near_ref[: 2 * rows] = block[: 2 * rows]
+
+        @pl.when(jnp.where(even, first, last) == d)
+        def _(block=block):
+            far_ref[: 2 * rows] = block[: 2 * rows]
+
+
+def edges(place, blocks):
+    out_rows, width = blocks[0].shape
+    rows = (out_rows - 16) // 4
+    at = lambda h, place: (0, h)
+    return pl.pallas_call(
+        edges_kernel,
+        out_shape=[
+            jax.ShapeDtypeStruct((2 * rows + 16, width), BF16),
+            jax.ShapeDtypeStruct((2 * rows + 16, width), BF16),
+            jax.ShapeDtypeStruct((16, width), BF16),
+        ],
+        grid_spec=pltpu.PrefetchScalarGridSpec(
+            num_scalar_prefetch=1,
+            grid=(width // HEAD_DIM,),
+            in_specs=[pl.BlockSpec((out_rows, HEAD_DIM), at)] * GROUP,
+            out_specs=[
+                pl.BlockSpec((2 * rows + 16, HEAD_DIM), at),
+                pl.BlockSpec((2 * rows + 16, HEAD_DIM), at),
+                pl.BlockSpec((16, HEAD_DIM), at),
+            ],
+        ),
+        compiler_params=params(),
+        cost_estimate=cost(1, 4 * out_rows * width * 2),
+        name="edges",
+    )(place, *blocks)
+
+
+def attend_kernel(
+    place_ref, b0, b1, b2, b3, own_g, near, far, mid,
+    q0, q1, q2, q3, a0, a1, a2, a3, near_out, far_out, mid_out, own_out,
+    pair, weights, sums, pair_g, sums_g,
+):
+    me, plane = place_ref[0], place_ref[1]
+    rows = (b0.shape[0] - 16) // 4
+    keys = slice(0, HEAD_DIM)
+    vals = slice(HEAD_DIM, 2 * HEAD_DIM)
+    blocks = (b0, b1, b2, b3)
+    for d, block in enumerate(blocks):
+        at = pl.multiple_of(((me ^ d) + 1) * rows, TILE)
+        pair[pl.ds(at, rows), keys] = block[0:rows]
+        pair[pl.ds(at, rows), vals] = block[rows : 2 * rows]
+    even = plane % 2 == 0
+    top = (GROUP + 1) * rows
+    near_at = pl.multiple_of(jnp.where(even, top, 0), TILE)
+    far_at = pl.multiple_of(jnp.where(even, 0, top), TILE)
+    for ref, at in ((near, near_at), (far, far_at)):
+        pair[pl.ds(at, rows), keys] = ref[0:rows]
+        pair[pl.ds(at, rows), vals] = ref[rows : 2 * rows]
+    globals_in = [
+        own_g[...].astype(F32),
+        near[2 * rows :].astype(F32),
+        mid[...].astype(F32),
+        far[2 * rows :].astype(F32),
+    ]
+    pair_g[:, keys] = jnp.concatenate([x[:8] for x in globals_in], axis=0).astype(BF16)
+    pair_g[:, vals] = jnp.concatenate([x[8:] for x in globals_in], axis=0).astype(BF16)
+    sums[...] = jnp.zeros_like(sums)
+    sums_g[...] = jnp.zeros_like(sums_g)
+    weights[...] = jnp.zeros_like(weights)
+    count_g = pair_g.shape[0]
+    row = lax.broadcasted_iota(jnp.int32, (count_g, HEAD_DIM), 0)
+    lane = lax.broadcasted_iota(jnp.int32, (count_g, HEAD_DIM), 1)
+    span = 4 * TILE
+    for d, (block, q_out) in enumerate(zip(blocks, (q0, q1, q2, q3))):
+        facts = block[4 * rows :].astype(F32)
+        live = jnp.sum(jnp.where(row == lane, facts[8:9], 0.0), axis=1, keepdims=True) > 0.0
+        for tile in range(rows // TILE):
+            start = jnp.max(facts[9 + tile : 10 + tile]).astype(jnp.int32)
+            at = pl.multiple_of(start * TILE, TILE)
+            here = slice(2 * rows + tile * TILE, 2 * rows + (tile + 1) * TILE)
+            there = slice(3 * rows + tile * TILE, 3 * rows + (tile + 1) * TILE)
+            weights[:TILE, keys] = block[here]
+            weights[TILE:, vals] = block[there]
+            w = weights[...]
+            both = jnp.concatenate([pair[pl.ds(at, span)], pair_g[...]], axis=0)
+            product = contract(both, w, ((1,), (1,)))
+            score = product[:, :TILE] * FACTOR
+            dprob = product[:, TILE:]
+            score_g = jnp.where(live, score[span:], -jnp.inf)
+            score = jnp.concatenate([score[:span], score_g], axis=0)
+            largest = jnp.max(score, axis=0, keepdims=True)
+            probs = jnp.exp(score - largest)
+            probs = probs * (1.0 / jnp.sum(probs, axis=0, keepdims=True))
+            delta = jnp.sum(probs * dprob, axis=0, keepdims=True)
+            dscore = (probs * (dprob - delta) * FACTOR).astype(BF16)
+            grads = contract(
+                jnp.concatenate([dscore, probs.astype(BF16)], axis=1), w, ((1,), (0,))
+            )
+            sums[pl.ds(at, span)] += grads[:span]
+            sums_g[...] += grads[span:]
+            grad_query = contract(dscore, both[:, keys], ((0,), (0,)))
+            q_out[tile * TILE : (tile + 1) * TILE] = grad_query.astype(BF16)
+    for d, out in enumerate((a0, a1, a2, a3)):
+        at = pl.multiple_of(((me ^ d) + 1) * rows, TILE)
+        out[0] = sums[pl.ds(at, rows), keys]
+        out[1] = sums[pl.ds(at, rows), vals]
+    global_rows = [
+        jnp.concatenate(
+            [sums_g[8 * e : 8 * e + 8, keys], sums_g[8 * e : 8 * e + 8, vals]], axis=0
+        )
+        for e in range(GROUP)
+    ]
+    own_out[...] = global_rows[0]
+    mid_out[...] = global_rows[2].astype(BF16)
+    for out, at, part in (
+        (near_out, near_at, global_rows[1]),
+        (far_out, far_at, global_rows[3]),
+    ):
+        out[:rows] = sums[pl.ds(at, rows), keys].astype(BF16)
+        out[rows : 2 * rows] = sums[pl.ds(at, rows), vals].astype(BF16)
+        out[2 * rows :] = part.astype(BF16)
+
+
+def attend(place, blocks, own_g, near, far, mid):
+    out_rows, width = blocks[0].shape
+    rows = (out_rows - 16) // 4
+    count = width // HEAD_DIM
+    at = lambda h, place: (0, h)
+    deep = lambda h, place: (0, 0, h)
+    tall = pl.BlockSpec((out_rows, HEAD_DIM), at)
+    edge = pl.BlockSpec((2 * rows + 16, HEAD_DIM), at)
+    few = pl.BlockSpec((16, HEAD_DIM), at)
+    return pl.pallas_call(
+        attend_kernel,
+        out_shape=[jax.ShapeDtypeStruct((rows, width), BF16)] * GROUP
+        + [jax.ShapeDtypeStruct((2, rows, width), F32)] * GROUP
+        + [jax.ShapeDtypeStruct((2 * rows + 16, width), BF16)] * 2
+        + [jax.ShapeDtypeStruct((16, width), BF16), jax.ShapeDtypeStruct((16, width), F32)],
+        grid_spec=pltpu.PrefetchScalarGridSpec(
+            num_scalar_prefetch=1,
+            grid=(count,),
+            in_specs=[tall] * GROUP + [few, edge, edge, few],
+            out_specs=[pl.BlockSpec((rows, HEAD_DIM), at)] * GROUP
+            + [pl.BlockSpec((2, rows, HEAD_DIM), deep)] * GROUP
+            + [edge, edge, few, few],
+            scratch_shapes=[
+                pltpu.VMEM(((GROUP + 2) * rows, 2 * HEAD_DIM), BF16),
+                pltpu.VMEM((2 * TILE, 2 * HEAD_DIM), BF16),
+                pltpu.VMEM(((GROUP + 2) * rows, 2 * HEAD_DIM), F32),
+                pltpu.VMEM((8 * GROUP, 2 * HEAD_DIM), BF16),
+                pltpu.VMEM((8 * GROUP, 2 * HEAD_DIM), F32),
+            ],
+        ),
+        compiler_params=params(),
+        cost_estimate=cost(count * 5e9, 4 * out_rows * width * 4),
+        name="attend",
+    )(place, *blocks, own_g, near, far, mid)
+
+
+def settle_kernel(
+    place_ref, f0, f1, f2, f3, q0, q1, q2, q3, a0, a1, a2, a3, own_g, near, far, mid,
+    o0, o1, o2, o3,
+):
+    me, plane = place_ref[0], place_ref[1]
+    rows = q0.shape[0]
+    even = plane % 2 == 0
+    part = (
+        own_g[...]
+        + near[2 * rows :].astype(F32)
+        + mid[...].astype(F32)
+        + far[2 * rows :].astype(F32)
+    )
+    inner = (plane == 1) | (plane == 2)
+    lane = lax.broadcasted_iota(jnp.int32, (8, HEAD_DIM), 1)
+    for d, (fact, dq, acc, out) in enumerate(
+        zip((f0, f1, f2, f3), (q0, q1, q2, q3), (a0, a1, a2, a3), (o0, o1, o2, o3))
+    ):
+        j = me ^ d
+        facts = fact[...].astype(F32)[:8].astype(jnp.int32)
+        hot = jnp.concatenate([facts == lane, facts == lane + HEAD_DIM], axis=1).astype(F32)
+        near_here = j == jnp.where(even, GROUP - 1, 0)
+        far_here = (j == jnp.where(even, 0, GROUP - 1)) & inner
+        out[:rows] = dq[...]
+        for i in range(2):
+            total = acc[i] + contract(
+                hot, part[8 * i : 8 * i + 8], ((0,), (0,)), lax.Precision.HIGHEST
+            )
+            rest = slice(i * rows, (i + 1) * rows)
+            total = total + jnp.where(near_here, near[rest].astype(F32), 0.0)
+            total = total + jnp.where(far_here, far[rest].astype(F32), 0.0)
+            out[(i + 1) * rows : (i + 2) * rows] = total.astype(BF16)
+
+
+def settle(place, blocks, dqs, accs, own_g, near, far, mid):
+    rows, width = dqs[0].shape
+    at = lambda h, place: (0, h)
+    deep = lambda h, place: (0, 0, h)
+    edge = pl.BlockSpec((2 * rows + 16, HEAD_DIM), at)
+    few = pl.BlockSpec((16, HEAD_DIM), at)
+    facts = pl.BlockSpec((16, HEAD_DIM), lambda h, place: (4 * rows // 16, h))
+    return pl.pallas_call(
+        settle_kernel,
+        out_shape=[jax.ShapeDtypeStruct((3 * rows, width), BF16)] * GROUP,
+        grid_spec=pltpu.PrefetchScalarGridSpec(
+            num_scalar_prefetch=1,
+            grid=(width // HEAD_DIM,),
+            in_specs=[facts] * GROUP
+            + [pl.BlockSpec((rows, HEAD_DIM), at)] * GROUP
+            + [pl.BlockSpec((2, rows, HEAD_DIM), deep)] * GROUP
+            + [few, edge, edge, few],
+            out_specs=[pl.BlockSpec((3 * rows, HEAD_DIM), at)] * GROUP,
+        ),
+        compiler_params=params(),
+        cost_estimate=cost(1, 16 * rows * width * 4),
+        name="settle",
+    )(place, *blocks, *dqs, *accs, own_g, near, far, mid)
+
+
+def dots_kernel(place_ref, *refs):
+    out_ref = refs[-1]
+    rows = out_ref.shape[0]
+    step = pl.program_id(0)
+    totals = [jnp.zeros((rows, HEAD_DIM), F32), jnp.zeros((rows, HEAD_DIM), F32)]
+    for d in range(GROUP):
+        grads, query, key, query_gain, key_gain = refs[5 * d : 5 * d + 5]
+        totals[0] += grads[:rows].astype(F32) * query_gain[...] * query[...].astype(F32)
+        totals[1] += grads[rows:].astype(F32) * key_gain[...] * key[...].astype(F32)
+    part = lane_pair(
+        jnp.sum(totals[0], axis=1, keepdims=True), jnp.sum(totals[1], axis=1, keepdims=True), rows
+    )
+
+    @pl.when(step == 0)
+    def _():
+        out_ref[...] = part
+
+    @pl.when(step > 0)
+    def _():
+        out_ref[...] += part
+
+
+def dots(place, grads, query_raw, key_raw, gains, first):
+    rows, full = query_raw.shape
+    count = grads[0].shape[1] // HEAD_DIM
+    each = full // HEAD_DIM // GROUP
+    specs, operands = [], []
+    for d in range(GROUP):
+        at = lambda h, place, d=d: (0, (place[0] ^ d) * each + first + h)
+        specs += (
+            [pl.BlockSpec((2 * rows, HEAD_DIM), lambda h, place: (0, h))]
+            + [pl.BlockSpec((rows, HEAD_DIM), at)] * 2
+            + [pl.BlockSpec((1, HEAD_DIM), at)] * 2
+        )
+        operands += [grads[d], query_raw, key_raw, gains[0], gains[1]]
+    return pl.pallas_call(
+        dots_kernel,
+        out_shape=jax.ShapeDtypeStruct((rows, HEAD_DIM), F32),
+        grid_spec=pltpu.PrefetchScalarGridSpec(
+            num_scalar_prefetch=1,
+            grid=(count,),
+            in_specs=specs,
+            out_specs=pl.BlockSpec((rows, HEAD_DIM), lambda h, place: (0, 0)),
+        ),
+        compiler_params=params(),
+        cost_estimate=cost(1, 16 * rows * count * HEAD_DIM * 2),
+        name="dots",
+    )(place, *operands)
+
+
+def finish_kernel(chunks, place_ref, own_ref, other_ref, dot_ref, dot_other_ref, *refs):
+    me = place_ref[0]
+    grads = refs[: GROUP * len(chunks)]
+    query_ref, key_ref, query_gain, key_gain = refs[GROUP * len(chunks) : GROUP * len(chunks) + 4]
+    query_out, key_out, value_out = refs[GROUP * len(chunks) + 4 :]
+    rows, full = query_ref.shape
+    each = full // GROUP
+    inv = inverses(own_ref[...], other_ref[...])
+    total = dot_ref[...] + dot_other_ref[...]
+    dot = (total[:, :1], total[:, HEAD_DIM // 2 : HEAD_DIM // 2 + 1])
+    coeff = [inv[i] * inv[i] * inv[i] * (dot[i] / D) for i in range(2)]
+    for d in range(GROUP):
+        first = 0
+        for c, count in enumerate(chunks):
+            ref = grads[c * GROUP + d]
+            for h in range(count):
+                at = pl.multiple_of((me ^ d) * each + (first + h) * HEAD_DIM, HEAD_DIM)
+                here = pl.ds(at, HEAD_DIM)
+                col = slice(h * HEAD_DIM, (h + 1) * HEAD_DIM)
+                for i, (raw, gain, out) in enumerate(
+                    ((query_ref, query_gain, query_out), (key_ref, key_gain, key_out))
+                ):
+                    grad = ref[i * rows : (i + 1) * rows, col].astype(F32)
+                    out[:, here] = (
+                        inv[i] * (grad * gain[:, here]) - raw[:, here].astype(F32) * coeff[i]
+                    ).astype(BF16)
+                value_out[:, here] = ref[2 * rows :, col]
+            first += count
+
+
+def finish(place, own, other, dot, dot_other, grads, query_raw, key_raw, gains, chunks):
+    vmem = pl.BlockSpec(memory_space=pltpu.VMEM)
+    flat = [x for chunk in grads for x in chunk]
+    return pl.pallas_call(
+        functools.partial(finish_kernel, chunks),
+        out_shape=[jax.ShapeDtypeStruct(query_raw.shape, BF16)] * 3,
+        in_specs=[pl.BlockSpec(memory_space=pltpu.SMEM)] + [vmem] * (4 + len(flat) + 4),
+        out_specs=[vmem] * 3,
+        compiler_params=params(),
+        cost_estimate=cost(1, 16 * query_raw.size),
+        name="finish",
+    )(place, own, other, dot, dot_other, *flat, query_raw, key_raw, *gains)
+
+
+def swap_heads(x):
+    return lax.ppermute(x, "head", [(0, 1), (1, 0)])
+
+
+def plane_body(
+    query_raw, key_raw, values, out_grad, query_gain, key_gain, key_tiles, global_ids, readers
+):
+    device = lax.axis_index("ctx")
+    place = jnp.stack([device % GROUP, device // GROUP]).astype(jnp.int32)
+    gains = (query_gain[None, :], key_gain[None, :])
+    own = squares(query_raw, key_raw)
+    other = swap_heads(own)
+    arrays = (query_raw, key_raw, values, out_grad)
+    packed, first = [], 0
+    for count in CHUNKS:
+        sent = pack(
+            place, key_tiles, global_ids, readers, own, other, arrays, gains, first, count
+        )
+        packed.append([sent[0]] + [swapped(sent[d], d) for d in range(1, GROUP)])
+        first += count
+    homes, dot, first = [], None, 0
+    for count, blocks in zip(CHUNKS, packed):
+        near, far, own_g = edges(place, blocks)
+        near, far, mid = swapped(near, 4), swapped(far, 12), swapped(own_g, 8)
+        results = attend(place, blocks, own_g, near, far, mid)
+        dqs, accs = results[:GROUP], results[GROUP : 2 * GROUP]
+        near, far, mid, own_g = results[2 * GROUP :]
+        near, far, mid = swapped(near, 4), swapped(far, 12), swapped(mid, 8)
+        sent = settle(place, blocks, dqs, accs, own_g, near, far, mid)
+        home = [sent[0]] + [swapped(sent[d], d) for d in range(1, GROUP)]
+        part = dots(place, home, query_raw, key_raw, gains, first)
+        dot = part if dot is None else dot + part
+        homes.append(home)
+        first += count
+    dot_other = swap_heads(dot)
+    return tuple(
+        finish(place, own, other, dot, dot_other, homes, query_raw, key_raw, gains, CHUNKS)
+    )
 
 
 def passed_along(shard, axis, by):
@@ -174,8 +682,10 @@
 
 
 def solution(mesh):
+    sizes = dict(mesh.shape)
+    planes = sizes["ctx"] == GROUP * GROUP and sizes["head"] == 2
     return jax.shard_map(
-        body,
+        plane_body if planes else body,
         mesh=mesh,
         in_specs=(
             P("ctx", "head"),

time: 1270 us -> 185 us (0.15); the launches traced: 1260 us -> 185 us
  waiting for transfers between devices: 390 us -> 63.2 us
  other arithmetic: 251 us -> 0.1 us
  local copies, waits for them, and re-layouts: 244 us -> 2.71 us
  matrix products: 223 us -> 0 us
  blocking collectives: 83.7 us -> 0 us
  Pallas kernels: 0 us -> 63.1 us
  starting transfers between devices: 9.33 us -> 54.8 us
  loops' own time: 39.9 us -> 0 us
  between operations: 15.5 us -> 0.96 us
    dot_general x240 -> x0, matrix products: 223 us -> none  [the longest x20 38.5 us: head_block(): jnp.einsum('tqk,tqd->tkd', probs_low[..., :window_count], grad_head, pref...]
    ppermute x6 -> x38, waiting for transfers between devices: 273 us -> 63.2 us  [the longest x36 61 us: swapped(): return lax.ppermute(shard, 'ctx', [(i, i ^ bit) for i in range(count)])]
    scatter-add x2 -> x0, other arithmetic: 172 us -> none  [the longest x1 170 us: body(): window_grads.at[:, window_rows.reshape(-1)]]
    unnamed x2 -> x0, waiting for transfers between devices: 117 us -> none
    all_gather x1 -> x0, blocking collectives: 78.6 us -> none  [body(): global_pair = lax.all_gather(own_pair, 'ctx', axis=1, tiled=True)]
    pallas_call x0 -> x17, Pallas kernels: none -> 63.1 us  [the longest x3 31.6 us: attend(): pl.pallas_call(attend_kernel, out_shape=[jax.ShapeDtypeStruct((rows, widt...]
    another operation x6 -> x0, local copies, waits for them, and re-layouts: 60.2 us -> none  [the longest x3 60.1 us: body(): jnp.stack([window_dk, window_dv])]
    ppermute x6 -> x38, starting transfers between devices: 9.29 us -> 54.8 us  [the longest x36 54.2 us: swapped(): return lax.ppermute(shard, 'ctx', [(i, i ^ bit) for i in range(count)])]
  transfers between devices with their start and end apart: 7 -> 38, of which waited for: 5 -> 11; matrix products, arithmetic and copies ran while one was open for 2% -> 0% of each run, Pallas kernels for 0% -> 28%
where the time goes in v1:
time: 185 us
  waiting for transfers between devices  63.2 us (34%)
  Pallas kernels  63.1 us (34%)
  starting transfers between devices  54.8 us (30%)
  local copies, waits for them, and re-layouts  2.71 us (1%)
    ppermute x36, waiting for transfers between devices, swapped(): return lax.ppermute(shard, 'ctx', [(i, i ^ bit) for i in range(count)])  61 us
    ppermute x36, starting transfers between devices, swapped(): return lax.ppermute(shard, 'ctx', [(i, i ^ bit) for i in range(count)])  54.2 us
    pallas_call x3, Pallas kernels, attend(): pl.pallas_call(attend_kernel, out_shape=[jax.ShapeDtypeStruct((rows, widt...  31.6 us
    pallas_call x3, Pallas kernels, settle(): pl.pallas_call(settle_kernel, out_shape=[jax.ShapeDtypeStruct((3 * rows,...  9.73 us
    pallas_call x3, Pallas kernels, pack(): pl.pallas_call(pack_kernel, out_shape=[jax.ShapeDtypeStruct((out_rows, co...  7.63 us
    pallas_call x1, Pallas kernels, finish(): pl.pallas_call(functools.partial(finish_kernel, chunks), out_shape=[jax.S...  4.69 us
    pallas_call x3, Pallas kernels, dots(): pl.pallas_call(dots_kernel, out_shape=jax.ShapeDtypeStruct((rows, HEAD_DI...  4.28 us
    pallas_call x3, Pallas kernels, edges(): pl.pallas_call(edges_kernel, out_shape=[jax.ShapeDtypeStruct((2 * rows +...  4.02 us
  transfers between devices with their start and end apart: 38, of which 11 were waited for; matrix products, arithmetic and copies ran while one was open for 0% of the time, Pallas kernels for 28%

profile of v1, /device:TPU:0, one launch (start us, length us, event | category | flops | bytes accessed | tf_op | source)
XLA Modules:
  0.0 184.9 jit_solution(14851272171307944700)
XLA Ops:
  6.0 3.0 %pack.4 = (bf16[1040,256]{1,0:T(8,128)(2,1)S(1)}, bf16[1040,256]{1,0:T(8,128)(2,1)S(1)}, bf16[1040,256]{1,0:T(8,128)(2,1)S(1)}, bf16[1040,256]{1,0:T(8,128)(2,1)S(1)}) custom-call(s32[2]{0:T(128)S(1)} %pad_add_fusion.place_ref, s32[2,4]{1,0:T(2,128)S(1)} %copy-done.13, s32[2]{0:T(128)S(1)} %copy-done.14, s32[1,16]{1,0:T(1,128)S(1)} %copy-done.15, ...), custom_call_target="tpu_custom_call" | custom-call | flops 1 | bytes 4259840 | tf_op jit(solution)/shard_map/pack/pallas_call | solution.py:134
  9.0 2.9 %collective-permute-start.13 = (bf16[1040,256]{1,0:T(8,128)(2,1)S(1)}, bf16[1040,256]{1,0:T(8,128)(2,1)S(1)}, u32[]{:S(2)}, u32[]{:S(2)}) collective-permute-start(bf16[1040,256]{1,0:T(8,128)(2,1)S(1)} %get-tuple-element.96), channel_id=1, source_target_pairs={{0,2},{2,0},{4,6},{6,4},{8,10},{10,8},{12,14},{14,12},{16,18},{18,... | collective-permute-start | bytes 1597448 | tf_op jit(solution)/shard_map/ppermute | solution.py:28
  11.9 1.5 collective-permute-start.14
  13.4 2.9 %pack.3 = (bf16[1040,256]{1,0:T(8,128)(2,1)S(1)}, bf16[1040,256]{1,0:T(8,128)(2,1)S(1)}, bf16[1040,256]{1,0:T(8,128)(2,1)S(1)}, bf16[1040,256]{1,0:T(8,128)(2,1)S(1)}) custom-call(s32[2]{0:T(128)S(1)} %pad_add_fusion.place_ref, s32[2,4]{1,0:T(2,128)S(1)} %copy-done.13, s32[2]{0:T(128)S(1)} %copy-done.14, s32[1,16]{1,0:T(1,128)S(1)} %copy-done.15, ...), custom_call_target="tpu_custom_call" | custom-call | flops 1 | bytes 4259840 | tf_op jit(solution)/shard_map/pack/pallas_call | solution.py:134
  16.3 2.0 %collective-permute-start.1 = (bf16[1040,256]{1,0:T(8,128)(2,1)S(1)}, bf16[1040,256]{1,0:T(8,128)(2,1)S(1)}, u32[]{:S(2)}, u32[]{:S(2)}) collective-permute-start(bf16[1040,256]{1,0:T(8,128)(2,1)S(1)} %get-tuple-element.73), channel_id=1, source_target_pairs={{0,2},{2,0},{4,6},{6,4},{8,10},{10,8},{12,14},{14,12},{16,18},{18,... | collective-permute-start | bytes 1597448 | tf_op jit(solution)/shard_map/ppermute | solution.py:28
  18.3 1.5 collective-permute-start.2
  19.9 4.9 %collective-permute-done.13.b1.f1 = bf16[1040,256]{1,0:T(8,128)(2,1)S(1)} collective-permute-done((bf16[1040,256]{1,0:T(8,128)(2,1)S(1)}, bf16[1040,256]{1,0:T(8,128)(2,1)S(1)}, u32[]{:S(2)}, u32[]{:S(2)}) %collective-permute-start.13) | collective-permute-done | bytes 532512 | tf_op jit(solution)/shard_map/ppermute | solution.py:28
  24.8 3.0 %collective-permute-start.3 = (bf16[1040,256]{1,0:T(8,128)(2,1)S(1)}, bf16[1040,256]{1,0:T(8,128)(2,1)S(1)}, u32[]{:S(2)}, u32[]{:S(2)}) collective-permute-start(bf16[1040,256]{1,0:T(8,128)(2,1)S(1)} %get-tuple-element.75), channel_id=1, source_target_pairs={{0,6},{2,4},{4,2},{6,0},{8,14},{10,12},{12,10},{14,8},{16,22},{18,... | collective-permute-start | bytes 1597448 | tf_op jit(solution)/shard_map/ppermute | solution.py:28
  27.8 10.5 %collective-permute-done.14.b2.f2 = bf16[1040,256]{1,0:T(8,128)(2,1)S(1)} collective-permute-done((bf16[1040,256]{1,0:T(8,128)(2,1)S(1)}, bf16[1040,256]{1,0:T(8,128)(2,1)S(1)}, u32[]{:S(2)}, u32[]{:S(2)}) %collective-permute-start.14) | collective-permute-done | bytes 532512 | tf_op jit(solution)/shard_map/ppermute | solution.py:28
  38.3 1.5 edges.4
  39.8 1.6 collective-permute-start.16
  41.4 2.5 %collective-permute-start.17 = (bf16[528,256]{1,0:T(8,128)(2,1)S(1)}, bf16[528,256]{1,0:T(8,128)(2,1)S(1)}, u32[]{:S(2)}, u32[]{:S(2)}) collective-permute-start(bf16[528,256]{1,0:T(8,128)(2,1)S(1)} %get-tuple-element.101), channel_id=1, source_target_pairs={{0,24},{2,26},{4,28},{6,30},{8,16},{10,18},{12,20},{14,22},{16,8},... | collective-permute-start | bytes 811016 | tf_op jit(solution)/shard_map/ppermute | solution.py:28
  43.9 1.8 pack.5
  45.7 1.9 %collective-permute-done.1.b1.f1 = bf16[1040,256]{1,0:T(8,128)(2,1)S(1)} collective-permute-done((bf16[1040,256]{1,0:T(8,128)(2,1)S(1)}, bf16[1040,256]{1,0:T(8,128)(2,1)S(1)}, u32[]{:S(2)}, u32[]{:S(2)}) %collective-permute-start.1) | collective-permute-done | bytes 532512 | tf_op jit(solution)/shard_map/ppermute | solution.py:28
  47.6 2.1 %collective-permute-start.25 = (bf16[1040,128]{1,0:T(8,128)(2,1)S(1)}, bf16[1040,128]{1,0:T(8,128)(2,1)S(1)}, u32[]{:S(2)}, u32[]{:S(2)}) collective-permute-start(bf16[1040,128]{1,0:T(8,128)(2,1)S(1)} %get-tuple-element.119), channel_id=1, source_target_pairs={{0,2},{2,0},{4,6},{6,4},{8,10},{10,8},{12,14},{14,12},{16,18},{18,... | collective-permute-start | bytes 798728 | tf_op jit(solution)/shard_map/ppermute | solution.py:28
  49.7 9.6 %collective-permute-done.2.b2.f2 = bf16[1040,256]{1,0:T(8,128)(2,1)S(1)} collective-permute-done((bf16[1040,256]{1,0:T(8,128)(2,1)S(1)}, bf16[1040,256]{1,0:T(8,128)(2,1)S(1)}, u32[]{:S(2)}, u32[]{:S(2)}) %collective-permute-start.2) | collective-permute-done | bytes 532512 | tf_op jit(solution)/shard_map/ppermute | solution.py:28
  59.3 2.6 %collective-permute-start.18 = (bf16[16,256]{1,0:T(8,128)(2,1)S(1)}, bf16[16,256]{1,0:T(8,128)(2,1)S(1)}, u32[]{:S(2)}, u32[]{:S(2)}) collective-permute-start(bf16[16,256]{1,0:T(8,128)(2,1)S(1)} %get-tuple-element.99.own_g), channel_id=1, source_target_pairs={{0,16},{2,18},{4,20},{6,22},{8,24},{10,26},{12,28},{14,30},{16,0},... | collective-permute-start | bytes 24584 | tf_op jit(solution)/shard_map/ppermute | solution.py:28
  61.9 2.2 %collective-permute-start.26 = (bf16[1040,128]{1,0:T(8,128)(2,1)S(1)}, bf16[1040,128]{1,0:T(8,128)(2,1)S(1)}, u32[]{:S(2)}, u32[]{:S(2)}) collective-permute-start(bf16[1040,128]{1,0:T(8,128)(2,1)S(1)} %get-tuple-element.120), channel_id=1, source_target_pairs={{0,4},{2,6},{4,0},{6,2},{8,12},{10,14},{12,8},{14,10},{16,20},{18,... | collective-permute-start | bytes 798728 | tf_op jit(solution)/shard_map/ppermute | solution.py:28
  64.1 1.5 edges.3
  65.6 1.3 collective-permute-start.27
  67.0 1.6 collective-permute-start.4
  68.5 2.5 %collective-permute-start.5 = (bf16[528,256]{1,0:T(8,128)(2,1)S(1)}, bf16[528,256]{1,0:T(8,128)(2,1)S(1)}, u32[]{:S(2)}, u32[]{:S(2)}) collective-permute-start(bf16[528,256]{1,0:T(8,128)(2,1)S(1)} %get-tuple-element.78), channel_id=1, source_target_pairs={{0,24},{2,26},{4,28},{6,30},{8,16},{10,18},{12,20},{14,22},{16,8},... | collective-permute-start | bytes 811016 | tf_op jit(solution)/shard_map/ppermute | solution.py:28
  71.2 12.5 %attend.4 = (bf16[256,256]{1,0:T(8,128)(2,1)S(1)}, bf16[256,256]{1,0:T(8,128)(2,1)S(1)}, bf16[256,256]{1,0:T(8,128)(2,1)S(1)}, bf16[256,256]{1,0:T(8,128)(2,1)S(...) custom-call(s32[2]{0:T(128)S(1)} %pad_add_fusion.place_ref, ...), custom_call_target="tpu_custom_call" | custom-call | flops 10000000000 | bytes 4259840 | tf_op jit(solution)/shard_map/attend/pallas_call | solution.py:304
  83.7 2.8 %collective-permute-start.21 = (bf16[16,256]{1,0:T(8,128)(2,1)S(1)}, bf16[16,256]{1,0:T(8,128)(2,1)S(1)}, u32[]{:S(2)}, u32[]{:S(2)}) collective-permute-start(bf16[16,256]{1,0:T(8,128)(2,1)S(1)} %get-tuple-element.113), channel_id=1, source_target_pairs={{0,16},{2,18},{4,20},{6,22},{8,24},{10,26},{12,28},{14,30},{16,0},... | collective-permute-start | bytes 24584 | tf_op jit(solution)/shard_map/ppermute | solution.py:28
  89.2 1.8 collective-permute-start.30
  91.1 1.5 collective-permute-start.19
  93.6 13.1 %attend.3 = (bf16[256,256]{1,0:T(8,128)(2,1)S(1)}, bf16[256,256]{1,0:T(8,128)(2,1)S(1)}, bf16[256,256]{1,0:T(8,128)(2,1)S(1)}, bf16[256,256]{1,0:T(8,128)(2,1)S(...) custom-call(s32[2]{0:T(128)S(1)} %pad_add_fusion.place_ref, ...), custom_call_target="tpu_custom_call" | custom-call | flops 10000000000 | bytes 4259840 | tf_op jit(solution)/shard_map/attend/pallas_call | solution.py:304
  106.8 4.3 %settle.4 = (bf16[768,256]{1,0:T(8,128)(2,1)S(1)}, bf16[768,256]{1,0:T(8,128)(2,1)}, bf16[768,256]{1,0:T(8,128)(2,1)}, bf16[768,256]{1,0:T(8,128)(2,1)S(1)}) custom-call(s32[2]{0:T(128)S(1)} %pad_add_fusion.place_ref, bf16[1040,256]{1,0:T(8,128)(2,1)S(1)} %get-tuple-element.95.b0.f0, bf16[1040,256]{1,0:T(8,128)(2,1)S(1)} %collective-permute-done.13.b1.f1, ...), custom_call_target="tpu_custom_call" | custom-call | flops 1 | bytes 4194304 | tf_op jit(solution)/shard_map/settle/pallas_call | solution.py:372
  111.8 6.0 %attend.5 = (bf16[256,128]{1,0:T(8,128)(2,1)S(1)}, bf16[256,128]{1,0:T(8,128)(2,1)S(1)}, bf16[256,128]{1,0:T(8,128)(2,1)S(1)}, bf16[256,128]{1,0:T(8,128)(2,1)S(...) custom-call(s32[2]{0:T(128)S(1)} %pad_add_fusion.place_ref, ...), custom_call_target="tpu_custom_call" | custom-call | flops 5000000000 | bytes 2129920 | tf_op jit(solution)/shard_map/attend/pallas_call | solution.py:304
  117.8 2.1 %collective-permute-start.31 = (bf16[528,128]{1,0:T(8,128)(2,1)S(1)}, bf16[528,128]{1,0:T(8,128)(2,1)S(1)}, u32[]{:S(2)}, u32[]{:S(2)}) collective-permute-start(bf16[528,128]{1,0:T(8,128)(2,1)S(1)} %get-tuple-element.134), channel_id=1, source_target_pairs={{0,8},{2,10},{4,12},{6,14},{8,0},{10,2},{12,4},{14,6},{16,24},{18,... | collective-permute-start | bytes 405512 | tf_op jit(solution)/shard_map/ppermute | solution.py:28
  119.9 2.9 %collective-permute-start.32 = (bf16[528,128]{1,0:T(8,128)(2,1)S(1)}, bf16[528,128]{1,0:T(8,128)(2,1)S(1)}, u32[]{:S(2)}, u32[]{:S(2)}) collective-permute-start(bf16[528,128]{1,0:T(8,128)(2,1)S(1)} %get-tuple-element.135), channel_id=1, source_target_pairs={{0,24},{2,26},{4,28},{6,30},{8,16},{10,18},{12,20},{14,22},{16,8},... | collective-permute-start | bytes 405512 | tf_op jit(solution)/shard_map/ppermute | solution.py:28
  122.7 7.7 %collective-permute-done.33.mid = bf16[16,128]{1,0:T(8,128)(2,1)S(1)} collective-permute-done((bf16[16,128]{1,0:T(8,128)(2,1)S(1)}, bf16[16,128]{1,0:T(8,128)(2,1)S(1)}, u32[]{:S(2)}, u32[]{:S(2)}) %collective-permute-start.33) | collective-permute-done | bytes 4128 | tf_op jit(solution)/shard_map/ppermute | solution.py:28
  130.4 1.9 %collective-permute-start.8 = (bf16[528,256]{1,0:T(8,128)(2,1)S(1)}, bf16[528,256]{1,0:T(8,128)(2,1)S(1)}, u32[]{:S(2)}, u32[]{:S(2)}) collective-permute-start(bf16[528,256]{1,0:T(8,128)(2,1)S(1)} %get-tuple-element.89), channel_id=1, source_target_pairs={{0,24},{2,26},{4,28},{6,30},{8,16},{10,18},{12,20},{14,22},{16,8},... | collective-permute-start | bytes 811016 | tf_op jit(solution)/shard_map/ppermute | solution.py:28
  132.3 1.7 settle.5
  134.0 1.5 collective-permute-start.34
  135.5 2.1 %collective-permute-done.9.mid = bf16[16,256]{1,0:T(8,128)(2,1)S(1)} collective-permute-done((bf16[16,256]{1,0:T(8,128)(2,1)S(1)}, bf16[16,256]{1,0:T(8,128)(2,1)S(1)}, u32[]{:S(2)}, u32[]{:S(2)}) %collective-permute-start.9) | collective-permute-done | bytes 8224 | tf_op jit(solution)/shard_map/ppermute | solution.py:28
  138.2 2.4 %collective-permute-start.36 = (bf16[768,128]{1,0:T(8,128)(2,1)S(1)}, bf16[768,128]{1,0:T(8,128)(2,1)S(1)}, u32[]{:S(2)}, u32[]{:S(2)}) collective-permute-start(bf16[768,128]{1,0:T(8,128)(2,1)S(1)} %get-tuple-element.140), channel_id=1, source_target_pairs={{0,6},{2,4},{4,2},{6,0},{8,14},{10,12},{12,10},{14,8},{16,22},{18,... | collective-permute-start | bytes 589832 | tf_op jit(solution)/shard_map/ppermute | solution.py:28
  141.2 3.7 %settle.3 = (bf16[768,256]{1,0:T(8,128)(2,1)S(1)}, bf16[768,256]{1,0:T(8,128)(2,1)S(1)}, bf16[768,256]{1,0:T(8,128)(2,1)S(1)}, bf16[768,256]{1,0:T(8,128)(2,1)S(1)}) custom-call(s32[2]{0:T(128)S(1)} %pad_add_fusion.place_ref, bf16[1040,256]{1,0:T(8,128)(2,1)S(1)} %get-tuple-element.72.b0.f0, bf16[1040,256]{1,0:T(8,128)(2,1)S(1)} %collective-permute-done.1.b1.f1, ...), custom_call_target="tpu_custom_call" | custom-call | flops 1 | bytes 4194304 | tf_op jit(solution)/shard_map/settle/pallas_call | solution.py:372
  144.9 1.5 collective-permute-start.24
  146.4 7.7 %collective-permute-done.35.refs_10_ = bf16[768,128]{1,0:T(8,128)(2,1)S(1)} collective-permute-done((bf16[768,128]{1,0:T(8,128)(2,1)S(1)}, bf16[768,128]{1,0:T(8,128)(2,1)S(1)}, u32[]{:S(2)}, u32[]{:S(2)}) %collective-permute-start.35) | collective-permute-done | bytes 196640 | tf_op jit(solution)/shard_map/ppermute | solution.py:28
  154.2 2.3 %collective-permute-start.10 = (bf16[768,256]{1,0:T(8,128)(2,1)S(1)}, bf16[768,256]{1,0:T(8,128)(2,1)S(1)}, u32[]{:S(2)}, u32[]{:S(2)}) collective-permute-start(bf16[768,256]{1,0:T(8,128)(2,1)S(1)} %get-tuple-element.92), channel_id=1, source_target_pairs={{0,2},{2,0},{4,6},{6,4},{8,10},{10,8},{12,14},{14,12},{16,18},{18,... | collective-permute-start | bytes 1179656 | tf_op jit(solution)/shard_map/ppermute | solution.py:28
  156.5 1.5 collective-permute-start.12
  158.8 14.0 %collective-permute-done.23.refs_10_.refs_6_ = bf16[768,256]{1,0:T(8,128)(2,1)S(1)} collective-permute-done((bf16[768,256]{1,0:T(8,128)(2,1)}, bf16[768,256]{1,0:T(8,128)(2,1)S(1)}, u32[]{:S(2)}, u32[]{:S(2)}) %collective-permute-start.23) | collective-permute-done | bytes 393248 | tf_op jit(solution)/shard_map/ppermute | solution.py:28
  172.8 1.7 dots.4
  174.6 2.5 %collective-permute-done.11.refs_10_.refs_2_ = bf16[768,256]{1,0:T(8,128)(2,1)S(1)} collective-permute-done((bf16[768,256]{1,0:T(8,128)(2,1)S(1)}, bf16[768,256]{1,0:T(8,128)(2,1)S(1)}, u32[]{:S(2)}, u32[]{:S(2)}) %collective-permute-start.11) | collective-permute-done | bytes 393248 | tf_op jit(solution)/shard_map/ppermute | solution.py:28
  177.0 1.7 dots.3
  178.9 1.3 collective-permute-done.37.dot_other_ref
  180.2 4.7 %finish.1 = (bf16[256,2560]{1,0:T(8,128)(2,1)}, bf16[256,2560]{1,0:T(8,128)(2,1)}, bf16[256,2560]{1,0:T(8,128)(2,1)}) custom-call(s32[2]{0:T(128)S(1)} %pad_add_fusion.place_ref, f32[256,128]{1,0:T(8,128)S(1)} %squares.1.own_ref, f32[256,128]{1,0:T(8,128)S(1)} %collective-permute-done.other_ref, f32[256,128]{1,0:T(8,128)S(1)} %add_add_fusion.dot_ref, ...), custom_call_target="tpu_custom_call" | custom-call | flops 1 | bytes 10485760 | tf_op jit(solution)/shard_map/finish/pallas_call | solution.py:473
  (85 shorter events, 11.9 us)
Async XLA Ops:
  3.3 2.7 %copy-start.4 = (bf16[256,2560]{1,0:T(8,128)(2,1)S(1)}, bf16[256,2560]{1,0:T(8,128)(2,1)}, u32[]{:S(2)}) copy-start(bf16[256,2560]{1,0:T(8,128)(2,1)} %refs_19_.5) | copy-start | bytes 3932164
  4.5 1.5 collective-permute-start
  9.0 15.8 %collective-permute-start.13 = (bf16[1040,256]{1,0:T(8,128)(2,1)S(1)}, bf16[1040,256]{1,0:T(8,128)(2,1)S(1)}, u32[]{:S(2)}, u32[]{:S(2)}) collective-permute-start(bf16[1040,256]{1,0:T(8,128)(2,1)S(1)} %get-tuple-element.96), channel_id=1, source_target_pairs={{0,2},{2,0},{4,6},{6,4},{8,10},{10,8},{12,14},{14,12},{16,18},{18,... | collective-permute-start | bytes 1597448 | tf_op jit(solution)/shard_map/ppermute | solution.py:28
  11.9 26.4 %collective-permute-start.14 = (bf16[1040,256]{1,0:T(8,128)(2,1)S(1)}, bf16[1040,256]{1,0:T(8,128)(2,1)S(1)}, u32[]{:S(2)}, u32[]{:S(2)}) collective-permute-start(bf16[1040,256]{1,0:T(8,128)(2,1)S(1)} %get-tuple-element.97), channel_id=1, source_target_pairs={{0,4},{2,6},{4,0},{6,2},{8,12},{10,14},{12,8},{14,10},{16,20},{18,... | collective-permute-start | bytes 1597448 | tf_op jit(solution)/shard_map/ppermute | solution.py:28
  13.4 24.9 %collective-permute-start.15 = (bf16[1040,256]{1,0:T(8,128)(2,1)S(1)}, bf16[1040,256]{1,0:T(8,128)(2,1)S(1)}, u32[]{:S(2)}, u32[]{:S(2)}) collective-permute-start(bf16[1040,256]{1,0:T(8,128)(2,1)S(1)} %get-tuple-element.98), channel_id=1, source_target_pairs={{0,6},{2,4},{4,2},{6,0},{8,14},{10,12},{12,10},{14,8},{16,22},{18,... | collective-permute-start | bytes 1597448 | tf_op jit(solution)/shard_map/ppermute | solution.py:28
  16.3 27.6 %copy-start.1 = (bf16[256,2560]{1,0:T(8,128)(2,1)S(1)}, bf16[256,2560]{1,0:T(8,128)(2,1)}, u32[]{:S(2)}) copy-start(bf16[256,2560]{1,0:T(8,128)(2,1)} %refs_12_.13) | copy-start | bytes 3932164
  16.3 31.3 %collective-permute-start.1 = (bf16[1040,256]{1,0:T(8,128)(2,1)S(1)}, bf16[1040,256]{1,0:T(8,128)(2,1)S(1)}, u32[]{:S(2)}, u32[]{:S(2)}) collective-permute-start(bf16[1040,256]{1,0:T(8,128)(2,1)S(1)} %get-tuple-element.73), channel_id=1, source_target_pairs={{0,2},{2,0},{4,6},{6,4},{8,10},{10,8},{12,14},{14,12},{16,18},{18,... | collective-permute-start | bytes 1597448 | tf_op jit(solution)/shard_map/ppermute | solution.py:28
  18.3 41.0 %collective-permute-start.2 = (bf16[1040,256]{1,0:T(8,128)(2,1)S(1)}, bf16[1040,256]{1,0:T(8,128)(2,1)S(1)}, u32[]{:S(2)}, u32[]{:S(2)}) collective-permute-start(bf16[1040,256]{1,0:T(8,128)(2,1)S(1)} %get-tuple-element.74), channel_id=1, source_target_pairs={{0,4},{2,6},{4,0},{6,2},{8,12},{10,14},{12,8},{14,10},{16,20},{18,... | collective-permute-start | bytes 1597448 | tf_op jit(solution)/shard_map/ppermute | solution.py:28
  24.8 37.2 %collective-permute-start.3 = (bf16[1040,256]{1,0:T(8,128)(2,1)S(1)}, bf16[1040,256]{1,0:T(8,128)(2,1)S(1)}, u32[]{:S(2)}, u32[]{:S(2)}) collective-permute-start(bf16[1040,256]{1,0:T(8,128)(2,1)S(1)} %get-tuple-element.75), channel_id=1, source_target_pairs={{0,6},{2,4},{4,2},{6,0},{8,14},{10,12},{12,10},{14,8},{16,22},{18,... | collective-permute-start | bytes 1597448 | tf_op jit(solution)/shard_map/ppermute | solution.py:28
  38.3 32.9 %copy-start.7 = (bf16[1040,256]{1,0:T(8,128)(2,1)}, bf16[1040,256]{1,0:T(8,128)(2,1)S(1)}, u32[]{:S(2)}) copy-start(bf16[1040,256]{1,0:T(8,128)(2,1)S(1)} %collective-permute-done.14.b2.f2) | copy-start | bytes 1597444
  38.3 32.9 %copy-start.8 = (bf16[1040,256]{1,0:T(8,128)(2,1)}, bf16[1040,256]{1,0:T(8,128)(2,1)S(1)}, u32[]{:S(2)}) copy-start(bf16[1040,256]{1,0:T(8,128)(2,1)S(1)} %collective-permute-done.15.b3.f3) | copy-start | bytes 1597444
  39.8 28.7 %collective-permute-start.16 = (bf16[528,256]{1,0:T(8,128)(2,1)S(1)}, bf16[528,256]{1,0:T(8,128)(2,1)S(1)}, u32[]{:S(2)}, u32[]{:S(2)}) collective-permute-start(bf16[528,256]{1,0:T(8,128)(2,1)S(1)} %get-tuple-element.100), channel_id=1, source_target_pairs={{0,8},{2,10},{4,12},{6,14},{8,0},{10,2},{12,4},{14,6},{16,24},{18,... | collective-permute-start | bytes 811016 | tf_op jit(solution)/shard_map/ppermute | solution.py:28
  41.4 29.6 %collective-permute-start.17 = (bf16[528,256]{1,0:T(8,128)(2,1)S(1)}, bf16[528,256]{1,0:T(8,128)(2,1)S(1)}, u32[]{:S(2)}, u32[]{:S(2)}) collective-permute-start(bf16[528,256]{1,0:T(8,128)(2,1)S(1)} %get-tuple-element.101), channel_id=1, source_target_pairs={{0,24},{2,26},{4,28},{6,30},{8,16},{10,18},{12,20},{14,22},{16,8},... | collective-permute-start | bytes 811016 | tf_op jit(solution)/shard_map/ppermute | solution.py:28
  47.6 18.0 %collective-permute-start.25 = (bf16[1040,128]{1,0:T(8,128)(2,1)S(1)}, bf16[1040,128]{1,0:T(8,128)(2,1)S(1)}, u32[]{:S(2)}, u32[]{:S(2)}) collective-permute-start(bf16[1040,128]{1,0:T(8,128)(2,1)S(1)} %get-tuple-element.119), channel_id=1, source_target_pairs={{0,2},{2,0},{4,6},{6,4},{8,10},{10,8},{12,14},{14,12},{16,18},{18,... | collective-permute-start | bytes 798728 | tf_op jit(solution)/shard_map/ppermute | solution.py:28
  59.3 34.3 %copy-start.5 = (bf16[1040,256]{1,0:T(8,128)(2,1)}, bf16[1040,256]{1,0:T(8,128)(2,1)S(1)}, u32[]{:S(2)}) copy-start(bf16[1040,256]{1,0:T(8,128)(2,1)S(1)} %collective-permute-done.2.b2.f2) | copy-start | bytes 1597444
  59.3 7.6 %collective-permute-start.18 = (bf16[16,256]{1,0:T(8,128)(2,1)S(1)}, bf16[16,256]{1,0:T(8,128)(2,1)S(1)}, u32[]{:S(2)}, u32[]{:S(2)}) collective-permute-start(bf16[16,256]{1,0:T(8,128)(2,1)S(1)} %get-tuple-element.99.own_g), channel_id=1, source_target_pairs={{0,16},{2,18},{4,20},{6,22},{8,24},{10,26},{12,28},{14,30},{16,0},... | collective-permute-start | bytes 24584 | tf_op jit(solution)/shard_map/ppermute | solution.py:28
  61.9 31.7 %copy-start.6 = (bf16[1040,256]{1,0:T(8,128)(2,1)}, bf16[1040,256]{1,0:T(8,128)(2,1)S(1)}, u32[]{:S(2)}) copy-start(bf16[1040,256]{1,0:T(8,128)(2,1)S(1)} %collective-permute-done.3.b3.f3) | copy-start | bytes 1597444
  61.9 21.8 %collective-permute-start.26 = (bf16[1040,128]{1,0:T(8,128)(2,1)S(1)}, bf16[1040,128]{1,0:T(8,128)(2,1)S(1)}, u32[]{:S(2)}, u32[]{:S(2)}) collective-permute-start(bf16[1040,128]{1,0:T(8,128)(2,1)S(1)} %get-tuple-element.120), channel_id=1, source_target_pairs={{0,4},{2,6},{4,0},{6,2},{8,12},{10,14},{12,8},{14,10},{16,20},{18,... | collective-permute-start | bytes 798728 | tf_op jit(solution)/shard_map/ppermute | solution.py:28
  65.6 20.9 %collective-permute-start.27 = (bf16[1040,128]{1,0:T(8,128)(2,1)S(1)}, bf16[1040,128]{1,0:T(8,128)(2,1)S(1)}, u32[]{:S(2)}, u32[]{:S(2)}) collective-permute-start(bf16[1040,128]{1,0:T(8,128)(2,1)S(1)} %get-tuple-element.121), channel_id=1, source_target_pairs={{0,6},{2,4},{4,2},{6,0},{8,14},{10,12},{12,10},{14,8},{16,22},{18,... | collective-permute-start | bytes 798728 | tf_op jit(solution)/shard_map/ppermute | solution.py:28
  67.0 22.2 %collective-permute-start.4 = (bf16[528,256]{1,0:T(8,128)(2,1)S(1)}, bf16[528,256]{1,0:T(8,128)(2,1)S(1)}, u32[]{:S(2)}, u32[]{:S(2)}) collective-permute-start(bf16[528,256]{1,0:T(8,128)(2,1)S(1)} %get-tuple-element.77), channel_id=1, source_target_pairs={{0,8},{2,10},{4,12},{6,14},{8,0},{10,2},{12,4},{14,6},{16,24},{18,... | collective-permute-start | bytes 811016 | tf_op jit(solution)/shard_map/ppermute | solution.py:28
  68.5 22.5 %collective-permute-start.5 = (bf16[528,256]{1,0:T(8,128)(2,1)S(1)}, bf16[528,256]{1,0:T(8,128)(2,1)S(1)}, u32[]{:S(2)}, u32[]{:S(2)}) collective-permute-start(bf16[528,256]{1,0:T(8,128)(2,1)S(1)} %get-tuple-element.78), channel_id=1, source_target_pairs={{0,24},{2,26},{4,28},{6,30},{8,16},{10,18},{12,20},{14,22},{16,8},... | collective-permute-start | bytes 811016 | tf_op jit(solution)/shard_map/ppermute | solution.py:28
  71.0 17.2 %collective-permute-start.6 = (bf16[16,256]{1,0:T(8,128)(2,1)S(1)}, bf16[16,256]{1,0:T(8,128)(2,1)S(1)}, u32[]{:S(2)}, u32[]{:S(2)}) collective-permute-start(bf16[16,256]{1,0:T(8,128)(2,1)S(1)} %get-tuple-element.76.own_g), channel_id=1, source_target_pairs={{0,16},{2,18},{4,20},{6,22},{8,24},{10,26},{12,28},{14,30},{16,0},... | collective-permute-start | bytes 24584 | tf_op jit(solution)/shard_map/ppermute | solution.py:28
  83.7 8.9 %collective-permute-start.21 = (bf16[16,256]{1,0:T(8,128)(2,1)S(1)}, bf16[16,256]{1,0:T(8,128)(2,1)S(1)}, u32[]{:S(2)}, u32[]{:S(2)}) collective-permute-start(bf16[16,256]{1,0:T(8,128)(2,1)S(1)} %get-tuple-element.113), channel_id=1, source_target_pairs={{0,16},{2,18},{4,20},{6,22},{8,24},{10,26},{12,28},{14,30},{16,0},... | collective-permute-start | bytes 24584 | tf_op jit(solution)/shard_map/ppermute | solution.py:28
  87.5 24.3 %collective-permute-start.28 = (bf16[528,128]{1,0:T(8,128)(2,1)S(1)}, bf16[528,128]{1,0:T(8,128)(2,1)S(1)}, u32[]{:S(2)}, u32[]{:S(2)}) collective-permute-start(bf16[528,128]{1,0:T(8,128)(2,1)S(1)} %get-tuple-element.123), channel_id=1, source_target_pairs={{0,8},{2,10},{4,12},{6,14},{8,0},{10,2},{12,4},{14,6},{16,24},{18,... | collective-permute-start | bytes 405512 | tf_op jit(solution)/shard_map/ppermute | solution.py:28
  88.2 23.6 %collective-permute-start.29 = (bf16[528,128]{1,0:T(8,128)(2,1)S(1)}, bf16[528,128]{1,0:T(8,128)(2,1)S(1)}, u32[]{:S(2)}, u32[]{:S(2)}) collective-permute-start(bf16[528,128]{1,0:T(8,128)(2,1)S(1)} %get-tuple-element.124), channel_id=1, source_target_pairs={{0,24},{2,26},{4,28},{6,30},{8,16},{10,18},{12,20},{14,22},{16,8},... | collective-permute-start | bytes 405512 | tf_op jit(solution)/shard_map/ppermute | solution.py:28
  89.2 22.5 %collective-permute-start.30 = (bf16[16,128]{1,0:T(8,128)(2,1)S(1)}, bf16[16,128]{1,0:T(8,128)(2,1)S(1)}, u32[]{:S(2)}, u32[]{:S(2)}) collective-permute-start(bf16[16,128]{1,0:T(8,128)(2,1)S(1)} %get-tuple-element.122.own_g), channel_id=1, source_target_pairs={{0,16},{2,18},{4,20},{6,22},{8,24},{10,26},{12,28},{14,30},{16,0},... | collective-permute-start | bytes 12296 | tf_op jit(solution)/shard_map/ppermute | solution.py:28
  91.1 15.6 %collective-permute-start.19 = (bf16[528,256]{1,0:T(8,128)(2,1)S(1)}, bf16[528,256]{1,0:T(8,128)(2,1)S(1)}, u32[]{:S(2)}, u32[]{:S(2)}) collective-permute-start(bf16[528,256]{1,0:T(8,128)(2,1)S(1)} %get-tuple-element.111), channel_id=1, source_target_pairs={{0,8},{2,10},{4,12},{6,14},{8,0},{10,2},{12,4},{14,6},{16,24},{18,... | collective-permute-start | bytes 811016 | tf_op jit(solution)/shard_map/ppermute | solution.py:28
  92.6 14.2 %collective-permute-start.20 = (bf16[528,256]{1,0:T(8,128)(2,1)S(1)}, bf16[528,256]{1,0:T(8,128)(2,1)S(1)}, u32[]{:S(2)}, u32[]{:S(2)}) collective-permute-start(bf16[528,256]{1,0:T(8,128)(2,1)S(1)} %get-tuple-element.112), channel_id=1, source_target_pairs={{0,24},{2,26},{4,28},{6,30},{8,16},{10,18},{12,20},{14,22},{16,8},... | collective-permute-start | bytes 811016 | tf_op jit(solution)/shard_map/ppermute | solution.py:28
  106.7 4.4 %copy-start.9 = (bf16[256,256]{1,0:T(8,128)(2,1)}, bf16[256,256]{1,0:T(8,128)(2,1)S(1)}, u32[]{:S(2)}) copy-start(bf16[256,256]{1,0:T(8,128)(2,1)S(1)} %get-tuple-element.81.q2) | copy-start | bytes 393220
  106.7 4.4 %copy-start.11 = (bf16[256,256]{1,0:T(8,128)(2,1)}, bf16[256,256]{1,0:T(8,128)(2,1)S(1)}, u32[]{:S(2)}) copy-start(bf16[256,256]{1,0:T(8,128)(2,1)S(1)} %get-tuple-element.82.q3) | copy-start | bytes 393220
  106.7 31.5 %collective-permute-start.7 = (bf16[528,256]{1,0:T(8,128)(2,1)}, bf16[528,256]{1,0:T(8,128)(2,1)S(1)}, u32[]{:S(2)}, u32[]{:S(2)}) collective-permute-start(bf16[528,256]{1,0:T(8,128)(2,1)} %get-tuple-element.88), channel_id=1, source_target_pairs={{0,8},{2,10},{4,12},{6,14},{8,0},{10,2},{12,4},{14,6},{16,24},{18,... | collective-permute-start | bytes 811016 | tf_op jit(solution)/shard_map/ppermute | solution.py:28
  111.1 45.4 %collective-permute-start.22 = (bf16[768,256]{1,0:T(8,128)(2,1)}, bf16[768,256]{1,0:T(8,128)(2,1)S(1)}, u32[]{:S(2)}, u32[]{:S(2)}) collective-permute-start(bf16[768,256]{1,0:T(8,128)(2,1)} %get-tuple-element.115), channel_id=1, source_target_pairs={{0,2},{2,0},{4,6},{6,4},{8,10},{10,8},{12,14},{14,12},{16,18},{18,... | collective-permute-start | bytes 1179656 | tf_op jit(solution)/shard_map/ppermute | solution.py:28
  117.8 14.5 %collective-permute-start.31 = (bf16[528,128]{1,0:T(8,128)(2,1)S(1)}, bf16[528,128]{1,0:T(8,128)(2,1)S(1)}, u32[]{:S(2)}, u32[]{:S(2)}) collective-permute-start(bf16[528,128]{1,0:T(8,128)(2,1)S(1)} %get-tuple-element.134), channel_id=1, source_target_pairs={{0,8},{2,10},{4,12},{6,14},{8,0},{10,2},{12,4},{14,6},{16,24},{18,... | collective-permute-start | bytes 405512 | tf_op jit(solution)/shard_map/ppermute | solution.py:28
  119.9 12.5 %collective-permute-start.32 = (bf16[528,128]{1,0:T(8,128)(2,1)S(1)}, bf16[528,128]{1,0:T(8,128)(2,1)S(1)}, u32[]{:S(2)}, u32[]{:S(2)}) collective-permute-start(bf16[528,128]{1,0:T(8,128)(2,1)S(1)} %get-tuple-element.135), channel_id=1, source_target_pairs={{0,24},{2,26},{4,28},{6,30},{8,16},{10,18},{12,20},{14,22},{16,8},... | collective-permute-start | bytes 405512 | tf_op jit(solution)/shard_map/ppermute | solution.py:28
  122.7 7.7 %collective-permute-start.33 = (bf16[16,128]{1,0:T(8,128)(2,1)S(1)}, bf16[16,128]{1,0:T(8,128)(2,1)S(1)}, u32[]{:S(2)}, u32[]{:S(2)}) collective-permute-start(bf16[16,128]{1,0:T(8,128)(2,1)S(1)} %get-tuple-element.136), channel_id=1, source_target_pairs={{0,16},{2,18},{4,20},{6,22},{8,24},{10,26},{12,28},{14,30},{16,0},... | collective-permute-start | bytes 12296 | tf_op jit(solution)/shard_map/ppermute | solution.py:28
  130.4 10.2 %collective-permute-start.8 = (bf16[528,256]{1,0:T(8,128)(2,1)S(1)}, bf16[528,256]{1,0:T(8,128)(2,1)S(1)}, u32[]{:S(2)}, u32[]{:S(2)}) collective-permute-start(bf16[528,256]{1,0:T(8,128)(2,1)S(1)} %get-tuple-element.89), channel_id=1, source_target_pairs={{0,24},{2,26},{4,28},{6,30},{8,16},{10,18},{12,20},{14,22},{16,8},... | collective-permute-start | bytes 811016 | tf_op jit(solution)/shard_map/ppermute | solution.py:28
  132.3 5.3 %collective-permute-start.9 = (bf16[16,256]{1,0:T(8,128)(2,1)S(1)}, bf16[16,256]{1,0:T(8,128)(2,1)S(1)}, u32[]{:S(2)}, u32[]{:S(2)}) collective-permute-start(bf16[16,256]{1,0:T(8,128)(2,1)S(1)} %get-tuple-element.90), channel_id=1, source_target_pairs={{0,16},{2,18},{4,20},{6,22},{8,24},{10,26},{12,28},{14,30},{16,0},... | collective-permute-start | bytes 24584 | tf_op jit(solution)/shard_map/ppermute | solution.py:28
  132.3 8.8 %copy-start.10 = (bf16[256,256]{1,0:T(8,128)(2,1)S(1)}, bf16[256,256]{1,0:T(8,128)(2,1)}, u32[]{:S(2)}) copy-start(bf16[256,256]{1,0:T(8,128)(2,1)} %copy-done.9) | copy-start | bytes 393220
  132.3 8.8 %copy-start.12 = (bf16[256,256]{1,0:T(8,128)(2,1)S(1)}, bf16[256,256]{1,0:T(8,128)(2,1)}, u32[]{:S(2)}) copy-start(bf16[256,256]{1,0:T(8,128)(2,1)} %copy-done.11) | copy-start | bytes 393220
  134.0 10.9 %collective-permute-start.34 = (bf16[768,128]{1,0:T(8,128)(2,1)S(1)}, bf16[768,128]{1,0:T(8,128)(2,1)S(1)}, u32[]{:S(2)}, u32[]{:S(2)}) collective-permute-start(bf16[768,128]{1,0:T(8,128)(2,1)S(1)} %get-tuple-element.138), channel_id=1, source_target_pairs={{0,2},{2,0},{4,6},{6,4},{8,10},{10,8},{12,14},{14,12},{16,18},{18,... | collective-permute-start | bytes 589832 | tf_op jit(solution)/shard_map/ppermute | solution.py:28
  137.7 16.5 %collective-permute-start.35 = (bf16[768,128]{1,0:T(8,128)(2,1)S(1)}, bf16[768,128]{1,0:T(8,128)(2,1)S(1)}, u32[]{:S(2)}, u32[]{:S(2)}) collective-permute-start(bf16[768,128]{1,0:T(8,128)(2,1)S(1)} %get-tuple-element.139), channel_id=1, source_target_pairs={{0,4},{2,6},{4,0},{6,2},{8,12},{10,14},{12,8},{14,10},{16,20},{18,... | collective-permute-start | bytes 589832 | tf_op jit(solution)/shard_map/ppermute | solution.py:28
  138.2 18.3 %collective-permute-start.36 = (bf16[768,128]{1,0:T(8,128)(2,1)S(1)}, bf16[768,128]{1,0:T(8,128)(2,1)S(1)}, u32[]{:S(2)}, u32[]{:S(2)}) collective-permute-start(bf16[768,128]{1,0:T(8,128)(2,1)S(1)} %get-tuple-element.140), channel_id=1, source_target_pairs={{0,6},{2,4},{4,2},{6,0},{8,14},{10,12},{12,10},{14,8},{16,22},{18,... | collective-permute-start | bytes 589832 | tf_op jit(solution)/shard_map/ppermute | solution.py:28
  140.6 32.2 %collective-permute-start.23 = (bf16[768,256]{1,0:T(8,128)(2,1)}, bf16[768,256]{1,0:T(8,128)(2,1)S(1)}, u32[]{:S(2)}, u32[]{:S(2)}) collective-permute-start(bf16[768,256]{1,0:T(8,128)(2,1)} %get-tuple-element.116), channel_id=1, source_target_pairs={{0,4},{2,6},{4,0},{6,2},{8,12},{10,14},{12,8},{14,10},{16,20},{18,... | collective-permute-start | bytes 1179656 | tf_op jit(solution)/shard_map/ppermute | solution.py:28
  144.9 27.9 %collective-permute-start.24 = (bf16[768,256]{1,0:T(8,128)(2,1)S(1)}, bf16[768,256]{1,0:T(8,128)(2,1)S(1)}, u32[]{:S(2)}, u32[]{:S(2)}) collective-permute-start(bf16[768,256]{1,0:T(8,128)(2,1)S(1)} %get-tuple-element.117), channel_id=1, source_target_pairs={{0,6},{2,4},{4,2},{6,0},{8,14},{10,12},{12,10},{14,8},{16,22},{18,... | collective-permute-start | bytes 1179656 | tf_op jit(solution)/shard_map/ppermute | solution.py:28
  154.2 20.4 %collective-permute-start.10 = (bf16[768,256]{1,0:T(8,128)(2,1)S(1)}, bf16[768,256]{1,0:T(8,128)(2,1)S(1)}, u32[]{:S(2)}, u32[]{:S(2)}) collective-permute-start(bf16[768,256]{1,0:T(8,128)(2,1)S(1)} %get-tuple-element.92), channel_id=1, source_target_pairs={{0,2},{2,0},{4,6},{6,4},{8,10},{10,8},{12,14},{14,12},{16,18},{18,... | collective-permute-start | bytes 1179656 | tf_op jit(solution)/shard_map/ppermute | solution.py:28
  156.5 20.5 %collective-permute-start.11 = (bf16[768,256]{1,0:T(8,128)(2,1)S(1)}, bf16[768,256]{1,0:T(8,128)(2,1)S(1)}, u32[]{:S(2)}, u32[]{:S(2)}) collective-permute-start(bf16[768,256]{1,0:T(8,128)(2,1)S(1)} %get-tuple-element.93), channel_id=1, source_target_pairs={{0,4},{2,6},{4,0},{6,2},{8,12},{10,14},{12,8},{14,10},{16,20},{18,... | collective-permute-start | bytes 1179656 | tf_op jit(solution)/shard_map/ppermute | solution.py:28
  156.5 20.5 %collective-permute-start.12 = (bf16[768,256]{1,0:T(8,128)(2,1)S(1)}, bf16[768,256]{1,0:T(8,128)(2,1)S(1)}, u32[]{:S(2)}, u32[]{:S(2)}) collective-permute-start(bf16[768,256]{1,0:T(8,128)(2,1)S(1)} %get-tuple-element.94), channel_id=1, source_target_pairs={{0,6},{2,4},{4,2},{6,0},{8,14},{10,12},{12,10},{14,8},{16,22},{18,... | collective-permute-start | bytes 1179656 | tf_op jit(solution)/shard_map/ppermute | solution.py:28
  178.8 1.4 collective-permute-start.37
  (8 other events, 16.8 us)

commit v2 on v1

v2 whole, which is shorter than its diff:
```python
import functools

import jax
import jax.numpy as jnp
from jax import lax
from jax.experimental import pallas as pl
from jax.experimental.pallas import tpu as pltpu
from jax.sharding import PartitionSpec as P

HEAD_DIM = 128
D = 5120
TILE = 128
REACH = 1
G_DEV = 2
GROUP = 4
CHUNKS = (2, 2, 1)
ORDER = ("b0 i0 g0 b1", "i1 e0 b2 g1", "i2 s0 e1 g2", "s1 e2 s2")


EPSILON = 1e-06
FACTOR = HEAD_DIM ** (-0.5)
LOG2_E = 1.4426950408889634
FACTS = 32
EXTRA = 16
F32 = jnp.float32
BF16 = jnp.bfloat16
ANY = pl.BlockSpec(memory_space=pl.ANY)
VMEM_LIMIT = 48 * 1024 * 1024


def swapped(shard, bit):
    count = lax.axis_size("ctx")
    return lax.ppermute(shard, "ctx", [(i, i ^ bit) for i in range(count)])


def swapped_edges(shard):
    count = lax.axis_size("ctx")
    pairs = [(i, i ^ 12) for i in range(count) if i // GROUP % GROUP in (1, 2)]
    return lax.ppermute(shard, "ctx", pairs)


def params():
    return pltpu.CompilerParams(vmem_limit_bytes=VMEM_LIMIT)


def cost(flops, read):
    return pl.CostEstimate(flops=1, bytes_accessed=1, transcendentals=0)


def behind(kernel, inputs, tokens):
    def run(*refs):
        kernel(*refs[:inputs], *refs[inputs + tokens :])

    return run


def contract(a, b, dims, precision=None):
    return lax.dot_general(
        a, b, (dims, ((), ())), precision=precision, preferred_element_type=F32
    )


def lane_pair(first, second, rows):
    lane = lax.broadcasted_iota(jnp.int32, (rows, HEAD_DIM), 1)
    return jnp.where(lane < HEAD_DIM // 2, first, second)


def squares_kernel(query_ref, key_ref, out_ref):
    step = pl.program_id(0)
    query = query_ref[...].astype(F32)
    key = key_ref[...].astype(F32)
    part = lane_pair(
        jnp.sum(query * query, axis=1, keepdims=True),
        jnp.sum(key * key, axis=1, keepdims=True),
        query.shape[0],
    )

    @pl.when(step == 0)
    def _():
        out_ref[...] = part

    @pl.when(step > 0)
    def _():
        out_ref[...] += part


def squares(query_raw, key_raw):
    rows, width = query_raw.shape
    block = width // 4
    return pl.pallas_call(
        squares_kernel,
        out_shape=jax.ShapeDtypeStruct((rows, HEAD_DIM), F32),
        grid=(4,),
        in_specs=[pl.BlockSpec((rows, block), lambda i: (0, i))] * 2,
        out_specs=pl.BlockSpec((rows, HEAD_DIM), lambda i: (0, 0)),
        compiler_params=params(),
        cost_estimate=cost(4 * rows * width, 4 * rows * width),
        name="squares",
    )(query_raw, key_raw)


def inverses(own, other):
    both = lax.rsqrt((own + other) / D + EPSILON)
    return both[:, :1], both[:, HEAD_DIM // 2 : HEAD_DIM // 2 + 1]


def rows_kernel(place_ref, ids_ref, own_ref, other_ref, key_ref, value_ref, gain_ref, *outs):
    rows = key_ref.shape[0]
    _, key_inv = inverses(own_ref[...], other_ref[...])
    device = place_ref[1] * GROUP + place_ref[0]
    row = lax.broadcasted_iota(jnp.int32, (16 * GROUP, rows), 0)
    col = lax.broadcasted_iota(jnp.int32, (16 * GROUP, rows), 1)
    is_key = jnp.zeros((16 * GROUP, rows), jnp.bool_)
    is_value = is_key
    for r in range(G_DEV):
        here = col == ids_ref[r] - device * rows
        for e in range(GROUP):
            is_key = is_key | (here & (row == 16 * e + 2 * e + r))
            is_value = is_value | (here & (row == 16 * e + 8 + 2 * e + r))
    is_key = is_key.astype(F32).astype(BF16)
    is_value = is_value.astype(F32).astype(BF16)
    key = key_ref[...]
    normed = (key.astype(F32) * key_inv * gain_ref[...]).astype(BF16)
    total = contract(is_key, normed, ((1,), (0,))) + contract(
        is_value, value_ref[...], ((1,), (0,))
    )
    for e in range(GROUP):
        outs[e][...] = total[16 * e : 16 * e + 16].astype(BF16)
    outs[GROUP][...] = contract(is_key[:16], key, ((1,), (0,))).astype(BF16)


def global_rows(place, ids, own, other, key_raw, values, key_gain):
    rows, width = key_raw.shape
    block = width // 4
    smem = pl.BlockSpec(memory_space=pltpu.SMEM)
    whole = pl.BlockSpec((rows, HEAD_DIM), lambda i: (0, 0))
    return pl.pallas_call(
        rows_kernel,
        out_shape=[jax.ShapeDtypeStruct((16, width), BF16)] * (GROUP + 1),
        grid=(4,),
        in_specs=[smem, smem, whole, whole]
        + [pl.BlockSpec((rows, block), lambda i: (0, i))] * 2
        + [pl.BlockSpec((1, block), lambda i: (0, i))],
        out_specs=[pl.BlockSpec((16, block), lambda i: (0, i))] * (GROUP + 1),
        compiler_params=params(),
        cost_estimate=cost(1, 1),
        name="global_rows",
    )(place, ids, own, other, key_raw, values, key_gain)


def pack_kernel(place_ref, tiles_ref, readers_ref, own_ref, other_ref, *refs):
    per = 6 + GROUP
    me, plane = place_ref[0], place_ref[1]
    query_inv, key_inv = inverses(own_ref[...], other_ref[...])
    rows = own_ref.shape[0]
    row = lax.broadcasted_iota(jnp.int32, (16, HEAD_DIM), 0)
    lane = lax.broadcasted_iota(jnp.int32, (16, HEAD_DIM), 1)
    facts = jnp.zeros((16, HEAD_DIM), jnp.int32)
    for tile in range(rows // TILE):
        start = tiles_ref[tile, 0] - (plane * GROUP - 1) * (rows // TILE)
        facts = jnp.where(row == 1 + tile, start, facts)
    for e in range(GROUP):
        for j in range(GROUP):
            live = readers_ref[0, (plane ^ e) * GROUP + j]
            chosen = (row == 0) & (lane // G_DEV == GROUP * j + e)
            facts = jnp.where(chosen, live, facts)
    facts = facts.astype(F32).astype(BF16)
    refs[-1][...] = jnp.zeros((8, HEAD_DIM), F32)
    for d in range(GROUP):
        key, value, query, grad, key_gain, query_gain, *parts = refs[per * d : per * d + per]
        out = refs[per * GROUP + d]
        out[0:rows] = (key[...].astype(F32) * key_inv * key_gain[...]).astype(BF16)
        out[rows : 2 * rows] = value[...]
        out[2 * rows : 3 * rows] = (
            query[...].astype(F32) * query_inv * query_gain[...]
        ).astype(BF16)
        out[3 * rows : 4 * rows] = grad[...]
        out[4 * rows : 4 * rows + 16] = facts
        out[4 * rows + 16 :] = sum(part[...].astype(F32) for part in parts).astype(BF16)


def pack(place, tiles, readers, own, other, arrays, gains, parts, first, count, after):
    query_raw, key_raw, values, out_grad = arrays
    query_gain, key_gain = gains
    rows, width = query_raw.shape
    each = width // HEAD_DIM // GROUP
    smem = pl.BlockSpec(memory_space=pltpu.SMEM)
    whole = pl.BlockSpec((rows, HEAD_DIM), lambda h, place: (0, 0))
    specs, operands = [], []
    for d in range(GROUP):
        at = lambda h, place, d=d: (0, (place[0] ^ d) * each + first + h)
        specs += [pl.BlockSpec((rows, HEAD_DIM), at)] * 4
        specs += [pl.BlockSpec((1, HEAD_DIM), at)] * 2
        specs += [pl.BlockSpec((16, HEAD_DIM), at)] * GROUP
        operands += [key_raw, values, query_raw, out_grad, key_gain, query_gain, *parts]
    out_rows = 4 * rows + FACTS
    return pl.pallas_call(
        behind(pack_kernel, 5 + len(specs), len(after)),
        out_shape=[jax.ShapeDtypeStruct((out_rows, count * HEAD_DIM), BF16)] * GROUP
        + [jax.ShapeDtypeStruct((8, HEAD_DIM), F32)],
        grid_spec=pltpu.PrefetchScalarGridSpec(
            num_scalar_prefetch=1,
            grid=(count,),
            in_specs=[smem, smem, whole, whole] + specs + [ANY] * len(after),
            out_specs=[pl.BlockSpec((out_rows, HEAD_DIM), lambda h, place: (0, h))] * GROUP
            + [pl.BlockSpec((8, HEAD_DIM), lambda h, place: (0, 0))],
        ),
        compiler_params=params(),
        cost_estimate=cost(1, 1),
        name="pack",
    )(place, tiles, readers, own, other, *operands, *after)


def edges_kernel(place_ref, b0, b1, b2, b3, near_ref, far_ref, token):
    me, plane = place_ref[0], place_ref[1]
    token[...] = jnp.zeros((8, HEAD_DIM), F32)
    even = plane % 2 == 0
    last, first = me ^ (GROUP - 1), me
    for d, block in enumerate((b0, b1, b2, b3)):

        @pl.when(jnp.where(even, last, first) == d)
        def _(block=block):
            near_ref[...] = block[...]

        @pl.when(jnp.where(even, first, last) == d)
        def _(block=block):
            far_ref[...] = block[...]


def edges(place, blocks, after):
    out_rows, width = blocks[0].shape
    rows = (out_rows - FACTS) // 4
    whole = pl.BlockSpec((2 * rows, width), lambda i, place: (0, 0))
    return pl.pallas_call(
        behind(edges_kernel, 1 + GROUP, len(after)),
        out_shape=[jax.ShapeDtypeStruct((2 * rows, width), BF16)] * 2
        + [jax.ShapeDtypeStruct((8, HEAD_DIM), F32)],
        grid_spec=pltpu.PrefetchScalarGridSpec(
            num_scalar_prefetch=1,
            grid=(1,),
            in_specs=[whole] * GROUP + [ANY] * len(after),
            out_specs=[whole] * 2 + [pl.BlockSpec((8, HEAD_DIM), lambda i, place: (0, 0))],
        ),
        compiler_params=params(),
        cost_estimate=cost(1, 1),
        name="edges",
    )(place, *blocks, *after)


def attend_kernel(outer, place_ref, b0, b1, b2, b3, *refs):
    if outer:
        near, far, dq_out, acc_out, g_out, near_out, far_out = refs[:7]
    else:
        dq_out, acc_out, g_out = refs[:3]
    pair, weights, sums, raw_g, pair_g, sums_g, facts_at = refs[-7:]
    me, plane = place_ref[0], place_ref[1]
    rows = (b0.shape[0] - FACTS) // 4
    tiles = rows // TILE
    keys = slice(0, HEAD_DIM)
    vals = slice(HEAD_DIM, 2 * HEAD_DIM)

    @pl.when(pl.program_id(0) == 0)
    def _():
        weights[...] = jnp.zeros_like(weights)

    for d, block in enumerate((b0, b1, b2, b3)):
        j = me ^ d
        at = pl.multiple_of((j + 1) * rows, TILE)
        pair[pl.ds(at, rows), keys] = block[0:rows]
        pair[pl.ds(at, rows), vals] = block[rows : 2 * rows]
        for tile in range(tiles):
            here = 2 * rows + tile * TILE
            weights[j * tiles + tile, :TILE, keys] = block[here : here + TILE]
            weights[j * tiles + tile, TILE:, vals] = block[here + rows : here + rows + TILE]
        facts_at[j] = block[4 * rows : 4 * rows + 16].astype(F32)
        extra = block[4 * rows + 16 :].astype(F32)
        eight = pl.ds(pl.multiple_of(8 * j, 8), 8)
        raw_g[eight, keys] = extra[:8]
        raw_g[eight, vals] = extra[8:]
    pair_g[...] = raw_g[...].astype(BF16)
    if outer:
        even = plane % 2 == 0
        top = (GROUP + 1) * rows
        near_at = pl.multiple_of(jnp.where(even, top, 0), TILE)
        far_at = pl.multiple_of(jnp.where(even, 0, top), TILE)
        for ref, at in ((near, near_at), (far, far_at)):
            pair[pl.ds(at, rows), keys] = ref[0:rows]
            pair[pl.ds(at, rows), vals] = ref[rows : 2 * rows]
    sums[...] = jnp.zeros_like(sums)
    sums_g[...] = jnp.zeros_like(sums_g)
    count_g = pair_g.shape[0]
    row = lax.broadcasted_iota(jnp.int32, (count_g, HEAD_DIM), 0)
    lane = lax.broadcasted_iota(jnp.int32, (count_g, HEAD_DIM), 1)
    span = 4 * TILE
    units = []
    for j in (0, GROUP - 1) if outer else range(1, GROUP - 1):
        facts = facts_at[j]
        live = jnp.sum(jnp.where(row == lane, facts[0:1], 0.0), axis=1, keepdims=True) > 0.0
        for tile in range(tiles):
            start = jnp.max(facts[1 + tile : 2 + tile]).astype(jnp.int32)
            units.append((j * tiles + tile, pl.multiple_of(start * TILE, TILE), live))

    def products(unit):
        weight, at, _ = units[unit]
        both = jnp.concatenate([pair[pl.ds(at, span)], pair_g[...]], axis=0)
        return contract(both, weights[weight], ((1,), (1,)))

    ahead = products(0)
    for unit, (weight, at, live) in enumerate(units):
        product = ahead
        if unit + 1 < len(units):
            ahead = products(unit + 1)
        score = product[:, :TILE] * (FACTOR * LOG2_E)
        dprob = product[:, TILE:]
        score_g = jnp.where(live, score[span:], -jnp.inf)
        score = jnp.concatenate([score[:span], score_g], axis=0)
        largest = jnp.max(score, axis=0, keepdims=True)
        probs = jnp.exp2(score - largest)
        probs = probs * (1.0 / jnp.sum(probs, axis=0, keepdims=True))
        delta = jnp.sum(probs * dprob, axis=0, keepdims=True)
        dscore = (probs * ((dprob - delta) * FACTOR)).astype(BF16)
        grads = contract(
            jnp.concatenate([dscore, probs.astype(BF16)], axis=1), weights[weight], ((1,), (0,))
        )
        sums[pl.ds(at, span)] += grads[:span]
        sums_g[...] += grads[span:]
        both = jnp.concatenate([pair[pl.ds(at, span), keys], pair_g[:, keys]], axis=0)
        grad_query = contract(dscore, both, ((0,), (0,)))
        dq_out[unit * TILE : (unit + 1) * TILE] = grad_query.astype(BF16)
    acc_out[...] = sums[rows : (GROUP + 1) * rows].astype(BF16)
    g_out[...] = sums_g[...]
    if outer:
        for out, at in ((near_out, near_at), (far_out, far_at)):
            out[:rows] = sums[pl.ds(at, rows), keys].astype(BF16)
            out[rows : 2 * rows] = sums[pl.ds(at, rows), vals].astype(BF16)


def attend(place, blocks, halo, after):
    out_rows, width = blocks[0].shape
    rows = (out_rows - FACTS) // 4
    at = lambda h, place: (0, h)
    tall = pl.BlockSpec((out_rows, HEAD_DIM), at)
    edge = pl.BlockSpec((2 * rows, HEAD_DIM), at)
    wide = 2 * HEAD_DIM
    edge_shape = jax.ShapeDtypeStruct((2 * rows, width), BF16)
    return pl.pallas_call(
        behind(
            functools.partial(attend_kernel, len(halo) > 0), 1 + GROUP + len(halo), len(after)
        ),
        out_shape=[
            edge_shape,
            jax.ShapeDtypeStruct((GROUP * rows, 2 * width), BF16),
            jax.ShapeDtypeStruct((8 * GROUP, 2 * width), F32),
        ]
        + [edge_shape] * len(halo),
        grid_spec=pltpu.PrefetchScalarGridSpec(
            num_scalar_prefetch=1,
            grid=(width // HEAD_DIM,),
            in_specs=[tall] * GROUP + [edge] * len(halo) + [ANY] * len(after),
            out_specs=[
                edge,
                pl.BlockSpec((GROUP * rows, wide), at),
                pl.BlockSpec((8 * GROUP, wide), at),
            ]
            + [edge] * len(halo),
            scratch_shapes=[
                pltpu.VMEM(((GROUP + 2) * rows, wide), BF16),
                pltpu.VMEM((GROUP * rows // TILE, 2 * TILE, wide), BF16),
                pltpu.VMEM(((GROUP + 2) * rows, wide), F32),
                pltpu.VMEM((8 * GROUP, wide), F32),
                pltpu.VMEM((8 * GROUP, wide), BF16),
                pltpu.VMEM((8 * GROUP, wide), F32),
                pltpu.VMEM((GROUP, 16, HEAD_DIM), F32),
            ],
        ),
        compiler_params=params(),
        cost_estimate=cost(1, 1),
        name="outer" if halo else "inner",
    )(place, *blocks, *halo, *after)


def settle_kernel(
    place_ref, dq_in, acc_in, g_in, dq_out, acc_out, g_out, near, far, o0, o1, o2, o3, token,
    total_g,
):
    me, plane = place_ref[0], place_ref[1]
    token[...] = jnp.zeros((8, HEAD_DIM), F32)
    rows = dq_in.shape[0] // 2
    even = plane % 2 == 0
    inner = (plane == 1) | (plane == 2)
    total_g[...] = g_in[...] + g_out[...]
    for d, out in enumerate((o0, o1, o2, o3)):
        j = me ^ d
        near_here = j == jnp.where(even, GROUP - 1, 0)
        far_here = (j == jnp.where(even, 0, GROUP - 1)) & inner
        outside = (j == 0) | (j == GROUP - 1)

        @pl.when(outside)
        def _(out=out, j=j):
            out[:rows] = dq_out[pl.ds(pl.multiple_of(jnp.where(j == 0, 0, rows), TILE), rows)]

        @pl.when(~outside)
        def _(out=out, j=j):
            out[:rows] = dq_in[pl.ds(pl.multiple_of(jnp.where(j == 1, 0, rows), TILE), rows)]

        here = pl.ds(pl.multiple_of(j * rows, TILE), rows)
        for i in range(2):
            lanes = slice(i * HEAD_DIM, (i + 1) * HEAD_DIM)
            rest = slice(i * rows, (i + 1) * rows)
            total = acc_in[here, lanes].astype(F32) + acc_out[here, lanes].astype(F32)
            total = total + jnp.where(near_here, near[rest].astype(F32), 0.0)
            total = total + jnp.where(far_here, far[rest].astype(F32), 0.0)
            out[(i + 1) * rows : (i + 2) * rows] = total.astype(BF16)
        eight = pl.ds(pl.multiple_of(8 * j, 8), 8)
        both = total_g[eight]
        out[3 * rows :] = jnp.concatenate(
            [both[:, :HEAD_DIM], both[:, HEAD_DIM:]], axis=0
        ).astype(BF16)


def settle(place, inner, outer, near, far, after):
    rows, width = inner[0].shape
    rows = rows // 2
    at = lambda h, place: (0, h)
    wide = 2 * HEAD_DIM
    edge = pl.BlockSpec((2 * rows, HEAD_DIM), at)
    part = [edge, pl.BlockSpec((GROUP * rows, wide), at), pl.BlockSpec((8 * GROUP, wide), at)]
    return pl.pallas_call(
        behind(settle_kernel, 9, len(after)),
        out_shape=[jax.ShapeDtypeStruct((3 * rows + EXTRA, width), BF16)] * GROUP
        + [jax.ShapeDtypeStruct((8, HEAD_DIM), F32)],
        grid_spec=pltpu.PrefetchScalarGridSpec(
            num_scalar_prefetch=1,
            grid=(width // HEAD_DIM,),
            in_specs=part * 2 + [edge] * 2 + [ANY] * len(after),
            out_specs=[pl.BlockSpec((3 * rows + EXTRA, HEAD_DIM), at)] * GROUP
            + [pl.BlockSpec((8, HEAD_DIM), lambda h, place: (0, 0))],
            scratch_shapes=[pltpu.VMEM((8 * GROUP, wide), F32)],
        ),
        compiler_params=params(),
        cost_estimate=cost(1, 1),
        name="settle",
    )(place, *inner, *outer, near, far, *after)


def collect_kernel(chunks, place_ref, *refs):
    me = place_ref[0]
    out = refs[-1]
    each = out.shape[1] // GROUP
    for d in range(GROUP):
        first = 0
        for c, count in enumerate(chunks):
            at = pl.multiple_of((me ^ d) * each + first * HEAD_DIM, HEAD_DIM)
            out[:, pl.ds(at, count * HEAD_DIM)] = refs[c * GROUP + d][...]
            first += count


def collect(place, grads, width, chunks):
    flat = [x for chunk in grads for x in chunk]
    return pl.pallas_call(
        functools.partial(collect_kernel, chunks),
        out_shape=jax.ShapeDtypeStruct((EXTRA, width), BF16),
        grid_spec=pltpu.PrefetchScalarGridSpec(
            num_scalar_prefetch=1,
            grid=(1,),
            in_specs=[
                pl.BlockSpec(
                    (EXTRA, x.shape[1]),
                    lambda i, place, n=x.shape[0] // EXTRA - 1: (n, 0),
                )
                for x in flat
            ],
            out_specs=pl.BlockSpec((EXTRA, width), lambda i, place: (0, 0)),
        ),
        compiler_params=params(),
        cost_estimate=cost(1, 1),
        name="collect",
    )(place, *flat)


def global_sum(parts, row):
    return sum(
        part[row + 2 * e : row + 2 * e + 1].astype(F32) for e, part in enumerate(parts)
    )


def total_kernel(place_ref, ids_ref, raw_ref, gain_ref, p0, p1, p2, p3, *refs):
    out = refs[-1]
    rows = out.shape[0]
    device = place_ref[1] * GROUP + place_ref[0]
    total = refs[0][...]
    for ref in refs[1:-1]:
        total = total + ref[...]
    row = lax.broadcasted_iota(jnp.int32, (rows, HEAD_DIM), 0)
    lane = lax.broadcasted_iota(jnp.int32, (rows, HEAD_DIM), 1)
    parts = [p[...] for p in (p0, p1, p2, p3)]
    for r in range(G_DEV):
        raw = raw_ref[...].astype(F32)[r : r + 1]
        dot = jnp.sum(global_sum(parts, r) * gain_ref[...] * raw, axis=1, keepdims=True)
        here = (row == ids_ref[r] - device * rows) & (lane >= HEAD_DIM // 2)
        total = total + jnp.where(here, dot, 0.0)
    out[...] = total


def total_dots(place, ids, raw, gain, parts, dots):
    smem = pl.BlockSpec(memory_space=pltpu.SMEM)
    vmem = pl.BlockSpec(memory_space=pltpu.VMEM)
    return pl.pallas_call(
        total_kernel,
        out_shape=jax.ShapeDtypeStruct(dots[0].shape, F32),
        in_specs=[smem, smem] + [vmem] * (2 + GROUP + len(dots)),
        out_specs=vmem,
        compiler_params=params(),
        cost_estimate=cost(1, 1),
        name="total_dots",
    )(place, ids, raw, gain, *parts, *dots)


def dots_kernel(place_ref, *refs):
    out_ref = refs[-1]
    rows = out_ref.shape[0]
    step = pl.program_id(0)
    totals = [jnp.zeros((rows, HEAD_DIM), F32), jnp.zeros((rows, HEAD_DIM), F32)]
    for d in range(GROUP):
        grads, query, key, query_gain, key_gain = refs[5 * d : 5 * d + 5]
        totals[0] += grads[:rows].astype(F32) * query_gain[...] * query[...].astype(F32)
        totals[1] += grads[rows:].astype(F32) * key_gain[...] * key[...].astype(F32)
    part = lane_pair(
        jnp.sum(totals[0], axis=1, keepdims=True), jnp.sum(totals[1], axis=1, keepdims=True), rows
    )

    @pl.when(step == 0)
    def _():
        out_ref[...] = part

    @pl.when(step > 0)
    def _():
        out_ref[...] += part


def dots(place, grads, query_raw, key_raw, gains, first, after):
    rows, full = query_raw.shape
    count = grads[0].shape[1] // HEAD_DIM
    each = full // HEAD_DIM // GROUP
    specs, operands = [], []
    for d in range(GROUP):
        at = lambda h, place, d=d: (0, (place[0] ^ d) * each + first + h)
        specs += (
            [pl.BlockSpec((2 * rows, HEAD_DIM), lambda h, place: (0, h))]
            + [pl.BlockSpec((rows, HEAD_DIM), at)] * 2
            + [pl.BlockSpec((1, HEAD_DIM), at)] * 2
        )
        operands += [grads[d], query_raw, key_raw, gains[0], gains[1]]
    return pl.pallas_call(
        behind(dots_kernel, 1 + 5 * GROUP, len(after)),
        out_shape=jax.ShapeDtypeStruct((rows, HEAD_DIM), F32),
        grid_spec=pltpu.PrefetchScalarGridSpec(
            num_scalar_prefetch=1,
            grid=(count,),
            in_specs=specs + [ANY] * len(after),
            out_specs=pl.BlockSpec((rows, HEAD_DIM), lambda h, place: (0, 0)),
        ),
        compiler_params=params(),
        cost_estimate=cost(1, 16 * rows * count * HEAD_DIM * 2),
        name="dots",
    )(place, *operands, *after)


def finish_kernel(chunks, place_ref, ids_ref, own_ref, other_ref, dot_ref, dot_other_ref, *refs):
    me = place_ref[0]
    device = place_ref[1] * GROUP + me
    p0, p1, p2, p3, *refs = refs
    grads = refs[: GROUP * len(chunks)]
    query_ref, key_ref, query_gain, key_gain = refs[GROUP * len(chunks) : GROUP * len(chunks) + 4]
    query_out, key_out, value_out = refs[GROUP * len(chunks) + 4 :]
    rows, full = query_ref.shape
    each = full // GROUP
    inv = inverses(own_ref[...], other_ref[...])
    total = dot_ref[...] + dot_other_ref[...]
    dot = (total[:, :1], total[:, HEAD_DIM // 2 : HEAD_DIM // 2 + 1])
    coeff = [inv[i] * inv[i] * inv[i] * (dot[i] / D) for i in range(2)]
    row = lax.broadcasted_iota(jnp.int32, (rows, HEAD_DIM), 0)
    hot = [row == ids_ref[r] - device * rows for r in range(G_DEV)]
    for d in range(GROUP):
        first = 0
        for c, count in enumerate(chunks):
            ref = grads[c * GROUP + d]
            for h in range(count):
                at = pl.multiple_of((me ^ d) * each + (first + h) * HEAD_DIM, HEAD_DIM)
                here = pl.ds(at, HEAD_DIM)
                col = slice(h * HEAD_DIM, (h + 1) * HEAD_DIM)
                parts = [p[:, here] for p in (p0, p1, p2, p3)]
                grad = [ref[i * rows : (i + 1) * rows, col].astype(F32) for i in range(3)]
                for i in (1, 2):
                    for r in range(G_DEV):
                        more = global_sum(parts, 8 * (i - 1) + r)
                        grad[i] = grad[i] + jnp.where(hot[r], more, 0.0)
                for i, (raw, gain, out) in enumerate(
                    ((query_ref, query_gain, query_out), (key_ref, key_gain, key_out))
                ):
                    out[:, here] = (
                        inv[i] * (grad[i] * gain[:, here]) - raw[:, here].astype(F32) * coeff[i]
                    ).astype(BF16)
                value_out[:, here] = grad[2].astype(BF16)
            first += count


def finish(place, ids, own, other, dot, dot_other, parts, grads, query_raw, key_raw, gains, chunks):
    vmem = pl.BlockSpec(memory_space=pltpu.VMEM)
    smem = pl.BlockSpec(memory_space=pltpu.SMEM)
    flat = [x for chunk in grads for x in chunk]
    return pl.pallas_call(
        functools.partial(finish_kernel, chunks),
        out_shape=[jax.ShapeDtypeStruct(query_raw.shape, BF16)] * 3,
        in_specs=[smem, smem] + [vmem] * (4 + GROUP + len(flat) + 4),
        out_specs=[vmem] * 3,
        compiler_params=params(),
        cost_estimate=cost(1, 1),
        name="finish",
    )(place, ids, own, other, dot, dot_other, *parts, *flat, query_raw, key_raw, *gains)


def swap_heads(x):
    return lax.ppermute(x, "head", [(0, 1), (1, 0)])


def plane_body(
    query_raw, key_raw, values, out_grad, query_gain, key_gain, key_tiles, global_ids, readers
):
    device = lax.axis_index("ctx")
    place = jnp.stack([device % GROUP, device // GROUP]).astype(jnp.int32)
    gains = (query_gain[None, :], key_gain[None, :])
    own = squares(query_raw, key_raw)
    other = swap_heads(own)
    arrays = (query_raw, key_raw, values, out_grad)
    *sent, raw_rows = global_rows(place, global_ids, own, other, key_raw, values, gains[1])
    parts = [sent[0]] + [swapped(sent[e], 4 * e) for e in range(1, GROUP)]
    chunks = len(CHUNKS)
    firsts = [sum(CHUNKS[:c]) for c in range(chunks)]
    packed, token = [], ()
    for first, count in zip(firsts, CHUNKS):
        *sent, last = pack(
            place, key_tiles, readers, own, other, arrays, gains, parts, first, count, token
        )
        token = (last,)
        packed.append([sent[0]] + [swapped(sent[d], d) for d in range(1, GROUP)])
    edge, inner, outer, back, home, dot = ({} for _ in range(6))

    def begin(c, token):
        near, far, last = edges(place, packed[c], token)
        edge[c] = (swapped(near, 4), swapped_edges(far))
        return (last,)

    def inside(c, token):
        inner[c] = attend(place, packed[c], (), token)
        return (inner[c][2],)

    def outside(c, token):
        *outer[c], near, far = attend(place, packed[c], edge[c], token)
        back[c] = (swapped(near, 4), swapped_edges(far))
        return (outer[c][2],)

    def end(c, token):
        *sent, last = settle(place, inner[c], outer[c], *back[c], token)
        home[c] = [sent[0]] + [swapped(sent[d], d) for d in range(1, GROUP)]
        return (last,)

    def score(c, token):
        dot[c] = dots(place, home[c], query_raw, key_raw, gains, firsts[c], token)
        return (dot[c],)

    stages = {"b": begin, "i": inside, "g": outside, "e": end, "s": score}
    for step in " ".join(ORDER).split():
        name, *extra = step.split(":")
        held = tuple((packed if e[0] == "i" else home)[int(e[1])]["oxyd".index(e[2])] for e in extra)
        token = stages[name[0]](int(name[1]), token + held)
    homes = [home[c] for c in range(chunks)]
    mine = collect(place, homes, query_raw.shape[1], CHUNKS)
    parts = [mine] + [swapped(mine, 4 * e) for e in range(1, GROUP)]
    total = total_dots(
        place, global_ids, raw_rows, gains[1], parts, [dot[c] for c in range(chunks)]
    )
    return tuple(
        finish(
            place, global_ids, own, other, total, swap_heads(total), parts, homes,
            query_raw, key_raw, gains, CHUNKS,
        )
    )


def passed_along(shard, axis, by):
    count = lax.axis_size(axis)
    return lax.ppermute(shard, axis, [(i, (i + by) % count) for i in range(count)])


def normalize(as_float, gain, squares):
    inverse = lax.rsqrt(squares[:, None] / D + EPSILON)
    return (inverse, (as_float * inverse * gain).astype(jnp.bfloat16))


def norm_grad(as_float, inverse, scaled, coeffs):
    return (inverse * scaled - as_float * inverse**3 * (coeffs[:, None] / D)).astype(jnp.bfloat16)


def body(
    query_raw, key_raw, values, out_grad, query_gain, key_gain, key_tiles, global_ids, readers
):
    tokens_here, width_here = query_raw.shape
    heads_here = width_here // HEAD_DIM
    tiles_here = tokens_here // TILE
    factor = HEAD_DIM ** (-0.5)
    device = lax.axis_index("ctx")
    query_rows = query_raw.astype(jnp.float32)
    key_rows = key_raw.astype(jnp.float32)
    query_sq, key_sq = lax.psum(
        (jnp.sum(query_rows * query_rows, axis=1), jnp.sum(key_rows * key_rows, axis=1)), "head"
    )
    query_inv, query_norm = normalize(query_rows, query_gain, query_sq)
    key_inv, key_norm = normalize(key_rows, key_gain, key_sq)
    own_rows = global_ids - device * tokens_here
    own_pair = jnp.stack([key_norm[own_rows], values[own_rows]])
    global_pair = lax.all_gather(own_pair, "ctx", axis=1, tiled=True)
    global_keys = global_pair[0].reshape(-1, heads_here, HEAD_DIM)
    global_vals = global_pair[1].reshape(-1, heads_here, HEAD_DIM)
    live_mask = jnp.repeat(readers[0] > 0, G_DEV)
    key_value = jnp.stack([key_norm, values])
    current = passed_along(key_value, "ctx", -REACH)
    pieces = [current]
    for hop_index in range(2 * REACH):
        current = passed_along(current, "ctx", 1)
        pieces.append(current)
    pieces = pieces[::-1]
    window_pair = jnp.concatenate(pieces, axis=1)
    first_tile = (device - REACH) * tiles_here
    local_tiles = key_tiles - first_tile
    window_rows = (
        local_tiles[:, :, None] * TILE + jnp.arange(TILE, dtype=jnp.int32)[None, None, :]
    ).reshape(tiles_here, -1)
    window_count = window_rows.shape[1]
    window_keys = window_pair[0][window_rows].reshape(
        tiles_here, window_count, heads_here, HEAD_DIM
    )
    window_vals = window_pair[1][window_rows].reshape(
        tiles_here, window_count, heads_here, HEAD_DIM
    )
    query_four = query_norm.reshape(tiles_here, TILE, heads_here, HEAD_DIM)
    grad_four = out_grad.reshape(tiles_here, TILE, heads_here, HEAD_DIM)

    def head_block(head_number):
        query_head = lax.dynamic_index_in_dim(query_four, head_number, 2, keepdims=False)
        grad_head = lax.dynamic_index_in_dim(grad_four, head_number, 2, keepdims=False)
        wkeys = lax.dynamic_index_in_dim(window_keys, head_number, 2, keepdims=False)
        wvals = lax.dynamic_index_in_dim(window_vals, head_number, 2, keepdims=False)
        gkeys = lax.dynamic_index_in_dim(global_keys, head_number, 1, keepdims=False)
        gvals = lax.dynamic_index_in_dim(global_vals, head_number, 1, keepdims=False)
        score_window = (
            jnp.einsum("tqd,tkd->tqk", query_head, wkeys, preferred_element_type=jnp.float32)
            * factor
        )
        score_global = (
            jnp.einsum("tqd,kd->tqk", query_head, gkeys, preferred_element_type=jnp.float32)
            * factor
        )
        score_global = jnp.where(live_mask, score_global, -jnp.inf)
        scores = jnp.concatenate([score_window, score_global], axis=2)
        largest = jnp.max(scores, axis=2, keepdims=True)
        log_total = largest + jnp.log(jnp.sum(jnp.exp(scores - largest), axis=2, keepdims=True))
        probs = jnp.exp(scores - log_total)
        probs_low = probs.astype(jnp.bfloat16)
        attended = jnp.einsum(
            "tqk,tkd->tqd", probs_low[..., :window_count], wvals, preferred_element_type=jnp.float32
        )
        attended = attended + jnp.einsum(
            "tqk,kd->tqd", probs_low[..., window_count:], gvals, preferred_element_type=jnp.float32
        )
        attended = lax.optimization_barrier(attended.astype(jnp.bfloat16))
        delta_rows = jnp.sum(grad_head.astype(jnp.float32) * attended.astype(jnp.float32), axis=2)
        dprob = jnp.concatenate(
            [
                jnp.einsum("tqd,tkd->tqk", grad_head, wvals, preferred_element_type=jnp.float32),
                jnp.einsum("tqd,kd->tqk", grad_head, gvals, preferred_element_type=jnp.float32),
            ],
            axis=2,
        )
        dscore = (probs * (dprob - delta_rows[..., None]) * factor).astype(jnp.bfloat16)
        grad_query = jnp.einsum(
            "tqk,tkd->tqd", dscore[..., :window_count], wkeys, preferred_element_type=jnp.float32
        )
        grad_query = grad_query + jnp.einsum(
            "tqk,kd->tqd", dscore[..., window_count:], gkeys, preferred_element_type=jnp.float32
        )
        window_dk = jnp.einsum(
            "tqk,tqd->tkd",
            dscore[..., :window_count],
            query_head,
            preferred_element_type=jnp.float32,
        )
        window_dv = jnp.einsum(
            "tqk,tqd->tkd",
            probs_low[..., :window_count],
            grad_head,
            preferred_element_type=jnp.float32,
        )
        global_dk = jnp.einsum(
            "tqk,tqd->kd",
            dscore[..., window_count:],
            query_head,
            preferred_element_type=jnp.float32,
        )
        global_dv = jnp.einsum(
            "tqk,tqd->kd",
            probs_low[..., window_count:],
            grad_head,
            preferred_element_type=jnp.float32,
        )
        return (grad_query, window_dk, window_dv, global_dk, global_dv)

    head_results = lax.map(head_block, jnp.arange(heads_here, dtype=jnp.int32))
    grad_query = jnp.moveaxis(head_results[0], 0, 2).reshape(tokens_here, width_here)
    window_dk = jnp.moveaxis(head_results[1], 0, 2).reshape(-1, width_here)
    window_dv = jnp.moveaxis(head_results[2], 0, 2).reshape(-1, width_here)
    global_dk = jnp.moveaxis(head_results[3], 0, 1).reshape(-1, width_here)
    global_dv = jnp.moveaxis(head_results[4], 0, 1).reshape(-1, width_here)
    window_grads = jnp.zeros((2, window_pair.shape[1], width_here), jnp.float32)
    window_grads = window_grads.at[:, window_rows.reshape(-1)].add(
        jnp.stack([window_dk, window_dv])
    )
    spread_grads = window_grads.reshape(2, 2 * REACH + 1, tokens_here, width_here)
    slots = [spread_grads[:, slot_index] for slot_index in range(2 * REACH + 1)]
    carried = slots[2 * REACH]
    for hop_index in range(2 * REACH):
        carried = (
            passed_along(carried.astype(jnp.bfloat16), "ctx", 1).astype(carried.dtype)
            + slots[2 * REACH - 1 - hop_index]
        )
    home_grads = passed_along(carried.astype(jnp.bfloat16), "ctx", -REACH).astype(carried.dtype)
    global_part = lax.psum_scatter(
        jnp.stack([global_dk, global_dv]), "ctx", scatter_dimension=1, tiled=True
    )
    home_grads = home_grads.at[:, own_rows].add(global_part)
    scaled_query = grad_query * query_gain
    scaled_key = home_grads[0] * key_gain
    query_dot, key_dot = lax.psum(
        (jnp.sum(scaled_query * query_rows, axis=1), jnp.sum(scaled_key * key_rows, axis=1)), "head"
    )
    query_grad = norm_grad(query_rows, query_inv, scaled_query, query_dot)
    key_grad = norm_grad(key_rows, key_inv, scaled_key, key_dot)
    return (query_grad, key_grad, home_grads[1].astype(jnp.bfloat16))


def solution(mesh):
    sizes = dict(mesh.shape)
    planes = sizes["ctx"] == GROUP * GROUP and sizes["head"] == 2
    return jax.shard_map(
        plane_body if planes else body,
        mesh=mesh,
        in_specs=(
            P("ctx", "head"),
            P("ctx", "head"),
            P("ctx", "head"),
            P("ctx", "head"),
            P("head"),
            P("head"),
            P("ctx", None),
            P("ctx"),
            P("ctx", None),
        ),
        out_specs=(P("ctx", "head"), P("ctx", "head"), P("ctx", "head")),
        check_vma=False,
    )
```

time: 185 us -> 156 us (0.84)
  waiting for transfers between devices: 63.2 us -> 37.7 us
  Pallas kernels: 63.1 us -> 56.6 us
  starting transfers between devices: 54.8 us -> 57.5 us
    ppermute x36 -> x30, waiting for transfers between devices: 61 us -> 35.5 us  [swapped(): return lax.ppermute(shard, 'ctx', [(i, i ^ bit) for i in range(count)])]
    pallas_call x15 -> x21, Pallas kernels: 57.3 us -> 49.5 us  [the longest x6 26.4 us: attend(): pl.pallas_call(behind(functools.partial(attend_kernel, len(halo) > 0), 1...]
    ppermute x0 -> x6, starting transfers between devices: none -> 4.38 us  [swapped_edges(): return lax.ppermute(shard, 'ctx', pairs)]
    ppermute x36 -> x30, starting transfers between devices: 54.2 us -> 52.6 us  [swapped(): return lax.ppermute(shard, 'ctx', [(i, i ^ bit) for i in range(count)])]
  transfers between devices with their start and end apart: 38 -> 38, of which waited for: 11 -> 15; matrix products, arithmetic and copies ran while one was open for 0% -> 0% of each run, Pallas kernels for 28% -> 25%
where the time goes in v2:
time: 156 us
  starting transfers between devices  57.5 us (37%)
  Pallas kernels  56.6 us (36%)
  waiting for transfers between devices  37.7 us (24%)
  local copies, waits for them, and re-layouts  2.67 us (2%)
    ppermute x30, starting transfers between devices, swapped(): return lax.ppermute(shard, 'ctx', [(i, i ^ bit) for i in range(count)])  52.6 us
    ppermute x30, waiting for transfers between devices, swapped(): return lax.ppermute(shard, 'ctx', [(i, i ^ bit) for i in range(count)])  35.5 us
    pallas_call x6, Pallas kernels, attend(): pl.pallas_call(behind(functools.partial(attend_kernel, len(halo) > 0), 1...  26.4 us
    pallas_call x3, Pallas kernels, pack(): pl.pallas_call(behind(pack_kernel, 5 + len(specs), len(after)), out_shape...  8.45 us
    pallas_call x1, Pallas kernels, finish(): pl.pallas_call(functools.partial(finish_kernel, chunks), out_shape=[jax.S...  6.03 us
    pallas_call x3, Pallas kernels, settle(): pl.pallas_call(behind(settle_kernel, 9, len(after)), out_shape=[jax.Shape...  5.03 us
    ppermute x6, starting transfers between devices, swapped_edges(): return lax.ppermute(shard, 'ctx', pairs)  4.38 us
    pallas_call x3, Pallas kernels, dots(): pl.pallas_call(behind(dots_kernel, 1 + 5 * GROUP, len(after)), out_shape=...  4.3 us
  transfers between devices with their start and end apart: 38, of which 15 were waited for; matrix products, arithmetic and copies ran while one was open for 0% of the time, Pallas kernels for 25%

profile of v2, /device:TPU:0, one launch (start us, length us, event | category | flops | bytes accessed | tf_op | source)
XLA Modules:
  0.0 155.7 jit_solution(16207982540864732814)
XLA Ops:
  0.6 1.3 copy-done
  2.0 1.3 copy-done.2
  5.9 2.2 %global_rows.1 = (bf16[16,2560]{1,0:T(8,128)(2,1)S(1)}, bf16[16,2560]{1,0:T(8,128)(2,1)S(1)}, bf16[16,2560]{1,0:T(8,128)(2,1)S(1)}, bf16[16,2560]{1,0:T(8,128)(2,1)S(1)}, bf16[16,2560]{1,0:T(8,128)(2,1)S(1)}) custom-call(s32[2]{0:T(128)S(1)} %pad_add_fusion.place_ref.refs_0_, s32[2]{0:T(128)S(1)} %copy-done.7, f32[256,128]{1,0:T(8,128)S(1)} %squares.1.own_ref.refs_3_, ...), custom_call_target="tpu_custom_call" | custom-call | flops 1 | bytes 1 | tf_op jit(solution)/shard_map/global_rows/pallas_call | solution.py:137
  8.2 3.0 %collective-permute-start.1 = (bf16[16,2560]{1,0:T(8,128)(2,1)S(1)}, bf16[16,2560]{1,0:T(8,128)(2,1)S(1)}, u32[]{:S(2)}, u32[]{:S(2)}) collective-permute-start(bf16[16,2560]{1,0:T(8,128)(2,1)S(1)} %get-tuple-element.73), channel_id=1, source_target_pairs={{0,8},{2,10},{4,12},{6,14},{8,0},{10,2},{12,4},{14,6},{16,24},{18,... | collective-permute-start | bytes 245768 | tf_op jit(solution)/shard_map/ppermute | solution.py:33
  11.2 2.6 %collective-permute-start.2 = (bf16[16,2560]{1,0:T(8,128)(2,1)S(1)}, bf16[16,2560]{1,0:T(8,128)(2,1)S(1)}, u32[]{:S(2)}, u32[]{:S(2)}) collective-permute-start(bf16[16,2560]{1,0:T(8,128)(2,1)S(1)} %get-tuple-element.74), channel_id=1, source_target_pairs={{0,16},{2,18},{4,20},{6,22},{8,24},{10,26},{12,28},{14,30},{16,0},... | collective-permute-start | bytes 245768 | tf_op jit(solution)/shard_map/ppermute | solution.py:33
  13.9 6.7 %collective-permute-done.2.refs_13_.refs_23_.refs_33_.refs_43_ = bf16[16,2560]{1,0:T(8,128)(2,1)S(1)} collective-permute-done((bf16[16,2560]{1,0:T(8,128)(2,1)S(1)}, bf16[16,2560]{1,0:T(8,128)(2,1)S(1)}, u32[]{:S(2)}, u32[]{:S(2)}) %collective-permute-start.2) | collective-permute-done | bytes 81952 | tf_op jit(solution)/shard_map/ppermute | solution.py:33
  20.7 3.4 %pack.3 = (bf16[1056,256]{1,0:T(8,128)(2,1)S(1)}, bf16[1056,256]{1,0:T(8,128)(2,1)S(1)}, bf16[1056,256]{1,0:T(8,128)(2,1)S(1)}, bf16[1056,256]{1,0:T(8,128)(2,1)S(1)}, f32[8,128]{1,0:T(8,128)S(1)}) custom-call(s32[2]{0:T(128)S(1)} %pad_add_fusion.place_ref.refs_0_, s32[2,4]{1,0:T(2,128)S(1)} %copy-done.5, s32[1,16]{1,0:T(1,128)S(1)} %copy-done.6, ...), custom_call_target="tpu_custom_call" | custom-call | flops 1 | bytes 1 | tf_op jit(solution)/shard_map/pack/pallas_call | solution.py:197
  24.0 1.6 %collective-permute-start.4 = (bf16[1056,256]{1,0:T(8,128)(2,1)S(1)}, bf16[1056,256]{1,0:T(8,128)(2,1)S(1)}, u32[]{:S(2)}, u32[]{:S(2)}) collective-permute-start(bf16[1056,256]{1,0:T(8,128)(2,1)S(1)} %get-tuple-element.77), channel_id=1, source_target_pairs={{0,2},{2,0},{4,6},{6,4},{8,10},{10,8},{12,14},{14,12},{16,18},{18,... | collective-permute-start | bytes 1622024 | tf_op jit(solution)/shard_map/ppermute | solution.py:33
  25.6 1.5 collective-permute-start.5
  27.6 3.3 %pack.4 = (bf16[1056,256]{1,0:T(8,128)(2,1)S(1)}, bf16[1056,256]{1,0:T(8,128)(2,1)S(1)}, bf16[1056,256]{1,0:T(8,128)(2,1)S(1)}, bf16[1056,256]{1,0:T(8,128)(2,1)S(1)}, f32[8,128]{1,0:T(8,128)S(1)}) custom-call(s32[2]{0:T(128)S(1)} %pad_add_fusion.place_ref.refs_0_, s32[2,4]{1,0:T(2,128)S(1)} %copy-done.5, s32[1,16]{1,0:T(1,128)S(1)} %copy-done.6, ...), custom_call_target="tpu_custom_call" | custom-call | flops 1 | bytes 1 | tf_op jit(solution)/shard_map/pack/pallas_call | solution.py:197
  30.9 1.6 %collective-permute-start.11 = (bf16[1056,256]{1,0:T(8,128)(2,1)S(1)}, bf16[1056,256]{1,0:T(8,128)(2,1)S(1)}, u32[]{:S(2)}, u32[]{:S(2)}) collective-permute-start(bf16[1056,256]{1,0:T(8,128)(2,1)S(1)} %get-tuple-element.95), channel_id=1, source_target_pairs={{0,2},{2,0},{4,6},{6,4},{8,10},{10,8},{12,14},{14,12},{16,18},{18,... | collective-permute-start | bytes 1622024 | tf_op jit(solution)/shard_map/ppermute | solution.py:33
  32.5 1.5 collective-permute-start.12
  34.0 5.3 %collective-permute-done.4.refs_2_ = bf16[1056,256]{1,0:T(8,128)(2,1)S(1)} collective-permute-done((bf16[1056,256]{1,0:T(8,128)(2,1)S(1)}, bf16[1056,256]{1,0:T(8,128)(2,1)S(1)}, u32[]{:S(2)}, u32[]{:S(2)}) %collective-permute-start.4) | collective-permute-done | bytes 540704 | tf_op jit(solution)/shard_map/ppermute | solution.py:33
  39.3 2.5 %collective-permute-start.13 = (bf16[1056,256]{1,0:T(8,128)(2,1)S(1)}, bf16[1056,256]{1,0:T(8,128)(2,1)S(1)}, u32[]{:S(2)}, u32[]{:S(2)}) collective-permute-start(bf16[1056,256]{1,0:T(8,128)(2,1)S(1)} %get-tuple-element.97), channel_id=1, source_target_pairs={{0,6},{2,4},{4,2},{6,0},{8,14},{10,12},{12,10},{14,8},{16,22},{18,... | collective-permute-start | bytes 1622024 | tf_op jit(solution)/shard_map/ppermute | solution.py:33
  41.8 1.8 %pack.5 = (bf16[1056,128]{1,0:T(8,128)(2,1)S(1)}, bf16[1056,128]{1,0:T(8,128)(2,1)S(1)}, bf16[1056,128]{1,0:T(8,128)(2,1)S(1)}, bf16[1056,128]{1,0:T(8,128)(2,1)S(1)}, f32[8,128]{1,0:T(8,128)S(1)}) custom-call(s32[2]{0:T(128)S(1)} %pad_add_fusion.place_ref.refs_0_, s32[2,4]{1,0:T(2,128)S(1)} %copy-done.5, s32[1,16]{1,0:T(1,128)S(1)} %copy-done.6, ...), custom_call_target="tpu_custom_call" | custom-call | flops 1 | bytes 1 | tf_op jit(solution)/shard_map/pack/pallas_call | solution.py:197
  43.6 8.8 %collective-permute-done.5.refs_3_ = bf16[1056,256]{1,0:T(8,128)(2,1)S(1)} collective-permute-done((bf16[1056,256]{1,0:T(8,128)(2,1)S(1)}, bf16[1056,256]{1,0:T(8,128)(2,1)S(1)}, u32[]{:S(2)}, u32[]{:S(2)}) %collective-permute-start.5) | collective-permute-done | bytes 540704 | tf_op jit(solution)/shard_map/ppermute | solution.py:33
  53.0 1.5 collective-permute-start.7
  55.2 5.1 %inner.3 = (bf16[512,256]{1,0:T(8,128)(2,1)S(1)}, bf16[1024,512]{1,0:T(8,128)(2,1)S(1)}, f32[32,512]{1,0:T(8,128)S(1)}) custom-call(s32[2]{0:T(128)S(1)} %pad_add_fusion.place_ref.refs_0_, bf16[1056,256]{1,0:T(8,128)(2,1)S(1)} %get-tuple-element.76.refs_1_, bf16[1056,256]{1,0:T(8,128)(2,1)S(1)} %collective-permute-done.4.refs_2_, ...), custom_call_target="tpu_custom_call" | custom-call | flops 1 | bytes 1 | tf_op jit(solution)/shard_map/inner/pallas_call | solution.py:346
  60.4 5.5 %outer.3 = (bf16[512,256]{1,0:T(8,128)(2,1)S(1)}, bf16[1024,512]{1,0:T(8,128)(2,1)S(1)}, f32[32,512]{1,0:T(8,128)S(1)}, bf16[512,256]{1,0:T(8,128)(2,1)S(1)}, bf16[512,256]{1,0:T(8,128)(2,1)S(1)}) custom-call(s32[2]{0:T(128)S(1)} %pad_add_fusion.place_ref.refs_0_, bf16[1056,256]{1,0:T(8,128)(2,1)S(1)} %get-tuple-element.76.refs_1_, ...), custom_call_target="tpu_custom_call" | custom-call | flops 1 | bytes 1 | tf_op jit(solution)/shard_map/outer/pallas_call | solution.py:346
  65.9 3.5 %collective-permute-start.9 = (bf16[512,256]{1,0:T(8,128)(2,1)S(1)}, bf16[512,256]{1,0:T(8,128)(2,1)S(1)}, u32[]{:S(2)}, u32[]{:S(2)}) collective-permute-start(bf16[512,256]{1,0:T(8,128)(2,1)S(1)} %get-tuple-element.92), channel_id=1, source_target_pairs={{0,8},{2,10},{4,12},{6,14},{8,0},{10,2},{12,4},{14,6},{16,24},{18,... | collective-permute-start | bytes 786440 | tf_op jit(solution)/shard_map/ppermute | solution.py:33
  71.1 2.8 %collective-permute-start.20 = (bf16[1056,128]{1,0:T(8,128)(2,1)S(1)}, bf16[1056,128]{1,0:T(8,128)(2,1)S(1)}, u32[]{:S(2)}, u32[]{:S(2)}) collective-permute-start(bf16[1056,128]{1,0:T(8,128)(2,1)S(1)} %get-tuple-element.110), channel_id=1, source_target_pairs={{0,4},{2,6},{4,0},{6,2},{8,12},{10,14},{12,8},{14,10},{16,20},{18,... | collective-permute-start | bytes 811016 | tf_op jit(solution)/shard_map/ppermute | solution.py:33
  73.9 1.2 collective-permute-done.13.refs_4_
  75.2 1.4 collective-permute-start.21
  77.2 1.5 collective-permute-start.17
  79.6 5.1 %inner.4 = (bf16[512,256]{1,0:T(8,128)(2,1)S(1)}, bf16[1024,512]{1,0:T(8,128)(2,1)S(1)}, f32[32,512]{1,0:T(8,128)S(1)}) custom-call(s32[2]{0:T(128)S(1)} %pad_add_fusion.place_ref.refs_0_, bf16[1056,256]{1,0:T(8,128)(2,1)S(1)} %get-tuple-element.94.refs_1_, bf16[1056,256]{1,0:T(8,128)(2,1)S(1)} %collective-permute-done.11.refs_2_, ...), custom_call_target="tpu_custom_call" | custom-call | flops 1 | bytes 1 | tf_op jit(solution)/shard_map/inner/pallas_call | solution.py:346
  84.7 2.0 %settle.3 = (bf16[784,256]{1,0:T(8,128)(2,1)S(1)}, bf16[784,256]{1,0:T(8,128)(2,1)S(1)}, bf16[784,256]{1,0:T(8,128)(2,1)S(1)}, bf16[784,256]{1,0:T(8,128)(2,1)S(1)}, f32[8,128]{1,0:T(8,128)S(1)}) custom-call(s32[2]{0:T(128)S(1)} %pad_add_fusion.place_ref.refs_0_, bf16[512,256]{1,0:T(8,128)(2,1)S(1)} %get-tuple-element.84.refs_1_, ...), custom_call_target="tpu_custom_call" | custom-call | flops 1 | bytes 1 | tf_op jit(solution)/shard_map/settle/pallas_call | solution.py:428
  87.9 2.0 %collective-permute-start.15 = (bf16[784,256]{1,0:T(8,128)(2,1)S(1)}, bf16[784,256]{1,0:T(8,128)(2,1)S(1)}, u32[]{:S(2)}, u32[]{:S(2)}) collective-permute-start(bf16[784,256]{1,0:T(8,128)(2,1)S(1)} %get-tuple-element.102), channel_id=1, source_target_pairs={{0,4},{2,6},{4,0},{6,2},{8,12},{10,14},{12,8},{14,10},{16,20},{18,... | collective-permute-start | bytes 1204232 | tf_op jit(solution)/shard_map/ppermute | solution.py:33
  91.0 5.5 %outer.4 = (bf16[512,256]{1,0:T(8,128)(2,1)S(1)}, bf16[1024,512]{1,0:T(8,128)(2,1)S(1)}, f32[32,512]{1,0:T(8,128)S(1)}, bf16[512,256]{1,0:T(8,128)(2,1)S(1)}, bf16[512,256]{1,0:T(8,128)(2,1)S(1)}) custom-call(s32[2]{0:T(128)S(1)} %pad_add_fusion.place_ref.refs_0_, bf16[1056,256]{1,0:T(8,128)(2,1)S(1)} %get-tuple-element.94.refs_1_, ...), custom_call_target="tpu_custom_call" | custom-call | flops 1 | bytes 1 | tf_op jit(solution)/shard_map/outer/pallas_call | solution.py:346
  96.5 3.2 %collective-permute-start.22 = (bf16[512,256]{1,0:T(8,128)(2,1)S(1)}, bf16[512,256]{1,0:T(8,128)(2,1)S(1)}, u32[]{:S(2)}, u32[]{:S(2)}) collective-permute-start(bf16[512,256]{1,0:T(8,128)(2,1)S(1)} %get-tuple-element.117), channel_id=1, source_target_pairs={{0,8},{2,10},{4,12},{6,14},{8,0},{10,2},{12,4},{14,6},{16,24},{18,... | collective-permute-start | bytes 786440 | tf_op jit(solution)/shard_map/ppermute | solution.py:33
  100.3 2.5 %inner.5 = (bf16[512,128]{1,0:T(8,128)(2,1)S(1)}, bf16[1024,256]{1,0:T(8,128)(2,1)S(1)}, f32[32,256]{1,0:T(8,128)S(1)}) custom-call(s32[2]{0:T(128)S(1)} %pad_add_fusion.place_ref.refs_0_, bf16[1056,128]{1,0:T(8,128)(2,1)S(1)} %get-tuple-element.108.refs_1_, bf16[1056,128]{1,0:T(8,128)(2,1)S(1)} %collective-permute-done.19.refs_2_, ...), custom_call_target="tpu_custom_call" | custom-call | flops 1 | bytes 1 | tf_op jit(solution)/shard_map/inner/pallas_call | solution.py:346
  103.8 1.7 %dots.3.refs_9_.refs_0_ = f32[256,128]{1,0:T(8,128)S(1)} custom-call(s32[2]{0:T(128)S(1)} %pad_add_fusion.place_ref.refs_0_, bf16[784,256]{1,0:T(8,128)(2,1)S(1)} %get-tuple-element.100.refs_1_.refs_0_.refs_4_, bf16[256,2560]{1,0:T(8,128)(2,1)S(1)} %copy-done.3, bf16[256,2560]{1,0:T(8,128)(2,1)S(1)} %copy-done.1, ...), custom_call_target="tpu_custom_call" | custom-call | flops 1 | bytes 1 | tf_op jit(solution)/shard_map/dots/pallas_call | solution.py:554
  105.5 2.0 %settle.4 = (bf16[784,256]{1,0:T(8,128)(2,1)S(1)}, bf16[784,256]{1,0:T(8,128)(2,1)S(1)}, bf16[784,256]{1,0:T(8,128)(2,1)S(1)}, bf16[784,256]{1,0:T(8,128)(2,1)S(1)}, f32[8,128]{1,0:T(8,128)S(1)}) custom-call(s32[2]{0:T(128)S(1)} %pad_add_fusion.place_ref.refs_0_, bf16[512,256]{1,0:T(8,128)(2,1)S(1)} %get-tuple-element.104.refs_1_, ...), custom_call_target="tpu_custom_call" | custom-call | flops 1 | bytes 1 | tf_op jit(solution)/shard_map/settle/pallas_call | solution.py:428
  108.4 1.5 collective-permute-start.25
  109.9 1.2 collective-permute-start.26
  111.1 2.4 %collective-permute-start.27 = (bf16[512,128]{1,0:T(8,128)(2,1)S(1)}, bf16[512,128]{1,0:T(8,128)(2,1)S(1)}, u32[]{:S(2)}, u32[]{:S(2)}) collective-permute-start(bf16[512,128]{1,0:T(8,128)(2,1)S(1)} %get-tuple-element.126), channel_id=1, source_target_pairs={{0,8},{2,10},{4,12},{6,14},{8,0},{10,2},{12,4},{14,6},{16,24},{18,... | collective-permute-start | bytes 393224 | tf_op jit(solution)/shard_map/ppermute | solution.py:33
  114.2 2.6 %collective-permute-done.27.refs_5_ = bf16[512,128]{1,0:T(8,128)(2,1)S(1)} collective-permute-done((bf16[512,128]{1,0:T(8,128)(2,1)S(1)}, bf16[512,128]{1,0:T(8,128)(2,1)S(1)}, u32[]{:S(2)}, u32[]{:S(2)}) %collective-permute-start.27) | collective-permute-done | bytes 131104 | tf_op jit(solution)/shard_map/ppermute | solution.py:33
  116.8 2.6 %outer.5 = (bf16[512,128]{1,0:T(8,128)(2,1)S(1)}, bf16[1024,256]{1,0:T(8,128)(2,1)S(1)}, f32[32,256]{1,0:T(8,128)S(1)}, bf16[512,128]{1,0:T(8,128)(2,1)S(1)}, bf16[512,128]{1,0:T(8,128)(2,1)S(1)}) custom-call(s32[2]{0:T(128)S(1)} %pad_add_fusion.place_ref.refs_0_, bf16[1056,128]{1,0:T(8,128)(2,1)S(1)} %get-tuple-element.108.refs_1_, ...), custom_call_target="tpu_custom_call" | custom-call | flops 1 | bytes 1 | tf_op jit(solution)/shard_map/outer/pallas_call | solution.py:346
  119.4 4.3 %collective-permute-start.29 = (bf16[512,128]{1,0:T(8,128)(2,1)S(1)}, bf16[512,128]{1,0:T(8,128)(2,1)S(1)}, u32[]{:S(2)}, u32[]{:S(2)}) collective-permute-start(bf16[512,128]{1,0:T(8,128)(2,1)S(1)} %get-tuple-element.132), channel_id=1, source_target_pairs={{0,8},{2,10},{4,12},{6,14},{8,0},{10,2},{12,4},{14,6},{16,24},{18,... | collective-permute-start | bytes 393224 | tf_op jit(solution)/shard_map/ppermute | solution.py:33
  124.6 1.8 %dots.4.refs_9_.refs_1_ = f32[256,128]{1,0:T(8,128)S(1)} custom-call(s32[2]{0:T(128)S(1)} %pad_add_fusion.place_ref.refs_0_, bf16[784,256]{1,0:T(8,128)(2,1)S(1)} %get-tuple-element.120.refs_1_.refs_4_.refs_8_, bf16[256,2560]{1,0:T(8,128)(2,1)S(1)} %copy-done.3, bf16[256,2560]{1,0:T(8,128)(2,1)S(1)} %copy-done.1, ...), custom_call_target="tpu_custom_call" | custom-call | flops 1 | bytes 1 | tf_op jit(solution)/shard_map/dots/pallas_call | solution.py:554
  128.5 1.8 %collective-permute-start.32 = (bf16[784,128]{1,0:T(8,128)(2,1)S(1)}, bf16[784,128]{1,0:T(8,128)(2,1)S(1)}, u32[]{:S(2)}, u32[]{:S(2)}) collective-permute-start(bf16[784,128]{1,0:T(8,128)(2,1)S(1)} %get-tuple-element.136), channel_id=1, source_target_pairs={{0,4},{2,6},{4,0},{6,2},{8,12},{10,14},{12,8},{14,10},{16,20},{18,... | collective-permute-start | bytes 602120 | tf_op jit(solution)/shard_map/ppermute | solution.py:33
  131.2 2.1 %collective-permute-done.31.refs_9_.refs_6_.refs_13_ = bf16[784,128]{1,0:T(8,128)(2,1)S(1)} collective-permute-done((bf16[784,128]{1,0:T(8,128)(2,1)S(1)}, bf16[784,128]{1,0:T(8,128)(2,1)S(1)}, u32[]{:S(2)}, u32[]{:S(2)}) %collective-permute-start.31) | collective-permute-done | bytes 200736 | tf_op jit(solution)/shard_map/ppermute | solution.py:33
  133.3 2.3 %collective-permute-done.32.refs_10_.refs_11_.refs_14_ = bf16[784,128]{1,0:T(8,128)(2,1)S(1)} collective-permute-done((bf16[784,128]{1,0:T(8,128)(2,1)S(1)}, bf16[784,128]{1,0:T(8,128)(2,1)S(1)}, u32[]{:S(2)}, u32[]{:S(2)}) %collective-permute-start.32) | collective-permute-done | bytes 200736 | tf_op jit(solution)/shard_map/ppermute | solution.py:33
  135.6 1.5 collective-permute-done.33.refs_11_.refs_16_.refs_15_
  137.6 2.2 %collective-permute-start.36 = (bf16[16,2560]{1,0:T(8,128)(2,1)S(1)}, bf16[16,2560]{1,0:T(8,128)(2,1)S(1)}, u32[]{:S(2)}, u32[]{:S(2)}) collective-permute-start(bf16[16,2560]{1,0:T(8,128)(2,1)S(1)} %collect.1.p0.refs_0_), channel_id=1, source_target_pairs={{0,24},{2,26},{4,28},{6,30},{8,16},{10,18},{12,20},{14,22},{16,8},... | collective-permute-start | bytes 245768 | tf_op jit(solution)/shard_map/ppermute | solution.py:33
  139.8 3.3 %collective-permute-start.35 = (bf16[16,2560]{1,0:T(8,128)(2,1)S(1)}, bf16[16,2560]{1,0:T(8,128)(2,1)S(1)}, u32[]{:S(2)}, u32[]{:S(2)}) collective-permute-start(bf16[16,2560]{1,0:T(8,128)(2,1)S(1)} %collect.1.p0.refs_0_), channel_id=1, source_target_pairs={{0,16},{2,18},{4,20},{6,22},{8,24},{10,26},{12,28},{14,30},{16,0},... | collective-permute-start | bytes 245768 | tf_op jit(solution)/shard_map/ppermute | solution.py:33
  144.0 2.4 %collective-permute-done.35.p2.refs_2_ = bf16[16,2560]{1,0:T(8,128)(2,1)S(1)} collective-permute-done((bf16[16,2560]{1,0:T(8,128)(2,1)S(1)}, bf16[16,2560]{1,0:T(8,128)(2,1)S(1)}, u32[]{:S(2)}, u32[]{:S(2)}) %collective-permute-start.35) | collective-permute-done | bytes 81952 | tf_op jit(solution)/shard_map/ppermute | solution.py:33
  148.3 1.3 collective-permute-done.37.dot_other_ref
  149.7 6.0 %finish.1 = (bf16[256,2560]{1,0:T(8,128)(2,1)}, bf16[256,2560]{1,0:T(8,128)(2,1)}, bf16[256,2560]{1,0:T(8,128)(2,1)}) custom-call(s32[2]{0:T(128)S(1)} %pad_add_fusion.place_ref.refs_0_, s32[2]{0:T(128)S(1)} %copy-done.7, f32[256,128]{1,0:T(8,128)S(1)} %squares.1.own_ref.refs_3_, f32[256,128]{1,0:T(8,128)S(1)} %collective-permute-done.other_ref.refs_4_, ...), custom_call_target="tpu_custom_call" | custom-call | flops 1 | bytes 1 | tf_op jit(solution)/shard_map/finish/pallas_call | solution.py:612
  (74 shorter events, 20.4 us)
Async XLA Ops:
  0.6 1.3 copy-start
  2.0 1.3 copy-start.2
  3.3 1.7 %copy-start.8 = (f32[2560]{0:T(1024)S(1)}, f32[2560]{0:T(1024)}, u32[]{:S(2)}) copy-start(f32[2560]{0:T(1024)} %param.14) | copy-start | bytes 30724
  3.3 2.7 %copy-start.1 = (bf16[256,2560]{1,0:T(8,128)(2,1)S(1)}, bf16[256,2560]{1,0:T(8,128)(2,1)}, u32[]{:S(2)}) copy-start(bf16[256,2560]{1,0:T(8,128)(2,1)} %refs_17_.13) | copy-start | bytes 3932164
  3.3 2.7 %copy-start.4 = (bf16[256,2560]{1,0:T(8,128)(2,1)S(1)}, bf16[256,2560]{1,0:T(8,128)(2,1)}, u32[]{:S(2)}) copy-start(bf16[256,2560]{1,0:T(8,128)(2,1)} %refs_36_.5) | copy-start | bytes 3932164
  3.3 2.7 %copy-start.7 = (s32[2]{0:T(128)S(1)}, s32[2]{0:T(128)}, u32[]{:S(2)}) copy-start(s32[2]{0:T(128)} %ids_ref.5) | copy-start | bytes 28
  4.4 1.5 collective-permute-start
  5.0 8.7 %copy-start.9 = (f32[2560]{0:T(1024)S(1)}, f32[2560]{0:T(1024)}, u32[]{:S(2)}) copy-start(f32[2560]{0:T(1024)} %param.13) | copy-start | bytes 30724
  5.1 15.6 %copy-start.5 = (s32[2,4]{1,0:T(2,128)S(1)}, s32[2,4]{1,0:T(2,128)}, u32[]{:S(2)}) copy-start(s32[2,4]{1,0:T(2,128)} %refs_1_.5) | copy-start | bytes 100
  5.1 15.6 %copy-start.6 = (s32[1,16]{1,0:T(1,128)S(1)}, s32[1,16]{1,0:T(1,128)}, u32[]{:S(2)}) copy-start(s32[1,16]{1,0:T(1,128)} %refs_2_.8) | copy-start | bytes 196
  8.2 5.8 %collective-permute-start.1 = (bf16[16,2560]{1,0:T(8,128)(2,1)S(1)}, bf16[16,2560]{1,0:T(8,128)(2,1)S(1)}, u32[]{:S(2)}, u32[]{:S(2)}) collective-permute-start(bf16[16,2560]{1,0:T(8,128)(2,1)S(1)} %get-tuple-element.73), channel_id=1, source_target_pairs={{0,8},{2,10},{4,12},{6,14},{8,0},{10,2},{12,4},{14,6},{16,24},{18,... | collective-permute-start | bytes 245768 | tf_op jit(solution)/shard_map/ppermute | solution.py:33
  11.2 9.5 %collective-permute-start.2 = (bf16[16,2560]{1,0:T(8,128)(2,1)S(1)}, bf16[16,2560]{1,0:T(8,128)(2,1)S(1)}, u32[]{:S(2)}, u32[]{:S(2)}) collective-permute-start(bf16[16,2560]{1,0:T(8,128)(2,1)S(1)} %get-tuple-element.74), channel_id=1, source_target_pairs={{0,16},{2,18},{4,20},{6,22},{8,24},{10,26},{12,28},{14,30},{16,0},... | collective-permute-start | bytes 245768 | tf_op jit(solution)/shard_map/ppermute | solution.py:33
  13.8 6.9 %collective-permute-start.3 = (bf16[16,2560]{1,0:T(8,128)(2,1)S(1)}, bf16[16,2560]{1,0:T(8,128)(2,1)S(1)}, u32[]{:S(2)}, u32[]{:S(2)}) collective-permute-start(bf16[16,2560]{1,0:T(8,128)(2,1)S(1)} %get-tuple-element.75), channel_id=1, source_target_pairs={{0,24},{2,26},{4,28},{6,30},{8,16},{10,18},{12,20},{14,22},{16,8},... | collective-permute-start | bytes 245768 | tf_op jit(solution)/shard_map/ppermute | solution.py:33
  24.0 15.3 %collective-permute-start.4 = (bf16[1056,256]{1,0:T(8,128)(2,1)S(1)}, bf16[1056,256]{1,0:T(8,128)(2,1)S(1)}, u32[]{:S(2)}, u32[]{:S(2)}) collective-permute-start(bf16[1056,256]{1,0:T(8,128)(2,1)S(1)} %get-tuple-element.77), channel_id=1, source_target_pairs={{0,2},{2,0},{4,6},{6,4},{8,10},{10,8},{12,14},{14,12},{16,18},{18,... | collective-permute-start | bytes 1622024 | tf_op jit(solution)/shard_map/ppermute | solution.py:33
  25.6 26.8 %collective-permute-start.5 = (bf16[1056,256]{1,0:T(8,128)(2,1)S(1)}, bf16[1056,256]{1,0:T(8,128)(2,1)S(1)}, u32[]{:S(2)}, u32[]{:S(2)}) collective-permute-start(bf16[1056,256]{1,0:T(8,128)(2,1)S(1)} %get-tuple-element.78), channel_id=1, source_target_pairs={{0,4},{2,6},{4,0},{6,2},{8,12},{10,14},{12,8},{14,10},{16,20},{18,... | collective-permute-start | bytes 1622024 | tf_op jit(solution)/shard_map/ppermute | solution.py:33
  27.1 25.3 %collective-permute-start.6 = (bf16[1056,256]{1,0:T(8,128)(2,1)S(1)}, bf16[1056,256]{1,0:T(8,128)(2,1)S(1)}, u32[]{:S(2)}, u32[]{:S(2)}) collective-permute-start(bf16[1056,256]{1,0:T(8,128)(2,1)S(1)} %get-tuple-element.79), channel_id=1, source_target_pairs={{0,6},{2,4},{4,2},{6,0},{8,14},{10,12},{12,10},{14,8},{16,22},{18,... | collective-permute-start | bytes 1622024 | tf_op jit(solution)/shard_map/ppermute | solution.py:33
  27.6 14.2 %copy-start.3 = (bf16[256,2560]{1,0:T(8,128)(2,1)S(1)}, bf16[256,2560]{1,0:T(8,128)(2,1)}, u32[]{:S(2)}) copy-start(bf16[256,2560]{1,0:T(8,128)(2,1)} %refs_16_.7) | copy-start | bytes 3932164
  30.9 39.1 %collective-permute-start.11 = (bf16[1056,256]{1,0:T(8,128)(2,1)S(1)}, bf16[1056,256]{1,0:T(8,128)(2,1)S(1)}, u32[]{:S(2)}, u32[]{:S(2)}) collective-permute-start(bf16[1056,256]{1,0:T(8,128)(2,1)S(1)} %get-tuple-element.95), channel_id=1, source_target_pairs={{0,2},{2,0},{4,6},{6,4},{8,10},{10,8},{12,14},{14,12},{16,18},{18,... | collective-permute-start | bytes 1622024 | tf_op jit(solution)/shard_map/ppermute | solution.py:33
  32.5 38.7 %collective-permute-start.12 = (bf16[1056,256]{1,0:T(8,128)(2,1)S(1)}, bf16[1056,256]{1,0:T(8,128)(2,1)S(1)}, u32[]{:S(2)}, u32[]{:S(2)}) collective-permute-start(bf16[1056,256]{1,0:T(8,128)(2,1)S(1)} %get-tuple-element.96), channel_id=1, source_target_pairs={{0,4},{2,6},{4,0},{6,2},{8,12},{10,14},{12,8},{14,10},{16,20},{18,... | collective-permute-start | bytes 1622024 | tf_op jit(solution)/shard_map/ppermute | solution.py:33
  39.3 35.9 %collective-permute-start.13 = (bf16[1056,256]{1,0:T(8,128)(2,1)S(1)}, bf16[1056,256]{1,0:T(8,128)(2,1)S(1)}, u32[]{:S(2)}, u32[]{:S(2)}) collective-permute-start(bf16[1056,256]{1,0:T(8,128)(2,1)S(1)} %get-tuple-element.97), channel_id=1, source_target_pairs={{0,6},{2,4},{4,2},{6,0},{8,14},{10,12},{12,10},{14,8},{16,22},{18,... | collective-permute-start | bytes 1622024 | tf_op jit(solution)/shard_map/ppermute | solution.py:33
  53.0 7.3 %collective-permute-start.7 = (bf16[512,256]{1,0:T(8,128)(2,1)S(1)}, bf16[512,256]{1,0:T(8,128)(2,1)S(1)}, u32[]{:S(2)}, u32[]{:S(2)}) collective-permute-start(bf16[512,256]{1,0:T(8,128)(2,1)S(1)} %get-tuple-element.87), channel_id=1, source_target_pairs={{0,8},{2,10},{4,12},{6,14},{8,0},{10,2},{12,4},{14,6},{16,24},{18,... | collective-permute-start | bytes 786440 | tf_op jit(solution)/shard_map/ppermute | solution.py:33
  54.5 5.8 %collective-permute-start.8 = (bf16[512,256]{1,0:T(8,128)(2,1)S(1)}, bf16[512,256]{1,0:T(8,128)(2,1)S(1)}, u32[]{:S(2)}, u32[]{:S(2)}) collective-permute-start(bf16[512,256]{1,0:T(8,128)(2,1)S(1)} %get-tuple-element.88), channel_id=1, source_target_pairs={{8,16},{10,18},{12,20},{14,22},{16,8},{18,10},{20,12},{22,14},{9,1... | collective-permute-start | bytes 786440 | tf_op jit(solution)/shard_map/ppermute | solution.py:39
  65.9 11.3 %collective-permute-start.9 = (bf16[512,256]{1,0:T(8,128)(2,1)S(1)}, bf16[512,256]{1,0:T(8,128)(2,1)S(1)}, u32[]{:S(2)}, u32[]{:S(2)}) collective-permute-start(bf16[512,256]{1,0:T(8,128)(2,1)S(1)} %get-tuple-element.92), channel_id=1, source_target_pairs={{0,8},{2,10},{4,12},{6,14},{8,0},{10,2},{12,4},{14,6},{16,24},{18,... | collective-permute-start | bytes 786440 | tf_op jit(solution)/shard_map/ppermute | solution.py:33
  69.4 9.3 %collective-permute-start.10 = (bf16[512,256]{1,0:T(8,128)(2,1)S(1)}, bf16[512,256]{1,0:T(8,128)(2,1)S(1)}, u32[]{:S(2)}, u32[]{:S(2)}) collective-permute-start(bf16[512,256]{1,0:T(8,128)(2,1)S(1)} %get-tuple-element.93), channel_id=1, source_target_pairs={{8,16},{10,18},{12,20},{14,22},{16,8},{18,10},{20,12},{22,14},{9,1... | collective-permute-start | bytes 786440 | tf_op jit(solution)/shard_map/ppermute | solution.py:39
  70.0 16.7 %collective-permute-start.19 = (bf16[1056,128]{1,0:T(8,128)(2,1)S(1)}, bf16[1056,128]{1,0:T(8,128)(2,1)S(1)}, u32[]{:S(2)}, u32[]{:S(2)}) collective-permute-start(bf16[1056,128]{1,0:T(8,128)(2,1)S(1)} %get-tuple-element.109), channel_id=1, source_target_pairs={{0,2},{2,0},{4,6},{6,4},{8,10},{10,8},{12,14},{14,12},{16,18},{18,... | collective-permute-start | bytes 811016 | tf_op jit(solution)/shard_map/ppermute | solution.py:33
  71.1 16.8 %collective-permute-start.20 = (bf16[1056,128]{1,0:T(8,128)(2,1)S(1)}, bf16[1056,128]{1,0:T(8,128)(2,1)S(1)}, u32[]{:S(2)}, u32[]{:S(2)}) collective-permute-start(bf16[1056,128]{1,0:T(8,128)(2,1)S(1)} %get-tuple-element.110), channel_id=1, source_target_pairs={{0,4},{2,6},{4,0},{6,2},{8,12},{10,14},{12,8},{14,10},{16,20},{18,... | collective-permute-start | bytes 811016 | tf_op jit(solution)/shard_map/ppermute | solution.py:33
  75.2 14.8 %collective-permute-start.21 = (bf16[1056,128]{1,0:T(8,128)(2,1)S(1)}, bf16[1056,128]{1,0:T(8,128)(2,1)S(1)}, u32[]{:S(2)}, u32[]{:S(2)}) collective-permute-start(bf16[1056,128]{1,0:T(8,128)(2,1)S(1)} %get-tuple-element.111), channel_id=1, source_target_pairs={{0,6},{2,4},{4,2},{6,0},{8,14},{10,12},{12,10},{14,8},{16,22},{18,... | collective-permute-start | bytes 811016 | tf_op jit(solution)/shard_map/ppermute | solution.py:33
  77.2 13.7 %collective-permute-start.17 = (bf16[512,256]{1,0:T(8,128)(2,1)S(1)}, bf16[512,256]{1,0:T(8,128)(2,1)S(1)}, u32[]{:S(2)}, u32[]{:S(2)}) collective-permute-start(bf16[512,256]{1,0:T(8,128)(2,1)S(1)} %get-tuple-element.106), channel_id=1, source_target_pairs={{0,8},{2,10},{4,12},{6,14},{8,0},{10,2},{12,4},{14,6},{16,24},{18,... | collective-permute-start | bytes 786440 | tf_op jit(solution)/shard_map/ppermute | solution.py:33
  78.7 12.2 %collective-permute-start.18 = (bf16[512,256]{1,0:T(8,128)(2,1)S(1)}, bf16[512,256]{1,0:T(8,128)(2,1)S(1)}, u32[]{:S(2)}, u32[]{:S(2)}) collective-permute-start(bf16[512,256]{1,0:T(8,128)(2,1)S(1)} %get-tuple-element.107), channel_id=1, source_target_pairs={{8,16},{10,18},{12,20},{14,22},{16,8},{18,10},{20,12},{22,14},{9,1... | collective-permute-start | bytes 786440 | tf_op jit(solution)/shard_map/ppermute | solution.py:39
  86.8 16.1 %collective-permute-start.14 = (bf16[784,256]{1,0:T(8,128)(2,1)S(1)}, bf16[784,256]{1,0:T(8,128)(2,1)S(1)}, u32[]{:S(2)}, u32[]{:S(2)}) collective-permute-start(bf16[784,256]{1,0:T(8,128)(2,1)S(1)} %get-tuple-element.101), channel_id=1, source_target_pairs={{0,2},{2,0},{4,6},{6,4},{8,10},{10,8},{12,14},{14,12},{16,18},{18,... | collective-permute-start | bytes 1204232 | tf_op jit(solution)/shard_map/ppermute | solution.py:33
  87.9 14.9 %collective-permute-start.15 = (bf16[784,256]{1,0:T(8,128)(2,1)S(1)}, bf16[784,256]{1,0:T(8,128)(2,1)S(1)}, u32[]{:S(2)}, u32[]{:S(2)}) collective-permute-start(bf16[784,256]{1,0:T(8,128)(2,1)S(1)} %get-tuple-element.102), channel_id=1, source_target_pairs={{0,4},{2,6},{4,0},{6,2},{8,12},{10,14},{12,8},{14,10},{16,20},{18,... | collective-permute-start | bytes 1204232 | tf_op jit(solution)/shard_map/ppermute | solution.py:33
  90.0 13.8 %collective-permute-start.16 = (bf16[784,256]{1,0:T(8,128)(2,1)S(1)}, bf16[784,256]{1,0:T(8,128)(2,1)S(1)}, u32[]{:S(2)}, u32[]{:S(2)}) collective-permute-start(bf16[784,256]{1,0:T(8,128)(2,1)S(1)} %get-tuple-element.103), channel_id=1, source_target_pairs={{0,6},{2,4},{4,2},{6,0},{8,14},{10,12},{12,10},{14,8},{16,22},{18,... | collective-permute-start | bytes 1204232 | tf_op jit(solution)/shard_map/ppermute | solution.py:33
  96.5 9.0 %collective-permute-start.22 = (bf16[512,256]{1,0:T(8,128)(2,1)S(1)}, bf16[512,256]{1,0:T(8,128)(2,1)S(1)}, u32[]{:S(2)}, u32[]{:S(2)}) collective-permute-start(bf16[512,256]{1,0:T(8,128)(2,1)S(1)} %get-tuple-element.117), channel_id=1, source_target_pairs={{0,8},{2,10},{4,12},{6,14},{8,0},{10,2},{12,4},{14,6},{16,24},{18,... | collective-permute-start | bytes 786440 | tf_op jit(solution)/shard_map/ppermute | solution.py:33
  99.6 5.9 %collective-permute-start.23 = (bf16[512,256]{1,0:T(8,128)(2,1)S(1)}, bf16[512,256]{1,0:T(8,128)(2,1)S(1)}, u32[]{:S(2)}, u32[]{:S(2)}) collective-permute-start(bf16[512,256]{1,0:T(8,128)(2,1)S(1)} %get-tuple-element.118), channel_id=1, source_target_pairs={{8,16},{10,18},{12,20},{14,22},{16,8},{18,10},{20,12},{22,14},{9,1... | collective-permute-start | bytes 786440 | tf_op jit(solution)/shard_map/ppermute | solution.py:39
  107.6 17.0 %collective-permute-start.24 = (bf16[784,256]{1,0:T(8,128)(2,1)S(1)}, bf16[784,256]{1,0:T(8,128)(2,1)S(1)}, u32[]{:S(2)}, u32[]{:S(2)}) collective-permute-start(bf16[784,256]{1,0:T(8,128)(2,1)S(1)} %get-tuple-element.121), channel_id=1, source_target_pairs={{0,2},{2,0},{4,6},{6,4},{8,10},{10,8},{12,14},{14,12},{16,18},{18,... | collective-permute-start | bytes 1204232 | tf_op jit(solution)/shard_map/ppermute | solution.py:33
  108.4 16.1 %collective-permute-start.25 = (bf16[784,256]{1,0:T(8,128)(2,1)S(1)}, bf16[784,256]{1,0:T(8,128)(2,1)S(1)}, u32[]{:S(2)}, u32[]{:S(2)}) collective-permute-start(bf16[784,256]{1,0:T(8,128)(2,1)S(1)} %get-tuple-element.122), channel_id=1, source_target_pairs={{0,4},{2,6},{4,0},{6,2},{8,12},{10,14},{12,8},{14,10},{16,20},{18,... | collective-permute-start | bytes 1204232 | tf_op jit(solution)/shard_map/ppermute | solution.py:33
  109.9 14.6 %collective-permute-start.26 = (bf16[784,256]{1,0:T(8,128)(2,1)S(1)}, bf16[784,256]{1,0:T(8,128)(2,1)S(1)}, u32[]{:S(2)}, u32[]{:S(2)}) collective-permute-start(bf16[784,256]{1,0:T(8,128)(2,1)S(1)} %get-tuple-element.123), channel_id=1, source_target_pairs={{0,6},{2,4},{4,2},{6,0},{8,14},{10,12},{12,10},{14,8},{16,22},{18,... | collective-permute-start | bytes 1204232 | tf_op jit(solution)/shard_map/ppermute | solution.py:33
  111.1 5.6 %collective-permute-start.27 = (bf16[512,128]{1,0:T(8,128)(2,1)S(1)}, bf16[512,128]{1,0:T(8,128)(2,1)S(1)}, u32[]{:S(2)}, u32[]{:S(2)}) collective-permute-start(bf16[512,128]{1,0:T(8,128)(2,1)S(1)} %get-tuple-element.126), channel_id=1, source_target_pairs={{0,8},{2,10},{4,12},{6,14},{8,0},{10,2},{12,4},{14,6},{16,24},{18,... | collective-permute-start | bytes 393224 | tf_op jit(solution)/shard_map/ppermute | solution.py:33
  113.5 3.2 %collective-permute-start.28 = (bf16[512,128]{1,0:T(8,128)(2,1)S(1)}, bf16[512,128]{1,0:T(8,128)(2,1)S(1)}, u32[]{:S(2)}, u32[]{:S(2)}) collective-permute-start(bf16[512,128]{1,0:T(8,128)(2,1)S(1)} %get-tuple-element.127), channel_id=1, source_target_pairs={{8,16},{10,18},{12,20},{14,22},{16,8},{18,10},{20,12},{22,14},{9,1... | collective-permute-start | bytes 393224 | tf_op jit(solution)/shard_map/ppermute | solution.py:39
  119.4 7.2 %collective-permute-start.29 = (bf16[512,128]{1,0:T(8,128)(2,1)S(1)}, bf16[512,128]{1,0:T(8,128)(2,1)S(1)}, u32[]{:S(2)}, u32[]{:S(2)}) collective-permute-start(bf16[512,128]{1,0:T(8,128)(2,1)S(1)} %get-tuple-element.132), channel_id=1, source_target_pairs={{0,8},{2,10},{4,12},{6,14},{8,0},{10,2},{12,4},{14,6},{16,24},{18,... | collective-permute-start | bytes 393224 | tf_op jit(solution)/shard_map/ppermute | solution.py:33
  123.7 3.0 %collective-permute-start.30 = (bf16[512,128]{1,0:T(8,128)(2,1)S(1)}, bf16[512,128]{1,0:T(8,128)(2,1)S(1)}, u32[]{:S(2)}, u32[]{:S(2)}) collective-permute-start(bf16[512,128]{1,0:T(8,128)(2,1)S(1)} %get-tuple-element.133), channel_id=1, source_target_pairs={{8,16},{10,18},{12,20},{14,22},{16,8},{18,10},{20,12},{22,14},{9,1... | collective-permute-start | bytes 393224 | tf_op jit(solution)/shard_map/ppermute | solution.py:39
  127.5 5.8 %collective-permute-start.31 = (bf16[784,128]{1,0:T(8,128)(2,1)S(1)}, bf16[784,128]{1,0:T(8,128)(2,1)S(1)}, u32[]{:S(2)}, u32[]{:S(2)}) collective-permute-start(bf16[784,128]{1,0:T(8,128)(2,1)S(1)} %get-tuple-element.135), channel_id=1, source_target_pairs={{0,2},{2,0},{4,6},{6,4},{8,10},{10,8},{12,14},{14,12},{16,18},{18,... | collective-permute-start | bytes 602120 | tf_op jit(solution)/shard_map/ppermute | solution.py:33
  128.5 7.1 %collective-permute-start.32 = (bf16[784,128]{1,0:T(8,128)(2,1)S(1)}, bf16[784,128]{1,0:T(8,128)(2,1)S(1)}, u32[]{:S(2)}, u32[]{:S(2)}) collective-permute-start(bf16[784,128]{1,0:T(8,128)(2,1)S(1)} %get-tuple-element.136), channel_id=1, source_target_pairs={{0,4},{2,6},{4,0},{6,2},{8,12},{10,14},{12,8},{14,10},{16,20},{18,... | collective-permute-start | bytes 602120 | tf_op jit(solution)/shard_map/ppermute | solution.py:33
  130.2 6.9 %collective-permute-start.33 = (bf16[784,128]{1,0:T(8,128)(2,1)S(1)}, bf16[784,128]{1,0:T(8,128)(2,1)S(1)}, u32[]{:S(2)}, u32[]{:S(2)}) collective-permute-start(bf16[784,128]{1,0:T(8,128)(2,1)S(1)} %get-tuple-element.137), channel_id=1, source_target_pairs={{0,6},{2,4},{4,2},{6,0},{8,14},{10,12},{12,10},{14,8},{16,22},{18,... | collective-permute-start | bytes 602120 | tf_op jit(solution)/shard_map/ppermute | solution.py:33
  137.6 6.3 %collective-permute-start.36 = (bf16[16,2560]{1,0:T(8,128)(2,1)S(1)}, bf16[16,2560]{1,0:T(8,128)(2,1)S(1)}, u32[]{:S(2)}, u32[]{:S(2)}) collective-permute-start(bf16[16,2560]{1,0:T(8,128)(2,1)S(1)} %collect.1.p0.refs_0_), channel_id=1, source_target_pairs={{0,24},{2,26},{4,28},{6,30},{8,16},{10,18},{12,20},{14,22},{16,8},... | collective-permute-start | bytes 245768 | tf_op jit(solution)/shard_map/ppermute | solution.py:33
  139.8 6.6 %collective-permute-start.35 = (bf16[16,2560]{1,0:T(8,128)(2,1)S(1)}, bf16[16,2560]{1,0:T(8,128)(2,1)S(1)}, u32[]{:S(2)}, u32[]{:S(2)}) collective-permute-start(bf16[16,2560]{1,0:T(8,128)(2,1)S(1)} %collect.1.p0.refs_0_), channel_id=1, source_target_pairs={{0,16},{2,18},{4,20},{6,22},{8,24},{10,26},{12,28},{14,30},{16,0},... | collective-permute-start | bytes 245768 | tf_op jit(solution)/shard_map/ppermute | solution.py:33
  143.1 4.4 %collective-permute-start.34 = (bf16[16,2560]{1,0:T(8,128)(2,1)S(1)}, bf16[16,2560]{1,0:T(8,128)(2,1)S(1)}, u32[]{:S(2)}, u32[]{:S(2)}) collective-permute-start(bf16[16,2560]{1,0:T(8,128)(2,1)S(1)} %collect.1.p0.refs_0_), channel_id=1, source_target_pairs={{0,8},{2,10},{4,12},{6,14},{8,0},{10,2},{12,4},{14,6},{16,24},{18,... | collective-permute-start | bytes 245768 | tf_op jit(solution)/shard_map/ppermute | solution.py:33
  148.3 1.4 collective-permute-start.37

commit v3 on v2

--- a/solution.py
+++ b/solution.py
@@ -21,7 +21,6 @@
 FACTOR = HEAD_DIM ** (-0.5)
 LOG2_E = 1.4426950408889634
 FACTS = 32
-EXTRA = 16
 F32 = jnp.float32
 BF16 = jnp.bfloat16
 ANY = pl.BlockSpec(memory_space=pl.ANY)
@@ -54,6 +53,32 @@
     return run
 
 
+def heads_call(kernel, count, place, inputs, outputs, after=(), scratch=(), name=None):
+    widths = [w for _, w in inputs] + [w for _, w in outputs]
+
+    def run(place_ref, *refs):
+        refs = refs[: len(inputs)] + refs[len(inputs) + len(after) :]
+        for h in range(count):
+            views = [
+                ref.at[:, h * w : (h + 1) * w] if w else ref for ref, w in zip(refs, widths)
+            ]
+            kernel(h, place_ref, *views, *refs[len(widths) :])
+
+    vmem = pl.BlockSpec(memory_space=pltpu.VMEM)
+    return pl.pallas_call(
+        run,
+        out_shape=[shape for shape, _ in outputs],
+        in_specs=[pl.BlockSpec(memory_space=pltpu.SMEM)]
+        + [vmem] * len(inputs)
+        + [ANY] * len(after),
+        out_specs=[vmem] * len(outputs),
+        scratch_shapes=scratch,
+        compiler_params=params(),
+        cost_estimate=cost(1, 1),
+        name=name,
+    )(place, *[x for x, _ in inputs], *after)
+
+
 def contract(a, b, dims, precision=None):
     return lax.dot_general(
         a, b, (dims, ((), ())), precision=precision, preferred_element_type=F32
@@ -66,35 +91,26 @@
 
 
 def squares_kernel(query_ref, key_ref, out_ref):
-    step = pl.program_id(0)
-    query = query_ref[...].astype(F32)
-    key = key_ref[...].astype(F32)
-    part = lane_pair(
-        jnp.sum(query * query, axis=1, keepdims=True),
-        jnp.sum(key * key, axis=1, keepdims=True),
-        query.shape[0],
-    )
-
-    @pl.when(step == 0)
-    def _():
-        out_ref[...] = part
-
-    @pl.when(step > 0)
-    def _():
-        out_ref[...] += part
+    rows, width = query_ref.shape
+    step = rows // 4
+    for at in range(0, rows, step):
+        part = []
+        for ref in (query_ref, key_ref):
+            x = ref[at : at + step].astype(F32)
+            part.append(jnp.sum(x * x, axis=1, keepdims=True))
+        out_ref[at : at + step] = lane_pair(*part, step)
 
 
 def squares(query_raw, key_raw):
     rows, width = query_raw.shape
-    block = width // 4
+    vmem = pl.BlockSpec(memory_space=pltpu.VMEM)
     return pl.pallas_call(
         squares_kernel,
         out_shape=jax.ShapeDtypeStruct((rows, HEAD_DIM), F32),
-        grid=(4,),
-        in_specs=[pl.BlockSpec((rows, block), lambda i: (0, i))] * 2,
-        out_specs=pl.BlockSpec((rows, HEAD_DIM), lambda i: (0, 0)),
+        in_specs=[vmem] * 2,
+        out_specs=vmem,
         compiler_params=params(),
-        cost_estimate=cost(4 * rows * width, 4 * rows * width),
+        cost_estimate=cost(1, 1),
         name="squares",
     )(query_raw, key_raw)
 
@@ -104,52 +120,54 @@
     return both[:, :1], both[:, HEAD_DIM // 2 : HEAD_DIM // 2 + 1]
 
 
-def rows_kernel(place_ref, ids_ref, own_ref, other_ref, key_ref, value_ref, gain_ref, *outs):
-    rows = key_ref.shape[0]
-    _, key_inv = inverses(own_ref[...], other_ref[...])
+def rows_kernel(place_ref, ids_ref, own_ref, other_ref, key_ref, value_ref, gain_ref, out, raw):
+    rows, width = key_ref.shape
+    block = width // GROUP
     device = place_ref[1] * GROUP + place_ref[0]
-    row = lax.broadcasted_iota(jnp.int32, (16 * GROUP, rows), 0)
-    col = lax.broadcasted_iota(jnp.int32, (16 * GROUP, rows), 1)
-    is_key = jnp.zeros((16 * GROUP, rows), jnp.bool_)
-    is_value = is_key
+    row = lax.broadcasted_iota(jnp.int32, (16, width), 0)
+    keys, found, vals = [], [], []
     for r in range(G_DEV):
-        here = col == ids_ref[r] - device * rows
-        for e in range(GROUP):
-            is_key = is_key | (here & (row == 16 * e + 2 * e + r))
-            is_value = is_value | (here & (row == 16 * e + 8 + 2 * e + r))
-    is_key = is_key.astype(F32).astype(BF16)
-    is_value = is_value.astype(F32).astype(BF16)
-    key = key_ref[...]
-    normed = (key.astype(F32) * key_inv * gain_ref[...]).astype(BF16)
-    total = contract(is_key, normed, ((1,), (0,))) + contract(
-        is_value, value_ref[...], ((1,), (0,))
-    )
-    for e in range(GROUP):
-        outs[e][...] = total[16 * e : 16 * e + 16].astype(BF16)
-    outs[GROUP][...] = contract(is_key[:16], key, ((1,), (0,))).astype(BF16)
+        at = ids_ref[r] - device * rows
+        base = pl.multiple_of(at // 16 * 16, 16)
+        here = pl.ds(base, 16)
+        _, inv = inverses(own_ref[here], other_ref[here])
+        hot = row == at - base
+
+        def only(x):
+            return jnp.sum(jnp.where(hot, x, 0.0), axis=0, keepdims=True)
+
+        key = key_ref[here].astype(F32)
+        keys.append(only(key))
+        found.append(only((key * inv * gain_ref[...]).astype(BF16).astype(F32)))
+        vals.append(only(value_ref[here].astype(F32)))
+    raw[...] = jnp.where(row == 0, keys[0], keys[1]).astype(BF16)
+    total = jnp.zeros((16, block), F32)
+    row = lax.broadcasted_iota(jnp.int32, (16, block), 0)
+    for g in range(GROUP):
+        for i, x in enumerate(found + vals):
+            total = jnp.where(row == 4 * g + i, x[:, g * block : (g + 1) * block], total)
+    out[...] = total.astype(BF16)
 
 
 def global_rows(place, ids, own, other, key_raw, values, key_gain):
     rows, width = key_raw.shape
-    block = width // 4
     smem = pl.BlockSpec(memory_space=pltpu.SMEM)
-    whole = pl.BlockSpec((rows, HEAD_DIM), lambda i: (0, 0))
+    vmem = pl.BlockSpec(memory_space=pltpu.VMEM)
     return pl.pallas_call(
         rows_kernel,
-        out_shape=[jax.ShapeDtypeStruct((16, width), BF16)] * (GROUP + 1),
-        grid=(4,),
-        in_specs=[smem, smem, whole, whole]
-        + [pl.BlockSpec((rows, block), lambda i: (0, i))] * 2
-        + [pl.BlockSpec((1, block), lambda i: (0, i))],
-        out_specs=[pl.BlockSpec((16, block), lambda i: (0, i))] * (GROUP + 1),
+        out_shape=[
+            jax.ShapeDtypeStruct((16, width // GROUP), BF16),
+            jax.ShapeDtypeStruct((16, width), BF16),
+        ],
+        in_specs=[smem, smem] + [vmem] * 5,
+        out_specs=[vmem] * 2,
         compiler_params=params(),
         cost_estimate=cost(1, 1),
         name="global_rows",
     )(place, ids, own, other, key_raw, values, key_gain)
 
 
-def pack_kernel(place_ref, tiles_ref, readers_ref, own_ref, other_ref, *refs):
-    per = 6 + GROUP
+def pack_kernel(first, place_ref, tiles_ref, readers_ref, own_ref, other_ref, *refs):
     me, plane = place_ref[0], place_ref[1]
     query_inv, key_inv = inverses(own_ref[...], other_ref[...])
     rows = own_ref.shape[0]
@@ -165,53 +183,57 @@
             chosen = (row == 0) & (lane // G_DEV == GROUP * j + e)
             facts = jnp.where(chosen, live, facts)
     facts = facts.astype(F32).astype(BF16)
-    refs[-1][...] = jnp.zeros((8, HEAD_DIM), F32)
-    for d in range(GROUP):
-        key, value, query, grad, key_gain, query_gain, *parts = refs[per * d : per * d + per]
-        out = refs[per * GROUP + d]
-        out[0:rows] = (key[...].astype(F32) * key_inv * key_gain[...]).astype(BF16)
-        out[rows : 2 * rows] = value[...]
-        out[2 * rows : 3 * rows] = (
-            query[...].astype(F32) * query_inv * query_gain[...]
-        ).astype(BF16)
-        out[3 * rows : 4 * rows] = grad[...]
-        out[4 * rows : 4 * rows + 16] = facts
-        out[4 * rows + 16 :] = sum(part[...].astype(F32) for part in parts).astype(BF16)
+    key_ref, value_ref, query_ref, grad_ref, key_gain, query_gain = refs[:6]
+    *outs, token = refs[6 + GROUP :]
+    token[...] = jnp.zeros((8, HEAD_DIM), F32)
+    parts = jnp.concatenate([ref[...] for ref in refs[6 : 6 + GROUP]], axis=0)
+    row = lax.broadcasted_iota(jnp.int32, (16, 16 * GROUP), 0)
+    col = lax.broadcasted_iota(jnp.int32, (16, 16 * GROUP), 1)
+    each = key_ref.shape[1] // HEAD_DIM // GROUP
+    for d, out in enumerate(outs):
+        spot = col % 16 - 4 * (me ^ d)
+        hot = (spot >= 0) & (spot < 4)
+        hot = hot & (row == 2 * (col // 16) + spot % 2 + 8 * (spot // 2))
+        hot = hot.astype(F32).astype(BF16)
+        chosen = parts[:, first * HEAD_DIM : first * HEAD_DIM + out.shape[1]]
+        out[4 * rows + 16 :] = contract(hot, chosen, ((1,), (0,))).astype(BF16)
+        for h in range(out.shape[1] // HEAD_DIM):
+            at = pl.multiple_of(((me ^ d) * each + first + h) * HEAD_DIM, HEAD_DIM)
+            here = pl.ds(at, HEAD_DIM)
+            lanes = slice(h * HEAD_DIM, (h + 1) * HEAD_DIM)
+            key = key_ref[:, here].astype(F32)
+            query = query_ref[:, here].astype(F32)
+            out[0:rows, lanes] = (key * key_inv * key_gain[:, here]).astype(BF16)
+            out[rows : 2 * rows, lanes] = value_ref[:, here]
+            out[2 * rows : 3 * rows, lanes] = (query * query_inv * query_gain[:, here]).astype(BF16)
+            out[3 * rows : 4 * rows, lanes] = grad_ref[:, here]
+            out[4 * rows : 4 * rows + 16, lanes] = facts
 
 
 def pack(place, tiles, readers, own, other, arrays, gains, parts, first, count, after):
     query_raw, key_raw, values, out_grad = arrays
     query_gain, key_gain = gains
     rows, width = query_raw.shape
-    each = width // HEAD_DIM // GROUP
     smem = pl.BlockSpec(memory_space=pltpu.SMEM)
-    whole = pl.BlockSpec((rows, HEAD_DIM), lambda h, place: (0, 0))
-    specs, operands = [], []
-    for d in range(GROUP):
-        at = lambda h, place, d=d: (0, (place[0] ^ d) * each + first + h)
-        specs += [pl.BlockSpec((rows, HEAD_DIM), at)] * 4
-        specs += [pl.BlockSpec((1, HEAD_DIM), at)] * 2
-        specs += [pl.BlockSpec((16, HEAD_DIM), at)] * GROUP
-        operands += [key_raw, values, query_raw, out_grad, key_gain, query_gain, *parts]
+    vmem = pl.BlockSpec(memory_space=pltpu.VMEM)
     out_rows = 4 * rows + FACTS
+    kernel = functools.partial(pack_kernel, first)
     return pl.pallas_call(
-        behind(pack_kernel, 5 + len(specs), len(after)),
+        behind(kernel, 11 + GROUP, len(after)),
         out_shape=[jax.ShapeDtypeStruct((out_rows, count * HEAD_DIM), BF16)] * GROUP
         + [jax.ShapeDtypeStruct((8, HEAD_DIM), F32)],
-        grid_spec=pltpu.PrefetchScalarGridSpec(
-            num_scalar_prefetch=1,
-            grid=(count,),
-            in_specs=[smem, smem, whole, whole] + specs + [ANY] * len(after),
-            out_specs=[pl.BlockSpec((out_rows, HEAD_DIM), lambda h, place: (0, h))] * GROUP
-            + [pl.BlockSpec((8, HEAD_DIM), lambda h, place: (0, 0))],
-        ),
+        in_specs=[smem] * 3 + [vmem] * (8 + GROUP) + [ANY] * len(after),
+        out_specs=[vmem] * (GROUP + 1),
         compiler_params=params(),
         cost_estimate=cost(1, 1),
         name="pack",
-    )(place, tiles, readers, own, other, *operands, *after)
-
-
-def edges_kernel(place_ref, b0, b1, b2, b3, near_ref, far_ref, token):
+    )(
+        place, tiles, readers, own, other, key_raw, values, query_raw, out_grad,
+        key_gain, query_gain, *parts, *after,
+    )
+
+
+def edges_kernel(head, place_ref, b0, b1, b2, b3, near_ref, far_ref, token):
     me, plane = place_ref[0], place_ref[1]
     token[...] = jnp.zeros((8, HEAD_DIM), F32)
     even = plane % 2 == 0
@@ -220,36 +242,31 @@
 
         @pl.when(jnp.where(even, last, first) == d)
         def _(block=block):
-            near_ref[...] = block[...]
+            near_ref[...] = block[: near_ref.shape[0]]
 
         @pl.when(jnp.where(even, first, last) == d)
         def _(block=block):
-            far_ref[...] = block[...]
+            far_ref[...] = block[: far_ref.shape[0]]
 
 
 def edges(place, blocks, after):
     out_rows, width = blocks[0].shape
     rows = (out_rows - FACTS) // 4
-    whole = pl.BlockSpec((2 * rows, width), lambda i, place: (0, 0))
-    return pl.pallas_call(
-        behind(edges_kernel, 1 + GROUP, len(after)),
-        out_shape=[jax.ShapeDtypeStruct((2 * rows, width), BF16)] * 2
-        + [jax.ShapeDtypeStruct((8, HEAD_DIM), F32)],
-        grid_spec=pltpu.PrefetchScalarGridSpec(
-            num_scalar_prefetch=1,
-            grid=(1,),
-            in_specs=[whole] * GROUP + [ANY] * len(after),
-            out_specs=[whole] * 2 + [pl.BlockSpec((8, HEAD_DIM), lambda i, place: (0, 0))],
-        ),
-        compiler_params=params(),
-        cost_estimate=cost(1, 1),
+    half = jax.ShapeDtypeStruct((2 * rows, width), BF16)
+    return heads_call(
+        edges_kernel,
+        1,
+        place,
+        [(block, 0) for block in blocks],
+        [(half, 0), (half, 0), (jax.ShapeDtypeStruct((8, HEAD_DIM), F32), 0)],
+        after,
         name="edges",
-    )(place, *blocks, *after)
-
-
-def attend_kernel(outer, place_ref, b0, b1, b2, b3, *refs):
+    )
+
+
+def attend_kernel(outer, head, place_ref, b0, b1, b2, b3, *refs):
     if outer:
-        near, far, dq_out, acc_out, g_out, near_out, far_out = refs[:7]
+        near, far, g_in, dq_out, acc_out, g_out, near_out, far_out, mid_out, end_out = refs[:10]
     else:
         dq_out, acc_out, g_out = refs[:3]
     pair, weights, sums, raw_g, pair_g, sums_g, facts_at = refs[-7:]
@@ -259,8 +276,7 @@
     keys = slice(0, HEAD_DIM)
     vals = slice(HEAD_DIM, 2 * HEAD_DIM)
 
-    @pl.when(pl.program_id(0) == 0)
-    def _():
+    if head == 0:
         weights[...] = jnp.zeros_like(weights)
 
     for d, block in enumerate((b0, b1, b2, b3)):
@@ -328,67 +344,67 @@
         grad_query = contract(dscore, both, ((0,), (0,)))
         dq_out[unit * TILE : (unit + 1) * TILE] = grad_query.astype(BF16)
     acc_out[...] = sums[rows : (GROUP + 1) * rows].astype(BF16)
-    g_out[...] = sums_g[...]
-    if outer:
+    if not outer:
+        g_out[...] = sums_g[...]
+    else:
+        total_g = (g_in[...] + sums_g[...]).astype(BF16)
+        row = lax.broadcasted_iota(jnp.int32, (8, 8 * GROUP), 0)
+        col = lax.broadcasted_iota(jnp.int32, (8, 8 * GROUP), 1)
+        for e, out in enumerate((g_out, near_out, mid_out, end_out)):
+            hot = (col // 8 == row // G_DEV) & (col % 8 == G_DEV * e + row % G_DEV)
+            part = contract(hot.astype(F32).astype(BF16), total_g, ((1,), (0,)))
+            out[out.shape[0] - 16 :] = jnp.concatenate([part[:, keys], part[:, vals]], axis=0).astype(
+                BF16
+            )
         for out, at in ((near_out, near_at), (far_out, far_at)):
             out[:rows] = sums[pl.ds(at, rows), keys].astype(BF16)
             out[rows : 2 * rows] = sums[pl.ds(at, rows), vals].astype(BF16)
 
 
-def attend(place, blocks, halo, after):
+def attend(place, blocks, halo, inner_g, after):
     out_rows, width = blocks[0].shape
     rows = (out_rows - FACTS) // 4
-    at = lambda h, place: (0, h)
-    tall = pl.BlockSpec((out_rows, HEAD_DIM), at)
-    edge = pl.BlockSpec((2 * rows, HEAD_DIM), at)
     wide = 2 * HEAD_DIM
-    edge_shape = jax.ShapeDtypeStruct((2 * rows, width), BF16)
-    return pl.pallas_call(
-        behind(
-            functools.partial(attend_kernel, len(halo) > 0), 1 + GROUP + len(halo), len(after)
-        ),
-        out_shape=[
-            edge_shape,
-            jax.ShapeDtypeStruct((GROUP * rows, 2 * width), BF16),
-            jax.ShapeDtypeStruct((8 * GROUP, 2 * width), F32),
-        ]
-        + [edge_shape] * len(halo),
-        grid_spec=pltpu.PrefetchScalarGridSpec(
-            num_scalar_prefetch=1,
-            grid=(width // HEAD_DIM,),
-            in_specs=[tall] * GROUP + [edge] * len(halo) + [ANY] * len(after),
-            out_specs=[
-                edge,
-                pl.BlockSpec((GROUP * rows, wide), at),
-                pl.BlockSpec((8 * GROUP, wide), at),
-            ]
-            + [edge] * len(halo),
-            scratch_shapes=[
-                pltpu.VMEM(((GROUP + 2) * rows, wide), BF16),
-                pltpu.VMEM((GROUP * rows // TILE, 2 * TILE, wide), BF16),
-                pltpu.VMEM(((GROUP + 2) * rows, wide), F32),
-                pltpu.VMEM((8 * GROUP, wide), F32),
-                pltpu.VMEM((8 * GROUP, wide), BF16),
-                pltpu.VMEM((8 * GROUP, wide), F32),
-                pltpu.VMEM((GROUP, 16, HEAD_DIM), F32),
-            ],
-        ),
-        compiler_params=params(),
-        cost_estimate=cost(1, 1),
+    half = jax.ShapeDtypeStruct((2 * rows, width), BF16)
+    few = jax.ShapeDtypeStruct((16, width), BF16)
+    near = jax.ShapeDtypeStruct((2 * rows + 16, width), BF16)
+    outs = [(half, HEAD_DIM), (jax.ShapeDtypeStruct((GROUP * rows, 2 * width), BF16), wide)]
+    if halo:
+        outs += [(x, HEAD_DIM) for x in (few, near, half, few, few)]
+    else:
+        outs += [(jax.ShapeDtypeStruct((8 * GROUP, 2 * width), F32), wide)]
+    return heads_call(
+        functools.partial(attend_kernel, len(halo) > 0),
+        width // HEAD_DIM,
+        place,
+        [(x, HEAD_DIM) for x in (*blocks, *halo)] + [(x, wide) for x in inner_g],
+        outs,
+        after,
+        [
+            pltpu.VMEM(((GROUP + 2) * rows, wide), BF16),
+            pltpu.VMEM((GROUP * rows // TILE, 2 * TILE, wide), BF16),
+            pltpu.VMEM(((GROUP + 2) * rows, wide), F32),
+            pltpu.VMEM((8 * GROUP, wide), F32),
+            pltpu.VMEM((8 * GROUP, wide), BF16),
+            pltpu.VMEM((8 * GROUP, wide), F32),
+            pltpu.VMEM((GROUP, 16, HEAD_DIM), F32),
+        ],
         name="outer" if halo else "inner",
-    )(place, *blocks, *halo, *after)
+    )
 
 
 def settle_kernel(
-    place_ref, dq_in, acc_in, g_in, dq_out, acc_out, g_out, near, far, o0, o1, o2, o3, token,
-    total_g,
+    head, place_ref, dq_in, acc_in, dq_out, acc_out, own_g, near, far, *refs
 ):
+    *more, o0, o1, o2, o3, token = refs
     me, plane = place_ref[0], place_ref[1]
     token[...] = jnp.zeros((8, HEAD_DIM), F32)
     rows = dq_in.shape[0] // 2
     even = plane % 2 == 0
     inner = (plane == 1) | (plane == 2)
-    total_g[...] = g_in[...] + g_out[...]
+    part = (own_g[...].astype(F32) + near[2 * rows :].astype(F32)).astype(BF16)
+    if more and head == 0:
+        rest_g = (more[0][...].astype(F32) + more[1][...].astype(F32)).astype(BF16)
     for d, out in enumerate((o0, o1, o2, o3)):
         j = me ^ d
         near_here = j == jnp.where(even, GROUP - 1, 0)
@@ -411,213 +427,207 @@
             total = total + jnp.where(near_here, near[rest].astype(F32), 0.0)
             total = total + jnp.where(far_here, far[rest].astype(F32), 0.0)
             out[(i + 1) * rows : (i + 2) * rows] = total.astype(BF16)
-        eight = pl.ds(pl.multiple_of(8 * j, 8), 8)
-        both = total_g[eight]
-        out[3 * rows :] = jnp.concatenate(
-            [both[:, :HEAD_DIM], both[:, HEAD_DIM:]], axis=0
-        ).astype(BF16)
-
-
-def settle(place, inner, outer, near, far, after):
+        out[3 * rows : 3 * rows + 16] = part
+        if more and head == 0:
+            for h in range(rest_g.shape[1] // HEAD_DIM):
+                at = 3 * rows + 16 * (h + 1)
+                out[at : at + 16] = rest_g[:, h * HEAD_DIM : (h + 1) * HEAD_DIM]
+
+
+def settle(place, inner, outer, own_g, near, far, more, after):
     rows, width = inner[0].shape
     rows = rows // 2
-    at = lambda h, place: (0, h)
-    wide = 2 * HEAD_DIM
-    edge = pl.BlockSpec((2 * rows, HEAD_DIM), at)
-    part = [edge, pl.BlockSpec((GROUP * rows, wide), at), pl.BlockSpec((8 * GROUP, wide), at)]
-    return pl.pallas_call(
-        behind(settle_kernel, 9, len(after)),
-        out_shape=[jax.ShapeDtypeStruct((3 * rows + EXTRA, width), BF16)] * GROUP
-        + [jax.ShapeDtypeStruct((8, HEAD_DIM), F32)],
-        grid_spec=pltpu.PrefetchScalarGridSpec(
-            num_scalar_prefetch=1,
-            grid=(width // HEAD_DIM,),
-            in_specs=part * 2 + [edge] * 2 + [ANY] * len(after),
-            out_specs=[pl.BlockSpec((3 * rows + EXTRA, HEAD_DIM), at)] * GROUP
-            + [pl.BlockSpec((8, HEAD_DIM), lambda h, place: (0, 0))],
-            scratch_shapes=[pltpu.VMEM((8 * GROUP, wide), F32)],
-        ),
-        compiler_params=params(),
-        cost_estimate=cost(1, 1),
+    part = (HEAD_DIM, 2 * HEAD_DIM)
+    extra = 16 + 16 * (more[0].shape[1] // HEAD_DIM if more else 0)
+    home = jax.ShapeDtypeStruct((3 * rows + extra, width), BF16)
+    return heads_call(
+        settle_kernel,
+        width // HEAD_DIM,
+        place,
+        [*zip(inner, part), *zip(outer, part)]
+        + [(x, HEAD_DIM) for x in (own_g, near, far)]
+        + [(x, 0) for x in more],
+        [(home, HEAD_DIM)] * GROUP + [(jax.ShapeDtypeStruct((8, HEAD_DIM), F32), 0)],
+        after,
         name="settle",
-    )(place, *inner, *outer, near, far, *after)
-
-
-def collect_kernel(chunks, place_ref, *refs):
+    )
+
+
+def join_kernel(head, place_ref, *refs):
+    *parts, mid, end = refs
+    half = len(parts) // 2
+    for out, some in ((mid, parts[:half]), (end, parts[half:])):
+        first = 0
+        for part in some:
+            out[:, first : first + part.shape[1]] = part[...]
+            first += part.shape[1]
+
+
+def join(place, mids, ends):
+    shape = jax.ShapeDtypeStruct((16, sum(x.shape[1] for x in mids)), BF16)
+    return heads_call(
+        join_kernel,
+        1,
+        place,
+        [(x, 0) for x in (*mids, *ends)],
+        [(shape, 0), (shape, 0)],
+        name="join",
+    )
+
+
+def total_kernel(chunks, place_ref, ids_ref, raw_ref, gain_ref, *refs):
+    *refs, out, sums = refs
+    homes, dot_refs = refs[: GROUP * len(chunks)], refs[GROUP * len(chunks) :]
+    rows, width = out.shape[0], sums.shape[1]
     me = place_ref[0]
-    out = refs[-1]
-    each = out.shape[1] // GROUP
+    device = place_ref[1] * GROUP + me
+    total = dot_refs[0][...]
+    for ref in dot_refs[1:]:
+        total = total + ref[...]
+    few = lax.broadcasted_iota(jnp.int32, (16, HEAD_DIM), 0)
+    eight = lax.broadcasted_iota(jnp.int32, (8, HEAD_DIM), 0)
+    hot = [few == 8 * i + G_DEV * me + r for i in range(2) for r in range(G_DEV)]
+    dot = [jnp.zeros((1, HEAD_DIM), F32) for _ in range(G_DEV)]
     for d in range(GROUP):
         first = 0
         for c, count in enumerate(chunks):
-            at = pl.multiple_of((me ^ d) * each + first * HEAD_DIM, HEAD_DIM)
-            out[:, pl.ds(at, count * HEAD_DIM)] = refs[c * GROUP + d][...]
+            for h in range(count):
+                home = homes[c * GROUP + d]
+                last = homes[(len(chunks) - 1) * GROUP + d]
+                at = 3 * rows + 16 * (first + h + 1)
+                part = home[3 * rows : 3 * rows + 16, h * HEAD_DIM : (h + 1) * HEAD_DIM].astype(F32)
+                part = part + last[at : at + 16, :HEAD_DIM].astype(F32)
+                found = [jnp.sum(jnp.where(x, part, 0.0), axis=0, keepdims=True) for x in hot]
+                at = pl.multiple_of(
+                    (me ^ d) * (width // GROUP) + (first + h) * HEAD_DIM, HEAD_DIM
+                )
+                here = pl.ds(at, HEAD_DIM)
+                block = jnp.zeros((8, HEAD_DIM), F32)
+                for i, x in enumerate(found):
+                    block = jnp.where(eight == i, x, block)
+                sums[:, here] = block
+                raw = raw_ref[:, here].astype(F32)
+                for r in range(G_DEV):
+                    dot[r] = dot[r] + found[r] * gain_ref[:, here] * raw[r : r + 1]
             first += count
-
-
-def collect(place, grads, width, chunks):
-    flat = [x for chunk in grads for x in chunk]
-    return pl.pallas_call(
-        functools.partial(collect_kernel, chunks),
-        out_shape=jax.ShapeDtypeStruct((EXTRA, width), BF16),
-        grid_spec=pltpu.PrefetchScalarGridSpec(
-            num_scalar_prefetch=1,
-            grid=(1,),
-            in_specs=[
-                pl.BlockSpec(
-                    (EXTRA, x.shape[1]),
-                    lambda i, place, n=x.shape[0] // EXTRA - 1: (n, 0),
-                )
-                for x in flat
-            ],
-            out_specs=pl.BlockSpec((EXTRA, width), lambda i, place: (0, 0)),
-        ),
-        compiler_params=params(),
-        cost_estimate=cost(1, 1),
-        name="collect",
-    )(place, *flat)
-
-
-def global_sum(parts, row):
-    return sum(
-        part[row + 2 * e : row + 2 * e + 1].astype(F32) for e, part in enumerate(parts)
-    )
-
-
-def total_kernel(place_ref, ids_ref, raw_ref, gain_ref, p0, p1, p2, p3, *refs):
-    out = refs[-1]
-    rows = out.shape[0]
-    device = place_ref[1] * GROUP + place_ref[0]
-    total = refs[0][...]
-    for ref in refs[1:-1]:
-        total = total + ref[...]
     row = lax.broadcasted_iota(jnp.int32, (rows, HEAD_DIM), 0)
     lane = lax.broadcasted_iota(jnp.int32, (rows, HEAD_DIM), 1)
-    parts = [p[...] for p in (p0, p1, p2, p3)]
     for r in range(G_DEV):
-        raw = raw_ref[...].astype(F32)[r : r + 1]
-        dot = jnp.sum(global_sum(parts, r) * gain_ref[...] * raw, axis=1, keepdims=True)
         here = (row == ids_ref[r] - device * rows) & (lane >= HEAD_DIM // 2)
-        total = total + jnp.where(here, dot, 0.0)
+        total = total + jnp.where(here, jnp.sum(dot[r], axis=1, keepdims=True), 0.0)
     out[...] = total
 
 
-def total_dots(place, ids, raw, gain, parts, dots):
+def total_dots(place, ids, raw, gain, homes, dots, chunks):
     smem = pl.BlockSpec(memory_space=pltpu.SMEM)
     vmem = pl.BlockSpec(memory_space=pltpu.VMEM)
+    flat = [x for home in homes for x in home]
     return pl.pallas_call(
-        total_kernel,
-        out_shape=jax.ShapeDtypeStruct(dots[0].shape, F32),
-        in_specs=[smem, smem] + [vmem] * (2 + GROUP + len(dots)),
-        out_specs=vmem,
+        functools.partial(total_kernel, chunks),
+        out_shape=[
+            jax.ShapeDtypeStruct(dots[0].shape, F32),
+            jax.ShapeDtypeStruct((8, raw.shape[1]), F32),
+        ],
+        in_specs=[smem, smem] + [vmem] * (2 + len(flat) + len(dots)),
+        out_specs=[vmem, vmem],
         compiler_params=params(),
         cost_estimate=cost(1, 1),
         name="total_dots",
-    )(place, ids, raw, gain, *parts, *dots)
-
-
-def dots_kernel(place_ref, *refs):
-    out_ref = refs[-1]
+    )(place, ids, raw, gain, *flat, *dots)
+
+
+def dots_kernel(first, head, place_ref, g0, g1, g2, g3, query, key, query_gain, key_gain, out_ref):
     rows = out_ref.shape[0]
-    step = pl.program_id(0)
+    each = query.shape[1] // HEAD_DIM // GROUP
     totals = [jnp.zeros((rows, HEAD_DIM), F32), jnp.zeros((rows, HEAD_DIM), F32)]
-    for d in range(GROUP):
-        grads, query, key, query_gain, key_gain = refs[5 * d : 5 * d + 5]
-        totals[0] += grads[:rows].astype(F32) * query_gain[...] * query[...].astype(F32)
-        totals[1] += grads[rows:].astype(F32) * key_gain[...] * key[...].astype(F32)
-    part = lane_pair(
+    for d, grads in enumerate((g0, g1, g2, g3)):
+        for h in range(grads.shape[1] // HEAD_DIM):
+            at = ((place_ref[0] ^ d) * each + first + h) * HEAD_DIM
+            here = pl.ds(pl.multiple_of(at, HEAD_DIM), HEAD_DIM)
+            lanes = slice(h * HEAD_DIM, (h + 1) * HEAD_DIM)
+            for i, (raw, gain) in enumerate(((query, query_gain), (key, key_gain))):
+                grad = grads[i * rows : (i + 1) * rows, lanes].astype(F32)
+                totals[i] += grad * gain[:, here] * raw[:, here].astype(F32)
+    out_ref[...] = lane_pair(
         jnp.sum(totals[0], axis=1, keepdims=True), jnp.sum(totals[1], axis=1, keepdims=True), rows
     )
 
-    @pl.when(step == 0)
-    def _():
-        out_ref[...] = part
-
-    @pl.when(step > 0)
-    def _():
-        out_ref[...] += part
-
 
 def dots(place, grads, query_raw, key_raw, gains, first, after):
-    rows, full = query_raw.shape
-    count = grads[0].shape[1] // HEAD_DIM
-    each = full // HEAD_DIM // GROUP
-    specs, operands = [], []
-    for d in range(GROUP):
-        at = lambda h, place, d=d: (0, (place[0] ^ d) * each + first + h)
-        specs += (
-            [pl.BlockSpec((2 * rows, HEAD_DIM), lambda h, place: (0, h))]
-            + [pl.BlockSpec((rows, HEAD_DIM), at)] * 2
-            + [pl.BlockSpec((1, HEAD_DIM), at)] * 2
-        )
-        operands += [grads[d], query_raw, key_raw, gains[0], gains[1]]
-    return pl.pallas_call(
-        behind(dots_kernel, 1 + 5 * GROUP, len(after)),
-        out_shape=jax.ShapeDtypeStruct((rows, HEAD_DIM), F32),
-        grid_spec=pltpu.PrefetchScalarGridSpec(
-            num_scalar_prefetch=1,
-            grid=(count,),
-            in_specs=specs + [ANY] * len(after),
-            out_specs=pl.BlockSpec((rows, HEAD_DIM), lambda h, place: (0, 0)),
-        ),
-        compiler_params=params(),
-        cost_estimate=cost(1, 16 * rows * count * HEAD_DIM * 2),
+    return heads_call(
+        functools.partial(dots_kernel, first),
+        1,
+        place,
+        [(x, 0) for x in (*grads, query_raw, key_raw, *gains)],
+        [(jax.ShapeDtypeStruct((query_raw.shape[0], HEAD_DIM), F32), 0)],
+        after,
         name="dots",
-    )(place, *operands, *after)
+    )[0]
 
 
 def finish_kernel(chunks, place_ref, ids_ref, own_ref, other_ref, dot_ref, dot_other_ref, *refs):
-    me = place_ref[0]
-    device = place_ref[1] * GROUP + me
-    p0, p1, p2, p3, *refs = refs
+    device = place_ref[1] * GROUP + place_ref[0]
     grads = refs[: GROUP * len(chunks)]
-    query_ref, key_ref, query_gain, key_gain = refs[GROUP * len(chunks) : GROUP * len(chunks) + 4]
-    query_out, key_out, value_out = refs[GROUP * len(chunks) + 4 :]
-    rows, full = query_ref.shape
-    each = full // GROUP
+    sum_ref, query_ref, key_ref, query_gain, key_gain = refs[GROUP * len(chunks) : -3]
+    query_out, key_out, value_out = refs[-3:]
+    rows = query_ref.shape[0]
+    each = query_ref.shape[1] // GROUP
     inv = inverses(own_ref[...], other_ref[...])
     total = dot_ref[...] + dot_other_ref[...]
     dot = (total[:, :1], total[:, HEAD_DIM // 2 : HEAD_DIM // 2 + 1])
     coeff = [inv[i] * inv[i] * inv[i] * (dot[i] / D) for i in range(2)]
     row = lax.broadcasted_iota(jnp.int32, (rows, HEAD_DIM), 0)
     hot = [row == ids_ref[r] - device * rows for r in range(G_DEV)]
-    for d in range(GROUP):
+
+    def whole(d):
         first = 0
         for c, count in enumerate(chunks):
             ref = grads[c * GROUP + d]
             for h in range(count):
-                at = pl.multiple_of((me ^ d) * each + (first + h) * HEAD_DIM, HEAD_DIM)
+                at = (first + h) * HEAD_DIM
+                there = slice(at, at + HEAD_DIM)
+                at = pl.multiple_of((place_ref[0] ^ d) * each + at, HEAD_DIM)
                 here = pl.ds(at, HEAD_DIM)
                 col = slice(h * HEAD_DIM, (h + 1) * HEAD_DIM)
-                parts = [p[:, here] for p in (p0, p1, p2, p3)]
                 grad = [ref[i * rows : (i + 1) * rows, col].astype(F32) for i in range(3)]
                 for i in (1, 2):
                     for r in range(G_DEV):
-                        more = global_sum(parts, 8 * (i - 1) + r)
+                        more = sum_ref[2 * (i - 1) + r : 2 * (i - 1) + r + 1, here]
                         grad[i] = grad[i] + jnp.where(hot[r], more, 0.0)
                 for i, (raw, gain, out) in enumerate(
                     ((query_ref, query_gain, query_out), (key_ref, key_gain, key_out))
                 ):
-                    out[:, here] = (
+                    out[:, there] = (
                         inv[i] * (grad[i] * gain[:, here]) - raw[:, here].astype(F32) * coeff[i]
                     ).astype(BF16)
-                value_out[:, here] = grad[2].astype(BF16)
+                value_out[:, there] = grad[2].astype(BF16)
             first += count
 
-
-def finish(place, ids, own, other, dot, dot_other, parts, grads, query_raw, key_raw, gains, chunks):
+    for d in range(GROUP):
+        pl.when(pl.program_id(0) == d)(functools.partial(whole, d))
+
+
+def finish(place, ids, own, other, dot, dot_other, sums, grads, query_raw, key_raw, gains, chunks):
+    rows, width = query_raw.shape
+    block = width // GROUP
+    smem = pl.BlockSpec(memory_space=pltpu.SMEM)
+    at = lambda i, place: (0, place[0] ^ i)
     vmem = pl.BlockSpec(memory_space=pltpu.VMEM)
-    smem = pl.BlockSpec(memory_space=pltpu.SMEM)
     flat = [x for chunk in grads for x in chunk]
+    column = pl.BlockSpec((rows, block), at)
     return pl.pallas_call(
         functools.partial(finish_kernel, chunks),
         out_shape=[jax.ShapeDtypeStruct(query_raw.shape, BF16)] * 3,
-        in_specs=[smem, smem] + [vmem] * (4 + GROUP + len(flat) + 4),
-        out_specs=[vmem] * 3,
+        grid_spec=pltpu.PrefetchScalarGridSpec(
+            num_scalar_prefetch=1,
+            grid=(GROUP,),
+            in_specs=[smem] + [vmem] * (4 + len(flat) + 5),
+            out_specs=[column] * 3,
+        ),
         compiler_params=params(),
         cost_estimate=cost(1, 1),
         name="finish",
-    )(place, ids, own, other, dot, dot_other, *parts, *flat, query_raw, key_raw, *gains)
+    )(place, ids, own, other, dot, dot_other, *flat, sums, query_raw, key_raw, *gains)
 
 
 def swap_heads(x):
@@ -633,8 +643,8 @@
     own = squares(query_raw, key_raw)
     other = swap_heads(own)
     arrays = (query_raw, key_raw, values, out_grad)
-    *sent, raw_rows = global_rows(place, global_ids, own, other, key_raw, values, gains[1])
-    parts = [sent[0]] + [swapped(sent[e], 4 * e) for e in range(1, GROUP)]
+    mine, raw_rows = global_rows(place, global_ids, own, other, key_raw, values, gains[1])
+    parts = [mine] + [swapped(mine, 4 * e) for e in range(1, GROUP)]
     chunks = len(CHUNKS)
     firsts = [sum(CHUNKS[:c]) for c in range(chunks)]
     packed, token = [], ()
@@ -645,6 +655,7 @@
         token = (last,)
         packed.append([sent[0]] + [swapped(sent[d], d) for d in range(1, GROUP)])
     edge, inner, outer, back, home, dot = ({} for _ in range(6))
+    fars = []
 
     def begin(c, token):
         near, far, last = edges(place, packed[c], token)
@@ -652,16 +663,23 @@
         return (last,)
 
     def inside(c, token):
-        inner[c] = attend(place, packed[c], (), token)
+        inner[c] = attend(place, packed[c], (), (), token)
         return (inner[c][2],)
 
     def outside(c, token):
-        *outer[c], near, far = attend(place, packed[c], edge[c], token)
-        back[c] = (swapped(near, 4), swapped_edges(far))
-        return (outer[c][2],)
+        results = attend(place, packed[c], edge[c], (inner[c][2],), token)
+        outer[c], own_g, near, far, mid, last = results[:2], *results[2:]
+        fars.append((mid, last))
+        more = ()
+        if c == chunks - 1:
+            mids, lasts = zip(*fars)
+            mid, last = join(place, mids, lasts)
+            more = (swapped(mid, 8), swapped(last, 12))
+        back[c] = (own_g, swapped(near, 4), swapped_edges(far), more)
+        return (own_g,)
 
     def end(c, token):
-        *sent, last = settle(place, inner[c], outer[c], *back[c], token)
+        *sent, last = settle(place, inner[c][:2], outer[c], *back[c], token)
         home[c] = [sent[0]] + [swapped(sent[d], d) for d in range(1, GROUP)]
         return (last,)
 
@@ -675,14 +693,12 @@
         held = tuple((packed if e[0] == "i" else home)[int(e[1])]["oxyd".index(e[2])] for e in extra)
         token = stages[name[0]](int(name[1]), token + held)
     homes = [home[c] for c in range(chunks)]
-    mine = collect(place, homes, query_raw.shape[1], CHUNKS)
-    parts = [mine] + [swapped(mine, 4 * e) for e in range(1, GROUP)]
-    total = total_dots(
-        place, global_ids, raw_rows, gains[1], parts, [dot[c] for c in range(chunks)]
+    total, sums = total_dots(
+        place, global_ids, raw_rows, gains[1], homes, [dot[c] for c in range(chunks)], CHUNKS
     )
     return tuple(
         finish(
-            place, global_ids, own, other, total, swap_heads(total), parts, homes,
+            place, global_ids, own, other, total, swap_heads(total), sums, homes,
             query_raw, key_raw, gains, CHUNKS,
         )
     )

time: 156 us -> 144 us (0.923)
  Pallas kernels: 56.6 us -> 47.8 us
  starting transfers between devices: 57.5 us -> 49.7 us
  waiting for transfers between devices: 37.7 us -> 42.6 us
    pallas_call x21, Pallas kernels: 49.5 us -> 41 us  [the longest x16 32.5 us: heads_call(): pl.pallas_call(run, out_shape=[shape for shape, _ in outputs], in_specs=[...]
    ppermute x30 -> x29, starting transfers between devices: 52.6 us -> 44.9 us  [swapped(): return lax.ppermute(shard, 'ctx', [(i, i ^ bit) for i in range(count)])]
    ppermute x30 -> x29, waiting for transfers between devices: 35.5 us -> 40.3 us  [swapped(): return lax.ppermute(shard, 'ctx', [(i, i ^ bit) for i in range(count)])]
  transfers between devices with their start and end apart: 38 -> 37, of which waited for: 15 -> 15; matrix products, arithmetic and copies ran while one was open for 0% -> 0% of each run, Pallas kernels for 25% -> 24%
where the time goes in v3:
time: 144 us
  starting transfers between devices  49.7 us (35%)
  Pallas kernels  47.8 us (33%)
  waiting for transfers between devices  42.6 us (30%)
  local copies, waits for them, and re-layouts  2.92 us (2%)
    ppermute x29, starting transfers between devices, swapped(): return lax.ppermute(shard, 'ctx', [(i, i ^ bit) for i in range(count)])  44.9 us
    ppermute x29, waiting for transfers between devices, swapped(): return lax.ppermute(shard, 'ctx', [(i, i ^ bit) for i in range(count)])  40.3 us
    pallas_call x16, Pallas kernels, heads_call(): pl.pallas_call(run, out_shape=[shape for shape, _ in outputs], in_specs=[...  32.5 us
    pallas_call x3, Pallas kernels, pack(): pl.pallas_call(behind(kernel, 11 + GROUP, len(after)), out_shape=[jax.Sha...  6.95 us
    pallas_call x1, Pallas kernels, finish(): pl.pallas_call(functools.partial(finish_kernel, chunks), out_shape=[jax.S...  6.15 us
    ppermute x6, starting transfers between devices, swapped_edges(): return lax.ppermute(shard, 'ctx', pairs)  4.18 us
    unnamed x24, local copies, waits for them, and re-layouts  2.9 us
  transfers between devices with their start and end apart: 37, of which 15 were waited for; matrix products, arithmetic and copies ran while one was open for 0% of the time, Pallas kernels for 24%

profile of v3, /device:TPU:0, one launch (start us, length us, event | category | flops | bytes accessed | tf_op | source)
XLA Modules:
  0.0 143.9 jit_solution(17661274084440311297)
XLA Ops:
  0.6 1.3 copy-done
  2.0 1.3 copy-done.2
  6.2 5.0 %collective-permute-start.3 = (bf16[16,640]{1,0:T(8,128)(2,1)S(1)}, bf16[16,640]{1,0:T(8,128)(2,1)S(1)}, u32[]{:S(2)}, u32[]{:S(2)}) collective-permute-start(bf16[16,640]{1,0:T(8,128)(2,1)S(1)} %get-tuple-element.79.refs_11_), channel_id=1, source_target_pairs={{0,24},{2,26},{4,28},{6,30},{8,16},{10,18},{12,20},{14,22},{16,8},... | collective-permute-start | bytes 61448 | tf_op jit(solution)/shard_map/ppermute | solution.py:32
  11.8 1.1 collective-permute-done.3.refs_14_
  13.0 2.9 %collective-permute-done.2.refs_13_ = bf16[16,640]{1,0:T(8,128)(2,1)S(1)} collective-permute-done((bf16[16,640]{1,0:T(8,128)(2,1)S(1)}, bf16[16,640]{1,0:T(8,128)(2,1)S(1)}, u32[]{:S(2)}, u32[]{:S(2)}) %collective-permute-start.2) | collective-permute-done | bytes 20512 | tf_op jit(solution)/shard_map/ppermute | solution.py:32
  15.9 2.2 %pack.3 = (bf16[1056,256]{1,0:T(8,128)(2,1)S(1)}, bf16[1056,256]{1,0:T(8,128)(2,1)S(1)}, bf16[1056,256]{1,0:T(8,128)(2,1)S(1)}, bf16[1056,256]{1,0:T(8,128)(2,1)S(1)}, f32[8,128]{1,0:T(8,128)S(1)}) custom-call(s32[2]{0:T(128)S(1)} %pad_add_fusion.place_ref.refs_0_, s32[2,4]{1,0:T(2,128)S(1)} %copy-done.7, s32[1,16]{1,0:T(1,128)S(1)} %copy-done.8, ...), custom_call_target="tpu_custom_call" | custom-call | flops 1 | bytes 1 | tf_op jit(solution)/shard_map/pack/pallas_call | solution.py:221
  18.1 1.6 %collective-permute-start.4 = (bf16[1056,256]{1,0:T(8,128)(2,1)S(1)}, bf16[1056,256]{1,0:T(8,128)(2,1)S(1)}, u32[]{:S(2)}, u32[]{:S(2)}) collective-permute-start(bf16[1056,256]{1,0:T(8,128)(2,1)S(1)} %get-tuple-element.81), channel_id=1, source_target_pairs={{0,2},{2,0},{4,6},{6,4},{8,10},{10,8},{12,14},{14,12},{16,18},{18,... | collective-permute-start | bytes 1622024 | tf_op jit(solution)/shard_map/ppermute | solution.py:32
  19.7 1.5 %collective-permute-start.5 = (bf16[1056,256]{1,0:T(8,128)(2,1)S(1)}, bf16[1056,256]{1,0:T(8,128)(2,1)S(1)}, u32[]{:S(2)}, u32[]{:S(2)}) collective-permute-start(bf16[1056,256]{1,0:T(8,128)(2,1)S(1)} %get-tuple-element.82), channel_id=1, source_target_pairs={{0,4},{2,6},{4,0},{6,2},{8,12},{10,14},{12,8},{14,10},{16,20},{18,... | collective-permute-start | bytes 1622024 | tf_op jit(solution)/shard_map/ppermute | solution.py:32
  21.7 2.3 %pack.4 = (bf16[1056,256]{1,0:T(8,128)(2,1)S(1)}, bf16[1056,256]{1,0:T(8,128)(2,1)S(1)}, bf16[1056,256]{1,0:T(8,128)(2,1)S(1)}, bf16[1056,256]{1,0:T(8,128)(2,1)S(1)}, f32[8,128]{1,0:T(8,128)S(1)}) custom-call(s32[2]{0:T(128)S(1)} %pad_add_fusion.place_ref.refs_0_, s32[2,4]{1,0:T(2,128)S(1)} %copy-done.7, s32[1,16]{1,0:T(1,128)S(1)} %copy-done.8, ...), custom_call_target="tpu_custom_call" | custom-call | flops 1 | bytes 1 | tf_op jit(solution)/shard_map/pack/pallas_call | solution.py:221
  24.0 1.6 %collective-permute-start.11 = (bf16[1056,256]{1,0:T(8,128)(2,1)S(1)}, bf16[1056,256]{1,0:T(8,128)(2,1)S(1)}, u32[]{:S(2)}, u32[]{:S(2)}) collective-permute-start(bf16[1056,256]{1,0:T(8,128)(2,1)S(1)} %get-tuple-element.99), channel_id=1, source_target_pairs={{0,2},{2,0},{4,6},{6,4},{8,10},{10,8},{12,14},{14,12},{16,18},{18,... | collective-permute-start | bytes 1622024 | tf_op jit(solution)/shard_map/ppermute | solution.py:32
  25.6 1.5 %collective-permute-start.12 = (bf16[1056,256]{1,0:T(8,128)(2,1)S(1)}, bf16[1056,256]{1,0:T(8,128)(2,1)S(1)}, u32[]{:S(2)}, u32[]{:S(2)}) collective-permute-start(bf16[1056,256]{1,0:T(8,128)(2,1)S(1)} %get-tuple-element.100), channel_id=1, source_target_pairs={{0,4},{2,6},{4,0},{6,2},{8,12},{10,14},{12,8},{14,10},{16,20},{18,... | collective-permute-start | bytes 1622024 | tf_op jit(solution)/shard_map/ppermute | solution.py:32
  27.1 6.3 %collective-permute-done.4.refs_1_ = bf16[1056,256]{1,0:T(8,128)(2,1)S(1)} collective-permute-done((bf16[1056,256]{1,0:T(8,128)(2,1)S(1)}, bf16[1056,256]{1,0:T(8,128)(2,1)S(1)}, u32[]{:S(2)}, u32[]{:S(2)}) %collective-permute-start.4) | collective-permute-done | bytes 540704 | tf_op jit(solution)/shard_map/ppermute | solution.py:32
  33.4 2.4 %collective-permute-start.13 = (bf16[1056,256]{1,0:T(8,128)(2,1)S(1)}, bf16[1056,256]{1,0:T(8,128)(2,1)S(1)}, u32[]{:S(2)}, u32[]{:S(2)}) collective-permute-start(bf16[1056,256]{1,0:T(8,128)(2,1)S(1)} %get-tuple-element.101), channel_id=1, source_target_pairs={{0,6},{2,4},{4,2},{6,0},{8,14},{10,12},{12,10},{14,8},{16,22},{18,... | collective-permute-start | bytes 1622024 | tf_op jit(solution)/shard_map/ppermute | solution.py:32
  35.8 2.4 %pack.5 = (bf16[1056,128]{1,0:T(8,128)(2,1)S(1)}, bf16[1056,128]{1,0:T(8,128)(2,1)}, bf16[1056,128]{1,0:T(8,128)(2,1)}, bf16[1056,128]{1,0:T(8,128)(2,1)S(1)}, f32[8,128]{1,0:T(8,128)S(1)}) custom-call(s32[2]{0:T(128)S(1)} %pad_add_fusion.place_ref.refs_0_, s32[2,4]{1,0:T(2,128)S(1)} %copy-done.7, s32[1,16]{1,0:T(1,128)S(1)} %copy-done.8, ...), custom_call_target="tpu_custom_call" | custom-call | flops 1 | bytes 1 | tf_op jit(solution)/shard_map/pack/pallas_call | solution.py:221
  38.2 8.2 %collective-permute-done.5.refs_2_ = bf16[1056,256]{1,0:T(8,128)(2,1)S(1)} collective-permute-done((bf16[1056,256]{1,0:T(8,128)(2,1)S(1)}, bf16[1056,256]{1,0:T(8,128)(2,1)S(1)}, u32[]{:S(2)}, u32[]{:S(2)}) %collective-permute-start.5) | collective-permute-done | bytes 540704 | tf_op jit(solution)/shard_map/ppermute | solution.py:32
  47.9 4.3 %inner.3 = (bf16[512,256]{1,0:T(8,128)(2,1)S(1)}, bf16[1024,512]{1,0:T(8,128)(2,1)S(1)}, f32[32,512]{1,0:T(8,128)S(1)}) custom-call(s32[2]{0:T(128)S(1)} %pad_add_fusion.place_ref.refs_0_, bf16[1056,256]{1,0:T(8,128)(2,1)S(1)} %get-tuple-element.80.refs_0_, bf16[1056,256]{1,0:T(8,128)(2,1)S(1)} %collective-permute-done.4.refs_1_, ...), custom_call_target="tpu_custom_call" | custom-call | flops 1 | bytes 1 | tf_op jit(solution)/shard_map/inner/pallas_call | solution.py:68
  52.2 1.4 collective-permute-done.7.refs_4_
  53.5 4.8 %outer.3 = (bf16[512,256]{1,0:T(8,128)(2,1)S(1)}, bf16[1024,512]{1,0:T(8,128)(2,1)S(1)}, bf16[16,256]{1,0:T(8,128)(2,1)S(1)}, bf16[528,256]{1,0:T(8,128)(2,1)S(1...) custom-call(s32[2]{0:T(128)S(1)} %pad_add_fusion.place_ref.refs_0_, ...), custom_call_target="tpu_custom_call" | custom-call | flops 1 | bytes 1 | tf_op jit(solution)/shard_map/outer/pallas_call | solution.py:68
  58.4 4.0 %collective-permute-start.9 = (bf16[528,256]{1,0:T(8,128)(2,1)S(1)}, bf16[528,256]{1,0:T(8,128)(2,1)S(1)}, u32[]{:S(2)}, u32[]{:S(2)}) collective-permute-start(bf16[528,256]{1,0:T(8,128)(2,1)S(1)} %get-tuple-element.96), channel_id=1, source_target_pairs={{0,8},{2,10},{4,12},{6,14},{8,0},{10,2},{12,4},{14,6},{16,24},{18,... | collective-permute-start | bytes 811016 | tf_op jit(solution)/shard_map/ppermute | solution.py:32
  63.0 1.1 collective-permute-start.19
  64.1 3.0 %collective-permute-done.12.refs_2_ = bf16[1056,256]{1,0:T(8,128)(2,1)S(1)} collective-permute-done((bf16[1056,256]{1,0:T(8,128)(2,1)S(1)}, bf16[1056,256]{1,0:T(8,128)(2,1)S(1)}, u32[]{:S(2)}, u32[]{:S(2)}) %collective-permute-start.12) | collective-permute-done | bytes 540704 | tf_op jit(solution)/shard_map/ppermute | solution.py:32
  67.0 2.8 %collective-permute-start.20 = (bf16[1056,128]{1,0:T(8,128)(2,1)}, bf16[1056,128]{1,0:T(8,128)(2,1)S(1)}, u32[]{:S(2)}, u32[]{:S(2)}) collective-permute-start(bf16[1056,128]{1,0:T(8,128)(2,1)} %get-tuple-element.114), channel_id=1, source_target_pairs={{0,4},{2,6},{4,0},{6,2},{8,12},{10,14},{12,8},{14,10},{16,20},{18,... | collective-permute-start | bytes 811016 | tf_op jit(solution)/shard_map/ppermute | solution.py:32
  72.2 4.3 %inner.4 = (bf16[512,256]{1,0:T(8,128)(2,1)S(1)}, bf16[1024,512]{1,0:T(8,128)(2,1)S(1)}, f32[32,512]{1,0:T(8,128)S(1)}) custom-call(s32[2]{0:T(128)S(1)} %pad_add_fusion.place_ref.refs_0_, bf16[1056,256]{1,0:T(8,128)(2,1)S(1)} %get-tuple-element.98.refs_0_, bf16[1056,256]{1,0:T(8,128)(2,1)S(1)} %collective-permute-done.11.refs_1_, ...), custom_call_target="tpu_custom_call" | custom-call | flops 1 | bytes 1 | tf_op jit(solution)/shard_map/inner/pallas_call | solution.py:68
  76.5 1.4 settle.3
  78.7 2.2 %collective-permute-done.20.refs_2_ = bf16[1056,128]{1,0:T(8,128)(2,1)S(1)} collective-permute-done((bf16[1056,128]{1,0:T(8,128)(2,1)}, bf16[1056,128]{1,0:T(8,128)(2,1)S(1)}, u32[]{:S(2)}, u32[]{:S(2)}) %collective-permute-start.20) | collective-permute-done | bytes 270368 | tf_op jit(solution)/shard_map/ppermute | solution.py:32
  80.9 2.0 %collective-permute-start.15 = (bf16[784,256]{1,0:T(8,128)(2,1)S(1)}, bf16[784,256]{1,0:T(8,128)(2,1)S(1)}, u32[]{:S(2)}, u32[]{:S(2)}) collective-permute-start(bf16[784,256]{1,0:T(8,128)(2,1)S(1)} %get-tuple-element.106), channel_id=1, source_target_pairs={{0,4},{2,6},{4,0},{6,2},{8,12},{10,14},{12,8},{14,10},{16,20},{18,... | collective-permute-start | bytes 1204232 | tf_op jit(solution)/shard_map/ppermute | solution.py:32
  83.5 4.8 %outer.4 = (bf16[512,256]{1,0:T(8,128)(2,1)S(1)}, bf16[1024,512]{1,0:T(8,128)(2,1)S(1)}, bf16[16,256]{1,0:T(8,128)(2,1)S(1)}, bf16[528,256]{1,0:T(8,128)(2,1)S(1...) custom-call(s32[2]{0:T(128)S(1)} %pad_add_fusion.place_ref.refs_0_, ...), custom_call_target="tpu_custom_call" | custom-call | flops 1 | bytes 1 | tf_op jit(solution)/shard_map/outer/pallas_call | solution.py:68
  88.4 2.5 %collective-permute-start.22 = (bf16[528,256]{1,0:T(8,128)(2,1)S(1)}, bf16[528,256]{1,0:T(8,128)(2,1)S(1)}, u32[]{:S(2)}, u32[]{:S(2)}) collective-permute-start(bf16[528,256]{1,0:T(8,128)(2,1)S(1)} %get-tuple-element.121), channel_id=1, source_target_pairs={{0,8},{2,10},{4,12},{6,14},{8,0},{10,2},{12,4},{14,6},{16,24},{18,... | collective-permute-start | bytes 811016 | tf_op jit(solution)/shard_map/ppermute | solution.py:32
  91.5 2.5 %inner.5 = (bf16[512,128]{1,0:T(8,128)(2,1)S(1)}, bf16[1024,256]{1,0:T(8,128)(2,1)S(1)}, f32[32,256]{1,0:T(8,128)S(1)}) custom-call(s32[2]{0:T(128)S(1)} %pad_add_fusion.place_ref.refs_0_, bf16[1056,128]{1,0:T(8,128)(2,1)S(1)} %get-tuple-element.112.refs_0_, bf16[1056,128]{1,0:T(8,128)(2,1)S(1)} %collective-permute-done.19.refs_1_, ...), custom_call_target="tpu_custom_call" | custom-call | flops 1 | bytes 1 | tf_op jit(solution)/shard_map/inner/pallas_call | solution.py:68
  94.0 3.1 %collective-permute-done.15.refs_2_ = bf16[784,256]{1,0:T(8,128)(2,1)S(1)} collective-permute-done((bf16[784,256]{1,0:T(8,128)(2,1)S(1)}, bf16[784,256]{1,0:T(8,128)(2,1)S(1)}, u32[]{:S(2)}, u32[]{:S(2)}) %collective-permute-start.15) | collective-permute-done | bytes 401440 | tf_op jit(solution)/shard_map/ppermute | solution.py:32
  97.1 1.0 dots.3.refs_7_.refs_12_
  98.3 1.6 %settle.4 = (bf16[784,256]{1,0:T(8,128)(2,1)S(1)}, bf16[784,256]{1,0:T(8,128)(2,1)S(1)}, bf16[784,256]{1,0:T(8,128)(2,1)S(1)}, bf16[784,256]{1,0:T(8,128)(2,1)S(1)}, f32[8,128]{1,0:T(8,128)S(1)}) custom-call(s32[2]{0:T(128)S(1)} %pad_add_fusion.place_ref.refs_0_, bf16[512,256]{1,0:T(8,128)(2,1)S(1)} %get-tuple-element.108.refs_0_, ...), custom_call_target="tpu_custom_call" | custom-call | flops 1 | bytes 1 | tf_op jit(solution)/shard_map/settle/pallas_call | solution.py:68
  100.3 1.1 collective-permute-start.25
  101.4 2.1 %collective-permute-start.26 = (bf16[784,256]{1,0:T(8,128)(2,1)S(1)}, bf16[784,256]{1,0:T(8,128)(2,1)S(1)}, u32[]{:S(2)}, u32[]{:S(2)}) collective-permute-start(bf16[784,256]{1,0:T(8,128)(2,1)S(1)} %get-tuple-element.127), channel_id=1, source_target_pairs={{0,6},{2,4},{4,2},{6,0},{8,14},{10,12},{12,10},{14,8},{16,22},{18,... | collective-permute-start | bytes 1204232 | tf_op jit(solution)/shard_map/ppermute | solution.py:32
  105.0 3.5 %collective-permute-done.27.refs_4_ = bf16[512,128]{1,0:T(8,128)(2,1)S(1)} collective-permute-done((bf16[512,128]{1,0:T(8,128)(2,1)S(1)}, bf16[512,128]{1,0:T(8,128)(2,1)S(1)}, u32[]{:S(2)}, u32[]{:S(2)}) %collective-permute-start.27) | collective-permute-done | bytes 131104 | tf_op jit(solution)/shard_map/ppermute | solution.py:32
  108.5 2.7 %outer.5 = (bf16[512,128]{1,0:T(8,128)(2,1)S(1)}, bf16[1024,256]{1,0:T(8,128)(2,1)S(1)}, bf16[16,128]{1,0:T(8,128)(2,1)S(1)}, bf16[528,128]{1,0:T(8,128)(2,1)S(1...) custom-call(s32[2]{0:T(128)S(1)} %pad_add_fusion.place_ref.refs_0_, ...), custom_call_target="tpu_custom_call" | custom-call | flops 1 | bytes 1 | tf_op jit(solution)/shard_map/outer/pallas_call | solution.py:68
  111.2 4.0 %collective-permute-start.29 = (bf16[528,128]{1,0:T(8,128)(2,1)S(1)}, bf16[528,128]{1,0:T(8,128)(2,1)S(1)}, u32[]{:S(2)}, u32[]{:S(2)}) collective-permute-start(bf16[528,128]{1,0:T(8,128)(2,1)S(1)} %get-tuple-element.136), channel_id=1, source_target_pairs={{0,8},{2,10},{4,12},{6,14},{8,0},{10,2},{12,4},{14,6},{16,24},{18,... | collective-permute-start | bytes 405512 | tf_op jit(solution)/shard_map/ppermute | solution.py:32
  116.4 2.8 %collective-permute-start.31 = (bf16[16,640]{1,0:T(8,128)(2,1)S(1)}, bf16[16,640]{1,0:T(8,128)(2,1)S(1)}, u32[]{:S(2)}, u32[]{:S(2)}) collective-permute-start(bf16[16,640]{1,0:T(8,128)(2,1)S(1)} %get-tuple-element.144), channel_id=1, source_target_pairs={{0,16},{2,18},{4,20},{6,22},{8,24},{10,26},{12,28},{14,30},{16,0},... | collective-permute-start | bytes 61448 | tf_op jit(solution)/shard_map/ppermute | solution.py:32
  119.2 1.6 %collective-permute-start.32 = (bf16[16,640]{1,0:T(8,128)(2,1)S(1)}, bf16[16,640]{1,0:T(8,128)(2,1)S(1)}, u32[]{:S(2)}, u32[]{:S(2)}) collective-permute-start(bf16[16,640]{1,0:T(8,128)(2,1)S(1)} %get-tuple-element.145), channel_id=1, source_target_pairs={{0,24},{2,26},{4,28},{6,30},{8,16},{10,18},{12,20},{14,22},{16,8},... | collective-permute-start | bytes 61448 | tf_op jit(solution)/shard_map/ppermute | solution.py:32
  120.8 1.0 dots.4.refs_9_.refs_13_
  121.8 3.0 %collective-permute-done.32.refs_8_ = bf16[16,640]{1,0:T(8,128)(2,1)S(1)} collective-permute-done((bf16[16,640]{1,0:T(8,128)(2,1)S(1)}, bf16[16,640]{1,0:T(8,128)(2,1)S(1)}, u32[]{:S(2)}, u32[]{:S(2)}) %collective-permute-start.32) | collective-permute-done | bytes 20512 | tf_op jit(solution)/shard_map/ppermute | solution.py:32
  126.1 1.6 %collective-permute-start.34 = (bf16[864,128]{1,0:T(8,128)(2,1)S(1)}, bf16[864,128]{1,0:T(8,128)(2,1)S(1)}, u32[]{:S(2)}, u32[]{:S(2)}) collective-permute-start(bf16[864,128]{1,0:T(8,128)(2,1)S(1)} %get-tuple-element.148), channel_id=1, source_target_pairs={{0,4},{2,6},{4,0},{6,2},{8,12},{10,14},{12,8},{14,10},{16,20},{18,... | collective-permute-start | bytes 663560 | tf_op jit(solution)/shard_map/ppermute | solution.py:32
  127.6 1.6 %collective-permute-start.35 = (bf16[864,128]{1,0:T(8,128)(2,1)S(1)}, bf16[864,128]{1,0:T(8,128)(2,1)S(1)}, u32[]{:S(2)}, u32[]{:S(2)}) collective-permute-start(bf16[864,128]{1,0:T(8,128)(2,1)S(1)} %get-tuple-element.149), channel_id=1, source_target_pairs={{0,6},{2,4},{4,2},{6,0},{8,14},{10,12},{12,10},{14,8},{16,22},{18,... | collective-permute-start | bytes 663560 | tf_op jit(solution)/shard_map/ppermute | solution.py:32
  129.3 2.4 %collective-permute-done.33.refs_1_.refs_9_ = bf16[864,128]{1,0:T(8,128)(2,1)S(1)} collective-permute-done((bf16[864,128]{1,0:T(8,128)(2,1)S(1)}, bf16[864,128]{1,0:T(8,128)(2,1)S(1)}, u32[]{:S(2)}, u32[]{:S(2)}) %collective-permute-start.33) | collective-permute-done | bytes 221216 | tf_op jit(solution)/shard_map/ppermute | solution.py:32
  131.7 1.8 %collective-permute-done.34.refs_2_.refs_10_ = bf16[864,128]{1,0:T(8,128)(2,1)S(1)} collective-permute-done((bf16[864,128]{1,0:T(8,128)(2,1)S(1)}, bf16[864,128]{1,0:T(8,128)(2,1)S(1)}, u32[]{:S(2)}, u32[]{:S(2)}) %collective-permute-start.34) | collective-permute-done | bytes 221216 | tf_op jit(solution)/shard_map/ppermute | solution.py:32
  133.5 1.3 collective-permute-done.35.refs_3_.refs_11_
  136.5 1.3 collective-permute-done.36.dot_other_ref
  137.8 6.1 %finish.1 = (bf16[256,2560]{1,0:T(8,128)(2,1)}, bf16[256,2560]{1,0:T(8,128)(2,1)}, bf16[256,2560]{1,0:T(8,128)(2,1)}) custom-call(s32[2]{0:T(128)S(1)} %pad_add_fusion.place_ref.refs_0_, s32[2]{0:T(128)S(1)} %copy-done.9, f32[256,128]{1,0:T(8,128)S(1)} %squares.1.own_ref.refs_3_, f32[256,128]{1,0:T(8,128)S(1)} %collective-permute-done.other_ref.refs_4_, ...), custom_call_target="tpu_custom_call" | custom-call | flops 1 | bytes 1 | tf_op jit(solution)/shard_map/finish/pallas_call | solution.py:618
  (76 shorter events, 16.6 us)
Async XLA Ops:
  0.6 1.3 copy-start
  2.0 1.3 copy-start.2
  3.3 2.1 %copy-start.1 = (bf16[256,2560]{1,0:T(8,128)(2,1)S(1)}, bf16[256,2560]{1,0:T(8,128)(2,1)}, u32[]{:S(2)}) copy-start(bf16[256,2560]{1,0:T(8,128)(2,1)} %refs_14_.1) | copy-start | bytes 3932164
  3.3 2.1 %copy-start.4 = (bf16[256,2560]{1,0:T(8,128)(2,1)S(1)}, bf16[256,2560]{1,0:T(8,128)(2,1)}, u32[]{:S(2)}) copy-start(bf16[256,2560]{1,0:T(8,128)(2,1)} %refs_6_.5) | copy-start | bytes 3932164
  3.3 2.1 %copy-start.9 = (s32[2]{0:T(128)S(1)}, s32[2]{0:T(128)}, u32[]{:S(2)}) copy-start(s32[2]{0:T(128)} %ids_ref.5) | copy-start | bytes 28
  3.9 1.5 %collective-permute-start = (f32[256,128]{1,0:T(8,128)S(1)}, f32[256,128]{1,0:T(8,128)S(1)}, u32[]{:S(2)}, u32[]{:S(2)}) collective-permute-start(f32[256,128]{1,0:T(8,128)S(1)} %squares.1.own_ref.refs_3_), channel_id=1, source_target_pairs={{0,1},{1,0},{2,3},{3,2},{4,5},{5,4},{6,7},{7,6},{8,9},{9,8},{10,11... | collective-permute-start | bytes 393224 | tf_op jit(solution)/shard_map/ppermute | solution.py:634
  4.5 7.4 %copy-start.11 = (f32[2560]{0:T(1024)S(1)}, f32[2560]{0:T(1024)}, u32[]{:S(2)}) copy-start(f32[2560]{0:T(1024)} %param.13) | copy-start | bytes 30724
  4.5 11.4 %copy-start.7 = (s32[2,4]{1,0:T(2,128)S(1)}, s32[2,4]{1,0:T(2,128)}, u32[]{:S(2)}) copy-start(s32[2,4]{1,0:T(2,128)} %refs_1_.5) | copy-start | bytes 100
  4.5 11.4 %copy-start.8 = (s32[1,16]{1,0:T(1,128)S(1)}, s32[1,16]{1,0:T(1,128)}, u32[]{:S(2)}) copy-start(s32[1,16]{1,0:T(1,128)} %refs_2_.5) | copy-start | bytes 196
  6.2 6.8 %collective-permute-start.3 = (bf16[16,640]{1,0:T(8,128)(2,1)S(1)}, bf16[16,640]{1,0:T(8,128)(2,1)S(1)}, u32[]{:S(2)}, u32[]{:S(2)}) collective-permute-start(bf16[16,640]{1,0:T(8,128)(2,1)S(1)} %get-tuple-element.79.refs_11_), channel_id=1, source_target_pairs={{0,24},{2,26},{4,28},{6,30},{8,16},{10,18},{12,20},{14,22},{16,8},... | collective-permute-start | bytes 61448 | tf_op jit(solution)/shard_map/ppermute | solution.py:32
  11.2 4.7 %collective-permute-start.2 = (bf16[16,640]{1,0:T(8,128)(2,1)S(1)}, bf16[16,640]{1,0:T(8,128)(2,1)S(1)}, u32[]{:S(2)}, u32[]{:S(2)}) collective-permute-start(bf16[16,640]{1,0:T(8,128)(2,1)S(1)} %get-tuple-element.79.refs_11_), channel_id=1, source_target_pairs={{0,16},{2,18},{4,20},{6,22},{8,24},{10,26},{12,28},{14,30},{16,0},... | collective-permute-start | bytes 61448 | tf_op jit(solution)/shard_map/ppermute | solution.py:32
  11.2 4.7 %collective-permute-start.1 = (bf16[16,640]{1,0:T(8,128)(2,1)S(1)}, bf16[16,640]{1,0:T(8,128)(2,1)S(1)}, u32[]{:S(2)}, u32[]{:S(2)}) collective-permute-start(bf16[16,640]{1,0:T(8,128)(2,1)S(1)} %get-tuple-element.79.refs_11_), channel_id=1, source_target_pairs={{0,8},{2,10},{4,12},{6,14},{8,0},{10,2},{12,4},{14,6},{16,24},{18,... | collective-permute-start | bytes 61448 | tf_op jit(solution)/shard_map/ppermute | solution.py:32
  18.1 15.3 %collective-permute-start.4 = (bf16[1056,256]{1,0:T(8,128)(2,1)S(1)}, bf16[1056,256]{1,0:T(8,128)(2,1)S(1)}, u32[]{:S(2)}, u32[]{:S(2)}) collective-permute-start(bf16[1056,256]{1,0:T(8,128)(2,1)S(1)} %get-tuple-element.81), channel_id=1, source_target_pairs={{0,2},{2,0},{4,6},{6,4},{8,10},{10,8},{12,14},{14,12},{16,18},{18,... | collective-permute-start | bytes 1622024 | tf_op jit(solution)/shard_map/ppermute | solution.py:32
  19.7 26.8 %collective-permute-start.5 = (bf16[1056,256]{1,0:T(8,128)(2,1)S(1)}, bf16[1056,256]{1,0:T(8,128)(2,1)S(1)}, u32[]{:S(2)}, u32[]{:S(2)}) collective-permute-start(bf16[1056,256]{1,0:T(8,128)(2,1)S(1)} %get-tuple-element.82), channel_id=1, source_target_pairs={{0,4},{2,6},{4,0},{6,2},{8,12},{10,14},{12,8},{14,10},{16,20},{18,... | collective-permute-start | bytes 1622024 | tf_op jit(solution)/shard_map/ppermute | solution.py:32
  21.2 25.3 %collective-permute-start.6 = (bf16[1056,256]{1,0:T(8,128)(2,1)S(1)}, bf16[1056,256]{1,0:T(8,128)(2,1)S(1)}, u32[]{:S(2)}, u32[]{:S(2)}) collective-permute-start(bf16[1056,256]{1,0:T(8,128)(2,1)S(1)} %get-tuple-element.83), channel_id=1, source_target_pairs={{0,6},{2,4},{4,2},{6,0},{8,14},{10,12},{12,10},{14,8},{16,22},{18,... | collective-permute-start | bytes 1622024 | tf_op jit(solution)/shard_map/ppermute | solution.py:32
  21.7 14.2 %copy-start.3 = (bf16[256,2560]{1,0:T(8,128)(2,1)S(1)}, bf16[256,2560]{1,0:T(8,128)(2,1)}, u32[]{:S(2)}) copy-start(bf16[256,2560]{1,0:T(8,128)(2,1)} %refs_13_.1) | copy-start | bytes 3932164
  24.0 39.0 %collective-permute-start.11 = (bf16[1056,256]{1,0:T(8,128)(2,1)S(1)}, bf16[1056,256]{1,0:T(8,128)(2,1)S(1)}, u32[]{:S(2)}, u32[]{:S(2)}) collective-permute-start(bf16[1056,256]{1,0:T(8,128)(2,1)S(1)} %get-tuple-element.99), channel_id=1, source_target_pairs={{0,2},{2,0},{4,6},{6,4},{8,10},{10,8},{12,14},{14,12},{16,18},{18,... | collective-permute-start | bytes 1622024 | tf_op jit(solution)/shard_map/ppermute | solution.py:32
  25.6 41.5 %collective-permute-start.12 = (bf16[1056,256]{1,0:T(8,128)(2,1)S(1)}, bf16[1056,256]{1,0:T(8,128)(2,1)S(1)}, u32[]{:S(2)}, u32[]{:S(2)}) collective-permute-start(bf16[1056,256]{1,0:T(8,128)(2,1)S(1)} %get-tuple-element.100), channel_id=1, source_target_pairs={{0,4},{2,6},{4,0},{6,2},{8,12},{10,14},{12,8},{14,10},{16,20},{18,... | collective-permute-start | bytes 1622024 | tf_op jit(solution)/shard_map/ppermute | solution.py:32
  33.4 36.5 %collective-permute-start.13 = (bf16[1056,256]{1,0:T(8,128)(2,1)S(1)}, bf16[1056,256]{1,0:T(8,128)(2,1)S(1)}, u32[]{:S(2)}, u32[]{:S(2)}) collective-permute-start(bf16[1056,256]{1,0:T(8,128)(2,1)S(1)} %get-tuple-element.101), channel_id=1, source_target_pairs={{0,6},{2,4},{4,2},{6,0},{8,14},{10,12},{12,10},{14,8},{16,22},{18,... | collective-permute-start | bytes 1622024 | tf_op jit(solution)/shard_map/ppermute | solution.py:32
  47.1 6.4 %collective-permute-start.7 = (bf16[512,256]{1,0:T(8,128)(2,1)S(1)}, bf16[512,256]{1,0:T(8,128)(2,1)S(1)}, u32[]{:S(2)}, u32[]{:S(2)}) collective-permute-start(bf16[512,256]{1,0:T(8,128)(2,1)S(1)} %get-tuple-element.90), channel_id=1, source_target_pairs={{0,8},{2,10},{4,12},{6,14},{8,0},{10,2},{12,4},{14,6},{16,24},{18,... | collective-permute-start | bytes 786440 | tf_op jit(solution)/shard_map/ppermute | solution.py:32
  47.2 6.4 %collective-permute-start.8 = (bf16[512,256]{1,0:T(8,128)(2,1)S(1)}, bf16[512,256]{1,0:T(8,128)(2,1)S(1)}, u32[]{:S(2)}, u32[]{:S(2)}) collective-permute-start(bf16[512,256]{1,0:T(8,128)(2,1)S(1)} %get-tuple-element.91), channel_id=1, source_target_pairs={{8,16},{10,18},{12,20},{14,22},{16,8},{18,10},{20,12},{22,14},{9,1... | collective-permute-start | bytes 786440 | tf_op jit(solution)/shard_map/ppermute | solution.py:38
  58.4 13.0 %collective-permute-start.9 = (bf16[528,256]{1,0:T(8,128)(2,1)S(1)}, bf16[528,256]{1,0:T(8,128)(2,1)S(1)}, u32[]{:S(2)}, u32[]{:S(2)}) collective-permute-start(bf16[528,256]{1,0:T(8,128)(2,1)S(1)} %get-tuple-element.96), channel_id=1, source_target_pairs={{0,8},{2,10},{4,12},{6,14},{8,0},{10,2},{12,4},{14,6},{16,24},{18,... | collective-permute-start | bytes 811016 | tf_op jit(solution)/shard_map/ppermute | solution.py:32
  62.3 8.9 %collective-permute-start.10 = (bf16[512,256]{1,0:T(8,128)(2,1)S(1)}, bf16[512,256]{1,0:T(8,128)(2,1)S(1)}, u32[]{:S(2)}, u32[]{:S(2)}) collective-permute-start(bf16[512,256]{1,0:T(8,128)(2,1)S(1)} %get-tuple-element.97), channel_id=1, source_target_pairs={{8,16},{10,18},{12,20},{14,22},{16,8},{18,10},{20,12},{22,14},{9,1... | collective-permute-start | bytes 786440 | tf_op jit(solution)/shard_map/ppermute | solution.py:38
  63.0 14.9 %collective-permute-start.19 = (bf16[1056,128]{1,0:T(8,128)(2,1)}, bf16[1056,128]{1,0:T(8,128)(2,1)S(1)}, u32[]{:S(2)}, u32[]{:S(2)}) collective-permute-start(bf16[1056,128]{1,0:T(8,128)(2,1)} %get-tuple-element.113), channel_id=1, source_target_pairs={{0,2},{2,0},{4,6},{6,4},{8,10},{10,8},{12,14},{14,12},{16,18},{18,... | collective-permute-start | bytes 811016 | tf_op jit(solution)/shard_map/ppermute | solution.py:32
  67.0 13.9 %collective-permute-start.20 = (bf16[1056,128]{1,0:T(8,128)(2,1)}, bf16[1056,128]{1,0:T(8,128)(2,1)S(1)}, u32[]{:S(2)}, u32[]{:S(2)}) collective-permute-start(bf16[1056,128]{1,0:T(8,128)(2,1)} %get-tuple-element.114), channel_id=1, source_target_pairs={{0,4},{2,6},{4,0},{6,2},{8,12},{10,14},{12,8},{14,10},{16,20},{18,... | collective-permute-start | bytes 811016 | tf_op jit(solution)/shard_map/ppermute | solution.py:32
  69.9 13.0 %collective-permute-start.21 = (bf16[1056,128]{1,0:T(8,128)(2,1)S(1)}, bf16[1056,128]{1,0:T(8,128)(2,1)S(1)}, u32[]{:S(2)}, u32[]{:S(2)}) collective-permute-start(bf16[1056,128]{1,0:T(8,128)(2,1)S(1)} %get-tuple-element.115), channel_id=1, source_target_pairs={{0,6},{2,4},{4,2},{6,0},{8,14},{10,12},{12,10},{14,8},{16,22},{18,... | collective-permute-start | bytes 811016 | tf_op jit(solution)/shard_map/ppermute | solution.py:32
  71.3 12.2 %collective-permute-start.17 = (bf16[512,256]{1,0:T(8,128)(2,1)S(1)}, bf16[512,256]{1,0:T(8,128)(2,1)S(1)}, u32[]{:S(2)}, u32[]{:S(2)}) collective-permute-start(bf16[512,256]{1,0:T(8,128)(2,1)S(1)} %get-tuple-element.110), channel_id=1, source_target_pairs={{0,8},{2,10},{4,12},{6,14},{8,0},{10,2},{12,4},{14,6},{16,24},{18,... | collective-permute-start | bytes 786440 | tf_op jit(solution)/shard_map/ppermute | solution.py:32
  71.4 12.2 %collective-permute-start.18 = (bf16[512,256]{1,0:T(8,128)(2,1)S(1)}, bf16[512,256]{1,0:T(8,128)(2,1)S(1)}, u32[]{:S(2)}, u32[]{:S(2)}) collective-permute-start(bf16[512,256]{1,0:T(8,128)(2,1)S(1)} %get-tuple-element.111), channel_id=1, source_target_pairs={{8,16},{10,18},{12,20},{14,22},{16,8},{18,10},{20,12},{22,14},{9,1... | collective-permute-start | bytes 786440 | tf_op jit(solution)/shard_map/ppermute | solution.py:38
  77.9 16.1 %collective-permute-start.14 = (bf16[784,256]{1,0:T(8,128)(2,1)S(1)}, bf16[784,256]{1,0:T(8,128)(2,1)S(1)}, u32[]{:S(2)}, u32[]{:S(2)}) collective-permute-start(bf16[784,256]{1,0:T(8,128)(2,1)S(1)} %get-tuple-element.105), channel_id=1, source_target_pairs={{0,2},{2,0},{4,6},{6,4},{8,10},{10,8},{12,14},{14,12},{16,18},{18,... | collective-permute-start | bytes 1204232 | tf_op jit(solution)/shard_map/ppermute | solution.py:32
  80.9 16.2 %collective-permute-start.15 = (bf16[784,256]{1,0:T(8,128)(2,1)S(1)}, bf16[784,256]{1,0:T(8,128)(2,1)S(1)}, u32[]{:S(2)}, u32[]{:S(2)}) collective-permute-start(bf16[784,256]{1,0:T(8,128)(2,1)S(1)} %get-tuple-element.106), channel_id=1, source_target_pairs={{0,4},{2,6},{4,0},{6,2},{8,12},{10,14},{12,8},{14,10},{16,20},{18,... | collective-permute-start | bytes 1204232 | tf_op jit(solution)/shard_map/ppermute | solution.py:32
  82.9 14.2 %collective-permute-start.16 = (bf16[784,256]{1,0:T(8,128)(2,1)S(1)}, bf16[784,256]{1,0:T(8,128)(2,1)S(1)}, u32[]{:S(2)}, u32[]{:S(2)}) collective-permute-start(bf16[784,256]{1,0:T(8,128)(2,1)S(1)} %get-tuple-element.107), channel_id=1, source_target_pairs={{0,6},{2,4},{4,2},{6,0},{8,14},{10,12},{12,10},{14,8},{16,22},{18,... | collective-permute-start | bytes 1204232 | tf_op jit(solution)/shard_map/ppermute | solution.py:32
  88.4 8.8 %copy-start.5 = (bf16[1024,512]{1,0:T(8,128)(2,1)}, bf16[1024,512]{1,0:T(8,128)(2,1)S(1)}, u32[]{:S(2)}) copy-start(bf16[1024,512]{1,0:T(8,128)(2,1)S(1)} %get-tuple-element.119.refs_3_) | copy-start | bytes 3145732
  88.4 9.7 %collective-permute-start.22 = (bf16[528,256]{1,0:T(8,128)(2,1)S(1)}, bf16[528,256]{1,0:T(8,128)(2,1)S(1)}, u32[]{:S(2)}, u32[]{:S(2)}) collective-permute-start(bf16[528,256]{1,0:T(8,128)(2,1)S(1)} %get-tuple-element.121), channel_id=1, source_target_pairs={{0,8},{2,10},{4,12},{6,14},{8,0},{10,2},{12,4},{14,6},{16,24},{18,... | collective-permute-start | bytes 811016 | tf_op jit(solution)/shard_map/ppermute | solution.py:32
  90.8 7.3 %collective-permute-start.23 = (bf16[512,256]{1,0:T(8,128)(2,1)S(1)}, bf16[512,256]{1,0:T(8,128)(2,1)S(1)}, u32[]{:S(2)}, u32[]{:S(2)}) collective-permute-start(bf16[512,256]{1,0:T(8,128)(2,1)S(1)} %get-tuple-element.122), channel_id=1, source_target_pairs={{8,16},{10,18},{12,20},{14,22},{16,8},{18,10},{20,12},{22,14},{9,1... | collective-permute-start | bytes 786440 | tf_op jit(solution)/shard_map/ppermute | solution.py:38
  97.1 1.2 copy-start.6
  100.0 16.4 %collective-permute-start.24 = (bf16[784,256]{1,0:T(8,128)(2,1)S(1)}, bf16[784,256]{1,0:T(8,128)(2,1)S(1)}, u32[]{:S(2)}, u32[]{:S(2)}) collective-permute-start(bf16[784,256]{1,0:T(8,128)(2,1)S(1)} %get-tuple-element.125), channel_id=1, source_target_pairs={{0,2},{2,0},{4,6},{6,4},{8,10},{10,8},{12,14},{14,12},{16,18},{18,... | collective-permute-start | bytes 1204232 | tf_op jit(solution)/shard_map/ppermute | solution.py:32
  100.3 18.9 %collective-permute-start.25 = (bf16[784,256]{1,0:T(8,128)(2,1)S(1)}, bf16[784,256]{1,0:T(8,128)(2,1)S(1)}, u32[]{:S(2)}, u32[]{:S(2)}) collective-permute-start(bf16[784,256]{1,0:T(8,128)(2,1)S(1)} %get-tuple-element.126), channel_id=1, source_target_pairs={{0,4},{2,6},{4,0},{6,2},{8,12},{10,14},{12,8},{14,10},{16,20},{18,... | collective-permute-start | bytes 1204232 | tf_op jit(solution)/shard_map/ppermute | solution.py:32
  101.4 19.4 %collective-permute-start.26 = (bf16[784,256]{1,0:T(8,128)(2,1)S(1)}, bf16[784,256]{1,0:T(8,128)(2,1)S(1)}, u32[]{:S(2)}, u32[]{:S(2)}) collective-permute-start(bf16[784,256]{1,0:T(8,128)(2,1)S(1)} %get-tuple-element.127), channel_id=1, source_target_pairs={{0,6},{2,4},{4,2},{6,0},{8,14},{10,12},{12,10},{14,8},{16,22},{18,... | collective-permute-start | bytes 1204232 | tf_op jit(solution)/shard_map/ppermute | solution.py:32
  103.5 5.0 %collective-permute-start.27 = (bf16[512,128]{1,0:T(8,128)(2,1)S(1)}, bf16[512,128]{1,0:T(8,128)(2,1)S(1)}, u32[]{:S(2)}, u32[]{:S(2)}) collective-permute-start(bf16[512,128]{1,0:T(8,128)(2,1)S(1)} %get-tuple-element.130), channel_id=1, source_target_pairs={{0,8},{2,10},{4,12},{6,14},{8,0},{10,2},{12,4},{14,6},{16,24},{18,... | collective-permute-start | bytes 393224 | tf_op jit(solution)/shard_map/ppermute | solution.py:32
  104.3 4.2 %collective-permute-start.28 = (bf16[512,128]{1,0:T(8,128)(2,1)S(1)}, bf16[512,128]{1,0:T(8,128)(2,1)S(1)}, u32[]{:S(2)}, u32[]{:S(2)}) collective-permute-start(bf16[512,128]{1,0:T(8,128)(2,1)S(1)} %get-tuple-element.131), channel_id=1, source_target_pairs={{8,16},{10,18},{12,20},{14,22},{16,8},{18,10},{20,12},{22,14},{9,1... | collective-permute-start | bytes 393224 | tf_op jit(solution)/shard_map/ppermute | solution.py:38
  111.2 13.6 %collective-permute-start.29 = (bf16[528,128]{1,0:T(8,128)(2,1)S(1)}, bf16[528,128]{1,0:T(8,128)(2,1)S(1)}, u32[]{:S(2)}, u32[]{:S(2)}) collective-permute-start(bf16[528,128]{1,0:T(8,128)(2,1)S(1)} %get-tuple-element.136), channel_id=1, source_target_pairs={{0,8},{2,10},{4,12},{6,14},{8,0},{10,2},{12,4},{14,6},{16,24},{18,... | collective-permute-start | bytes 405512 | tf_op jit(solution)/shard_map/ppermute | solution.py:32
  115.2 9.6 %collective-permute-start.30 = (bf16[512,128]{1,0:T(8,128)(2,1)S(1)}, bf16[512,128]{1,0:T(8,128)(2,1)S(1)}, u32[]{:S(2)}, u32[]{:S(2)}) collective-permute-start(bf16[512,128]{1,0:T(8,128)(2,1)S(1)} %get-tuple-element.137), channel_id=1, source_target_pairs={{8,16},{10,18},{12,20},{14,22},{16,8},{18,10},{20,12},{22,14},{9,1... | collective-permute-start | bytes 393224 | tf_op jit(solution)/shard_map/ppermute | solution.py:38
  116.4 5.4 %collective-permute-start.31 = (bf16[16,640]{1,0:T(8,128)(2,1)S(1)}, bf16[16,640]{1,0:T(8,128)(2,1)S(1)}, u32[]{:S(2)}, u32[]{:S(2)}) collective-permute-start(bf16[16,640]{1,0:T(8,128)(2,1)S(1)} %get-tuple-element.144), channel_id=1, source_target_pairs={{0,16},{2,18},{4,20},{6,22},{8,24},{10,26},{12,28},{14,30},{16,0},... | collective-permute-start | bytes 61448 | tf_op jit(solution)/shard_map/ppermute | solution.py:32
  119.2 5.6 %collective-permute-start.32 = (bf16[16,640]{1,0:T(8,128)(2,1)S(1)}, bf16[16,640]{1,0:T(8,128)(2,1)S(1)}, u32[]{:S(2)}, u32[]{:S(2)}) collective-permute-start(bf16[16,640]{1,0:T(8,128)(2,1)S(1)} %get-tuple-element.145), channel_id=1, source_target_pairs={{0,24},{2,26},{4,28},{6,30},{8,16},{10,18},{12,20},{14,22},{16,8},... | collective-permute-start | bytes 61448 | tf_op jit(solution)/shard_map/ppermute | solution.py:32
  125.7 6.0 %collective-permute-start.33 = (bf16[864,128]{1,0:T(8,128)(2,1)S(1)}, bf16[864,128]{1,0:T(8,128)(2,1)S(1)}, u32[]{:S(2)}, u32[]{:S(2)}) collective-permute-start(bf16[864,128]{1,0:T(8,128)(2,1)S(1)} %get-tuple-element.147), channel_id=1, source_target_pairs={{0,2},{2,0},{4,6},{6,4},{8,10},{10,8},{12,14},{14,12},{16,18},{18,... | collective-permute-start | bytes 663560 | tf_op jit(solution)/shard_map/ppermute | solution.py:32
  126.1 7.4 %collective-permute-start.34 = (bf16[864,128]{1,0:T(8,128)(2,1)S(1)}, bf16[864,128]{1,0:T(8,128)(2,1)S(1)}, u32[]{:S(2)}, u32[]{:S(2)}) collective-permute-start(bf16[864,128]{1,0:T(8,128)(2,1)S(1)} %get-tuple-element.148), channel_id=1, source_target_pairs={{0,4},{2,6},{4,0},{6,2},{8,12},{10,14},{12,8},{14,10},{16,20},{18,... | collective-permute-start | bytes 663560 | tf_op jit(solution)/shard_map/ppermute | solution.py:32
  127.6 7.2 %collective-permute-start.35 = (bf16[864,128]{1,0:T(8,128)(2,1)S(1)}, bf16[864,128]{1,0:T(8,128)(2,1)S(1)}, u32[]{:S(2)}, u32[]{:S(2)}) collective-permute-start(bf16[864,128]{1,0:T(8,128)(2,1)S(1)} %get-tuple-element.149), channel_id=1, source_target_pairs={{0,6},{2,4},{4,2},{6,0},{8,14},{10,12},{12,10},{14,8},{16,22},{18,... | collective-permute-start | bytes 663560 | tf_op jit(solution)/shard_map/ppermute | solution.py:32
  136.4 1.4 collective-permute-start.36
  (1 other events, 1.1 us)

commit v4 on v3

--- a/solution.py
+++ b/solution.py
@@ -14,13 +14,14 @@
 G_DEV = 2
 GROUP = 4
 CHUNKS = (2, 2, 1)
-ORDER = ("b0 i0 g0 b1", "i1 e0 b2 g1", "i2 s0 e1 g2", "s1 e2 s2")
+ORDER = ("b0 i0 g0 b1", "i1 e0 b2 g1", "i2:z2 s0 e1 g2", "e2 s1",)
 
 
 EPSILON = 1e-06
 FACTOR = HEAD_DIM ** (-0.5)
 LOG2_E = 1.4426950408889634
 FACTS = 32
+FINISH_STEPS = 4
 F32 = jnp.float32
 BF16 = jnp.bfloat16
 ANY = pl.BlockSpec(memory_space=pl.ANY)
@@ -475,14 +476,16 @@
     )
 
 
-def total_kernel(chunks, place_ref, ids_ref, raw_ref, gain_ref, *refs):
+def total_kernel(chunks, place_ref, ids_ref, raw_ref, query, key, query_gain, gain_ref, *refs):
     *refs, out, sums = refs
     homes, dot_refs = refs[: GROUP * len(chunks)], refs[GROUP * len(chunks) :]
     rows, width = out.shape[0], sums.shape[1]
     me = place_ref[0]
     device = place_ref[1] * GROUP + me
-    total = dot_refs[0][...]
-    for ref in dot_refs[1:]:
+    total = part_dots(
+        sum(chunks[:-1]), me, homes[-GROUP:], query, key, query_gain, gain_ref
+    )
+    for ref in dot_refs:
         total = total + ref[...]
     few = lax.broadcasted_iota(jnp.int32, (16, HEAD_DIM), 0)
     eight = lax.broadcasted_iota(jnp.int32, (8, HEAD_DIM), 0)
@@ -518,39 +521,43 @@
     out[...] = total
 
 
-def total_dots(place, ids, raw, gain, homes, dots, chunks):
+def total_dots(place, ids, raw, query_raw, key_raw, gains, homes, dots, chunks):
     smem = pl.BlockSpec(memory_space=pltpu.SMEM)
     vmem = pl.BlockSpec(memory_space=pltpu.VMEM)
     flat = [x for home in homes for x in home]
+    raw_rows = query_raw.shape[0]
     return pl.pallas_call(
         functools.partial(total_kernel, chunks),
         out_shape=[
-            jax.ShapeDtypeStruct(dots[0].shape, F32),
+            jax.ShapeDtypeStruct((raw_rows, HEAD_DIM), F32),
             jax.ShapeDtypeStruct((8, raw.shape[1]), F32),
         ],
-        in_specs=[smem, smem] + [vmem] * (2 + len(flat) + len(dots)),
+        in_specs=[smem, smem] + [vmem] * (5 + len(flat) + len(dots)),
         out_specs=[vmem, vmem],
         compiler_params=params(),
         cost_estimate=cost(1, 1),
         name="total_dots",
-    )(place, ids, raw, gain, *flat, *dots)
-
-
-def dots_kernel(first, head, place_ref, g0, g1, g2, g3, query, key, query_gain, key_gain, out_ref):
-    rows = out_ref.shape[0]
-    each = query.shape[1] // HEAD_DIM // GROUP
+    )(place, ids, raw, query_raw, key_raw, *gains, *flat, *dots)
+
+
+def part_dots(first, me, homes, query, key, query_gain, key_gain):
+    rows, width = query.shape
+    each = width // HEAD_DIM // GROUP
     totals = [jnp.zeros((rows, HEAD_DIM), F32), jnp.zeros((rows, HEAD_DIM), F32)]
-    for d, grads in enumerate((g0, g1, g2, g3)):
+    for d, grads in enumerate(homes):
         for h in range(grads.shape[1] // HEAD_DIM):
-            at = ((place_ref[0] ^ d) * each + first + h) * HEAD_DIM
+            at = ((me ^ d) * each + first + h) * HEAD_DIM
             here = pl.ds(pl.multiple_of(at, HEAD_DIM), HEAD_DIM)
             lanes = slice(h * HEAD_DIM, (h + 1) * HEAD_DIM)
             for i, (raw, gain) in enumerate(((query, query_gain), (key, key_gain))):
                 grad = grads[i * rows : (i + 1) * rows, lanes].astype(F32)
                 totals[i] += grad * gain[:, here] * raw[:, here].astype(F32)
-    out_ref[...] = lane_pair(
-        jnp.sum(totals[0], axis=1, keepdims=True), jnp.sum(totals[1], axis=1, keepdims=True), rows
-    )
+    sums = [jnp.sum(x, axis=1, keepdims=True) for x in totals]
+    return lane_pair(*sums, rows)
+
+
+def dots_kernel(first, head, place_ref, *refs):
+    refs[-1][...] = part_dots(first, place_ref[0], refs[:GROUP], *refs[GROUP:-1])
 
 
 def dots(place, grads, query_raw, key_raw, gains, first, after):
@@ -566,30 +573,34 @@
 
 
 def finish_kernel(chunks, place_ref, ids_ref, own_ref, other_ref, dot_ref, dot_other_ref, *refs):
-    device = place_ref[1] * GROUP + place_ref[0]
+    me = place_ref[0]
+    device = place_ref[1] * GROUP + me
     grads = refs[: GROUP * len(chunks)]
     sum_ref, query_ref, key_ref, query_gain, key_gain = refs[GROUP * len(chunks) : -3]
     query_out, key_out, value_out = refs[-3:]
-    rows = query_ref.shape[0]
-    each = query_ref.shape[1] // GROUP
-    inv = inverses(own_ref[...], other_ref[...])
-    total = dot_ref[...] + dot_other_ref[...]
+    rows, width = query_ref.shape
+    block = query_out.shape[0]
+    each = width // GROUP
+    start = pl.program_id(0) * block
+    now = pl.ds(pl.multiple_of(start, block), block)
+    inv = inverses(own_ref[now], other_ref[now])
+    total = dot_ref[now] + dot_other_ref[now]
     dot = (total[:, :1], total[:, HEAD_DIM // 2 : HEAD_DIM // 2 + 1])
     coeff = [inv[i] * inv[i] * inv[i] * (dot[i] / D) for i in range(2)]
-    row = lax.broadcasted_iota(jnp.int32, (rows, HEAD_DIM), 0)
+    row = lax.broadcasted_iota(jnp.int32, (block, HEAD_DIM), 0) + start
     hot = [row == ids_ref[r] - device * rows for r in range(G_DEV)]
-
-    def whole(d):
+    for d in range(GROUP):
         first = 0
         for c, count in enumerate(chunks):
             ref = grads[c * GROUP + d]
             for h in range(count):
-                at = (first + h) * HEAD_DIM
-                there = slice(at, at + HEAD_DIM)
-                at = pl.multiple_of((place_ref[0] ^ d) * each + at, HEAD_DIM)
+                at = pl.multiple_of((me ^ d) * each + (first + h) * HEAD_DIM, HEAD_DIM)
                 here = pl.ds(at, HEAD_DIM)
                 col = slice(h * HEAD_DIM, (h + 1) * HEAD_DIM)
-                grad = [ref[i * rows : (i + 1) * rows, col].astype(F32) for i in range(3)]
+                grad = [
+                    ref[pl.ds(pl.multiple_of(start + i * rows, block), block), col].astype(F32)
+                    for i in range(3)
+                ]
                 for i in (1, 2):
                     for r in range(G_DEV):
                         more = sum_ref[2 * (i - 1) + r : 2 * (i - 1) + r + 1, here]
@@ -597,33 +608,25 @@
                 for i, (raw, gain, out) in enumerate(
                     ((query_ref, query_gain, query_out), (key_ref, key_gain, key_out))
                 ):
-                    out[:, there] = (
-                        inv[i] * (grad[i] * gain[:, here]) - raw[:, here].astype(F32) * coeff[i]
+                    out[:, here] = (
+                        inv[i] * (grad[i] * gain[:, here]) - raw[now, here].astype(F32) * coeff[i]
                     ).astype(BF16)
-                value_out[:, there] = grad[2].astype(BF16)
+                value_out[:, here] = grad[2].astype(BF16)
             first += count
-
-    for d in range(GROUP):
-        pl.when(pl.program_id(0) == d)(functools.partial(whole, d))
 
 
 def finish(place, ids, own, other, dot, dot_other, sums, grads, query_raw, key_raw, gains, chunks):
     rows, width = query_raw.shape
-    block = width // GROUP
     smem = pl.BlockSpec(memory_space=pltpu.SMEM)
-    at = lambda i, place: (0, place[0] ^ i)
     vmem = pl.BlockSpec(memory_space=pltpu.VMEM)
     flat = [x for chunk in grads for x in chunk]
-    column = pl.BlockSpec((rows, block), at)
+    block = pl.BlockSpec((rows // FINISH_STEPS, width), lambda i: (i, 0))
     return pl.pallas_call(
         functools.partial(finish_kernel, chunks),
         out_shape=[jax.ShapeDtypeStruct(query_raw.shape, BF16)] * 3,
-        grid_spec=pltpu.PrefetchScalarGridSpec(
-            num_scalar_prefetch=1,
-            grid=(GROUP,),
-            in_specs=[smem] + [vmem] * (4 + len(flat) + 5),
-            out_specs=[column] * 3,
-        ),
+        grid=(FINISH_STEPS,),
+        in_specs=[smem, smem] + [vmem] * (4 + len(flat) + 5),
+        out_specs=[block] * 3,
         compiler_params=params(),
         cost_estimate=cost(1, 1),
         name="finish",
@@ -690,11 +693,11 @@
     stages = {"b": begin, "i": inside, "g": outside, "e": end, "s": score}
     for step in " ".join(ORDER).split():
         name, *extra = step.split(":")
-        held = tuple((packed if e[0] == "i" else home)[int(e[1])]["oxyd".index(e[2])] for e in extra)
+        held = tuple(x for e in extra for x in edge[int(e[1])])
         token = stages[name[0]](int(name[1]), token + held)
     homes = [home[c] for c in range(chunks)]
     total, sums = total_dots(
-        place, global_ids, raw_rows, gains[1], homes, [dot[c] for c in range(chunks)], CHUNKS
+        place, global_ids, raw_rows, query_raw, key_raw, gains, homes, list(dot.values()), CHUNKS
     )
     return tuple(
         finish(

time: 144 us -> 139 us (0.965); the launches traced: 144 us -> 137 us
  waiting for transfers between devices: 42.6 us -> 35.1 us
  starting transfers between devices: 49.7 us -> 52.1 us
    ppermute x29, waiting for transfers between devices: 40.3 us -> 32.9 us  [swapped(): return lax.ppermute(shard, 'ctx', [(i, i ^ bit) for i in range(count)])]
    ppermute x29, starting transfers between devices: 44.9 us -> 47.4 us  [swapped(): return lax.ppermute(shard, 'ctx', [(i, i ^ bit) for i in range(count)])]
    pallas_call x16 -> x15, Pallas kernels: 32.5 us -> 31.7 us  [heads_call(): pl.pallas_call(run, out_shape=[shape for shape, _ in outputs], in_specs=[...]
  transfers between devices with their start and end apart: 37 -> 37, of which waited for: 15 -> 15; matrix products, arithmetic and copies ran while one was open for 0% -> 0% of each run, Pallas kernels for 24% -> 25%
where the time goes in v4:
time: 139 us; the launch traced here: 137 us
  starting transfers between devices  52.1 us (37%)
  Pallas kernels  46.4 us (33%)
  waiting for transfers between devices  35.1 us (25%)
  local copies, waits for them, and re-layouts  2.71 us (2%)
    ppermute x29, starting transfers between devices, swapped(): return lax.ppermute(shard, 'ctx', [(i, i ^ bit) for i in range(count)])  47.4 us
    ppermute x29, waiting for transfers between devices, swapped(): return lax.ppermute(shard, 'ctx', [(i, i ^ bit) for i in range(count)])  32.9 us
    pallas_call x15, Pallas kernels, heads_call(): pl.pallas_call(run, out_shape=[shape for shape, _ in outputs], in_specs=[...  31.7 us
    pallas_call x3, Pallas kernels, pack(): pl.pallas_call(behind(kernel, 11 + GROUP, len(after)), out_shape=[jax.Sha...  6.87 us
    pallas_call x1, Pallas kernels, finish(): pl.pallas_call(functools.partial(finish_kernel, chunks), out_shape=[jax.S...  4.72 us
    ppermute x6, starting transfers between devices, swapped_edges(): return lax.ppermute(shard, 'ctx', pairs)  4.18 us
  transfers between devices with their start and end apart: 37, of which 15 were waited for; matrix products, arithmetic and copies ran while one was open for 0% of the time, Pallas kernels for 25%

profile of v4, /device:TPU:0, one launch (start us, length us, event | category | flops | bytes accessed | tf_op | source)
XLA Modules:
  0.0 137.4 jit_solution(857565212422549296)
XLA Ops:
  0.6 1.3 copy-done
  2.0 1.3 copy-done.2
  6.2 5.0 %collective-permute-start.3 = (bf16[16,640]{1,0:T(8,128)(2,1)S(1)}, bf16[16,640]{1,0:T(8,128)(2,1)S(1)}, u32[]{:S(2)}, u32[]{:S(2)}) collective-permute-start(bf16[16,640]{1,0:T(8,128)(2,1)S(1)} %get-tuple-element.79.refs_11_), channel_id=1, source_target_pairs={{0,24},{2,26},{4,28},{6,30},{8,16},{10,18},{12,20},{14,22},{16,8},... | collective-permute-start | bytes 61448 | tf_op jit(solution)/shard_map/ppermute | solution.py:33
  11.8 1.1 collective-permute-done.3.refs_14_
  13.0 2.9 %collective-permute-done.2.refs_13_ = bf16[16,640]{1,0:T(8,128)(2,1)S(1)} collective-permute-done((bf16[16,640]{1,0:T(8,128)(2,1)S(1)}, bf16[16,640]{1,0:T(8,128)(2,1)S(1)}, u32[]{:S(2)}, u32[]{:S(2)}) %collective-permute-start.2) | collective-permute-done | bytes 20512 | tf_op jit(solution)/shard_map/ppermute | solution.py:33
  15.9 2.2 %pack.3 = (bf16[1056,256]{1,0:T(8,128)(2,1)S(1)}, bf16[1056,256]{1,0:T(8,128)(2,1)S(1)}, bf16[1056,256]{1,0:T(8,128)(2,1)S(1)}, bf16[1056,256]{1,0:T(8,128)(2,1)S(1)}, f32[8,128]{1,0:T(8,128)S(1)}) custom-call(s32[2]{0:T(128)S(1)} %pad_add_fusion.place_ref.refs_0_, s32[2,4]{1,0:T(2,128)S(1)} %copy-done.7, s32[1,16]{1,0:T(1,128)S(1)} %copy-done.8, ...), custom_call_target="tpu_custom_call" | custom-call | flops 1 | bytes 1 | tf_op jit(solution)/shard_map/pack/pallas_call | solution.py:222
  18.1 1.6 %collective-permute-start.4 = (bf16[1056,256]{1,0:T(8,128)(2,1)S(1)}, bf16[1056,256]{1,0:T(8,128)(2,1)S(1)}, u32[]{:S(2)}, u32[]{:S(2)}) collective-permute-start(bf16[1056,256]{1,0:T(8,128)(2,1)S(1)} %get-tuple-element.81), channel_id=1, source_target_pairs={{0,2},{2,0},{4,6},{6,4},{8,10},{10,8},{12,14},{14,12},{16,18},{18,... | collective-permute-start | bytes 1622024 | tf_op jit(solution)/shard_map/ppermute | solution.py:33
  19.7 1.5 %collective-permute-start.5 = (bf16[1056,256]{1,0:T(8,128)(2,1)S(1)}, bf16[1056,256]{1,0:T(8,128)(2,1)S(1)}, u32[]{:S(2)}, u32[]{:S(2)}) collective-permute-start(bf16[1056,256]{1,0:T(8,128)(2,1)S(1)} %get-tuple-element.82), channel_id=1, source_target_pairs={{0,4},{2,6},{4,0},{6,2},{8,12},{10,14},{12,8},{14,10},{16,20},{18,... | collective-permute-start | bytes 1622024 | tf_op jit(solution)/shard_map/ppermute | solution.py:33
  21.7 2.3 %pack.4 = (bf16[1056,256]{1,0:T(8,128)(2,1)S(1)}, bf16[1056,256]{1,0:T(8,128)(2,1)S(1)}, bf16[1056,256]{1,0:T(8,128)(2,1)S(1)}, bf16[1056,256]{1,0:T(8,128)(2,1)S(1)}, f32[8,128]{1,0:T(8,128)S(1)}) custom-call(s32[2]{0:T(128)S(1)} %pad_add_fusion.place_ref.refs_0_, s32[2,4]{1,0:T(2,128)S(1)} %copy-done.7, s32[1,16]{1,0:T(1,128)S(1)} %copy-done.8, ...), custom_call_target="tpu_custom_call" | custom-call | flops 1 | bytes 1 | tf_op jit(solution)/shard_map/pack/pallas_call | solution.py:222
  24.0 1.6 %collective-permute-start.11 = (bf16[1056,256]{1,0:T(8,128)(2,1)S(1)}, bf16[1056,256]{1,0:T(8,128)(2,1)S(1)}, u32[]{:S(2)}, u32[]{:S(2)}) collective-permute-start(bf16[1056,256]{1,0:T(8,128)(2,1)S(1)} %get-tuple-element.99), channel_id=1, source_target_pairs={{0,2},{2,0},{4,6},{6,4},{8,10},{10,8},{12,14},{14,12},{16,18},{18,... | collective-permute-start | bytes 1622024 | tf_op jit(solution)/shard_map/ppermute | solution.py:33
  25.6 1.5 %collective-permute-start.12 = (bf16[1056,256]{1,0:T(8,128)(2,1)S(1)}, bf16[1056,256]{1,0:T(8,128)(2,1)S(1)}, u32[]{:S(2)}, u32[]{:S(2)}) collective-permute-start(bf16[1056,256]{1,0:T(8,128)(2,1)S(1)} %get-tuple-element.100), channel_id=1, source_target_pairs={{0,4},{2,6},{4,0},{6,2},{8,12},{10,14},{12,8},{14,10},{16,20},{18,... | collective-permute-start | bytes 1622024 | tf_op jit(solution)/shard_map/ppermute | solution.py:33
  27.1 6.3 %collective-permute-done.4.refs_1_ = bf16[1056,256]{1,0:T(8,128)(2,1)S(1)} collective-permute-done((bf16[1056,256]{1,0:T(8,128)(2,1)S(1)}, bf16[1056,256]{1,0:T(8,128)(2,1)S(1)}, u32[]{:S(2)}, u32[]{:S(2)}) %collective-permute-start.4) | collective-permute-done | bytes 540704 | tf_op jit(solution)/shard_map/ppermute | solution.py:33
  33.4 2.4 %collective-permute-start.13 = (bf16[1056,256]{1,0:T(8,128)(2,1)S(1)}, bf16[1056,256]{1,0:T(8,128)(2,1)S(1)}, u32[]{:S(2)}, u32[]{:S(2)}) collective-permute-start(bf16[1056,256]{1,0:T(8,128)(2,1)S(1)} %get-tuple-element.101), channel_id=1, source_target_pairs={{0,6},{2,4},{4,2},{6,0},{8,14},{10,12},{12,10},{14,8},{16,22},{18,... | collective-permute-start | bytes 1622024 | tf_op jit(solution)/shard_map/ppermute | solution.py:33
  35.8 2.3 %pack.5 = (bf16[1056,128]{1,0:T(8,128)(2,1)S(1)}, bf16[1056,128]{1,0:T(8,128)(2,1)}, bf16[1056,128]{1,0:T(8,128)(2,1)S(1)}, bf16[1056,128]{1,0:T(8,128)(2,1)S(1)}, f32[8,128]{1,0:T(8,128)S(1)}) custom-call(s32[2]{0:T(128)S(1)} %pad_add_fusion.place_ref.refs_0_, s32[2,4]{1,0:T(2,128)S(1)} %copy-done.7, s32[1,16]{1,0:T(1,128)S(1)} %copy-done.8, ...), custom_call_target="tpu_custom_call" | custom-call | flops 1 | bytes 1 | tf_op jit(solution)/shard_map/pack/pallas_call | solution.py:222
  38.2 8.3 %collective-permute-done.5.refs_2_ = bf16[1056,256]{1,0:T(8,128)(2,1)S(1)} collective-permute-done((bf16[1056,256]{1,0:T(8,128)(2,1)S(1)}, bf16[1056,256]{1,0:T(8,128)(2,1)S(1)}, u32[]{:S(2)}, u32[]{:S(2)}) %collective-permute-start.5) | collective-permute-done | bytes 540704 | tf_op jit(solution)/shard_map/ppermute | solution.py:33
  47.9 4.3 %inner.3 = (bf16[512,256]{1,0:T(8,128)(2,1)S(1)}, bf16[1024,512]{1,0:T(8,128)(2,1)S(1)}, f32[32,512]{1,0:T(8,128)S(1)}) custom-call(s32[2]{0:T(128)S(1)} %pad_add_fusion.place_ref.refs_0_, bf16[1056,256]{1,0:T(8,128)(2,1)S(1)} %get-tuple-element.80.refs_0_, bf16[1056,256]{1,0:T(8,128)(2,1)S(1)} %collective-permute-done.4.refs_1_, ...), custom_call_target="tpu_custom_call" | custom-call | flops 1 | bytes 1 | tf_op jit(solution)/shard_map/inner/pallas_call | solution.py:69
  52.2 1.4 collective-permute-done.7.refs_4_
  53.5 4.8 %outer.3 = (bf16[512,256]{1,0:T(8,128)(2,1)S(1)}, bf16[1024,512]{1,0:T(8,128)(2,1)S(1)}, bf16[16,256]{1,0:T(8,128)(2,1)S(1)}, bf16[528,256]{1,0:T(8,128)(2,1)S(1...) custom-call(s32[2]{0:T(128)S(1)} %pad_add_fusion.place_ref.refs_0_, ...), custom_call_target="tpu_custom_call" | custom-call | flops 1 | bytes 1 | tf_op jit(solution)/shard_map/outer/pallas_call | solution.py:69
  58.4 4.0 %collective-permute-start.9 = (bf16[528,256]{1,0:T(8,128)(2,1)S(1)}, bf16[528,256]{1,0:T(8,128)(2,1)S(1)}, u32[]{:S(2)}, u32[]{:S(2)}) collective-permute-start(bf16[528,256]{1,0:T(8,128)(2,1)S(1)} %get-tuple-element.96), channel_id=1, source_target_pairs={{0,8},{2,10},{4,12},{6,14},{8,0},{10,2},{12,4},{14,6},{16,24},{18,... | collective-permute-start | bytes 811016 | tf_op jit(solution)/shard_map/ppermute | solution.py:33
  63.0 1.1 collective-permute-start.19
  64.1 3.0 %collective-permute-done.12.refs_2_ = bf16[1056,256]{1,0:T(8,128)(2,1)S(1)} collective-permute-done((bf16[1056,256]{1,0:T(8,128)(2,1)S(1)}, bf16[1056,256]{1,0:T(8,128)(2,1)S(1)}, u32[]{:S(2)}, u32[]{:S(2)}) %collective-permute-start.12) | collective-permute-done | bytes 540704 | tf_op jit(solution)/shard_map/ppermute | solution.py:33
  67.0 2.8 %collective-permute-start.20 = (bf16[1056,128]{1,0:T(8,128)(2,1)S(1)}, bf16[1056,128]{1,0:T(8,128)(2,1)S(1)}, u32[]{:S(2)}, u32[]{:S(2)}) collective-permute-start(bf16[1056,128]{1,0:T(8,128)(2,1)S(1)} %get-tuple-element.114), channel_id=1, source_target_pairs={{0,4},{2,6},{4,0},{6,2},{8,12},{10,14},{12,8},{14,10},{16,20},{18,... | collective-permute-start | bytes 811016 | tf_op jit(solution)/shard_map/ppermute | solution.py:33
  72.2 4.3 %inner.4 = (bf16[512,256]{1,0:T(8,128)(2,1)S(1)}, bf16[1024,512]{1,0:T(8,128)(2,1)S(1)}, f32[32,512]{1,0:T(8,128)S(1)}) custom-call(s32[2]{0:T(128)S(1)} %pad_add_fusion.place_ref.refs_0_, bf16[1056,256]{1,0:T(8,128)(2,1)S(1)} %get-tuple-element.98.refs_0_, bf16[1056,256]{1,0:T(8,128)(2,1)S(1)} %collective-permute-done.11.refs_1_, ...), custom_call_target="tpu_custom_call" | custom-call | flops 1 | bytes 1 | tf_op jit(solution)/shard_map/inner/pallas_call | solution.py:69
  76.5 1.4 %settle.3 = (bf16[784,256]{1,0:T(8,128)(2,1)S(1)}, bf16[784,256]{1,0:T(8,128)(2,1)S(1)}, bf16[784,256]{1,0:T(8,128)(2,1)S(1)}, bf16[784,256]{1,0:T(8,128)(2,1)S(1)}, f32[8,128]{1,0:T(8,128)S(1)}) custom-call(s32[2]{0:T(128)S(1)} %pad_add_fusion.place_ref.refs_0_, bf16[512,256]{1,0:T(8,128)(2,1)S(1)} %get-tuple-element.88.refs_0_, ...), custom_call_target="tpu_custom_call" | custom-call | flops 1 | bytes 1 | tf_op jit(solution)/shard_map/settle/pallas_call | solution.py:69
  78.7 2.0 %collective-permute-done.20.refs_2_ = bf16[1056,128]{1,0:T(8,128)(2,1)S(1)} collective-permute-done((bf16[1056,128]{1,0:T(8,128)(2,1)S(1)}, bf16[1056,128]{1,0:T(8,128)(2,1)S(1)}, u32[]{:S(2)}, u32[]{:S(2)}) %collective-permute-start.20) | collective-permute-done | bytes 270368 | tf_op jit(solution)/shard_map/ppermute | solution.py:33
  80.7 2.0 %collective-permute-start.15 = (bf16[784,256]{1,0:T(8,128)(2,1)S(1)}, bf16[784,256]{1,0:T(8,128)(2,1)S(1)}, u32[]{:S(2)}, u32[]{:S(2)}) collective-permute-start(bf16[784,256]{1,0:T(8,128)(2,1)S(1)} %get-tuple-element.106), channel_id=1, source_target_pairs={{0,4},{2,6},{4,0},{6,2},{8,12},{10,14},{12,8},{14,10},{16,20},{18,... | collective-permute-start | bytes 1204232 | tf_op jit(solution)/shard_map/ppermute | solution.py:33
  83.3 2.7 %collective-permute-start.24 = (bf16[512,128]{1,0:T(8,128)(2,1)S(1)}, bf16[512,128]{1,0:T(8,128)(2,1)S(1)}, u32[]{:S(2)}, u32[]{:S(2)}) collective-permute-start(bf16[512,128]{1,0:T(8,128)(2,1)S(1)} %get-tuple-element.123), channel_id=1, source_target_pairs={{0,8},{2,10},{4,12},{6,14},{8,0},{10,2},{12,4},{14,6},{16,24},{18,... | collective-permute-start | bytes 393224 | tf_op jit(solution)/shard_map/ppermute | solution.py:33
  86.7 4.8 %outer.4 = (bf16[512,256]{1,0:T(8,128)(2,1)S(1)}, bf16[1024,512]{1,0:T(8,128)(2,1)S(1)}, bf16[16,256]{1,0:T(8,128)(2,1)S(1)}, bf16[528,256]{1,0:T(8,128)(2,1)S(1...) custom-call(s32[2]{0:T(128)S(1)} %pad_add_fusion.place_ref.refs_0_, ...), custom_call_target="tpu_custom_call" | custom-call | flops 1 | bytes 1 | tf_op jit(solution)/shard_map/outer/pallas_call | solution.py:69
  91.5 2.8 %collective-permute-start.22 = (bf16[528,256]{1,0:T(8,128)(2,1)S(1)}, bf16[528,256]{1,0:T(8,128)(2,1)S(1)}, u32[]{:S(2)}, u32[]{:S(2)}) collective-permute-start(bf16[528,256]{1,0:T(8,128)(2,1)S(1)} %get-tuple-element.121), channel_id=1, source_target_pairs={{0,8},{2,10},{4,12},{6,14},{8,0},{10,2},{12,4},{14,6},{16,24},{18,... | collective-permute-start | bytes 811016 | tf_op jit(solution)/shard_map/ppermute | solution.py:33
  95.0 2.5 %inner.5 = (bf16[512,128]{1,0:T(8,128)(2,1)S(1)}, bf16[1024,256]{1,0:T(8,128)(2,1)S(1)}, f32[32,256]{1,0:T(8,128)S(1)}) custom-call(s32[2]{0:T(128)S(1)} %pad_add_fusion.place_ref.refs_0_, bf16[1056,128]{1,0:T(8,128)(2,1)S(1)} %get-tuple-element.112.refs_0_, bf16[1056,128]{1,0:T(8,128)(2,1)S(1)} %collective-permute-done.19.refs_1_, ...), custom_call_target="tpu_custom_call" | custom-call | flops 1 | bytes 1 | tf_op jit(solution)/shard_map/inner/pallas_call | solution.py:69
  97.5 1.0 dots.2.refs_7_.refs_12_
  98.7 1.6 %settle.4 = (bf16[784,256]{1,0:T(8,128)(2,1)S(1)}, bf16[784,256]{1,0:T(8,128)(2,1)S(1)}, bf16[784,256]{1,0:T(8,128)(2,1)S(1)}, bf16[784,256]{1,0:T(8,128)(2,1)S(1)}, f32[8,128]{1,0:T(8,128)S(1)}) custom-call(s32[2]{0:T(128)S(1)} %pad_add_fusion.place_ref.refs_0_, bf16[512,256]{1,0:T(8,128)(2,1)S(1)} %get-tuple-element.108.refs_0_, ...), custom_call_target="tpu_custom_call" | custom-call | flops 1 | bytes 1 | tf_op jit(solution)/shard_map/settle/pallas_call | solution.py:69
  101.2 2.0 %collective-permute-start.27 = (bf16[784,256]{1,0:T(8,128)(2,1)S(1)}, bf16[784,256]{1,0:T(8,128)(2,1)S(1)}, u32[]{:S(2)}, u32[]{:S(2)}) collective-permute-start(bf16[784,256]{1,0:T(8,128)(2,1)S(1)} %get-tuple-element.128), channel_id=1, source_target_pairs={{0,4},{2,6},{4,0},{6,2},{8,12},{10,14},{12,8},{14,10},{16,20},{18,... | collective-permute-start | bytes 1204232 | tf_op jit(solution)/shard_map/ppermute | solution.py:33
  103.9 2.7 %outer.5 = (bf16[512,128]{1,0:T(8,128)(2,1)S(1)}, bf16[1024,256]{1,0:T(8,128)(2,1)S(1)}, bf16[16,128]{1,0:T(8,128)(2,1)S(1)}, bf16[528,128]{1,0:T(8,128)(2,1)S(1...) custom-call(s32[2]{0:T(128)S(1)} %pad_add_fusion.place_ref.refs_0_, ...), custom_call_target="tpu_custom_call" | custom-call | flops 1 | bytes 1 | tf_op jit(solution)/shard_map/outer/pallas_call | solution.py:69
  107.2 4.2 %collective-permute-start.31 = (bf16[16,640]{1,0:T(8,128)(2,1)S(1)}, bf16[16,640]{1,0:T(8,128)(2,1)S(1)}, u32[]{:S(2)}, u32[]{:S(2)}) collective-permute-start(bf16[16,640]{1,0:T(8,128)(2,1)S(1)} %get-tuple-element.144), channel_id=1, source_target_pairs={{0,16},{2,18},{4,20},{6,22},{8,24},{10,26},{12,28},{14,30},{16,0},... | collective-permute-start | bytes 61448 | tf_op jit(solution)/shard_map/ppermute | solution.py:33
  111.4 2.1 %collective-permute-start.32 = (bf16[16,640]{1,0:T(8,128)(2,1)S(1)}, bf16[16,640]{1,0:T(8,128)(2,1)S(1)}, u32[]{:S(2)}, u32[]{:S(2)}) collective-permute-start(bf16[16,640]{1,0:T(8,128)(2,1)S(1)} %get-tuple-element.145), channel_id=1, source_target_pairs={{0,24},{2,26},{4,28},{6,30},{8,16},{10,18},{12,20},{14,22},{16,8},... | collective-permute-start | bytes 61448 | tf_op jit(solution)/shard_map/ppermute | solution.py:33
  113.5 2.3 %collective-permute-start.29 = (bf16[528,128]{1,0:T(8,128)(2,1)S(1)}, bf16[528,128]{1,0:T(8,128)(2,1)S(1)}, u32[]{:S(2)}, u32[]{:S(2)}) collective-permute-start(bf16[528,128]{1,0:T(8,128)(2,1)S(1)} %get-tuple-element.136), channel_id=1, source_target_pairs={{0,8},{2,10},{4,12},{6,14},{8,0},{10,2},{12,4},{14,6},{16,24},{18,... | collective-permute-start | bytes 405512 | tf_op jit(solution)/shard_map/ppermute | solution.py:33
  115.8 1.2 collective-permute-done.32.refs_8_
  117.7 1.1 collective-permute-done.29.refs_5_
  119.7 1.0 collective-permute-start.33
  120.7 2.0 %collective-permute-start.34 = (bf16[864,128]{1,0:T(8,128)(2,1)S(1)}, bf16[864,128]{1,0:T(8,128)(2,1)S(1)}, u32[]{:S(2)}, u32[]{:S(2)}) collective-permute-start(bf16[864,128]{1,0:T(8,128)(2,1)S(1)} %get-tuple-element.148), channel_id=1, source_target_pairs={{0,4},{2,6},{4,0},{6,2},{8,12},{10,14},{12,8},{14,10},{16,20},{18,... | collective-permute-start | bytes 663560 | tf_op jit(solution)/shard_map/ppermute | solution.py:33
  123.3 1.0 dots.3.refs_13_
  124.2 1.5 %collective-permute-done.33.refs_9_ = bf16[864,128]{1,0:T(8,128)(2,1)S(1)} collective-permute-done((bf16[864,128]{1,0:T(8,128)(2,1)S(1)}, bf16[864,128]{1,0:T(8,128)(2,1)S(1)}, u32[]{:S(2)}, u32[]{:S(2)}) %collective-permute-start.33) | collective-permute-done | bytes 221216 | tf_op jit(solution)/shard_map/ppermute | solution.py:33
  125.7 2.8 %collective-permute-done.34.refs_10_ = bf16[864,128]{1,0:T(8,128)(2,1)S(1)} collective-permute-done((bf16[864,128]{1,0:T(8,128)(2,1)S(1)}, bf16[864,128]{1,0:T(8,128)(2,1)S(1)}, u32[]{:S(2)}, u32[]{:S(2)}) %collective-permute-start.34) | collective-permute-done | bytes 221216 | tf_op jit(solution)/shard_map/ppermute | solution.py:33
  128.5 1.0 collective-permute-done.35.refs_11_
  129.5 1.7 %total_dots.1 = (f32[256,128]{1,0:T(8,128)S(1)}, f32[8,2560]{1,0:T(8,128)S(1)}) custom-call(s32[2]{0:T(128)S(1)} %pad_add_fusion.place_ref.refs_0_, s32[2]{0:T(128)S(1)} %copy-done.9, bf16[16,2560]{1,0:T(8,128)(2,1)S(1)} %get-tuple-element.78.raw_ref, bf16[256,2560]{1,0:T(8,128)(2,1)S(1)} %copy-done.3, bf16[256,2560]{1,0:T(8,128)(2,1)} %refs_14_.1, ...), custom_call_target="tpu_custom_call" | custom-call | flops 1 | bytes 1 | tf_op jit(solution)/shard_map/total_dots/pallas_call | solution.py:529
  131.4 1.3 collective-permute-done.36.dot_other_ref
  132.7 4.7 %finish.1 = (bf16[256,2560]{1,0:T(8,128)(2,1)}, bf16[256,2560]{1,0:T(8,128)(2,1)}, bf16[256,2560]{1,0:T(8,128)(2,1)}) custom-call(s32[2]{0:T(128)S(1)} %pad_add_fusion.place_ref.refs_0_, s32[2]{0:T(128)S(1)} %copy-done.9, f32[256,128]{1,0:T(8,128)S(1)} %squares.1.own_ref.refs_3_, f32[256,128]{1,0:T(8,128)S(1)} %collective-permute-done.other_ref.refs_4_, ...), custom_call_target="tpu_custom_call" | custom-call | flops 1 | bytes 1 | tf_op jit(solution)/shard_map/finish/pallas_call | solution.py:624
  (75 shorter events, 15.7 us)
Async XLA Ops:
  0.6 1.3 copy-start
  2.0 1.3 copy-start.2
  3.3 2.1 %copy-start.1 = (bf16[256,2560]{1,0:T(8,128)(2,1)S(1)}, bf16[256,2560]{1,0:T(8,128)(2,1)}, u32[]{:S(2)}) copy-start(bf16[256,2560]{1,0:T(8,128)(2,1)} %refs_14_.1) | copy-start | bytes 3932164
  3.3 2.1 %copy-start.4 = (bf16[256,2560]{1,0:T(8,128)(2,1)S(1)}, bf16[256,2560]{1,0:T(8,128)(2,1)}, u32[]{:S(2)}) copy-start(bf16[256,2560]{1,0:T(8,128)(2,1)} %refs_6_.5) | copy-start | bytes 3932164
  3.3 2.1 %copy-start.9 = (s32[2]{0:T(128)S(1)}, s32[2]{0:T(128)}, u32[]{:S(2)}) copy-start(s32[2]{0:T(128)} %ids_ref.5) | copy-start | bytes 28
  3.9 1.5 %collective-permute-start = (f32[256,128]{1,0:T(8,128)S(1)}, f32[256,128]{1,0:T(8,128)S(1)}, u32[]{:S(2)}, u32[]{:S(2)}) collective-permute-start(f32[256,128]{1,0:T(8,128)S(1)} %squares.1.own_ref.refs_3_), channel_id=1, source_target_pairs={{0,1},{1,0},{2,3},{3,2},{4,5},{5,4},{6,7},{7,6},{8,9},{9,8},{10,11... | collective-permute-start | bytes 393224 | tf_op jit(solution)/shard_map/ppermute | solution.py:637
  4.5 7.4 %copy-start.11 = (f32[2560]{0:T(1024)S(1)}, f32[2560]{0:T(1024)}, u32[]{:S(2)}) copy-start(f32[2560]{0:T(1024)} %param.13) | copy-start | bytes 30724
  4.5 11.4 %copy-start.7 = (s32[2,4]{1,0:T(2,128)S(1)}, s32[2,4]{1,0:T(2,128)}, u32[]{:S(2)}) copy-start(s32[2,4]{1,0:T(2,128)} %refs_1_.5) | copy-start | bytes 100
  4.5 11.4 %copy-start.8 = (s32[1,16]{1,0:T(1,128)S(1)}, s32[1,16]{1,0:T(1,128)}, u32[]{:S(2)}) copy-start(s32[1,16]{1,0:T(1,128)} %refs_2_.5) | copy-start | bytes 196
  6.2 6.8 %collective-permute-start.3 = (bf16[16,640]{1,0:T(8,128)(2,1)S(1)}, bf16[16,640]{1,0:T(8,128)(2,1)S(1)}, u32[]{:S(2)}, u32[]{:S(2)}) collective-permute-start(bf16[16,640]{1,0:T(8,128)(2,1)S(1)} %get-tuple-element.79.refs_11_), channel_id=1, source_target_pairs={{0,24},{2,26},{4,28},{6,30},{8,16},{10,18},{12,20},{14,22},{16,8},... | collective-permute-start | bytes 61448 | tf_op jit(solution)/shard_map/ppermute | solution.py:33
  11.2 4.7 %collective-permute-start.2 = (bf16[16,640]{1,0:T(8,128)(2,1)S(1)}, bf16[16,640]{1,0:T(8,128)(2,1)S(1)}, u32[]{:S(2)}, u32[]{:S(2)}) collective-permute-start(bf16[16,640]{1,0:T(8,128)(2,1)S(1)} %get-tuple-element.79.refs_11_), channel_id=1, source_target_pairs={{0,16},{2,18},{4,20},{6,22},{8,24},{10,26},{12,28},{14,30},{16,0},... | collective-permute-start | bytes 61448 | tf_op jit(solution)/shard_map/ppermute | solution.py:33
  11.2 4.7 %collective-permute-start.1 = (bf16[16,640]{1,0:T(8,128)(2,1)S(1)}, bf16[16,640]{1,0:T(8,128)(2,1)S(1)}, u32[]{:S(2)}, u32[]{:S(2)}) collective-permute-start(bf16[16,640]{1,0:T(8,128)(2,1)S(1)} %get-tuple-element.79.refs_11_), channel_id=1, source_target_pairs={{0,8},{2,10},{4,12},{6,14},{8,0},{10,2},{12,4},{14,6},{16,24},{18,... | collective-permute-start | bytes 61448 | tf_op jit(solution)/shard_map/ppermute | solution.py:33
  18.1 15.3 %collective-permute-start.4 = (bf16[1056,256]{1,0:T(8,128)(2,1)S(1)}, bf16[1056,256]{1,0:T(8,128)(2,1)S(1)}, u32[]{:S(2)}, u32[]{:S(2)}) collective-permute-start(bf16[1056,256]{1,0:T(8,128)(2,1)S(1)} %get-tuple-element.81), channel_id=1, source_target_pairs={{0,2},{2,0},{4,6},{6,4},{8,10},{10,8},{12,14},{14,12},{16,18},{18,... | collective-permute-start | bytes 1622024 | tf_op jit(solution)/shard_map/ppermute | solution.py:33
  19.7 26.8 %collective-permute-start.5 = (bf16[1056,256]{1,0:T(8,128)(2,1)S(1)}, bf16[1056,256]{1,0:T(8,128)(2,1)S(1)}, u32[]{:S(2)}, u32[]{:S(2)}) collective-permute-start(bf16[1056,256]{1,0:T(8,128)(2,1)S(1)} %get-tuple-element.82), channel_id=1, source_target_pairs={{0,4},{2,6},{4,0},{6,2},{8,12},{10,14},{12,8},{14,10},{16,20},{18,... | collective-permute-start | bytes 1622024 | tf_op jit(solution)/shard_map/ppermute | solution.py:33
  21.2 25.3 %collective-permute-start.6 = (bf16[1056,256]{1,0:T(8,128)(2,1)S(1)}, bf16[1056,256]{1,0:T(8,128)(2,1)S(1)}, u32[]{:S(2)}, u32[]{:S(2)}) collective-permute-start(bf16[1056,256]{1,0:T(8,128)(2,1)S(1)} %get-tuple-element.83), channel_id=1, source_target_pairs={{0,6},{2,4},{4,2},{6,0},{8,14},{10,12},{12,10},{14,8},{16,22},{18,... | collective-permute-start | bytes 1622024 | tf_op jit(solution)/shard_map/ppermute | solution.py:33
  21.7 14.2 %copy-start.3 = (bf16[256,2560]{1,0:T(8,128)(2,1)S(1)}, bf16[256,2560]{1,0:T(8,128)(2,1)}, u32[]{:S(2)}) copy-start(bf16[256,2560]{1,0:T(8,128)(2,1)} %refs_13_.1) | copy-start | bytes 3932164
  24.0 39.0 %collective-permute-start.11 = (bf16[1056,256]{1,0:T(8,128)(2,1)S(1)}, bf16[1056,256]{1,0:T(8,128)(2,1)S(1)}, u32[]{:S(2)}, u32[]{:S(2)}) collective-permute-start(bf16[1056,256]{1,0:T(8,128)(2,1)S(1)} %get-tuple-element.99), channel_id=1, source_target_pairs={{0,2},{2,0},{4,6},{6,4},{8,10},{10,8},{12,14},{14,12},{16,18},{18,... | collective-permute-start | bytes 1622024 | tf_op jit(solution)/shard_map/ppermute | solution.py:33
  25.6 41.5 %collective-permute-start.12 = (bf16[1056,256]{1,0:T(8,128)(2,1)S(1)}, bf16[1056,256]{1,0:T(8,128)(2,1)S(1)}, u32[]{:S(2)}, u32[]{:S(2)}) collective-permute-start(bf16[1056,256]{1,0:T(8,128)(2,1)S(1)} %get-tuple-element.100), channel_id=1, source_target_pairs={{0,4},{2,6},{4,0},{6,2},{8,12},{10,14},{12,8},{14,10},{16,20},{18,... | collective-permute-start | bytes 1622024 | tf_op jit(solution)/shard_map/ppermute | solution.py:33
  33.4 36.5 %collective-permute-start.13 = (bf16[1056,256]{1,0:T(8,128)(2,1)S(1)}, bf16[1056,256]{1,0:T(8,128)(2,1)S(1)}, u32[]{:S(2)}, u32[]{:S(2)}) collective-permute-start(bf16[1056,256]{1,0:T(8,128)(2,1)S(1)} %get-tuple-element.101), channel_id=1, source_target_pairs={{0,6},{2,4},{4,2},{6,0},{8,14},{10,12},{12,10},{14,8},{16,22},{18,... | collective-permute-start | bytes 1622024 | tf_op jit(solution)/shard_map/ppermute | solution.py:33
  47.1 6.4 %collective-permute-start.7 = (bf16[512,256]{1,0:T(8,128)(2,1)S(1)}, bf16[512,256]{1,0:T(8,128)(2,1)S(1)}, u32[]{:S(2)}, u32[]{:S(2)}) collective-permute-start(bf16[512,256]{1,0:T(8,128)(2,1)S(1)} %get-tuple-element.90), channel_id=1, source_target_pairs={{0,8},{2,10},{4,12},{6,14},{8,0},{10,2},{12,4},{14,6},{16,24},{18,... | collective-permute-start | bytes 786440 | tf_op jit(solution)/shard_map/ppermute | solution.py:33
  47.2 6.4 %collective-permute-start.8 = (bf16[512,256]{1,0:T(8,128)(2,1)S(1)}, bf16[512,256]{1,0:T(8,128)(2,1)S(1)}, u32[]{:S(2)}, u32[]{:S(2)}) collective-permute-start(bf16[512,256]{1,0:T(8,128)(2,1)S(1)} %get-tuple-element.91), channel_id=1, source_target_pairs={{8,16},{10,18},{12,20},{14,22},{16,8},{18,10},{20,12},{22,14},{9,1... | collective-permute-start | bytes 786440 | tf_op jit(solution)/shard_map/ppermute | solution.py:39
  58.4 13.0 %collective-permute-start.9 = (bf16[528,256]{1,0:T(8,128)(2,1)S(1)}, bf16[528,256]{1,0:T(8,128)(2,1)S(1)}, u32[]{:S(2)}, u32[]{:S(2)}) collective-permute-start(bf16[528,256]{1,0:T(8,128)(2,1)S(1)} %get-tuple-element.96), channel_id=1, source_target_pairs={{0,8},{2,10},{4,12},{6,14},{8,0},{10,2},{12,4},{14,6},{16,24},{18,... | collective-permute-start | bytes 811016 | tf_op jit(solution)/shard_map/ppermute | solution.py:33
  62.3 8.9 %collective-permute-start.10 = (bf16[512,256]{1,0:T(8,128)(2,1)S(1)}, bf16[512,256]{1,0:T(8,128)(2,1)S(1)}, u32[]{:S(2)}, u32[]{:S(2)}) collective-permute-start(bf16[512,256]{1,0:T(8,128)(2,1)S(1)} %get-tuple-element.97), channel_id=1, source_target_pairs={{8,16},{10,18},{12,20},{14,22},{16,8},{18,10},{20,12},{22,14},{9,1... | collective-permute-start | bytes 786440 | tf_op jit(solution)/shard_map/ppermute | solution.py:39
  63.0 14.9 %collective-permute-start.19 = (bf16[1056,128]{1,0:T(8,128)(2,1)}, bf16[1056,128]{1,0:T(8,128)(2,1)S(1)}, u32[]{:S(2)}, u32[]{:S(2)}) collective-permute-start(bf16[1056,128]{1,0:T(8,128)(2,1)} %get-tuple-element.113), channel_id=1, source_target_pairs={{0,2},{2,0},{4,6},{6,4},{8,10},{10,8},{12,14},{14,12},{16,18},{18,... | collective-permute-start | bytes 811016 | tf_op jit(solution)/shard_map/ppermute | solution.py:33
  67.0 13.7 %collective-permute-start.20 = (bf16[1056,128]{1,0:T(8,128)(2,1)S(1)}, bf16[1056,128]{1,0:T(8,128)(2,1)S(1)}, u32[]{:S(2)}, u32[]{:S(2)}) collective-permute-start(bf16[1056,128]{1,0:T(8,128)(2,1)S(1)} %get-tuple-element.114), channel_id=1, source_target_pairs={{0,4},{2,6},{4,0},{6,2},{8,12},{10,14},{12,8},{14,10},{16,20},{18,... | collective-permute-start | bytes 811016 | tf_op jit(solution)/shard_map/ppermute | solution.py:33
  69.9 12.8 %collective-permute-start.21 = (bf16[1056,128]{1,0:T(8,128)(2,1)S(1)}, bf16[1056,128]{1,0:T(8,128)(2,1)S(1)}, u32[]{:S(2)}, u32[]{:S(2)}) collective-permute-start(bf16[1056,128]{1,0:T(8,128)(2,1)S(1)} %get-tuple-element.115), channel_id=1, source_target_pairs={{0,6},{2,4},{4,2},{6,0},{8,14},{10,12},{12,10},{14,8},{16,22},{18,... | collective-permute-start | bytes 811016 | tf_op jit(solution)/shard_map/ppermute | solution.py:33
  71.3 12.0 %collective-permute-start.17 = (bf16[512,256]{1,0:T(8,128)(2,1)S(1)}, bf16[512,256]{1,0:T(8,128)(2,1)S(1)}, u32[]{:S(2)}, u32[]{:S(2)}) collective-permute-start(bf16[512,256]{1,0:T(8,128)(2,1)S(1)} %get-tuple-element.110), channel_id=1, source_target_pairs={{0,8},{2,10},{4,12},{6,14},{8,0},{10,2},{12,4},{14,6},{16,24},{18,... | collective-permute-start | bytes 786440 | tf_op jit(solution)/shard_map/ppermute | solution.py:33
  71.4 14.6 %collective-permute-start.18 = (bf16[512,256]{1,0:T(8,128)(2,1)S(1)}, bf16[512,256]{1,0:T(8,128)(2,1)S(1)}, u32[]{:S(2)}, u32[]{:S(2)}) collective-permute-start(bf16[512,256]{1,0:T(8,128)(2,1)S(1)} %get-tuple-element.111), channel_id=1, source_target_pairs={{8,16},{10,18},{12,20},{14,22},{16,8},{18,10},{20,12},{22,14},{9,1... | collective-permute-start | bytes 786440 | tf_op jit(solution)/shard_map/ppermute | solution.py:39
  77.9 19.5 %collective-permute-start.14 = (bf16[784,256]{1,0:T(8,128)(2,1)S(1)}, bf16[784,256]{1,0:T(8,128)(2,1)S(1)}, u32[]{:S(2)}, u32[]{:S(2)}) collective-permute-start(bf16[784,256]{1,0:T(8,128)(2,1)S(1)} %get-tuple-element.105), channel_id=1, source_target_pairs={{0,2},{2,0},{4,6},{6,4},{8,10},{10,8},{12,14},{14,12},{16,18},{18,... | collective-permute-start | bytes 1204232 | tf_op jit(solution)/shard_map/ppermute | solution.py:33
  80.7 16.8 %collective-permute-start.15 = (bf16[784,256]{1,0:T(8,128)(2,1)S(1)}, bf16[784,256]{1,0:T(8,128)(2,1)S(1)}, u32[]{:S(2)}, u32[]{:S(2)}) collective-permute-start(bf16[784,256]{1,0:T(8,128)(2,1)S(1)} %get-tuple-element.106), channel_id=1, source_target_pairs={{0,4},{2,6},{4,0},{6,2},{8,12},{10,14},{12,8},{14,10},{16,20},{18,... | collective-permute-start | bytes 1204232 | tf_op jit(solution)/shard_map/ppermute | solution.py:33
  82.7 14.8 %collective-permute-start.16 = (bf16[784,256]{1,0:T(8,128)(2,1)S(1)}, bf16[784,256]{1,0:T(8,128)(2,1)S(1)}, u32[]{:S(2)}, u32[]{:S(2)}) collective-permute-start(bf16[784,256]{1,0:T(8,128)(2,1)S(1)} %get-tuple-element.107), channel_id=1, source_target_pairs={{0,6},{2,4},{4,2},{6,0},{8,14},{10,12},{12,10},{14,8},{16,22},{18,... | collective-permute-start | bytes 1204232 | tf_op jit(solution)/shard_map/ppermute | solution.py:33
  83.3 8.2 %collective-permute-start.24 = (bf16[512,128]{1,0:T(8,128)(2,1)S(1)}, bf16[512,128]{1,0:T(8,128)(2,1)S(1)}, u32[]{:S(2)}, u32[]{:S(2)}) collective-permute-start(bf16[512,128]{1,0:T(8,128)(2,1)S(1)} %get-tuple-element.123), channel_id=1, source_target_pairs={{0,8},{2,10},{4,12},{6,14},{8,0},{10,2},{12,4},{14,6},{16,24},{18,... | collective-permute-start | bytes 393224 | tf_op jit(solution)/shard_map/ppermute | solution.py:33
  86.0 8.3 %collective-permute-start.25 = (bf16[512,128]{1,0:T(8,128)(2,1)S(1)}, bf16[512,128]{1,0:T(8,128)(2,1)S(1)}, u32[]{:S(2)}, u32[]{:S(2)}) collective-permute-start(bf16[512,128]{1,0:T(8,128)(2,1)S(1)} %get-tuple-element.124), channel_id=1, source_target_pairs={{8,16},{10,18},{12,20},{14,22},{16,8},{18,10},{20,12},{22,14},{9,1... | collective-permute-start | bytes 393224 | tf_op jit(solution)/shard_map/ppermute | solution.py:39
  91.5 6.0 %copy-start.5 = (bf16[1024,512]{1,0:T(8,128)(2,1)}, bf16[1024,512]{1,0:T(8,128)(2,1)S(1)}, u32[]{:S(2)}) copy-start(bf16[1024,512]{1,0:T(8,128)(2,1)S(1)} %get-tuple-element.119.refs_3_) | copy-start | bytes 3145732
  91.5 7.2 %collective-permute-start.22 = (bf16[528,256]{1,0:T(8,128)(2,1)S(1)}, bf16[528,256]{1,0:T(8,128)(2,1)S(1)}, u32[]{:S(2)}, u32[]{:S(2)}) collective-permute-start(bf16[528,256]{1,0:T(8,128)(2,1)S(1)} %get-tuple-element.121), channel_id=1, source_target_pairs={{0,8},{2,10},{4,12},{6,14},{8,0},{10,2},{12,4},{14,6},{16,24},{18,... | collective-permute-start | bytes 811016 | tf_op jit(solution)/shard_map/ppermute | solution.py:33
  94.3 4.2 %collective-permute-start.23 = (bf16[512,256]{1,0:T(8,128)(2,1)S(1)}, bf16[512,256]{1,0:T(8,128)(2,1)S(1)}, u32[]{:S(2)}, u32[]{:S(2)}) collective-permute-start(bf16[512,256]{1,0:T(8,128)(2,1)S(1)} %get-tuple-element.122), channel_id=1, source_target_pairs={{8,16},{10,18},{12,20},{14,22},{16,8},{18,10},{20,12},{22,14},{9,1... | collective-permute-start | bytes 786440 | tf_op jit(solution)/shard_map/ppermute | solution.py:39
  97.5 1.2 copy-start.6
  100.4 22.3 %collective-permute-start.26 = (bf16[784,256]{1,0:T(8,128)(2,1)S(1)}, bf16[784,256]{1,0:T(8,128)(2,1)S(1)}, u32[]{:S(2)}, u32[]{:S(2)}) collective-permute-start(bf16[784,256]{1,0:T(8,128)(2,1)S(1)} %get-tuple-element.127), channel_id=1, source_target_pairs={{0,2},{2,0},{4,6},{6,4},{8,10},{10,8},{12,14},{14,12},{16,18},{18,... | collective-permute-start | bytes 1204232 | tf_op jit(solution)/shard_map/ppermute | solution.py:33
  101.2 22.1 %collective-permute-start.27 = (bf16[784,256]{1,0:T(8,128)(2,1)S(1)}, bf16[784,256]{1,0:T(8,128)(2,1)S(1)}, u32[]{:S(2)}, u32[]{:S(2)}) collective-permute-start(bf16[784,256]{1,0:T(8,128)(2,1)S(1)} %get-tuple-element.128), channel_id=1, source_target_pairs={{0,4},{2,6},{4,0},{6,2},{8,12},{10,14},{12,8},{14,10},{16,20},{18,... | collective-permute-start | bytes 1204232 | tf_op jit(solution)/shard_map/ppermute | solution.py:33
  103.2 20.1 %collective-permute-start.28 = (bf16[784,256]{1,0:T(8,128)(2,1)S(1)}, bf16[784,256]{1,0:T(8,128)(2,1)S(1)}, u32[]{:S(2)}, u32[]{:S(2)}) collective-permute-start(bf16[784,256]{1,0:T(8,128)(2,1)S(1)} %get-tuple-element.129), channel_id=1, source_target_pairs={{0,6},{2,4},{4,2},{6,0},{8,14},{10,12},{12,10},{14,8},{16,22},{18,... | collective-permute-start | bytes 1204232 | tf_op jit(solution)/shard_map/ppermute | solution.py:33
  107.2 6.3 %collective-permute-start.31 = (bf16[16,640]{1,0:T(8,128)(2,1)S(1)}, bf16[16,640]{1,0:T(8,128)(2,1)S(1)}, u32[]{:S(2)}, u32[]{:S(2)}) collective-permute-start(bf16[16,640]{1,0:T(8,128)(2,1)S(1)} %get-tuple-element.144), channel_id=1, source_target_pairs={{0,16},{2,18},{4,20},{6,22},{8,24},{10,26},{12,28},{14,30},{16,0},... | collective-permute-start | bytes 61448 | tf_op jit(solution)/shard_map/ppermute | solution.py:33
  111.4 5.6 %collective-permute-start.32 = (bf16[16,640]{1,0:T(8,128)(2,1)S(1)}, bf16[16,640]{1,0:T(8,128)(2,1)S(1)}, u32[]{:S(2)}, u32[]{:S(2)}) collective-permute-start(bf16[16,640]{1,0:T(8,128)(2,1)S(1)} %get-tuple-element.145), channel_id=1, source_target_pairs={{0,24},{2,26},{4,28},{6,30},{8,16},{10,18},{12,20},{14,22},{16,8},... | collective-permute-start | bytes 61448 | tf_op jit(solution)/shard_map/ppermute | solution.py:33
  113.5 5.3 %collective-permute-start.29 = (bf16[528,128]{1,0:T(8,128)(2,1)S(1)}, bf16[528,128]{1,0:T(8,128)(2,1)S(1)}, u32[]{:S(2)}, u32[]{:S(2)}) collective-permute-start(bf16[528,128]{1,0:T(8,128)(2,1)S(1)} %get-tuple-element.136), channel_id=1, source_target_pairs={{0,8},{2,10},{4,12},{6,14},{8,0},{10,2},{12,4},{14,6},{16,24},{18,... | collective-permute-start | bytes 405512 | tf_op jit(solution)/shard_map/ppermute | solution.py:33
  117.0 0.7 collective-permute-start.30
  119.7 6.0 %collective-permute-start.33 = (bf16[864,128]{1,0:T(8,128)(2,1)S(1)}, bf16[864,128]{1,0:T(8,128)(2,1)S(1)}, u32[]{:S(2)}, u32[]{:S(2)}) collective-permute-start(bf16[864,128]{1,0:T(8,128)(2,1)S(1)} %get-tuple-element.147), channel_id=1, source_target_pairs={{0,2},{2,0},{4,6},{6,4},{8,10},{10,8},{12,14},{14,12},{16,18},{18,... | collective-permute-start | bytes 663560 | tf_op jit(solution)/shard_map/ppermute | solution.py:33
  120.7 7.8 %collective-permute-start.34 = (bf16[864,128]{1,0:T(8,128)(2,1)S(1)}, bf16[864,128]{1,0:T(8,128)(2,1)S(1)}, u32[]{:S(2)}, u32[]{:S(2)}) collective-permute-start(bf16[864,128]{1,0:T(8,128)(2,1)S(1)} %get-tuple-element.148), channel_id=1, source_target_pairs={{0,4},{2,6},{4,0},{6,2},{8,12},{10,14},{12,8},{14,10},{16,20},{18,... | collective-permute-start | bytes 663560 | tf_op jit(solution)/shard_map/ppermute | solution.py:33
  122.7 6.8 %collective-permute-start.35 = (bf16[864,128]{1,0:T(8,128)(2,1)S(1)}, bf16[864,128]{1,0:T(8,128)(2,1)S(1)}, u32[]{:S(2)}, u32[]{:S(2)}) collective-permute-start(bf16[864,128]{1,0:T(8,128)(2,1)S(1)} %get-tuple-element.149), channel_id=1, source_target_pairs={{0,6},{2,4},{4,2},{6,0},{8,14},{10,12},{12,10},{14,8},{16,22},{18,... | collective-permute-start | bytes 663560 | tf_op jit(solution)/shard_map/ppermute | solution.py:33
  131.3 1.4 %collective-permute-start.36 = (f32[256,128]{1,0:T(8,128)S(1)}, f32[256,128]{1,0:T(8,128)S(1)}, u32[]{:S(2)}, u32[]{:S(2)}) collective-permute-start(f32[256,128]{1,0:T(8,128)S(1)} %get-tuple-element.151.dot_ref), channel_id=1, source_target_pairs={{0,1},{1,0},{2,3},{3,2},{4,5},{5,4},{6,7},{7,6},{8,9},{9,8},{10,11... | collective-permute-start | bytes 393224 | tf_op jit(solution)/shard_map/ppermute | solution.py:637
  (1 other events, 1.1 us)

commit v5 on v4

--- a/solution.py
+++ b/solution.py
@@ -168,7 +168,7 @@
     )(place, ids, own, other, key_raw, values, key_gain)
 
 
-def pack_kernel(first, place_ref, tiles_ref, readers_ref, own_ref, other_ref, *refs):
+def pack_kernel(first, whole, place_ref, tiles_ref, readers_ref, own_ref, other_ref, *refs):
     me, plane = place_ref[0], place_ref[1]
     query_inv, key_inv = inverses(own_ref[...], other_ref[...])
     rows = own_ref.shape[0]
@@ -197,28 +197,32 @@
         hot = hot & (row == 2 * (col // 16) + spot % 2 + 8 * (spot // 2))
         hot = hot.astype(F32).astype(BF16)
         chosen = parts[:, first * HEAD_DIM : first * HEAD_DIM + out.shape[1]]
-        out[4 * rows + 16 :] = contract(hot, chosen, ((1,), (0,))).astype(BF16)
+        top = 2 * rows if whole else 0
+        out[top + 2 * rows + 16 :] = contract(hot, chosen, ((1,), (0,))).astype(BF16)
         for h in range(out.shape[1] // HEAD_DIM):
             at = pl.multiple_of(((me ^ d) * each + first + h) * HEAD_DIM, HEAD_DIM)
             here = pl.ds(at, HEAD_DIM)
             lanes = slice(h * HEAD_DIM, (h + 1) * HEAD_DIM)
             key = key_ref[:, here].astype(F32)
             query = query_ref[:, here].astype(F32)
-            out[0:rows, lanes] = (key * key_inv * key_gain[:, here]).astype(BF16)
-            out[rows : 2 * rows, lanes] = value_ref[:, here]
-            out[2 * rows : 3 * rows, lanes] = (query * query_inv * query_gain[:, here]).astype(BF16)
-            out[3 * rows : 4 * rows, lanes] = grad_ref[:, here]
-            out[4 * rows : 4 * rows + 16, lanes] = facts
-
-
-def pack(place, tiles, readers, own, other, arrays, gains, parts, first, count, after):
+            if whole:
+                out[0:rows, lanes] = value_ref[:, here]
+                out[rows : 2 * rows, lanes] = grad_ref[:, here]
+            out[top : top + rows, lanes] = (key * key_inv * key_gain[:, here]).astype(BF16)
+            out[top + rows : top + 2 * rows, lanes] = (
+                query * query_inv * query_gain[:, here]
+            ).astype(BF16)
+            out[top + 2 * rows : top + 2 * rows + 16, lanes] = facts
+
+
+def pack(place, tiles, readers, own, other, arrays, gains, parts, first, count, whole, after):
     query_raw, key_raw, values, out_grad = arrays
     query_gain, key_gain = gains
     rows, width = query_raw.shape
     smem = pl.BlockSpec(memory_space=pltpu.SMEM)
     vmem = pl.BlockSpec(memory_space=pltpu.VMEM)
-    out_rows = 4 * rows + FACTS
-    kernel = functools.partial(pack_kernel, first)
+    out_rows = (4 if whole else 2) * rows + FACTS
+    kernel = functools.partial(pack_kernel, first, whole)
     return pl.pallas_call(
         behind(kernel, 11 + GROUP, len(after)),
         out_shape=[jax.ShapeDtypeStruct((out_rows, count * HEAD_DIM), BF16)] * GROUP
@@ -234,25 +238,61 @@
     )
 
 
-def edges_kernel(head, place_ref, b0, b1, b2, b3, near_ref, far_ref, token):
+def raw_kernel(first, head, place_ref, value_ref, grad_ref, *outs):
+    rows, width = value_ref.shape
+    for d, out in enumerate(outs):
+        wide = out.shape[1]
+        at = (place_ref[0] ^ d) * (width // GROUP) + first * HEAD_DIM
+        here = pl.ds(pl.multiple_of(at, HEAD_DIM), wide)
+        out[:rows] = value_ref[:, here]
+        out[rows:] = grad_ref[:, here]
+
+
+def pack_raw(place, values, out_grad, first, count):
+    shape = jax.ShapeDtypeStruct((2 * values.shape[0], count * HEAD_DIM), BF16)
+    return heads_call(
+        functools.partial(raw_kernel, first),
+        1,
+        place,
+        [(values, 0), (out_grad, 0)],
+        [(shape, 0)] * GROUP,
+        name="pack_raw",
+    )
+
+
+def halves(refs, rows):
+    if len(refs) == 2 * GROUP:
+        return list(zip(refs[:GROUP], refs[GROUP:]))
+    return [(ref.at[0 : 2 * rows], ref.at[2 * rows : ref.shape[0]]) for ref in refs]
+
+
+def edges_kernel(head, place_ref, *refs):
+    *blocks, near_ref, far_ref, token = refs
+    rows = near_ref.shape[0] // 2
     me, plane = place_ref[0], place_ref[1]
     token[...] = jnp.zeros((8, HEAD_DIM), F32)
     even = plane % 2 == 0
     last, first = me ^ (GROUP - 1), me
-    for d, block in enumerate((b0, b1, b2, b3)):
+    for d, block in enumerate(halves(blocks, rows)):
 
         @pl.when(jnp.where(even, last, first) == d)
         def _(block=block):
-            near_ref[...] = block[: near_ref.shape[0]]
+            near_ref[:rows] = block[1][:rows]
+            near_ref[rows:] = block[0][:rows]
 
         @pl.when(jnp.where(even, first, last) == d)
         def _(block=block):
-            far_ref[...] = block[: far_ref.shape[0]]
+            far_ref[:rows] = block[1][:rows]
+            far_ref[rows:] = block[0][:rows]
+
+
+def block_rows(blocks):
+    return (sum(x.shape[0] for x in blocks) // GROUP - FACTS) // 4
 
 
 def edges(place, blocks, after):
-    out_rows, width = blocks[0].shape
-    rows = (out_rows - FACTS) // 4
+    width = blocks[0].shape[1]
+    rows = block_rows(blocks)
     half = jax.ShapeDtypeStruct((2 * rows, width), BF16)
     return heads_call(
         edges_kernel,
@@ -265,14 +305,15 @@
     )
 
 
-def attend_kernel(outer, head, place_ref, b0, b1, b2, b3, *refs):
+def attend_kernel(outer, inputs, head, place_ref, *refs):
+    blocks, refs = refs[:inputs], refs[inputs:]
     if outer:
         near, far, g_in, dq_out, acc_out, g_out, near_out, far_out, mid_out, end_out = refs[:10]
     else:
         dq_out, acc_out, g_out = refs[:3]
     pair, weights, sums, raw_g, pair_g, sums_g, facts_at = refs[-7:]
     me, plane = place_ref[0], place_ref[1]
-    rows = (b0.shape[0] - FACTS) // 4
+    rows = block_rows(blocks)
     tiles = rows // TILE
     keys = slice(0, HEAD_DIM)
     vals = slice(HEAD_DIM, 2 * HEAD_DIM)
@@ -280,17 +321,17 @@
     if head == 0:
         weights[...] = jnp.zeros_like(weights)
 
-    for d, block in enumerate((b0, b1, b2, b3)):
+    for d, (raw, normed) in enumerate(halves(blocks, rows)):
         j = me ^ d
         at = pl.multiple_of((j + 1) * rows, TILE)
-        pair[pl.ds(at, rows), keys] = block[0:rows]
-        pair[pl.ds(at, rows), vals] = block[rows : 2 * rows]
+        pair[pl.ds(at, rows), keys] = normed[0:rows]
+        pair[pl.ds(at, rows), vals] = raw[0:rows]
         for tile in range(tiles):
-            here = 2 * rows + tile * TILE
-            weights[j * tiles + tile, :TILE, keys] = block[here : here + TILE]
-            weights[j * tiles + tile, TILE:, vals] = block[here + rows : here + rows + TILE]
-        facts_at[j] = block[4 * rows : 4 * rows + 16].astype(F32)
-        extra = block[4 * rows + 16 :].astype(F32)
+            here = rows + tile * TILE
+            weights[j * tiles + tile, :TILE, keys] = normed[here : here + TILE]
+            weights[j * tiles + tile, TILE:, vals] = raw[here : here + TILE]
+        facts_at[j] = normed[2 * rows : 2 * rows + 16].astype(F32)
+        extra = normed[2 * rows + 16 : 2 * rows + 32].astype(F32)
         eight = pl.ds(pl.multiple_of(8 * j, 8), 8)
         raw_g[eight, keys] = extra[:8]
         raw_g[eight, vals] = extra[8:]
@@ -363,8 +404,8 @@
 
 
 def attend(place, blocks, halo, inner_g, after):
-    out_rows, width = blocks[0].shape
-    rows = (out_rows - FACTS) // 4
+    width = blocks[0].shape[1]
+    rows = block_rows(blocks)
     wide = 2 * HEAD_DIM
     half = jax.ShapeDtypeStruct((2 * rows, width), BF16)
     few = jax.ShapeDtypeStruct((16, width), BF16)
@@ -375,7 +416,7 @@
     else:
         outs += [(jax.ShapeDtypeStruct((8 * GROUP, 2 * width), F32), wide)]
     return heads_call(
-        functools.partial(attend_kernel, len(halo) > 0),
+        functools.partial(attend_kernel, len(halo) > 0, len(blocks)),
         width // HEAD_DIM,
         place,
         [(x, HEAD_DIM) for x in (*blocks, *halo)] + [(x, wide) for x in inner_g],
@@ -651,12 +692,19 @@
     chunks = len(CHUNKS)
     firsts = [sum(CHUNKS[:c]) for c in range(chunks)]
     packed, token = [], ()
+
+    def spread(sent):
+        return [sent[0]] + [swapped(sent[d], d) for d in range(1, GROUP)]
+
+    raw = spread(pack_raw(place, values, out_grad, 0, CHUNKS[0]))
+    token = tuple(raw[1:])
     for first, count in zip(firsts, CHUNKS):
         *sent, last = pack(
-            place, key_tiles, readers, own, other, arrays, gains, parts, first, count, token
+            place, key_tiles, readers, own, other, arrays, gains, parts, first, count, first > 0,
+            token,
         )
         token = (last,)
-        packed.append([sent[0]] + [swapped(sent[d], d) for d in range(1, GROUP)])
+        packed.append((raw if first == 0 else []) + spread(sent))
     edge, inner, outer, back, home, dot = ({} for _ in range(6))
     fars = []
 

time: 139 us -> 134 us (0.964)
  waiting for transfers between devices: 35.1 us -> 20.6 us
  starting transfers between devices: 52.1 us -> 61.3 us
    ppermute x29 -> x32, waiting for transfers between devices: 32.9 us -> 18 us  [swapped(): return lax.ppermute(shard, 'ctx', [(i, i ^ bit) for i in range(count)])]
    ppermute x29 -> x32, starting transfers between devices: 47.4 us -> 57.2 us  [swapped(): return lax.ppermute(shard, 'ctx', [(i, i ^ bit) for i in range(count)])]
    pallas_call x15 -> x16, Pallas kernels: 31.7 us -> 32.5 us  [heads_call(): pl.pallas_call(run, out_shape=[shape for shape, _ in outputs], in_specs=[...]
  transfers between devices with their start and end apart: 37 -> 40, of which waited for: 15 -> 17; matrix products, arithmetic and copies ran while one was open for 0% -> 0% of each run, Pallas kernels for 25% -> 28%
where the time goes in v5:
time: 134 us; the launch traced here: 133 us
  starting transfers between devices  61.3 us (46%)
  Pallas kernels  46.9 us (35%)
  waiting for transfers between devices  20.6 us (15%)
  local copies, waits for them, and re-layouts  2.7 us (2%)
    ppermute x32, starting transfers between devices, swapped(): return lax.ppermute(shard, 'ctx', [(i, i ^ bit) for i in range(count)])  57.2 us
    pallas_call x16, Pallas kernels, heads_call(): pl.pallas_call(run, out_shape=[shape for shape, _ in outputs], in_specs=[...  32.5 us
    ppermute x32, waiting for transfers between devices, swapped(): return lax.ppermute(shard, 'ctx', [(i, i ^ bit) for i in range(count)])  18 us
    pallas_call x3, Pallas kernels, pack(): pl.pallas_call(behind(kernel, 11 + GROUP, len(after)), out_shape=[jax.Sha...  6.51 us
    pallas_call x1, Pallas kernels, finish(): pl.pallas_call(functools.partial(finish_kernel, chunks), out_shape=[jax.S...  4.73 us
    ppermute x6, starting transfers between devices, swapped_edges(): return lax.ppermute(shard, 'ctx', pairs)  3.98 us
    unnamed x22, local copies, waits for them, and re-layouts  2.68 us
  transfers between devices with their start and end apart: 40, of which 17 were waited for; matrix products, arithmetic and copies ran while one was open for 0% of the time, Pallas kernels for 28%

profile of v5, /device:TPU:0, one launch (start us, length us, event | category | flops | bytes accessed | tf_op | source)
XLA Modules:
  0.0 132.6 jit_solution(9263104122752102428)
XLA Ops:
  0.7 1.3 copy-done.3
  2.0 1.3 copy-done.5
  4.0 3.0 %collective-permute-start.1 = (bf16[512,256]{1,0:T(8,128)(2,1)S(1)}, bf16[512,256]{1,0:T(8,128)(2,1)S(1)}, u32[]{:S(2)}, u32[]{:S(2)}) collective-permute-start(bf16[512,256]{1,0:T(8,128)(2,1)S(1)} %get-tuple-element.84), channel_id=1, source_target_pairs={{0,2},{2,0},{4,6},{6,4},{8,10},{10,8},{12,14},{14,12},{16,18},{18,... | collective-permute-start | bytes 786440 | tf_op jit(solution)/shard_map/ppermute | solution.py:33
  7.0 1.5 %collective-permute-start.2 = (bf16[512,256]{1,0:T(8,128)(2,1)S(1)}, bf16[512,256]{1,0:T(8,128)(2,1)S(1)}, u32[]{:S(2)}, u32[]{:S(2)}) collective-permute-start(bf16[512,256]{1,0:T(8,128)(2,1)S(1)} %get-tuple-element.85), channel_id=1, source_target_pairs={{0,4},{2,6},{4,0},{6,2},{8,12},{10,14},{12,8},{14,10},{16,20},{18,... | collective-permute-start | bytes 786440 | tf_op jit(solution)/shard_map/ppermute | solution.py:33
  9.3 1.3 collective-permute-done.other_ref.refs_4_
  11.4 4.1 %collective-permute-start.6 = (bf16[16,640]{1,0:T(8,128)(2,1)S(1)}, bf16[16,640]{1,0:T(8,128)(2,1)S(1)}, u32[]{:S(2)}, u32[]{:S(2)}) collective-permute-start(bf16[16,640]{1,0:T(8,128)(2,1)S(1)} %get-tuple-element.87.refs_11_), channel_id=1, source_target_pairs={{0,24},{2,26},{4,28},{6,30},{8,16},{10,18},{12,20},{14,22},{16,8},... | collective-permute-start | bytes 61448 | tf_op jit(solution)/shard_map/ppermute | solution.py:33
  15.5 1.8 %collective-permute-done.6.refs_14_ = bf16[16,640]{1,0:T(8,128)(2,1)S(1)} collective-permute-done((bf16[16,640]{1,0:T(8,128)(2,1)S(1)}, bf16[16,640]{1,0:T(8,128)(2,1)S(1)}, u32[]{:S(2)}, u32[]{:S(2)}) %collective-permute-start.6) | collective-permute-done | bytes 20512 | tf_op jit(solution)/shard_map/ppermute | solution.py:33
  17.4 2.7 %collective-permute-done.5.refs_13_ = bf16[16,640]{1,0:T(8,128)(2,1)S(1)} collective-permute-done((bf16[16,640]{1,0:T(8,128)(2,1)S(1)}, bf16[16,640]{1,0:T(8,128)(2,1)S(1)}, u32[]{:S(2)}, u32[]{:S(2)}) %collective-permute-start.5) | collective-permute-done | bytes 20512 | tf_op jit(solution)/shard_map/ppermute | solution.py:33
  21.0 1.7 %pack.3 = (bf16[544,256]{1,0:T(8,128)(2,1)S(1)}, bf16[544,256]{1,0:T(8,128)(2,1)S(1)}, bf16[544,256]{1,0:T(8,128)(2,1)S(1)}, bf16[544,256]{1,0:T(8,128)(2,1)S(1)}, f32[8,128]{1,0:T(8,128)S(1)}) custom-call(s32[2]{0:T(128)S(1)} %pad_add_fusion.place_ref.refs_0_, s32[2,4]{1,0:T(2,128)S(1)} %copy-done.6, s32[1,16]{1,0:T(1,128)S(1)} %copy-done.7, ...), custom_call_target="tpu_custom_call" | custom-call | flops 1 | bytes 1 | tf_op jit(solution)/shard_map/pack/pallas_call | solution.py:226
  22.8 1.8 %collective-permute-start.7 = (bf16[544,256]{1,0:T(8,128)(2,1)S(1)}, bf16[544,256]{1,0:T(8,128)(2,1)S(1)}, u32[]{:S(2)}, u32[]{:S(2)}) collective-permute-start(bf16[544,256]{1,0:T(8,128)(2,1)S(1)} %get-tuple-element.89), channel_id=1, source_target_pairs={{0,2},{2,0},{4,6},{6,4},{8,10},{10,8},{12,14},{14,12},{16,18},{18,... | collective-permute-start | bytes 835592 | tf_op jit(solution)/shard_map/ppermute | solution.py:33
  24.5 1.5 %collective-permute-start.8 = (bf16[544,256]{1,0:T(8,128)(2,1)S(1)}, bf16[544,256]{1,0:T(8,128)(2,1)S(1)}, u32[]{:S(2)}, u32[]{:S(2)}) collective-permute-start(bf16[544,256]{1,0:T(8,128)(2,1)S(1)} %get-tuple-element.90), channel_id=1, source_target_pairs={{0,4},{2,6},{4,0},{6,2},{8,12},{10,14},{12,8},{14,10},{16,20},{18,... | collective-permute-start | bytes 835592 | tf_op jit(solution)/shard_map/ppermute | solution.py:33
  26.3 2.3 %pack.4 = (bf16[1056,256]{1,0:T(8,128)(2,1)S(1)}, bf16[1056,256]{1,0:T(8,128)(2,1)S(1)}, bf16[1056,256]{1,0:T(8,128)(2,1)S(1)}, bf16[1056,256]{1,0:T(8,128)(2,1)S(1)}, f32[8,128]{1,0:T(8,128)S(1)}) custom-call(s32[2]{0:T(128)S(1)} %pad_add_fusion.place_ref.refs_0_, s32[2,4]{1,0:T(2,128)S(1)} %copy-done.6, s32[1,16]{1,0:T(1,128)S(1)} %copy-done.7, ...), custom_call_target="tpu_custom_call" | custom-call | flops 1 | bytes 1 | tf_op jit(solution)/shard_map/pack/pallas_call | solution.py:226
  28.6 1.8 %collective-permute-start.14 = (bf16[1056,256]{1,0:T(8,128)(2,1)S(1)}, bf16[1056,256]{1,0:T(8,128)(2,1)S(1)}, u32[]{:S(2)}, u32[]{:S(2)}) collective-permute-start(bf16[1056,256]{1,0:T(8,128)(2,1)S(1)} %get-tuple-element.107), channel_id=1, source_target_pairs={{0,2},{2,0},{4,6},{6,4},{8,10},{10,8},{12,14},{14,12},{16,18},{18,... | collective-permute-start | bytes 1622024 | tf_op jit(solution)/shard_map/ppermute | solution.py:33
  30.4 1.5 %collective-permute-start.15 = (bf16[1056,256]{1,0:T(8,128)(2,1)S(1)}, bf16[1056,256]{1,0:T(8,128)(2,1)S(1)}, u32[]{:S(2)}, u32[]{:S(2)}) collective-permute-start(bf16[1056,256]{1,0:T(8,128)(2,1)S(1)} %get-tuple-element.108), channel_id=1, source_target_pairs={{0,4},{2,6},{4,0},{6,2},{8,12},{10,14},{12,8},{14,10},{16,20},{18,... | collective-permute-start | bytes 1622024 | tf_op jit(solution)/shard_map/ppermute | solution.py:33
  32.4 2.7 %collective-permute-start.16 = (bf16[1056,256]{1,0:T(8,128)(2,1)S(1)}, bf16[1056,256]{1,0:T(8,128)(2,1)S(1)}, u32[]{:S(2)}, u32[]{:S(2)}) collective-permute-start(bf16[1056,256]{1,0:T(8,128)(2,1)S(1)} %get-tuple-element.109), channel_id=1, source_target_pairs={{0,6},{2,4},{4,2},{6,0},{8,14},{10,12},{12,10},{14,8},{16,22},{18,... | collective-permute-start | bytes 1622024 | tf_op jit(solution)/shard_map/ppermute | solution.py:33
  35.1 2.5 %pack.5 = (bf16[1056,128]{1,0:T(8,128)(2,1)S(1)}, bf16[1056,128]{1,0:T(8,128)(2,1)}, bf16[1056,128]{1,0:T(8,128)(2,1)}, bf16[1056,128]{1,0:T(8,128)(2,1)}, f32[8,128]{1,0:T(8,128)S(1)}) custom-call(s32[2]{0:T(128)S(1)} %pad_add_fusion.place_ref.refs_0_, s32[2,4]{1,0:T(2,128)S(1)} %copy-done.6, s32[1,16]{1,0:T(1,128)S(1)} %copy-done.7, ...), custom_call_target="tpu_custom_call" | custom-call | flops 1 | bytes 1 | tf_op jit(solution)/shard_map/pack/pallas_call | solution.py:226
  38.4 1.1 collective-permute-done.9.refs_7_
  41.6 4.3 %inner.3 = (bf16[512,256]{1,0:T(8,128)(2,1)S(1)}, bf16[1024,512]{1,0:T(8,128)(2,1)S(1)}, f32[32,512]{1,0:T(8,128)S(1)}) custom-call(s32[2]{0:T(128)S(1)} %pad_add_fusion.place_ref.refs_0_, bf16[512,256]{1,0:T(8,128)(2,1)S(1)} %get-tuple-element.83.refs_0_, bf16[512,256]{1,0:T(8,128)(2,1)S(1)} %collective-permute-done.1.refs_15_.refs_1_, ...), custom_call_target="tpu_custom_call" | custom-call | flops 1 | bytes 1 | tf_op jit(solution)/shard_map/inner/pallas_call | solution.py:69
  46.6 4.8 %outer.3 = (bf16[512,256]{1,0:T(8,128)(2,1)S(1)}, bf16[1024,512]{1,0:T(8,128)(2,1)S(1)}, bf16[16,256]{1,0:T(8,128)(2,1)S(1)}, bf16[528,256]{1,0:T(8,128)(2,1)S(1...) custom-call(s32[2]{0:T(128)S(1)} %pad_add_fusion.place_ref.refs_0_, ...), custom_call_target="tpu_custom_call" | custom-call | flops 1 | bytes 1 | tf_op jit(solution)/shard_map/outer/pallas_call | solution.py:69
  51.5 4.7 %collective-permute-start.12 = (bf16[528,256]{1,0:T(8,128)(2,1)S(1)}, bf16[528,256]{1,0:T(8,128)(2,1)S(1)}, u32[]{:S(2)}, u32[]{:S(2)}) collective-permute-start(bf16[528,256]{1,0:T(8,128)(2,1)S(1)} %get-tuple-element.104), channel_id=1, source_target_pairs={{0,8},{2,10},{4,12},{6,14},{8,0},{10,2},{12,4},{14,6},{16,24},{18,... | collective-permute-start | bytes 811016 | tf_op jit(solution)/shard_map/ppermute | solution.py:33
  56.8 1.6 %collective-permute-start.22 = (bf16[1056,128]{1,0:T(8,128)(2,1)}, bf16[1056,128]{1,0:T(8,128)(2,1)S(1)}, u32[]{:S(2)}, u32[]{:S(2)}) collective-permute-start(bf16[1056,128]{1,0:T(8,128)(2,1)} %get-tuple-element.121), channel_id=1, source_target_pairs={{0,2},{2,0},{4,6},{6,4},{8,10},{10,8},{12,14},{14,12},{16,18},{18,... | collective-permute-start | bytes 811016 | tf_op jit(solution)/shard_map/ppermute | solution.py:33
  58.4 1.2 collective-permute-done.15.refs_2_
  59.5 3.0 %collective-permute-start.23 = (bf16[1056,128]{1,0:T(8,128)(2,1)}, bf16[1056,128]{1,0:T(8,128)(2,1)S(1)}, u32[]{:S(2)}, u32[]{:S(2)}) collective-permute-start(bf16[1056,128]{1,0:T(8,128)(2,1)} %get-tuple-element.122), channel_id=1, source_target_pairs={{0,4},{2,6},{4,0},{6,2},{8,12},{10,14},{12,8},{14,10},{16,20},{18,... | collective-permute-start | bytes 811016 | tf_op jit(solution)/shard_map/ppermute | solution.py:33
  62.8 1.4 %collective-permute-start.24 = (bf16[1056,128]{1,0:T(8,128)(2,1)}, bf16[1056,128]{1,0:T(8,128)(2,1)S(1)}, u32[]{:S(2)}, u32[]{:S(2)}) collective-permute-start(bf16[1056,128]{1,0:T(8,128)(2,1)} %get-tuple-element.123), channel_id=1, source_target_pairs={{0,6},{2,4},{4,2},{6,0},{8,14},{10,12},{12,10},{14,8},{16,22},{18,... | collective-permute-start | bytes 811016 | tf_op jit(solution)/shard_map/ppermute | solution.py:33
  66.2 4.3 %inner.4 = (bf16[512,256]{1,0:T(8,128)(2,1)S(1)}, bf16[1024,512]{1,0:T(8,128)(2,1)S(1)}, f32[32,512]{1,0:T(8,128)S(1)}) custom-call(s32[2]{0:T(128)S(1)} %pad_add_fusion.place_ref.refs_0_, bf16[1056,256]{1,0:T(8,128)(2,1)S(1)} %get-tuple-element.106.refs_0_, bf16[1056,256]{1,0:T(8,128)(2,1)S(1)} %collective-permute-done.14.refs_1_, ...), custom_call_target="tpu_custom_call" | custom-call | flops 1 | bytes 1 | tf_op jit(solution)/shard_map/inner/pallas_call | solution.py:69
  70.5 1.4 %settle.3 = (bf16[784,256]{1,0:T(8,128)(2,1)S(1)}, bf16[784,256]{1,0:T(8,128)(2,1)S(1)}, bf16[784,256]{1,0:T(8,128)(2,1)S(1)}, bf16[784,256]{1,0:T(8,128)(2,1)S(1)}, f32[8,128]{1,0:T(8,128)S(1)}) custom-call(s32[2]{0:T(128)S(1)} %pad_add_fusion.place_ref.refs_0_, bf16[512,256]{1,0:T(8,128)(2,1)S(1)} %get-tuple-element.96.refs_0_, ...), custom_call_target="tpu_custom_call" | custom-call | flops 1 | bytes 1 | tf_op jit(solution)/shard_map/settle/pallas_call | solution.py:69
  72.9 2.4 %collective-permute-start.18 = (bf16[784,256]{1,0:T(8,128)(2,1)S(1)}, bf16[784,256]{1,0:T(8,128)(2,1)S(1)}, u32[]{:S(2)}, u32[]{:S(2)}) collective-permute-start(bf16[784,256]{1,0:T(8,128)(2,1)S(1)} %get-tuple-element.114), channel_id=1, source_target_pairs={{0,4},{2,6},{4,0},{6,2},{8,12},{10,14},{12,8},{14,10},{16,20},{18,... | collective-permute-start | bytes 1204232 | tf_op jit(solution)/shard_map/ppermute | solution.py:33
  76.1 5.6 %collective-permute-start.27 = (bf16[512,128]{1,0:T(8,128)(2,1)S(1)}, bf16[512,128]{1,0:T(8,128)(2,1)S(1)}, u32[]{:S(2)}, u32[]{:S(2)}) collective-permute-start(bf16[512,128]{1,0:T(8,128)(2,1)S(1)} %get-tuple-element.131), channel_id=1, source_target_pairs={{0,8},{2,10},{4,12},{6,14},{8,0},{10,2},{12,4},{14,6},{16,24},{18,... | collective-permute-start | bytes 393224 | tf_op jit(solution)/shard_map/ppermute | solution.py:33
  82.4 4.8 %outer.4 = (bf16[512,256]{1,0:T(8,128)(2,1)S(1)}, bf16[1024,512]{1,0:T(8,128)(2,1)S(1)}, bf16[16,256]{1,0:T(8,128)(2,1)S(1)}, bf16[528,256]{1,0:T(8,128)(2,1)S(1...) custom-call(s32[2]{0:T(128)S(1)} %pad_add_fusion.place_ref.refs_0_, ...), custom_call_target="tpu_custom_call" | custom-call | flops 1 | bytes 1 | tf_op jit(solution)/shard_map/outer/pallas_call | solution.py:69
  87.2 1.3 %collective-permute-start.25 = (bf16[528,256]{1,0:T(8,128)(2,1)S(1)}, bf16[528,256]{1,0:T(8,128)(2,1)S(1)}, u32[]{:S(2)}, u32[]{:S(2)}) collective-permute-start(bf16[528,256]{1,0:T(8,128)(2,1)S(1)} %get-tuple-element.129), channel_id=1, source_target_pairs={{0,8},{2,10},{4,12},{6,14},{8,0},{10,2},{12,4},{14,6},{16,24},{18,... | collective-permute-start | bytes 811016 | tf_op jit(solution)/shard_map/ppermute | solution.py:33
  89.2 2.5 %inner.5 = (bf16[512,128]{1,0:T(8,128)(2,1)S(1)}, bf16[1024,256]{1,0:T(8,128)(2,1)S(1)}, f32[32,256]{1,0:T(8,128)S(1)}) custom-call(s32[2]{0:T(128)S(1)} %pad_add_fusion.place_ref.refs_0_, bf16[1056,128]{1,0:T(8,128)(2,1)S(1)} %get-tuple-element.120.refs_0_, bf16[1056,128]{1,0:T(8,128)(2,1)S(1)} %collective-permute-done.22.refs_1_, ...), custom_call_target="tpu_custom_call" | custom-call | flops 1 | bytes 1 | tf_op jit(solution)/shard_map/inner/pallas_call | solution.py:69
  91.8 1.0 dots.2.refs_7_.refs_12_
  93.7 1.6 %settle.4 = (bf16[784,256]{1,0:T(8,128)(2,1)S(1)}, bf16[784,256]{1,0:T(8,128)(2,1)S(1)}, bf16[784,256]{1,0:T(8,128)(2,1)S(1)}, bf16[784,256]{1,0:T(8,128)(2,1)S(1)}, f32[8,128]{1,0:T(8,128)S(1)}) custom-call(s32[2]{0:T(128)S(1)} %pad_add_fusion.place_ref.refs_0_, bf16[512,256]{1,0:T(8,128)(2,1)S(1)} %get-tuple-element.116.refs_0_, ...), custom_call_target="tpu_custom_call" | custom-call | flops 1 | bytes 1 | tf_op jit(solution)/shard_map/settle/pallas_call | solution.py:69
  96.0 1.5 %collective-permute-start.30 = (bf16[784,256]{1,0:T(8,128)(2,1)S(1)}, bf16[784,256]{1,0:T(8,128)(2,1)S(1)}, u32[]{:S(2)}, u32[]{:S(2)}) collective-permute-start(bf16[784,256]{1,0:T(8,128)(2,1)S(1)} %get-tuple-element.136), channel_id=1, source_target_pairs={{0,4},{2,6},{4,0},{6,2},{8,12},{10,14},{12,8},{14,10},{16,20},{18,... | collective-permute-start | bytes 1204232 | tf_op jit(solution)/shard_map/ppermute | solution.py:33
  97.5 1.4 %collective-permute-start.31 = (bf16[784,256]{1,0:T(8,128)(2,1)S(1)}, bf16[784,256]{1,0:T(8,128)(2,1)S(1)}, u32[]{:S(2)}, u32[]{:S(2)}) collective-permute-start(bf16[784,256]{1,0:T(8,128)(2,1)S(1)} %get-tuple-element.137), channel_id=1, source_target_pairs={{0,6},{2,4},{4,2},{6,0},{8,14},{10,12},{12,10},{14,8},{16,22},{18,... | collective-permute-start | bytes 1204232 | tf_op jit(solution)/shard_map/ppermute | solution.py:33
  98.9 2.7 %outer.5 = (bf16[512,128]{1,0:T(8,128)(2,1)S(1)}, bf16[1024,256]{1,0:T(8,128)(2,1)S(1)}, bf16[16,128]{1,0:T(8,128)(2,1)S(1)}, bf16[528,128]{1,0:T(8,128)(2,1)S(1...) custom-call(s32[2]{0:T(128)S(1)} %pad_add_fusion.place_ref.refs_0_, ...), custom_call_target="tpu_custom_call" | custom-call | flops 1 | bytes 1 | tf_op jit(solution)/shard_map/outer/pallas_call | solution.py:69
  102.2 4.6 %collective-permute-start.34 = (bf16[16,640]{1,0:T(8,128)(2,1)S(1)}, bf16[16,640]{1,0:T(8,128)(2,1)S(1)}, u32[]{:S(2)}, u32[]{:S(2)}) collective-permute-start(bf16[16,640]{1,0:T(8,128)(2,1)S(1)} %get-tuple-element.152), channel_id=1, source_target_pairs={{0,16},{2,18},{4,20},{6,22},{8,24},{10,26},{12,28},{14,30},{16,0},... | collective-permute-start | bytes 61448 | tf_op jit(solution)/shard_map/ppermute | solution.py:33
  106.8 2.3 %collective-permute-start.35 = (bf16[16,640]{1,0:T(8,128)(2,1)S(1)}, bf16[16,640]{1,0:T(8,128)(2,1)S(1)}, u32[]{:S(2)}, u32[]{:S(2)}) collective-permute-start(bf16[16,640]{1,0:T(8,128)(2,1)S(1)} %get-tuple-element.153), channel_id=1, source_target_pairs={{0,24},{2,26},{4,28},{6,30},{8,16},{10,18},{12,20},{14,22},{16,8},... | collective-permute-start | bytes 61448 | tf_op jit(solution)/shard_map/ppermute | solution.py:33
  109.1 2.3 %collective-permute-start.32 = (bf16[528,128]{1,0:T(8,128)(2,1)S(1)}, bf16[528,128]{1,0:T(8,128)(2,1)S(1)}, u32[]{:S(2)}, u32[]{:S(2)}) collective-permute-start(bf16[528,128]{1,0:T(8,128)(2,1)S(1)} %get-tuple-element.144), channel_id=1, source_target_pairs={{0,8},{2,10},{4,12},{6,14},{8,0},{10,2},{12,4},{14,6},{16,24},{18,... | collective-permute-start | bytes 405512 | tf_op jit(solution)/shard_map/ppermute | solution.py:33
  113.1 1.4 %collective-permute-done.32.refs_5_ = bf16[528,128]{1,0:T(8,128)(2,1)S(1)} collective-permute-done((bf16[528,128]{1,0:T(8,128)(2,1)S(1)}, bf16[528,128]{1,0:T(8,128)(2,1)S(1)}, u32[]{:S(2)}, u32[]{:S(2)}) %collective-permute-start.32) | collective-permute-done | bytes 135200 | tf_op jit(solution)/shard_map/ppermute | solution.py:33
  116.0 1.5 %collective-permute-start.37 = (bf16[864,128]{1,0:T(8,128)(2,1)S(1)}, bf16[864,128]{1,0:T(8,128)(2,1)S(1)}, u32[]{:S(2)}, u32[]{:S(2)}) collective-permute-start(bf16[864,128]{1,0:T(8,128)(2,1)S(1)} %get-tuple-element.156), channel_id=1, source_target_pairs={{0,4},{2,6},{4,0},{6,2},{8,12},{10,14},{12,8},{14,10},{16,20},{18,... | collective-permute-start | bytes 663560 | tf_op jit(solution)/shard_map/ppermute | solution.py:33
  117.5 1.4 %collective-permute-start.38 = (bf16[864,128]{1,0:T(8,128)(2,1)S(1)}, bf16[864,128]{1,0:T(8,128)(2,1)S(1)}, u32[]{:S(2)}, u32[]{:S(2)}) collective-permute-start(bf16[864,128]{1,0:T(8,128)(2,1)S(1)} %get-tuple-element.157), channel_id=1, source_target_pairs={{0,6},{2,4},{4,2},{6,0},{8,14},{10,12},{12,10},{14,8},{16,22},{18,... | collective-permute-start | bytes 663560 | tf_op jit(solution)/shard_map/ppermute | solution.py:33
  119.9 1.5 %collective-permute-done.36.refs_9_ = bf16[864,128]{1,0:T(8,128)(2,1)S(1)} collective-permute-done((bf16[864,128]{1,0:T(8,128)(2,1)S(1)}, bf16[864,128]{1,0:T(8,128)(2,1)S(1)}, u32[]{:S(2)}, u32[]{:S(2)}) %collective-permute-start.36) | collective-permute-done | bytes 221216 | tf_op jit(solution)/shard_map/ppermute | solution.py:33
  121.4 2.0 %collective-permute-done.37.refs_10_ = bf16[864,128]{1,0:T(8,128)(2,1)S(1)} collective-permute-done((bf16[864,128]{1,0:T(8,128)(2,1)S(1)}, bf16[864,128]{1,0:T(8,128)(2,1)S(1)}, u32[]{:S(2)}, u32[]{:S(2)}) %collective-permute-start.37) | collective-permute-done | bytes 221216 | tf_op jit(solution)/shard_map/ppermute | solution.py:33
  123.4 1.3 %collective-permute-done.38.refs_11_ = bf16[864,128]{1,0:T(8,128)(2,1)S(1)} collective-permute-done((bf16[864,128]{1,0:T(8,128)(2,1)S(1)}, bf16[864,128]{1,0:T(8,128)(2,1)S(1)}, u32[]{:S(2)}, u32[]{:S(2)}) %collective-permute-start.38) | collective-permute-done | bytes 221216 | tf_op jit(solution)/shard_map/ppermute | solution.py:33
  124.7 1.7 %total_dots.1 = (f32[256,128]{1,0:T(8,128)S(1)}, f32[8,2560]{1,0:T(8,128)S(1)}) custom-call(s32[2]{0:T(128)S(1)} %pad_add_fusion.place_ref.refs_0_, s32[2]{0:T(128)S(1)} %copy-done.8, bf16[16,2560]{1,0:T(8,128)(2,1)S(1)} %get-tuple-element.82.raw_ref, bf16[256,2560]{1,0:T(8,128)(2,1)S(1)} %copy-done.2, bf16[256,2560]{1,0:T(8,128)(2,1)} %refs_14_.1, ...), custom_call_target="tpu_custom_call" | custom-call | flops 1 | bytes 1 | tf_op jit(solution)/shard_map/total_dots/pallas_call | solution.py:570
  126.5 1.3 %collective-permute-done.39.dot_other_ref = f32[256,128]{1,0:T(8,128)S(1)} collective-permute-done((f32[256,128]{1,0:T(8,128)S(1)}, f32[256,128]{1,0:T(8,128)S(1)}, u32[]{:S(2)}, u32[]{:S(2)}) %collective-permute-start.39) | collective-permute-done | bytes 131104 | tf_op jit(solution)/shard_map/ppermute | solution.py:678
  127.9 4.7 %finish.1 = (bf16[256,2560]{1,0:T(8,128)(2,1)}, bf16[256,2560]{1,0:T(8,128)(2,1)}, bf16[256,2560]{1,0:T(8,128)(2,1)}) custom-call(s32[2]{0:T(128)S(1)} %pad_add_fusion.place_ref.refs_0_, s32[2]{0:T(128)S(1)} %copy-done.8, f32[256,128]{1,0:T(8,128)S(1)} %squares.1.own_ref.refs_3_, f32[256,128]{1,0:T(8,128)S(1)} %collective-permute-done.other_ref.refs_4_, ...), custom_call_target="tpu_custom_call" | custom-call | flops 1 | bytes 1 | tf_op jit(solution)/shard_map/finish/pallas_call | solution.py:665
  (80 shorter events, 20.0 us)
Async XLA Ops:
  3.4 5.2 %copy-start = (bf16[256,2560]{1,0:T(8,128)(2,1)S(1)}, bf16[256,2560]{1,0:T(8,128)(2,1)}, u32[]{:S(2)}) copy-start(bf16[256,2560]{1,0:T(8,128)(2,1)} %refs_14_.1) | copy-start | bytes 3932164
  3.4 5.2 %copy-start.1 = (bf16[256,2560]{1,0:T(8,128)(2,1)S(1)}, bf16[256,2560]{1,0:T(8,128)(2,1)}, u32[]{:S(2)}) copy-start(bf16[256,2560]{1,0:T(8,128)(2,1)} %refs_13_.1) | copy-start | bytes 3932164
  4.0 17.0 %collective-permute-start.1 = (bf16[512,256]{1,0:T(8,128)(2,1)S(1)}, bf16[512,256]{1,0:T(8,128)(2,1)S(1)}, u32[]{:S(2)}, u32[]{:S(2)}) collective-permute-start(bf16[512,256]{1,0:T(8,128)(2,1)S(1)} %get-tuple-element.84), channel_id=1, source_target_pairs={{0,2},{2,0},{4,6},{6,4},{8,10},{10,8},{12,14},{14,12},{16,18},{18,... | collective-permute-start | bytes 786440 | tf_op jit(solution)/shard_map/ppermute | solution.py:33
  7.0 14.0 %collective-permute-start.2 = (bf16[512,256]{1,0:T(8,128)(2,1)S(1)}, bf16[512,256]{1,0:T(8,128)(2,1)S(1)}, u32[]{:S(2)}, u32[]{:S(2)}) collective-permute-start(bf16[512,256]{1,0:T(8,128)(2,1)S(1)} %get-tuple-element.85), channel_id=1, source_target_pairs={{0,4},{2,6},{4,0},{6,2},{8,12},{10,14},{12,8},{14,10},{16,20},{18,... | collective-permute-start | bytes 786440 | tf_op jit(solution)/shard_map/ppermute | solution.py:33
  8.5 2.0 %copy-start.4 = (bf16[256,2560]{1,0:T(8,128)(2,1)S(1)}, bf16[256,2560]{1,0:T(8,128)(2,1)}, u32[]{:S(2)}) copy-start(bf16[256,2560]{1,0:T(8,128)(2,1)} %refs_6_.5) | copy-start | bytes 3932164
  8.5 2.0 %copy-start.8 = (s32[2]{0:T(128)S(1)}, s32[2]{0:T(128)}, u32[]{:S(2)}) copy-start(s32[2]{0:T(128)} %ids_ref.5) | copy-start | bytes 28
  8.5 12.5 %collective-permute-start.3 = (bf16[512,256]{1,0:T(8,128)(2,1)S(1)}, bf16[512,256]{1,0:T(8,128)(2,1)S(1)}, u32[]{:S(2)}, u32[]{:S(2)}) collective-permute-start(bf16[512,256]{1,0:T(8,128)(2,1)S(1)} %get-tuple-element.86), channel_id=1, source_target_pairs={{0,6},{2,4},{4,2},{6,0},{8,14},{10,12},{12,10},{14,8},{16,22},{18,... | collective-permute-start | bytes 786440 | tf_op jit(solution)/shard_map/ppermute | solution.py:33
  9.2 1.4 %collective-permute-start = (f32[256,128]{1,0:T(8,128)S(1)}, f32[256,128]{1,0:T(8,128)S(1)}, u32[]{:S(2)}, u32[]{:S(2)}) collective-permute-start(f32[256,128]{1,0:T(8,128)S(1)} %squares.1.own_ref.refs_3_), channel_id=1, source_target_pairs={{0,1},{1,0},{2,3},{3,2},{4,5},{5,4},{6,7},{7,6},{8,9},{9,8},{10,11... | collective-permute-start | bytes 393224 | tf_op jit(solution)/shard_map/ppermute | solution.py:678
  9.2 8.2 %copy-start.10 = (f32[2560]{0:T(1024)S(1)}, f32[2560]{0:T(1024)}, u32[]{:S(2)}) copy-start(f32[2560]{0:T(1024)} %param.13) | copy-start | bytes 30724
  9.2 11.8 %copy-start.6 = (s32[2,4]{1,0:T(2,128)S(1)}, s32[2,4]{1,0:T(2,128)}, u32[]{:S(2)}) copy-start(s32[2,4]{1,0:T(2,128)} %refs_1_.7) | copy-start | bytes 100
  9.3 11.8 %copy-start.7 = (s32[1,16]{1,0:T(1,128)S(1)}, s32[1,16]{1,0:T(1,128)}, u32[]{:S(2)}) copy-start(s32[1,16]{1,0:T(1,128)} %refs_2_.5) | copy-start | bytes 196
  11.4 5.9 %collective-permute-start.6 = (bf16[16,640]{1,0:T(8,128)(2,1)S(1)}, bf16[16,640]{1,0:T(8,128)(2,1)S(1)}, u32[]{:S(2)}, u32[]{:S(2)}) collective-permute-start(bf16[16,640]{1,0:T(8,128)(2,1)S(1)} %get-tuple-element.87.refs_11_), channel_id=1, source_target_pairs={{0,24},{2,26},{4,28},{6,30},{8,16},{10,18},{12,20},{14,22},{16,8},... | collective-permute-start | bytes 61448 | tf_op jit(solution)/shard_map/ppermute | solution.py:33
  15.5 4.7 %collective-permute-start.5 = (bf16[16,640]{1,0:T(8,128)(2,1)S(1)}, bf16[16,640]{1,0:T(8,128)(2,1)S(1)}, u32[]{:S(2)}, u32[]{:S(2)}) collective-permute-start(bf16[16,640]{1,0:T(8,128)(2,1)S(1)} %get-tuple-element.87.refs_11_), channel_id=1, source_target_pairs={{0,16},{2,18},{4,20},{6,22},{8,24},{10,26},{12,28},{14,30},{16,0},... | collective-permute-start | bytes 61448 | tf_op jit(solution)/shard_map/ppermute | solution.py:33
  17.2 3.8 %collective-permute-start.4 = (bf16[16,640]{1,0:T(8,128)(2,1)S(1)}, bf16[16,640]{1,0:T(8,128)(2,1)S(1)}, u32[]{:S(2)}, u32[]{:S(2)}) collective-permute-start(bf16[16,640]{1,0:T(8,128)(2,1)S(1)} %get-tuple-element.87.refs_11_), channel_id=1, source_target_pairs={{0,8},{2,10},{4,12},{6,14},{8,0},{10,2},{12,4},{14,6},{16,24},{18,... | collective-permute-start | bytes 61448 | tf_op jit(solution)/shard_map/ppermute | solution.py:33
  22.8 9.7 %collective-permute-start.7 = (bf16[544,256]{1,0:T(8,128)(2,1)S(1)}, bf16[544,256]{1,0:T(8,128)(2,1)S(1)}, u32[]{:S(2)}, u32[]{:S(2)}) collective-permute-start(bf16[544,256]{1,0:T(8,128)(2,1)S(1)} %get-tuple-element.89), channel_id=1, source_target_pairs={{0,2},{2,0},{4,6},{6,4},{8,10},{10,8},{12,14},{14,12},{16,18},{18,... | collective-permute-start | bytes 835592 | tf_op jit(solution)/shard_map/ppermute | solution.py:33
  24.5 13.9 %collective-permute-start.8 = (bf16[544,256]{1,0:T(8,128)(2,1)S(1)}, bf16[544,256]{1,0:T(8,128)(2,1)S(1)}, u32[]{:S(2)}, u32[]{:S(2)}) collective-permute-start(bf16[544,256]{1,0:T(8,128)(2,1)S(1)} %get-tuple-element.90), channel_id=1, source_target_pairs={{0,4},{2,6},{4,0},{6,2},{8,12},{10,14},{12,8},{14,10},{16,20},{18,... | collective-permute-start | bytes 835592 | tf_op jit(solution)/shard_map/ppermute | solution.py:33
  26.0 13.5 %collective-permute-start.9 = (bf16[544,256]{1,0:T(8,128)(2,1)S(1)}, bf16[544,256]{1,0:T(8,128)(2,1)S(1)}, u32[]{:S(2)}, u32[]{:S(2)}) collective-permute-start(bf16[544,256]{1,0:T(8,128)(2,1)S(1)} %get-tuple-element.91), channel_id=1, source_target_pairs={{0,6},{2,4},{4,2},{6,0},{8,14},{10,12},{12,10},{14,8},{16,22},{18,... | collective-permute-start | bytes 835592 | tf_op jit(solution)/shard_map/ppermute | solution.py:33
  26.3 8.8 %copy-start.2 = (bf16[256,2560]{1,0:T(8,128)(2,1)S(1)}, bf16[256,2560]{1,0:T(8,128)(2,1)}, u32[]{:S(2)}) copy-start(bf16[256,2560]{1,0:T(8,128)(2,1)} %refs_13_.1) | copy-start | bytes 3932164
  28.6 28.2 %collective-permute-start.14 = (bf16[1056,256]{1,0:T(8,128)(2,1)S(1)}, bf16[1056,256]{1,0:T(8,128)(2,1)S(1)}, u32[]{:S(2)}, u32[]{:S(2)}) collective-permute-start(bf16[1056,256]{1,0:T(8,128)(2,1)S(1)} %get-tuple-element.107), channel_id=1, source_target_pairs={{0,2},{2,0},{4,6},{6,4},{8,10},{10,8},{12,14},{14,12},{16,18},{18,... | collective-permute-start | bytes 1622024 | tf_op jit(solution)/shard_map/ppermute | solution.py:33
  30.4 29.1 %collective-permute-start.15 = (bf16[1056,256]{1,0:T(8,128)(2,1)S(1)}, bf16[1056,256]{1,0:T(8,128)(2,1)S(1)}, u32[]{:S(2)}, u32[]{:S(2)}) collective-permute-start(bf16[1056,256]{1,0:T(8,128)(2,1)S(1)} %get-tuple-element.108), channel_id=1, source_target_pairs={{0,4},{2,6},{4,0},{6,2},{8,12},{10,14},{12,8},{14,10},{16,20},{18,... | collective-permute-start | bytes 1622024 | tf_op jit(solution)/shard_map/ppermute | solution.py:33
  32.4 30.4 %collective-permute-start.16 = (bf16[1056,256]{1,0:T(8,128)(2,1)S(1)}, bf16[1056,256]{1,0:T(8,128)(2,1)S(1)}, u32[]{:S(2)}, u32[]{:S(2)}) collective-permute-start(bf16[1056,256]{1,0:T(8,128)(2,1)S(1)} %get-tuple-element.109), channel_id=1, source_target_pairs={{0,6},{2,4},{4,2},{6,0},{8,14},{10,12},{12,10},{14,8},{16,22},{18,... | collective-permute-start | bytes 1622024 | tf_op jit(solution)/shard_map/ppermute | solution.py:33
  40.2 6.4 %collective-permute-start.10 = (bf16[512,256]{1,0:T(8,128)(2,1)S(1)}, bf16[512,256]{1,0:T(8,128)(2,1)S(1)}, u32[]{:S(2)}, u32[]{:S(2)}) collective-permute-start(bf16[512,256]{1,0:T(8,128)(2,1)S(1)} %get-tuple-element.98), channel_id=1, source_target_pairs={{0,8},{2,10},{4,12},{6,14},{8,0},{10,2},{12,4},{14,6},{16,24},{18,... | collective-permute-start | bytes 786440 | tf_op jit(solution)/shard_map/ppermute | solution.py:33
  41.0 5.7 %collective-permute-start.11 = (bf16[512,256]{1,0:T(8,128)(2,1)S(1)}, bf16[512,256]{1,0:T(8,128)(2,1)S(1)}, u32[]{:S(2)}, u32[]{:S(2)}) collective-permute-start(bf16[512,256]{1,0:T(8,128)(2,1)S(1)} %get-tuple-element.99), channel_id=1, source_target_pairs={{8,16},{10,18},{12,20},{14,22},{16,8},{18,10},{20,12},{22,14},{9,1... | collective-permute-start | bytes 786440 | tf_op jit(solution)/shard_map/ppermute | solution.py:39
  51.5 14.1 %collective-permute-start.12 = (bf16[528,256]{1,0:T(8,128)(2,1)S(1)}, bf16[528,256]{1,0:T(8,128)(2,1)S(1)}, u32[]{:S(2)}, u32[]{:S(2)}) collective-permute-start(bf16[528,256]{1,0:T(8,128)(2,1)S(1)} %get-tuple-element.104), channel_id=1, source_target_pairs={{0,8},{2,10},{4,12},{6,14},{8,0},{10,2},{12,4},{14,6},{16,24},{18,... | collective-permute-start | bytes 811016 | tf_op jit(solution)/shard_map/ppermute | solution.py:33
  56.1 8.9 %collective-permute-start.13 = (bf16[512,256]{1,0:T(8,128)(2,1)S(1)}, bf16[512,256]{1,0:T(8,128)(2,1)S(1)}, u32[]{:S(2)}, u32[]{:S(2)}) collective-permute-start(bf16[512,256]{1,0:T(8,128)(2,1)S(1)} %get-tuple-element.105), channel_id=1, source_target_pairs={{8,16},{10,18},{12,20},{14,22},{16,8},{18,10},{20,12},{22,14},{9,1... | collective-permute-start | bytes 786440 | tf_op jit(solution)/shard_map/ppermute | solution.py:39
  56.8 15.1 %collective-permute-start.22 = (bf16[1056,128]{1,0:T(8,128)(2,1)}, bf16[1056,128]{1,0:T(8,128)(2,1)S(1)}, u32[]{:S(2)}, u32[]{:S(2)}) collective-permute-start(bf16[1056,128]{1,0:T(8,128)(2,1)} %get-tuple-element.121), channel_id=1, source_target_pairs={{0,2},{2,0},{4,6},{6,4},{8,10},{10,8},{12,14},{14,12},{16,18},{18,... | collective-permute-start | bytes 811016 | tf_op jit(solution)/shard_map/ppermute | solution.py:33
  59.5 13.3 %collective-permute-start.23 = (bf16[1056,128]{1,0:T(8,128)(2,1)}, bf16[1056,128]{1,0:T(8,128)(2,1)S(1)}, u32[]{:S(2)}, u32[]{:S(2)}) collective-permute-start(bf16[1056,128]{1,0:T(8,128)(2,1)} %get-tuple-element.122), channel_id=1, source_target_pairs={{0,4},{2,6},{4,0},{6,2},{8,12},{10,14},{12,8},{14,10},{16,20},{18,... | collective-permute-start | bytes 811016 | tf_op jit(solution)/shard_map/ppermute | solution.py:33
  62.8 12.5 %collective-permute-start.24 = (bf16[1056,128]{1,0:T(8,128)(2,1)}, bf16[1056,128]{1,0:T(8,128)(2,1)S(1)}, u32[]{:S(2)}, u32[]{:S(2)}) collective-permute-start(bf16[1056,128]{1,0:T(8,128)(2,1)} %get-tuple-element.123), channel_id=1, source_target_pairs={{0,6},{2,4},{4,2},{6,0},{8,14},{10,12},{12,10},{14,8},{16,22},{18,... | collective-permute-start | bytes 811016 | tf_op jit(solution)/shard_map/ppermute | solution.py:33
  65.0 11.1 %collective-permute-start.20 = (bf16[512,256]{1,0:T(8,128)(2,1)S(1)}, bf16[512,256]{1,0:T(8,128)(2,1)S(1)}, u32[]{:S(2)}, u32[]{:S(2)}) collective-permute-start(bf16[512,256]{1,0:T(8,128)(2,1)S(1)} %get-tuple-element.118), channel_id=1, source_target_pairs={{0,8},{2,10},{4,12},{6,14},{8,0},{10,2},{12,4},{14,6},{16,24},{18,... | collective-permute-start | bytes 786440 | tf_op jit(solution)/shard_map/ppermute | solution.py:33
  65.6 16.1 %collective-permute-start.21 = (bf16[512,256]{1,0:T(8,128)(2,1)S(1)}, bf16[512,256]{1,0:T(8,128)(2,1)S(1)}, u32[]{:S(2)}, u32[]{:S(2)}) collective-permute-start(bf16[512,256]{1,0:T(8,128)(2,1)S(1)} %get-tuple-element.119), channel_id=1, source_target_pairs={{8,16},{10,18},{12,20},{14,22},{16,8},{18,10},{20,12},{22,14},{9,1... | collective-permute-start | bytes 786440 | tf_op jit(solution)/shard_map/ppermute | solution.py:39
  72.0 19.8 %collective-permute-start.17 = (bf16[784,256]{1,0:T(8,128)(2,1)S(1)}, bf16[784,256]{1,0:T(8,128)(2,1)S(1)}, u32[]{:S(2)}, u32[]{:S(2)}) collective-permute-start(bf16[784,256]{1,0:T(8,128)(2,1)S(1)} %get-tuple-element.113), channel_id=1, source_target_pairs={{0,2},{2,0},{4,6},{6,4},{8,10},{10,8},{12,14},{14,12},{16,18},{18,... | collective-permute-start | bytes 1204232 | tf_op jit(solution)/shard_map/ppermute | solution.py:33
  72.9 18.9 %collective-permute-start.18 = (bf16[784,256]{1,0:T(8,128)(2,1)S(1)}, bf16[784,256]{1,0:T(8,128)(2,1)S(1)}, u32[]{:S(2)}, u32[]{:S(2)}) collective-permute-start(bf16[784,256]{1,0:T(8,128)(2,1)S(1)} %get-tuple-element.114), channel_id=1, source_target_pairs={{0,4},{2,6},{4,0},{6,2},{8,12},{10,14},{12,8},{14,10},{16,20},{18,... | collective-permute-start | bytes 1204232 | tf_op jit(solution)/shard_map/ppermute | solution.py:33
  75.2 16.5 %collective-permute-start.19 = (bf16[784,256]{1,0:T(8,128)(2,1)S(1)}, bf16[784,256]{1,0:T(8,128)(2,1)S(1)}, u32[]{:S(2)}, u32[]{:S(2)}) collective-permute-start(bf16[784,256]{1,0:T(8,128)(2,1)S(1)} %get-tuple-element.115), channel_id=1, source_target_pairs={{0,6},{2,4},{4,2},{6,0},{8,14},{10,12},{12,10},{14,8},{16,22},{18,... | collective-permute-start | bytes 1204232 | tf_op jit(solution)/shard_map/ppermute | solution.py:33
  76.1 11.0 %collective-permute-start.27 = (bf16[512,128]{1,0:T(8,128)(2,1)S(1)}, bf16[512,128]{1,0:T(8,128)(2,1)S(1)}, u32[]{:S(2)}, u32[]{:S(2)}) collective-permute-start(bf16[512,128]{1,0:T(8,128)(2,1)S(1)} %get-tuple-element.131), channel_id=1, source_target_pairs={{0,8},{2,10},{4,12},{6,14},{8,0},{10,2},{12,4},{14,6},{16,24},{18,... | collective-permute-start | bytes 393224 | tf_op jit(solution)/shard_map/ppermute | solution.py:33
  81.7 6.8 %collective-permute-start.28 = (bf16[512,128]{1,0:T(8,128)(2,1)S(1)}, bf16[512,128]{1,0:T(8,128)(2,1)S(1)}, u32[]{:S(2)}, u32[]{:S(2)}) collective-permute-start(bf16[512,128]{1,0:T(8,128)(2,1)S(1)} %get-tuple-element.132), channel_id=1, source_target_pairs={{8,16},{10,18},{12,20},{14,22},{16,8},{18,10},{20,12},{22,14},{9,1... | collective-permute-start | bytes 393224 | tf_op jit(solution)/shard_map/ppermute | solution.py:39
  87.2 6.5 %collective-permute-start.25 = (bf16[528,256]{1,0:T(8,128)(2,1)S(1)}, bf16[528,256]{1,0:T(8,128)(2,1)S(1)}, u32[]{:S(2)}, u32[]{:S(2)}) collective-permute-start(bf16[528,256]{1,0:T(8,128)(2,1)S(1)} %get-tuple-element.129), channel_id=1, source_target_pairs={{0,8},{2,10},{4,12},{6,14},{8,0},{10,2},{12,4},{14,6},{16,24},{18,... | collective-permute-start | bytes 811016 | tf_op jit(solution)/shard_map/ppermute | solution.py:33
  88.5 4.2 %collective-permute-start.26 = (bf16[512,256]{1,0:T(8,128)(2,1)S(1)}, bf16[512,256]{1,0:T(8,128)(2,1)S(1)}, u32[]{:S(2)}, u32[]{:S(2)}) collective-permute-start(bf16[512,256]{1,0:T(8,128)(2,1)S(1)} %get-tuple-element.130), channel_id=1, source_target_pairs={{8,16},{10,18},{12,20},{14,22},{16,8},{18,10},{20,12},{22,14},{9,1... | collective-permute-start | bytes 786440 | tf_op jit(solution)/shard_map/ppermute | solution.py:39
  95.3 22.2 %collective-permute-start.29 = (bf16[784,256]{1,0:T(8,128)(2,1)S(1)}, bf16[784,256]{1,0:T(8,128)(2,1)S(1)}, u32[]{:S(2)}, u32[]{:S(2)}) collective-permute-start(bf16[784,256]{1,0:T(8,128)(2,1)S(1)} %get-tuple-element.135), channel_id=1, source_target_pairs={{0,2},{2,0},{4,6},{6,4},{8,10},{10,8},{12,14},{14,12},{16,18},{18,... | collective-permute-start | bytes 1204232 | tf_op jit(solution)/shard_map/ppermute | solution.py:33
  96.0 23.0 %collective-permute-start.30 = (bf16[784,256]{1,0:T(8,128)(2,1)S(1)}, bf16[784,256]{1,0:T(8,128)(2,1)S(1)}, u32[]{:S(2)}, u32[]{:S(2)}) collective-permute-start(bf16[784,256]{1,0:T(8,128)(2,1)S(1)} %get-tuple-element.136), channel_id=1, source_target_pairs={{0,4},{2,6},{4,0},{6,2},{8,12},{10,14},{12,8},{14,10},{16,20},{18,... | collective-permute-start | bytes 1204232 | tf_op jit(solution)/shard_map/ppermute | solution.py:33
  97.5 21.5 %collective-permute-start.31 = (bf16[784,256]{1,0:T(8,128)(2,1)S(1)}, bf16[784,256]{1,0:T(8,128)(2,1)S(1)}, u32[]{:S(2)}, u32[]{:S(2)}) collective-permute-start(bf16[784,256]{1,0:T(8,128)(2,1)S(1)} %get-tuple-element.137), channel_id=1, source_target_pairs={{0,6},{2,4},{4,2},{6,0},{8,14},{10,12},{12,10},{14,8},{16,22},{18,... | collective-permute-start | bytes 1204232 | tf_op jit(solution)/shard_map/ppermute | solution.py:33
  102.2 7.0 %collective-permute-start.34 = (bf16[16,640]{1,0:T(8,128)(2,1)S(1)}, bf16[16,640]{1,0:T(8,128)(2,1)S(1)}, u32[]{:S(2)}, u32[]{:S(2)}) collective-permute-start(bf16[16,640]{1,0:T(8,128)(2,1)S(1)} %get-tuple-element.152), channel_id=1, source_target_pairs={{0,16},{2,18},{4,20},{6,22},{8,24},{10,26},{12,28},{14,30},{16,0},... | collective-permute-start | bytes 61448 | tf_op jit(solution)/shard_map/ppermute | solution.py:33
  106.8 5.6 %collective-permute-start.35 = (bf16[16,640]{1,0:T(8,128)(2,1)S(1)}, bf16[16,640]{1,0:T(8,128)(2,1)S(1)}, u32[]{:S(2)}, u32[]{:S(2)}) collective-permute-start(bf16[16,640]{1,0:T(8,128)(2,1)S(1)} %get-tuple-element.153), channel_id=1, source_target_pairs={{0,24},{2,26},{4,28},{6,30},{8,16},{10,18},{12,20},{14,22},{16,8},... | collective-permute-start | bytes 61448 | tf_op jit(solution)/shard_map/ppermute | solution.py:33
  109.1 5.3 %collective-permute-start.32 = (bf16[528,128]{1,0:T(8,128)(2,1)S(1)}, bf16[528,128]{1,0:T(8,128)(2,1)S(1)}, u32[]{:S(2)}, u32[]{:S(2)}) collective-permute-start(bf16[528,128]{1,0:T(8,128)(2,1)S(1)} %get-tuple-element.144), channel_id=1, source_target_pairs={{0,8},{2,10},{4,12},{6,14},{8,0},{10,2},{12,4},{14,6},{16,24},{18,... | collective-permute-start | bytes 405512 | tf_op jit(solution)/shard_map/ppermute | solution.py:33
  112.4 0.7 collective-permute-start.33
  115.4 6.0 %collective-permute-start.36 = (bf16[864,128]{1,0:T(8,128)(2,1)S(1)}, bf16[864,128]{1,0:T(8,128)(2,1)S(1)}, u32[]{:S(2)}, u32[]{:S(2)}) collective-permute-start(bf16[864,128]{1,0:T(8,128)(2,1)S(1)} %get-tuple-element.155), channel_id=1, source_target_pairs={{0,2},{2,0},{4,6},{6,4},{8,10},{10,8},{12,14},{14,12},{16,18},{18,... | collective-permute-start | bytes 663560 | tf_op jit(solution)/shard_map/ppermute | solution.py:33
  116.0 7.4 %collective-permute-start.37 = (bf16[864,128]{1,0:T(8,128)(2,1)S(1)}, bf16[864,128]{1,0:T(8,128)(2,1)S(1)}, u32[]{:S(2)}, u32[]{:S(2)}) collective-permute-start(bf16[864,128]{1,0:T(8,128)(2,1)S(1)} %get-tuple-element.156), channel_id=1, source_target_pairs={{0,4},{2,6},{4,0},{6,2},{8,12},{10,14},{12,8},{14,10},{16,20},{18,... | collective-permute-start | bytes 663560 | tf_op jit(solution)/shard_map/ppermute | solution.py:33
  117.5 7.2 %collective-permute-start.38 = (bf16[864,128]{1,0:T(8,128)(2,1)S(1)}, bf16[864,128]{1,0:T(8,128)(2,1)S(1)}, u32[]{:S(2)}, u32[]{:S(2)}) collective-permute-start(bf16[864,128]{1,0:T(8,128)(2,1)S(1)} %get-tuple-element.157), channel_id=1, source_target_pairs={{0,6},{2,4},{4,2},{6,0},{8,14},{10,12},{12,10},{14,8},{16,22},{18,... | collective-permute-start | bytes 663560 | tf_op jit(solution)/shard_map/ppermute | solution.py:33
  126.4 1.4 %collective-permute-start.39 = (f32[256,128]{1,0:T(8,128)S(1)}, f32[256,128]{1,0:T(8,128)S(1)}, u32[]{:S(2)}, u32[]{:S(2)}) collective-permute-start(f32[256,128]{1,0:T(8,128)S(1)} %get-tuple-element.159.dot_ref), channel_id=1, source_target_pairs={{0,1},{1,0},{2,3},{3,2},{4,5},{5,4},{6,7},{7,6},{8,9},{9,8},{10,11... | collective-permute-start | bytes 393224 | tf_op jit(solution)/shard_map/ppermute | solution.py:678
  (3 other events, 3.3 us)

commit v6 on v5

--- a/solution.py
+++ b/solution.py
@@ -54,26 +54,30 @@
     return run
 
 
-def heads_call(kernel, count, place, inputs, outputs, after=(), scratch=(), name=None):
-    widths = [w for _, w in inputs] + [w for _, w in outputs]
+def heads_call(
+    kernel, count, place, inputs, outputs, after=(), scratch=(), aliases={}, name=None
+):
+    lanes = [(entry[1], entry[2] if len(entry) > 2 else 0) for entry in (*inputs, *outputs)]
 
     def run(place_ref, *refs):
         refs = refs[: len(inputs)] + refs[len(inputs) + len(after) :]
         for h in range(count):
             views = [
-                ref.at[:, h * w : (h + 1) * w] if w else ref for ref, w in zip(refs, widths)
+                ref.at[:, at + h * w : at + (h + 1) * w] if w else ref
+                for ref, (w, at) in zip(refs, lanes)
             ]
-            kernel(h, place_ref, *views, *refs[len(widths) :])
+            kernel(h, place_ref, *views, *refs[len(lanes) :])
 
     vmem = pl.BlockSpec(memory_space=pltpu.VMEM)
     return pl.pallas_call(
         run,
-        out_shape=[shape for shape, _ in outputs],
+        out_shape=[entry[0] for entry in outputs],
         in_specs=[pl.BlockSpec(memory_space=pltpu.SMEM)]
         + [vmem] * len(inputs)
         + [ANY] * len(after),
         out_specs=[vmem] * len(outputs),
         scratch_shapes=scratch,
+        input_output_aliases={1 + i: o for i, o in aliases.items()},
         compiler_params=params(),
         cost_estimate=cost(1, 1),
         name=name,
@@ -166,6 +170,36 @@
         cost_estimate=cost(1, 1),
         name="global_rows",
     )(place, ids, own, other, key_raw, values, key_gain)
+
+
+def add_globals(me, d, first, parts, out):
+    parts = jnp.concatenate([ref[...] for ref in parts], axis=0)
+    row = lax.broadcasted_iota(jnp.int32, (16, 16 * GROUP), 0)
+    col = lax.broadcasted_iota(jnp.int32, (16, 16 * GROUP), 1)
+    spot = col % 16 - 4 * (me ^ d)
+    hot = (spot >= 0) & (spot < 4)
+    hot = hot & (row == 2 * (col // 16) + spot % 2 + 8 * (spot // 2))
+    hot = hot.astype(F32).astype(BF16)
+    chosen = parts[:, first * HEAD_DIM : first * HEAD_DIM + out.shape[1]]
+    out[out.shape[0] - 16 :] = contract(hot, chosen, ((1,), (0,))).astype(BF16)
+
+
+def append_kernel(first, head, place_ref, *refs):
+    for d, out in enumerate(refs[2 * GROUP :]):
+        add_globals(place_ref[0], d, first, refs[GROUP : 2 * GROUP], out)
+
+
+def append(place, sent, parts, first, after):
+    return heads_call(
+        functools.partial(append_kernel, first),
+        1,
+        place,
+        [(x, 0) for x in (*sent, *parts)],
+        [(jax.ShapeDtypeStruct(x.shape, BF16), 0) for x in sent],
+        after,
+        aliases={d: d for d in range(GROUP)},
+        name="append",
+    )
 
 
 def pack_kernel(first, whole, place_ref, tiles_ref, readers_ref, own_ref, other_ref, *refs):
@@ -185,20 +219,13 @@
             facts = jnp.where(chosen, live, facts)
     facts = facts.astype(F32).astype(BF16)
     key_ref, value_ref, query_ref, grad_ref, key_gain, query_gain = refs[:6]
-    *outs, token = refs[6 + GROUP :]
+    *outs, token = refs[-GROUP - 1 :]
     token[...] = jnp.zeros((8, HEAD_DIM), F32)
-    parts = jnp.concatenate([ref[...] for ref in refs[6 : 6 + GROUP]], axis=0)
-    row = lax.broadcasted_iota(jnp.int32, (16, 16 * GROUP), 0)
-    col = lax.broadcasted_iota(jnp.int32, (16, 16 * GROUP), 1)
     each = key_ref.shape[1] // HEAD_DIM // GROUP
     for d, out in enumerate(outs):
-        spot = col % 16 - 4 * (me ^ d)
-        hot = (spot >= 0) & (spot < 4)
-        hot = hot & (row == 2 * (col // 16) + spot % 2 + 8 * (spot // 2))
-        hot = hot.astype(F32).astype(BF16)
-        chosen = parts[:, first * HEAD_DIM : first * HEAD_DIM + out.shape[1]]
         top = 2 * rows if whole else 0
-        out[top + 2 * rows + 16 :] = contract(hot, chosen, ((1,), (0,))).astype(BF16)
+        if whole:
+            add_globals(me, d, first, refs[6 : 6 + GROUP], out)
         for h in range(out.shape[1] // HEAD_DIM):
             at = pl.multiple_of(((me ^ d) * each + first + h) * HEAD_DIM, HEAD_DIM)
             here = pl.ds(at, HEAD_DIM)
@@ -224,10 +251,10 @@
     out_rows = (4 if whole else 2) * rows + FACTS
     kernel = functools.partial(pack_kernel, first, whole)
     return pl.pallas_call(
-        behind(kernel, 11 + GROUP, len(after)),
+        behind(kernel, 11 + len(parts), len(after)),
         out_shape=[jax.ShapeDtypeStruct((out_rows, count * HEAD_DIM), BF16)] * GROUP
         + [jax.ShapeDtypeStruct((8, HEAD_DIM), F32)],
-        in_specs=[smem] * 3 + [vmem] * (8 + GROUP) + [ANY] * len(after),
+        in_specs=[smem] * 3 + [vmem] * (8 + len(parts)) + [ANY] * len(after),
         out_specs=[vmem] * (GROUP + 1),
         compiler_params=params(),
         cost_estimate=cost(1, 1),
@@ -308,7 +335,8 @@
 def attend_kernel(outer, inputs, head, place_ref, *refs):
     blocks, refs = refs[:inputs], refs[inputs:]
     if outer:
-        near, far, g_in, dq_out, acc_out, g_out, near_out, far_out, mid_out, end_out = refs[:10]
+        near, far, g_in = refs[:3]
+        dq_out, acc_out, g_out, near_out, far_out, mid_out, end_out = refs[-14:-7]
     else:
         dq_out, acc_out, g_out = refs[:3]
     pair, weights, sums, raw_g, pair_g, sums_g, facts_at = refs[-7:]
@@ -403,7 +431,7 @@
             out[rows : 2 * rows] = sums[pl.ds(at, rows), vals].astype(BF16)
 
 
-def attend(place, blocks, halo, inner_g, after):
+def attend(place, blocks, halo, inner_g, fars, first, each, after):
     width = blocks[0].shape[1]
     rows = block_rows(blocks)
     wide = 2 * HEAD_DIM
@@ -412,14 +440,17 @@
     near = jax.ShapeDtypeStruct((2 * rows + 16, width), BF16)
     outs = [(half, HEAD_DIM), (jax.ShapeDtypeStruct((GROUP * rows, 2 * width), BF16), wide)]
     if halo:
-        outs += [(x, HEAD_DIM) for x in (few, near, half, few, few)]
+        outs += [(x, HEAD_DIM) for x in (few, near, half)]
+        outs += [(jax.ShapeDtypeStruct((16, each * HEAD_DIM), BF16), HEAD_DIM, first * HEAD_DIM)] * 2
     else:
         outs += [(jax.ShapeDtypeStruct((8 * GROUP, 2 * width), F32), wide)]
     return heads_call(
         functools.partial(attend_kernel, len(halo) > 0, len(blocks)),
         width // HEAD_DIM,
         place,
-        [(x, HEAD_DIM) for x in (*blocks, *halo)] + [(x, wide) for x in inner_g],
+        [(x, HEAD_DIM) for x in (*blocks, *halo)]
+        + [(x, wide) for x in inner_g]
+        + [(x, 0) for x in fars],
         outs,
         after,
         [
@@ -431,6 +462,7 @@
             pltpu.VMEM((8 * GROUP, wide), F32),
             pltpu.VMEM((GROUP, 16, HEAD_DIM), F32),
         ],
+        {len(blocks) + 3 + i: 5 + i for i in range(len(fars))},
         name="outer" if halo else "inner",
     )
 
@@ -492,28 +524,6 @@
         [(home, HEAD_DIM)] * GROUP + [(jax.ShapeDtypeStruct((8, HEAD_DIM), F32), 0)],
         after,
         name="settle",
-    )
-
-
-def join_kernel(head, place_ref, *refs):
-    *parts, mid, end = refs
-    half = len(parts) // 2
-    for out, some in ((mid, parts[:half]), (end, parts[half:])):
-        first = 0
-        for part in some:
-            out[:, first : first + part.shape[1]] = part[...]
-            first += part.shape[1]
-
-
-def join(place, mids, ends):
-    shape = jax.ShapeDtypeStruct((16, sum(x.shape[1] for x in mids)), BF16)
-    return heads_call(
-        join_kernel,
-        1,
-        place,
-        [(x, 0) for x in (*mids, *ends)],
-        [(shape, 0), (shape, 0)],
-        name="join",
     )
 
 
@@ -697,16 +707,20 @@
         return [sent[0]] + [swapped(sent[d], d) for d in range(1, GROUP)]
 
     raw = spread(pack_raw(place, values, out_grad, 0, CHUNKS[0]))
-    token = tuple(raw[1:])
+    token = (raw_rows,)
     for first, count in zip(firsts, CHUNKS):
         *sent, last = pack(
-            place, key_tiles, readers, own, other, arrays, gains, parts, first, count, first > 0,
-            token,
-        )
+            place, key_tiles, readers, own, other, arrays, gains, parts if first else (), first,
+            count, first > 0, token,
+        )
+        if first == 0:
+            sent = append(place, sent, parts, first, tuple(raw[1:]))
+            last = sent[0]
         token = (last,)
         packed.append((raw if first == 0 else []) + spread(sent))
     edge, inner, outer, back, home, dot = ({} for _ in range(6))
     fars = []
+    each = query_raw.shape[1] // HEAD_DIM // GROUP
 
     def begin(c, token):
         near, far, last = edges(place, packed[c], token)
@@ -714,18 +728,18 @@
         return (last,)
 
     def inside(c, token):
-        inner[c] = attend(place, packed[c], (), (), token)
+        inner[c] = attend(place, packed[c], (), (), (), firsts[c], each, token)
         return (inner[c][2],)
 
     def outside(c, token):
-        results = attend(place, packed[c], edge[c], (inner[c][2],), token)
-        outer[c], own_g, near, far, mid, last = results[:2], *results[2:]
-        fars.append((mid, last))
+        results = attend(
+            place, packed[c], edge[c], (inner[c][2],), tuple(fars), firsts[c], each, token
+        )
+        outer[c], own_g, near, far = results[:2], *results[2:5]
+        fars[:] = results[5:]
         more = ()
         if c == chunks - 1:
-            mids, lasts = zip(*fars)
-            mid, last = join(place, mids, lasts)
-            more = (swapped(mid, 8), swapped(last, 12))
+            more = (swapped(fars[0], 8), swapped(fars[1], 12))
         back[c] = (own_g, swapped(near, 4), swapped_edges(far), more)
         return (own_g,)
 

time: 134 us -> 133 us (level)
  waiting for transfers between devices: 20.6 us -> 17.9 us
    ppermute x32, waiting for transfers between devices: 18 us -> 15.3 us  [swapped(): return lax.ppermute(shard, 'ctx', [(i, i ^ bit) for i in range(count)])]
  transfers between devices with their start and end apart: 40 -> 40, of which waited for: 17 -> 16; matrix products, arithmetic and copies ran while one was open for 0% -> 0% of each run, Pallas kernels for 28% -> 30%
where the time goes in v6:
time: 133 us; the launch traced here: 131 us
  starting transfers between devices  61 us (46%)
  Pallas kernels  48.2 us (36%)
  waiting for transfers between devices  17.9 us (13%)
  local copies, waits for them, and re-layouts  2.7 us (2%)
    ppermute x32, starting transfers between devices, swapped(): return lax.ppermute(shard, 'ctx', [(i, i ^ bit) for i in range(count)])  56.9 us
    pallas_call x16, Pallas kernels, heads_call(): pl.pallas_call(run, out_shape=[entry[0] for entry in outputs], in_specs=[...  32.7 us
    ppermute x32, waiting for transfers between devices, swapped(): return lax.ppermute(shard, 'ctx', [(i, i ^ bit) for i in range(count)])  15.3 us
    pallas_call x3, Pallas kernels, pack(): pl.pallas_call(behind(kernel, 11 + len(parts), len(after)), out_shape=[ja...  7.71 us
    pallas_call x1, Pallas kernels, finish(): pl.pallas_call(functools.partial(finish_kernel, chunks), out_shape=[jax.S...  4.73 us
    ppermute x6, starting transfers between devices, swapped_edges(): return lax.ppermute(shard, 'ctx', pairs)  3.98 us
    unnamed x22, local copies, waits for them, and re-layouts  2.68 us
  transfers between devices with their start and end apart: 40, of which 16 were waited for; matrix products, arithmetic and copies ran while one was open for 0% of the time, Pallas kernels for 30%

profile of v6, /device:TPU:0, one launch (start us, length us, event | category | flops | bytes accessed | tf_op | source)
XLA Modules:
  0.0 131.0 jit_solution(17237913768167358110)
XLA Ops:
  0.7 1.3 %copy-done.3 = bf16[256,2560]{1,0:T(8,128)(2,1)S(1)} copy-done((bf16[256,2560]{1,0:T(8,128)(2,1)S(1)}, bf16[256,2560]{1,0:T(8,128)(2,1)}, u32[]{:S(2)}) %copy-start.3) | copy-done | bytes 1310744
  2.0 1.3 %copy-done.5 = bf16[256,2560]{1,0:T(8,128)(2,1)S(1)} copy-done((bf16[256,2560]{1,0:T(8,128)(2,1)S(1)}, bf16[256,2560]{1,0:T(8,128)(2,1)}, u32[]{:S(2)}) %copy-start.5) | copy-done | bytes 1310744
  4.0 3.0 %collective-permute-start.1 = (bf16[512,256]{1,0:T(8,128)(2,1)S(1)}, bf16[512,256]{1,0:T(8,128)(2,1)S(1)}, u32[]{:S(2)}, u32[]{:S(2)}) collective-permute-start(bf16[512,256]{1,0:T(8,128)(2,1)S(1)} %get-tuple-element.85), channel_id=1, source_target_pairs={{0,2},{2,0},{4,6},{6,4},{8,10},{10,8},{12,14},{14,12},{16,18},{18,... | collective-permute-start | bytes 786440 | tf_op jit(solution)/shard_map/ppermute | solution.py:33
  7.0 1.5 %collective-permute-start.2 = (bf16[512,256]{1,0:T(8,128)(2,1)S(1)}, bf16[512,256]{1,0:T(8,128)(2,1)S(1)}, u32[]{:S(2)}, u32[]{:S(2)}) collective-permute-start(bf16[512,256]{1,0:T(8,128)(2,1)S(1)} %get-tuple-element.86), channel_id=1, source_target_pairs={{0,4},{2,6},{4,0},{6,2},{8,12},{10,14},{12,8},{14,10},{16,20},{18,... | collective-permute-start | bytes 786440 | tf_op jit(solution)/shard_map/ppermute | solution.py:33
  9.3 1.3 collective-permute-done.other_ref.refs_4_
  11.4 4.1 %collective-permute-start.6 = (bf16[16,640]{1,0:T(8,128)(2,1)S(1)}, bf16[16,640]{1,0:T(8,128)(2,1)S(1)}, u32[]{:S(2)}, u32[]{:S(2)}) collective-permute-start(bf16[16,640]{1,0:T(8,128)(2,1)S(1)} %get-tuple-element.92.refs_4_.refs_11_), channel_id=1, source_target_pairs={{0,24},{2,26},{4,28},{6,30},{8,16},{10,18},{12,20},{14,22},{16,8},... | collective-permute-start | bytes 61448 | tf_op jit(solution)/shard_map/ppermute | solution.py:33
  15.5 1.8 %collective-permute-done.6.refs_7_.refs_14_ = bf16[16,640]{1,0:T(8,128)(2,1)S(1)} collective-permute-done((bf16[16,640]{1,0:T(8,128)(2,1)S(1)}, bf16[16,640]{1,0:T(8,128)(2,1)S(1)}, u32[]{:S(2)}, u32[]{:S(2)}) %collective-permute-start.6) | collective-permute-done | bytes 20512 | tf_op jit(solution)/shard_map/ppermute | solution.py:33
  17.5 2.3 %pack.3 = (bf16[544,256]{1,0:T(8,128)(2,1)S(1)}, bf16[544,256]{1,0:T(8,128)(2,1)S(1)}, bf16[544,256]{1,0:T(8,128)(2,1)S(1)}, bf16[544,256]{1,0:T(8,128)(2,1)S(1)}, f32[8,128]{1,0:T(8,128)}) custom-call(s32[2]{0:T(128)S(1)} %pad_add_fusion.place_ref.refs_0_, s32[2,4]{1,0:T(2,128)S(1)} %copy-done.6, s32[1,16]{1,0:T(1,128)S(1)} %copy-done.7, ...), custom_call_target="tpu_custom_call" | custom-call | flops 1 | bytes 1 | tf_op jit(solution)/shard_map/pack/pallas_call | solution.py:253
  21.7 1.8 %collective-permute-start.7 = (bf16[544,256]{1,0:T(8,128)(2,1)S(1)}, bf16[544,256]{1,0:T(8,128)(2,1)S(1)}, u32[]{:S(2)}, u32[]{:S(2)}) collective-permute-start(bf16[544,256]{1,0:T(8,128)(2,1)S(1)} %get-tuple-element.94), channel_id=1, source_target_pairs={{0,2},{2,0},{4,6},{6,4},{8,10},{10,8},{12,14},{14,12},{16,18},{18,... | collective-permute-start | bytes 835592 | tf_op jit(solution)/shard_map/ppermute | solution.py:33
  23.5 1.5 %collective-permute-start.8 = (bf16[544,256]{1,0:T(8,128)(2,1)S(1)}, bf16[544,256]{1,0:T(8,128)(2,1)S(1)}, u32[]{:S(2)}, u32[]{:S(2)}) collective-permute-start(bf16[544,256]{1,0:T(8,128)(2,1)S(1)} %get-tuple-element.95), channel_id=1, source_target_pairs={{0,4},{2,6},{4,0},{6,2},{8,12},{10,14},{12,8},{14,10},{16,20},{18,... | collective-permute-start | bytes 835592 | tf_op jit(solution)/shard_map/ppermute | solution.py:33
  25.3 3.1 %pack.4 = (bf16[1056,256]{1,0:T(8,128)(2,1)S(1)}, bf16[1056,256]{1,0:T(8,128)(2,1)}, bf16[1056,256]{1,0:T(8,128)(2,1)S(1)}, bf16[1056,256]{1,0:T(8,128)(2,1)S(1)}, f32[8,128]{1,0:T(8,128)S(1)}) custom-call(s32[2]{0:T(128)S(1)} %pad_add_fusion.place_ref.refs_0_, s32[2,4]{1,0:T(2,128)S(1)} %copy-done.6, s32[1,16]{1,0:T(1,128)S(1)} %copy-done.7, ...), custom_call_target="tpu_custom_call" | custom-call | flops 1 | bytes 1 | tf_op jit(solution)/shard_map/pack/pallas_call | solution.py:253
  28.4 1.7 %collective-permute-start.14 = (bf16[1056,256]{1,0:T(8,128)(2,1)}, bf16[1056,256]{1,0:T(8,128)(2,1)S(1)}, u32[]{:S(2)}, u32[]{:S(2)}) collective-permute-start(bf16[1056,256]{1,0:T(8,128)(2,1)} %get-tuple-element.111), channel_id=1, source_target_pairs={{0,2},{2,0},{4,6},{6,4},{8,10},{10,8},{12,14},{14,12},{16,18},{18,... | collective-permute-start | bytes 1622024 | tf_op jit(solution)/shard_map/ppermute | solution.py:33
  30.1 1.5 %collective-permute-start.15 = (bf16[1056,256]{1,0:T(8,128)(2,1)S(1)}, bf16[1056,256]{1,0:T(8,128)(2,1)S(1)}, u32[]{:S(2)}, u32[]{:S(2)}) collective-permute-start(bf16[1056,256]{1,0:T(8,128)(2,1)S(1)} %get-tuple-element.112), channel_id=1, source_target_pairs={{0,4},{2,6},{4,0},{6,2},{8,12},{10,14},{12,8},{14,10},{16,20},{18,... | collective-permute-start | bytes 1622024 | tf_op jit(solution)/shard_map/ppermute | solution.py:33
  31.6 2.4 %collective-permute-start.16 = (bf16[1056,256]{1,0:T(8,128)(2,1)S(1)}, bf16[1056,256]{1,0:T(8,128)(2,1)S(1)}, u32[]{:S(2)}, u32[]{:S(2)}) collective-permute-start(bf16[1056,256]{1,0:T(8,128)(2,1)S(1)} %get-tuple-element.113), channel_id=1, source_target_pairs={{0,6},{2,4},{4,2},{6,0},{8,14},{10,12},{12,10},{14,8},{16,22},{18,... | collective-permute-start | bytes 1622024 | tf_op jit(solution)/shard_map/ppermute | solution.py:33
  34.0 2.3 %pack.5 = (bf16[1056,128]{1,0:T(8,128)(2,1)S(1)}, bf16[1056,128]{1,0:T(8,128)(2,1)}, bf16[1056,128]{1,0:T(8,128)(2,1)S(1)}, bf16[1056,128]{1,0:T(8,128)(2,1)S(1)}, f32[8,128]{1,0:T(8,128)S(1)}) custom-call(s32[2]{0:T(128)S(1)} %pad_add_fusion.place_ref.refs_0_, s32[2,4]{1,0:T(2,128)S(1)} %copy-done.6, s32[1,16]{1,0:T(1,128)S(1)} %copy-done.7, ...), custom_call_target="tpu_custom_call" | custom-call | flops 1 | bytes 1 | tf_op jit(solution)/shard_map/pack/pallas_call | solution.py:253
  36.8 1.7 %collective-permute-done.9.refs_7_ = bf16[544,256]{1,0:T(8,128)(2,1)S(1)} collective-permute-done((bf16[544,256]{1,0:T(8,128)(2,1)S(1)}, bf16[544,256]{1,0:T(8,128)(2,1)S(1)}, u32[]{:S(2)}, u32[]{:S(2)}) %collective-permute-start.9) | collective-permute-done | bytes 278560 | tf_op jit(solution)/shard_map/ppermute | solution.py:33
  40.6 4.3 %inner.3 = (bf16[512,256]{1,0:T(8,128)(2,1)S(1)}, bf16[1024,512]{1,0:T(8,128)(2,1)S(1)}, f32[32,512]{1,0:T(8,128)S(1)}) custom-call(s32[2]{0:T(128)S(1)} %pad_add_fusion.place_ref.refs_0_, bf16[512,256]{1,0:T(8,128)(2,1)S(1)} %get-tuple-element.84.refs_0_, bf16[512,256]{1,0:T(8,128)(2,1)S(1)} %collective-permute-done.1.refs_8_.refs_1_, ...), custom_call_target="tpu_custom_call" | custom-call | flops 1 | bytes 1 | tf_op jit(solution)/shard_map/inner/pallas_call | solution.py:72
  45.6 4.8 %outer.3 = (bf16[512,256]{1,0:T(8,128)(2,1)S(1)}, bf16[1024,512]{1,0:T(8,128)(2,1)S(1)}, bf16[16,256]{1,0:T(8,128)(2,1)S(1)}, bf16[528,256]{1,0:T(8,128)(2,1)S(1...) custom-call(s32[2]{0:T(128)S(1)} %pad_add_fusion.place_ref.refs_0_, ...), custom_call_target="tpu_custom_call" | custom-call | flops 1 | bytes 1 | tf_op jit(solution)/shard_map/outer/pallas_call | solution.py:72
  50.4 4.7 %collective-permute-start.12 = (bf16[528,256]{1,0:T(8,128)(2,1)S(1)}, bf16[528,256]{1,0:T(8,128)(2,1)S(1)}, u32[]{:S(2)}, u32[]{:S(2)}) collective-permute-start(bf16[528,256]{1,0:T(8,128)(2,1)S(1)} %get-tuple-element.108), channel_id=1, source_target_pairs={{0,8},{2,10},{4,12},{6,14},{8,0},{10,2},{12,4},{14,6},{16,24},{18,... | collective-permute-start | bytes 811016 | tf_op jit(solution)/shard_map/ppermute | solution.py:33
  55.8 1.6 %collective-permute-start.22 = (bf16[1056,128]{1,0:T(8,128)(2,1)}, bf16[1056,128]{1,0:T(8,128)(2,1)S(1)}, u32[]{:S(2)}, u32[]{:S(2)}) collective-permute-start(bf16[1056,128]{1,0:T(8,128)(2,1)} %get-tuple-element.127), channel_id=1, source_target_pairs={{0,2},{2,0},{4,6},{6,4},{8,10},{10,8},{12,14},{14,12},{16,18},{18,... | collective-permute-start | bytes 811016 | tf_op jit(solution)/shard_map/ppermute | solution.py:33
  57.3 1.2 collective-permute-done.15.refs_2_
  58.5 3.0 %collective-permute-start.23 = (bf16[1056,128]{1,0:T(8,128)(2,1)S(1)}, bf16[1056,128]{1,0:T(8,128)(2,1)S(1)}, u32[]{:S(2)}, u32[]{:S(2)}) collective-permute-start(bf16[1056,128]{1,0:T(8,128)(2,1)S(1)} %get-tuple-element.128), channel_id=1, source_target_pairs={{0,4},{2,6},{4,0},{6,2},{8,12},{10,14},{12,8},{14,10},{16,20},{18,... | collective-permute-start | bytes 811016 | tf_op jit(solution)/shard_map/ppermute | solution.py:33
  61.7 1.4 %collective-permute-start.24 = (bf16[1056,128]{1,0:T(8,128)(2,1)S(1)}, bf16[1056,128]{1,0:T(8,128)(2,1)S(1)}, u32[]{:S(2)}, u32[]{:S(2)}) collective-permute-start(bf16[1056,128]{1,0:T(8,128)(2,1)S(1)} %get-tuple-element.129), channel_id=1, source_target_pairs={{0,6},{2,4},{4,2},{6,0},{8,14},{10,12},{12,10},{14,8},{16,22},{18,... | collective-permute-start | bytes 811016 | tf_op jit(solution)/shard_map/ppermute | solution.py:33
  65.3 4.3 %inner.4 = (bf16[512,256]{1,0:T(8,128)(2,1)S(1)}, bf16[1024,512]{1,0:T(8,128)(2,1)S(1)}, f32[32,512]{1,0:T(8,128)S(1)}) custom-call(s32[2]{0:T(128)S(1)} %pad_add_fusion.place_ref.refs_0_, bf16[1056,256]{1,0:T(8,128)(2,1)S(1)} %get-tuple-element.110.refs_0_, bf16[1056,256]{1,0:T(8,128)(2,1)S(1)} %collective-permute-done.14.refs_1_, ...), custom_call_target="tpu_custom_call" | custom-call | flops 1 | bytes 1 | tf_op jit(solution)/shard_map/inner/pallas_call | solution.py:72
  69.6 1.4 %settle.3 = (bf16[784,256]{1,0:T(8,128)(2,1)S(1)}, bf16[784,256]{1,0:T(8,128)(2,1)S(1)}, bf16[784,256]{1,0:T(8,128)(2,1)S(1)}, bf16[784,256]{1,0:T(8,128)(2,1)S(1)}, f32[8,128]{1,0:T(8,128)S(1)}) custom-call(s32[2]{0:T(128)S(1)} %pad_add_fusion.place_ref.refs_0_, bf16[512,256]{1,0:T(8,128)(2,1)S(1)} %get-tuple-element.100.refs_0_, ...), custom_call_target="tpu_custom_call" | custom-call | flops 1 | bytes 1 | tf_op jit(solution)/shard_map/settle/pallas_call | solution.py:72
  71.8 2.2 %collective-permute-start.18 = (bf16[784,256]{1,0:T(8,128)(2,1)S(1)}, bf16[784,256]{1,0:T(8,128)(2,1)S(1)}, u32[]{:S(2)}, u32[]{:S(2)}) collective-permute-start(bf16[784,256]{1,0:T(8,128)(2,1)S(1)} %get-tuple-element.118), channel_id=1, source_target_pairs={{0,4},{2,6},{4,0},{6,2},{8,12},{10,14},{12,8},{14,10},{16,20},{18,... | collective-permute-start | bytes 1204232 | tf_op jit(solution)/shard_map/ppermute | solution.py:33
  75.2 5.4 %collective-permute-start.27 = (bf16[512,128]{1,0:T(8,128)(2,1)S(1)}, bf16[512,128]{1,0:T(8,128)(2,1)S(1)}, u32[]{:S(2)}, u32[]{:S(2)}) collective-permute-start(bf16[512,128]{1,0:T(8,128)(2,1)S(1)} %get-tuple-element.137), channel_id=1, source_target_pairs={{0,8},{2,10},{4,12},{6,14},{8,0},{10,2},{12,4},{14,6},{16,24},{18,... | collective-permute-start | bytes 393224 | tf_op jit(solution)/shard_map/ppermute | solution.py:33
  81.3 4.8 %outer.4 = (bf16[512,256]{1,0:T(8,128)(2,1)S(1)}, bf16[1024,512]{1,0:T(8,128)(2,1)S(1)}, bf16[16,256]{1,0:T(8,128)(2,1)S(1)}, bf16[528,256]{1,0:T(8,128)(2,1)S(1...) custom-call(s32[2]{0:T(128)S(1)} %pad_add_fusion.place_ref.refs_0_, ...), custom_call_target="tpu_custom_call", output_to_operand_aliasing={{5}: (8, {}), {6}: (9, {})} | custom-call | flops 1 | bytes 1 | tf_op jit(solution)/shard_map/outer/pallas_call | solution.py:72
  86.1 1.4 %collective-permute-start.25 = (bf16[528,256]{1,0:T(8,128)(2,1)S(1)}, bf16[528,256]{1,0:T(8,128)(2,1)S(1)}, u32[]{:S(2)}, u32[]{:S(2)}) collective-permute-start(bf16[528,256]{1,0:T(8,128)(2,1)S(1)} %get-tuple-element.135), channel_id=1, source_target_pairs={{0,8},{2,10},{4,12},{6,14},{8,0},{10,2},{12,4},{14,6},{16,24},{18,... | collective-permute-start | bytes 811016 | tf_op jit(solution)/shard_map/ppermute | solution.py:33
  88.2 2.5 %inner.5 = (bf16[512,128]{1,0:T(8,128)(2,1)S(1)}, bf16[1024,256]{1,0:T(8,128)(2,1)S(1)}, f32[32,256]{1,0:T(8,128)S(1)}) custom-call(s32[2]{0:T(128)S(1)} %pad_add_fusion.place_ref.refs_0_, bf16[1056,128]{1,0:T(8,128)(2,1)S(1)} %get-tuple-element.126.refs_0_, bf16[1056,128]{1,0:T(8,128)(2,1)S(1)} %collective-permute-done.22.refs_1_, ...), custom_call_target="tpu_custom_call" | custom-call | flops 1 | bytes 1 | tf_op jit(solution)/shard_map/inner/pallas_call | solution.py:72
  90.7 1.0 dots.2.refs_7_.refs_12_
  92.7 1.6 %settle.4 = (bf16[784,256]{1,0:T(8,128)(2,1)S(1)}, bf16[784,256]{1,0:T(8,128)(2,1)S(1)}, bf16[784,256]{1,0:T(8,128)(2,1)S(1)}, bf16[784,256]{1,0:T(8,128)(2,1)S(1)}, f32[8,128]{1,0:T(8,128)S(1)}) custom-call(s32[2]{0:T(128)S(1)} %pad_add_fusion.place_ref.refs_0_, bf16[512,256]{1,0:T(8,128)(2,1)S(1)} %get-tuple-element.120.refs_0_, ...), custom_call_target="tpu_custom_call" | custom-call | flops 1 | bytes 1 | tf_op jit(solution)/shard_map/settle/pallas_call | solution.py:72
  94.9 1.5 %collective-permute-start.30 = (bf16[784,256]{1,0:T(8,128)(2,1)S(1)}, bf16[784,256]{1,0:T(8,128)(2,1)S(1)}, u32[]{:S(2)}, u32[]{:S(2)}) collective-permute-start(bf16[784,256]{1,0:T(8,128)(2,1)S(1)} %get-tuple-element.142), channel_id=1, source_target_pairs={{0,4},{2,6},{4,0},{6,2},{8,12},{10,14},{12,8},{14,10},{16,20},{18,... | collective-permute-start | bytes 1204232 | tf_op jit(solution)/shard_map/ppermute | solution.py:33
  96.4 1.4 %collective-permute-start.31 = (bf16[784,256]{1,0:T(8,128)(2,1)S(1)}, bf16[784,256]{1,0:T(8,128)(2,1)S(1)}, u32[]{:S(2)}, u32[]{:S(2)}) collective-permute-start(bf16[784,256]{1,0:T(8,128)(2,1)S(1)} %get-tuple-element.143), channel_id=1, source_target_pairs={{0,6},{2,4},{4,2},{6,0},{8,14},{10,12},{12,10},{14,8},{16,22},{18,... | collective-permute-start | bytes 1204232 | tf_op jit(solution)/shard_map/ppermute | solution.py:33
  97.8 2.7 %outer.5 = (bf16[512,128]{1,0:T(8,128)(2,1)S(1)}, bf16[1024,256]{1,0:T(8,128)(2,1)S(1)}, bf16[16,128]{1,0:T(8,128)(2,1)S(1)}, bf16[528,128]{1,0:T(8,128)(2,1)S(1...) custom-call(s32[2]{0:T(128)S(1)} %pad_add_fusion.place_ref.refs_0_, ...), custom_call_target="tpu_custom_call", output_to_operand_aliasing={{5}: (8, {}), {6}: (9, {})} | custom-call | flops 1 | bytes 1 | tf_op jit(solution)/shard_map/outer/pallas_call | solution.py:72
  100.6 4.6 %collective-permute-start.34 = (bf16[16,640]{1,0:T(8,128)(2,1)S(1)}, bf16[16,640]{1,0:T(8,128)(2,1)S(1)}, u32[]{:S(2)}, u32[]{:S(2)}) collective-permute-start(bf16[16,640]{1,0:T(8,128)(2,1)S(1)} %get-tuple-element.154), channel_id=1, source_target_pairs={{0,16},{2,18},{4,20},{6,22},{8,24},{10,26},{12,28},{14,30},{16,0},... | collective-permute-start | bytes 61448 | tf_op jit(solution)/shard_map/ppermute | solution.py:33
  105.2 2.3 %collective-permute-start.35 = (bf16[16,640]{1,0:T(8,128)(2,1)S(1)}, bf16[16,640]{1,0:T(8,128)(2,1)S(1)}, u32[]{:S(2)}, u32[]{:S(2)}) collective-permute-start(bf16[16,640]{1,0:T(8,128)(2,1)S(1)} %get-tuple-element.155), channel_id=1, source_target_pairs={{0,24},{2,26},{4,28},{6,30},{8,16},{10,18},{12,20},{14,22},{16,8},... | collective-permute-start | bytes 61448 | tf_op jit(solution)/shard_map/ppermute | solution.py:33
  107.5 2.3 %collective-permute-start.32 = (bf16[528,128]{1,0:T(8,128)(2,1)S(1)}, bf16[528,128]{1,0:T(8,128)(2,1)S(1)}, u32[]{:S(2)}, u32[]{:S(2)}) collective-permute-start(bf16[528,128]{1,0:T(8,128)(2,1)S(1)} %get-tuple-element.152), channel_id=1, source_target_pairs={{0,8},{2,10},{4,12},{6,14},{8,0},{10,2},{12,4},{14,6},{16,24},{18,... | collective-permute-start | bytes 405512 | tf_op jit(solution)/shard_map/ppermute | solution.py:33
  111.4 1.4 %collective-permute-done.32.refs_5_ = bf16[528,128]{1,0:T(8,128)(2,1)S(1)} collective-permute-done((bf16[528,128]{1,0:T(8,128)(2,1)S(1)}, bf16[528,128]{1,0:T(8,128)(2,1)S(1)}, u32[]{:S(2)}, u32[]{:S(2)}) %collective-permute-start.32) | collective-permute-done | bytes 135200 | tf_op jit(solution)/shard_map/ppermute | solution.py:33
  114.3 1.5 %collective-permute-start.37 = (bf16[864,128]{1,0:T(8,128)(2,1)S(1)}, bf16[864,128]{1,0:T(8,128)(2,1)S(1)}, u32[]{:S(2)}, u32[]{:S(2)}) collective-permute-start(bf16[864,128]{1,0:T(8,128)(2,1)S(1)} %get-tuple-element.158), channel_id=1, source_target_pairs={{0,4},{2,6},{4,0},{6,2},{8,12},{10,14},{12,8},{14,10},{16,20},{18,... | collective-permute-start | bytes 663560 | tf_op jit(solution)/shard_map/ppermute | solution.py:33
  115.9 1.4 %collective-permute-start.38 = (bf16[864,128]{1,0:T(8,128)(2,1)S(1)}, bf16[864,128]{1,0:T(8,128)(2,1)S(1)}, u32[]{:S(2)}, u32[]{:S(2)}) collective-permute-start(bf16[864,128]{1,0:T(8,128)(2,1)S(1)} %get-tuple-element.159), channel_id=1, source_target_pairs={{0,6},{2,4},{4,2},{6,0},{8,14},{10,12},{12,10},{14,8},{16,22},{18,... | collective-permute-start | bytes 663560 | tf_op jit(solution)/shard_map/ppermute | solution.py:33
  117.3 1.0 dots.3.refs_13_
  118.3 1.5 %collective-permute-done.36.refs_9_ = bf16[864,128]{1,0:T(8,128)(2,1)S(1)} collective-permute-done((bf16[864,128]{1,0:T(8,128)(2,1)S(1)}, bf16[864,128]{1,0:T(8,128)(2,1)S(1)}, u32[]{:S(2)}, u32[]{:S(2)}) %collective-permute-start.36) | collective-permute-done | bytes 221216 | tf_op jit(solution)/shard_map/ppermute | solution.py:33
  119.7 2.0 %collective-permute-done.37.refs_10_ = bf16[864,128]{1,0:T(8,128)(2,1)S(1)} collective-permute-done((bf16[864,128]{1,0:T(8,128)(2,1)S(1)}, bf16[864,128]{1,0:T(8,128)(2,1)S(1)}, u32[]{:S(2)}, u32[]{:S(2)}) %collective-permute-start.37) | collective-permute-done | bytes 221216 | tf_op jit(solution)/shard_map/ppermute | solution.py:33
  121.7 1.3 %collective-permute-done.38.refs_11_ = bf16[864,128]{1,0:T(8,128)(2,1)S(1)} collective-permute-done((bf16[864,128]{1,0:T(8,128)(2,1)S(1)}, bf16[864,128]{1,0:T(8,128)(2,1)S(1)}, u32[]{:S(2)}, u32[]{:S(2)}) %collective-permute-start.38) | collective-permute-done | bytes 221216 | tf_op jit(solution)/shard_map/ppermute | solution.py:33
  123.1 1.7 %total_dots.1 = (f32[256,128]{1,0:T(8,128)S(1)}, f32[8,2560]{1,0:T(8,128)S(1)}) custom-call(s32[2]{0:T(128)S(1)} %pad_add_fusion.place_ref.refs_0_, s32[2]{0:T(128)S(1)} %copy-done.8, bf16[16,2560]{1,0:T(8,128)(2,1)S(1)} %get-tuple-element.83.refs_11_.raw_ref, bf16[256,2560]{1,0:T(8,128)(2,1)S(1)} %copy-done.2, bf16[256,2560]{1,0:T(8,128)(2,1)} %refs_14_.1, ...), custom_call_target="tpu_custom_call" | custom-call | flops 1 | bytes 1 | tf_op jit(solution)/shard_map/total_dots/pallas_call | solution.py:580
  124.9 1.3 %collective-permute-done.39.dot_other_ref = f32[256,128]{1,0:T(8,128)S(1)} collective-permute-done((f32[256,128]{1,0:T(8,128)S(1)}, f32[256,128]{1,0:T(8,128)S(1)}, u32[]{:S(2)}, u32[]{:S(2)}) %collective-permute-start.39) | collective-permute-done | bytes 131104 | tf_op jit(solution)/shard_map/ppermute | solution.py:688
  126.2 4.7 %finish.1 = (bf16[256,2560]{1,0:T(8,128)(2,1)}, bf16[256,2560]{1,0:T(8,128)(2,1)}, bf16[256,2560]{1,0:T(8,128)(2,1)}) custom-call(s32[2]{0:T(128)S(1)} %pad_add_fusion.place_ref.refs_0_, s32[2]{0:T(128)S(1)} %copy-done.8, f32[256,128]{1,0:T(8,128)S(1)} %squares.1.own_ref.refs_3_, f32[256,128]{1,0:T(8,128)S(1)} %collective-permute-done.other_ref.refs_4_, ...), custom_call_target="tpu_custom_call" | custom-call | flops 1 | bytes 1 | tf_op jit(solution)/shard_map/finish/pallas_call | solution.py:675
  (80 shorter events, 19.1 us)
Async XLA Ops:
  3.4 5.2 %copy-start = (bf16[256,2560]{1,0:T(8,128)(2,1)S(1)}, bf16[256,2560]{1,0:T(8,128)(2,1)}, u32[]{:S(2)}) copy-start(bf16[256,2560]{1,0:T(8,128)(2,1)} %refs_14_.1) | copy-start | bytes 3932164
  3.4 5.2 %copy-start.1 = (bf16[256,2560]{1,0:T(8,128)(2,1)S(1)}, bf16[256,2560]{1,0:T(8,128)(2,1)}, u32[]{:S(2)}) copy-start(bf16[256,2560]{1,0:T(8,128)(2,1)} %refs_13_.1) | copy-start | bytes 3932164
  4.0 17.0 %collective-permute-start.1 = (bf16[512,256]{1,0:T(8,128)(2,1)S(1)}, bf16[512,256]{1,0:T(8,128)(2,1)S(1)}, u32[]{:S(2)}, u32[]{:S(2)}) collective-permute-start(bf16[512,256]{1,0:T(8,128)(2,1)S(1)} %get-tuple-element.85), channel_id=1, source_target_pairs={{0,2},{2,0},{4,6},{6,4},{8,10},{10,8},{12,14},{14,12},{16,18},{18,... | collective-permute-start | bytes 786440 | tf_op jit(solution)/shard_map/ppermute | solution.py:33
  7.0 14.0 %collective-permute-start.2 = (bf16[512,256]{1,0:T(8,128)(2,1)S(1)}, bf16[512,256]{1,0:T(8,128)(2,1)S(1)}, u32[]{:S(2)}, u32[]{:S(2)}) collective-permute-start(bf16[512,256]{1,0:T(8,128)(2,1)S(1)} %get-tuple-element.86), channel_id=1, source_target_pairs={{0,4},{2,6},{4,0},{6,2},{8,12},{10,14},{12,8},{14,10},{16,20},{18,... | collective-permute-start | bytes 786440 | tf_op jit(solution)/shard_map/ppermute | solution.py:33
  8.5 2.0 %copy-start.4 = (bf16[256,2560]{1,0:T(8,128)(2,1)S(1)}, bf16[256,2560]{1,0:T(8,128)(2,1)}, u32[]{:S(2)}) copy-start(bf16[256,2560]{1,0:T(8,128)(2,1)} %refs_6_.5) | copy-start | bytes 3932164
  8.5 2.0 %copy-start.8 = (s32[2]{0:T(128)S(1)}, s32[2]{0:T(128)}, u32[]{:S(2)}) copy-start(s32[2]{0:T(128)} %ids_ref.5) | copy-start | bytes 28
  8.5 12.5 %collective-permute-start.3 = (bf16[512,256]{1,0:T(8,128)(2,1)S(1)}, bf16[512,256]{1,0:T(8,128)(2,1)S(1)}, u32[]{:S(2)}, u32[]{:S(2)}) collective-permute-start(bf16[512,256]{1,0:T(8,128)(2,1)S(1)} %get-tuple-element.87), channel_id=1, source_target_pairs={{0,6},{2,4},{4,2},{6,0},{8,14},{10,12},{12,10},{14,8},{16,22},{18,... | collective-permute-start | bytes 786440 | tf_op jit(solution)/shard_map/ppermute | solution.py:33
  9.2 1.4 %collective-permute-start = (f32[256,128]{1,0:T(8,128)S(1)}, f32[256,128]{1,0:T(8,128)S(1)}, u32[]{:S(2)}, u32[]{:S(2)}) collective-permute-start(f32[256,128]{1,0:T(8,128)S(1)} %squares.1.own_ref.refs_3_), channel_id=1, source_target_pairs={{0,1},{1,0},{2,3},{3,2},{4,5},{5,4},{6,7},{7,6},{8,9},{9,8},{10,11... | collective-permute-start | bytes 393224 | tf_op jit(solution)/shard_map/ppermute | solution.py:688
  9.2 8.2 %copy-start.10 = (f32[2560]{0:T(1024)S(1)}, f32[2560]{0:T(1024)}, u32[]{:S(2)}) copy-start(f32[2560]{0:T(1024)} %param.13) | copy-start | bytes 30724
  9.2 8.2 %copy-start.6 = (s32[2,4]{1,0:T(2,128)S(1)}, s32[2,4]{1,0:T(2,128)}, u32[]{:S(2)}) copy-start(s32[2,4]{1,0:T(2,128)} %refs_1_.7) | copy-start | bytes 100
  9.3 8.2 %copy-start.7 = (s32[1,16]{1,0:T(1,128)S(1)}, s32[1,16]{1,0:T(1,128)}, u32[]{:S(2)}) copy-start(s32[1,16]{1,0:T(1,128)} %refs_2_.5) | copy-start | bytes 196
  11.4 5.9 %collective-permute-start.6 = (bf16[16,640]{1,0:T(8,128)(2,1)S(1)}, bf16[16,640]{1,0:T(8,128)(2,1)S(1)}, u32[]{:S(2)}, u32[]{:S(2)}) collective-permute-start(bf16[16,640]{1,0:T(8,128)(2,1)S(1)} %get-tuple-element.92.refs_4_.refs_11_), channel_id=1, source_target_pairs={{0,24},{2,26},{4,28},{6,30},{8,16},{10,18},{12,20},{14,22},{16,8},... | collective-permute-start | bytes 61448 | tf_op jit(solution)/shard_map/ppermute | solution.py:33
  15.5 4.7 %collective-permute-start.5 = (bf16[16,640]{1,0:T(8,128)(2,1)S(1)}, bf16[16,640]{1,0:T(8,128)(2,1)S(1)}, u32[]{:S(2)}, u32[]{:S(2)}) collective-permute-start(bf16[16,640]{1,0:T(8,128)(2,1)S(1)} %get-tuple-element.92.refs_4_.refs_11_), channel_id=1, source_target_pairs={{0,16},{2,18},{4,20},{6,22},{8,24},{10,26},{12,28},{14,30},{16,0},... | collective-permute-start | bytes 61448 | tf_op jit(solution)/shard_map/ppermute | solution.py:33
  17.2 3.8 %collective-permute-start.4 = (bf16[16,640]{1,0:T(8,128)(2,1)S(1)}, bf16[16,640]{1,0:T(8,128)(2,1)S(1)}, u32[]{:S(2)}, u32[]{:S(2)}) collective-permute-start(bf16[16,640]{1,0:T(8,128)(2,1)S(1)} %get-tuple-element.92.refs_4_.refs_11_), channel_id=1, source_target_pairs={{0,8},{2,10},{4,12},{6,14},{8,0},{10,2},{12,4},{14,6},{16,24},{18,... | collective-permute-start | bytes 61448 | tf_op jit(solution)/shard_map/ppermute | solution.py:33
  21.7 9.9 %collective-permute-start.7 = (bf16[544,256]{1,0:T(8,128)(2,1)S(1)}, bf16[544,256]{1,0:T(8,128)(2,1)S(1)}, u32[]{:S(2)}, u32[]{:S(2)}) collective-permute-start(bf16[544,256]{1,0:T(8,128)(2,1)S(1)} %get-tuple-element.94), channel_id=1, source_target_pairs={{0,2},{2,0},{4,6},{6,4},{8,10},{10,8},{12,14},{14,12},{16,18},{18,... | collective-permute-start | bytes 835592 | tf_op jit(solution)/shard_map/ppermute | solution.py:33
  23.5 13.4 %collective-permute-start.8 = (bf16[544,256]{1,0:T(8,128)(2,1)S(1)}, bf16[544,256]{1,0:T(8,128)(2,1)S(1)}, u32[]{:S(2)}, u32[]{:S(2)}) collective-permute-start(bf16[544,256]{1,0:T(8,128)(2,1)S(1)} %get-tuple-element.95), channel_id=1, source_target_pairs={{0,4},{2,6},{4,0},{6,2},{8,12},{10,14},{12,8},{14,10},{16,20},{18,... | collective-permute-start | bytes 835592 | tf_op jit(solution)/shard_map/ppermute | solution.py:33
  25.0 13.5 %collective-permute-start.9 = (bf16[544,256]{1,0:T(8,128)(2,1)S(1)}, bf16[544,256]{1,0:T(8,128)(2,1)S(1)}, u32[]{:S(2)}, u32[]{:S(2)}) collective-permute-start(bf16[544,256]{1,0:T(8,128)(2,1)S(1)} %get-tuple-element.96), channel_id=1, source_target_pairs={{0,6},{2,4},{4,2},{6,0},{8,14},{10,12},{12,10},{14,8},{16,22},{18,... | collective-permute-start | bytes 835592 | tf_op jit(solution)/shard_map/ppermute | solution.py:33
  25.3 8.8 %copy-start.2 = (bf16[256,2560]{1,0:T(8,128)(2,1)S(1)}, bf16[256,2560]{1,0:T(8,128)(2,1)}, u32[]{:S(2)}) copy-start(bf16[256,2560]{1,0:T(8,128)(2,1)} %refs_13_.1) | copy-start | bytes 3932164
  28.4 27.4 %collective-permute-start.14 = (bf16[1056,256]{1,0:T(8,128)(2,1)}, bf16[1056,256]{1,0:T(8,128)(2,1)S(1)}, u32[]{:S(2)}, u32[]{:S(2)}) collective-permute-start(bf16[1056,256]{1,0:T(8,128)(2,1)} %get-tuple-element.111), channel_id=1, source_target_pairs={{0,2},{2,0},{4,6},{6,4},{8,10},{10,8},{12,14},{14,12},{16,18},{18,... | collective-permute-start | bytes 1622024 | tf_op jit(solution)/shard_map/ppermute | solution.py:33
  30.1 28.4 %collective-permute-start.15 = (bf16[1056,256]{1,0:T(8,128)(2,1)S(1)}, bf16[1056,256]{1,0:T(8,128)(2,1)S(1)}, u32[]{:S(2)}, u32[]{:S(2)}) collective-permute-start(bf16[1056,256]{1,0:T(8,128)(2,1)S(1)} %get-tuple-element.112), channel_id=1, source_target_pairs={{0,4},{2,6},{4,0},{6,2},{8,12},{10,14},{12,8},{14,10},{16,20},{18,... | collective-permute-start | bytes 1622024 | tf_op jit(solution)/shard_map/ppermute | solution.py:33
  31.6 30.1 %collective-permute-start.16 = (bf16[1056,256]{1,0:T(8,128)(2,1)S(1)}, bf16[1056,256]{1,0:T(8,128)(2,1)S(1)}, u32[]{:S(2)}, u32[]{:S(2)}) collective-permute-start(bf16[1056,256]{1,0:T(8,128)(2,1)S(1)} %get-tuple-element.113), channel_id=1, source_target_pairs={{0,6},{2,4},{4,2},{6,0},{8,14},{10,12},{12,10},{14,8},{16,22},{18,... | collective-permute-start | bytes 1622024 | tf_op jit(solution)/shard_map/ppermute | solution.py:33
  39.1 6.4 %collective-permute-start.10 = (bf16[512,256]{1,0:T(8,128)(2,1)S(1)}, bf16[512,256]{1,0:T(8,128)(2,1)S(1)}, u32[]{:S(2)}, u32[]{:S(2)}) collective-permute-start(bf16[512,256]{1,0:T(8,128)(2,1)S(1)} %get-tuple-element.102), channel_id=1, source_target_pairs={{0,8},{2,10},{4,12},{6,14},{8,0},{10,2},{12,4},{14,6},{16,24},{18,... | collective-permute-start | bytes 786440 | tf_op jit(solution)/shard_map/ppermute | solution.py:33
  40.0 5.6 %collective-permute-start.11 = (bf16[512,256]{1,0:T(8,128)(2,1)S(1)}, bf16[512,256]{1,0:T(8,128)(2,1)S(1)}, u32[]{:S(2)}, u32[]{:S(2)}) collective-permute-start(bf16[512,256]{1,0:T(8,128)(2,1)S(1)} %get-tuple-element.103), channel_id=1, source_target_pairs={{8,16},{10,18},{12,20},{14,22},{16,8},{18,10},{20,12},{22,14},{9,1... | collective-permute-start | bytes 786440 | tf_op jit(solution)/shard_map/ppermute | solution.py:39
  50.4 14.3 %collective-permute-start.12 = (bf16[528,256]{1,0:T(8,128)(2,1)S(1)}, bf16[528,256]{1,0:T(8,128)(2,1)S(1)}, u32[]{:S(2)}, u32[]{:S(2)}) collective-permute-start(bf16[528,256]{1,0:T(8,128)(2,1)S(1)} %get-tuple-element.108), channel_id=1, source_target_pairs={{0,8},{2,10},{4,12},{6,14},{8,0},{10,2},{12,4},{14,6},{16,24},{18,... | collective-permute-start | bytes 811016 | tf_op jit(solution)/shard_map/ppermute | solution.py:33
  55.1 8.9 %collective-permute-start.13 = (bf16[512,256]{1,0:T(8,128)(2,1)S(1)}, bf16[512,256]{1,0:T(8,128)(2,1)S(1)}, u32[]{:S(2)}, u32[]{:S(2)}) collective-permute-start(bf16[512,256]{1,0:T(8,128)(2,1)S(1)} %get-tuple-element.109), channel_id=1, source_target_pairs={{8,16},{10,18},{12,20},{14,22},{16,8},{18,10},{20,12},{22,14},{9,1... | collective-permute-start | bytes 786440 | tf_op jit(solution)/shard_map/ppermute | solution.py:39
  55.8 15.3 %collective-permute-start.22 = (bf16[1056,128]{1,0:T(8,128)(2,1)}, bf16[1056,128]{1,0:T(8,128)(2,1)S(1)}, u32[]{:S(2)}, u32[]{:S(2)}) collective-permute-start(bf16[1056,128]{1,0:T(8,128)(2,1)} %get-tuple-element.127), channel_id=1, source_target_pairs={{0,2},{2,0},{4,6},{6,4},{8,10},{10,8},{12,14},{14,12},{16,18},{18,... | collective-permute-start | bytes 811016 | tf_op jit(solution)/shard_map/ppermute | solution.py:33
  58.5 13.3 %collective-permute-start.23 = (bf16[1056,128]{1,0:T(8,128)(2,1)S(1)}, bf16[1056,128]{1,0:T(8,128)(2,1)S(1)}, u32[]{:S(2)}, u32[]{:S(2)}) collective-permute-start(bf16[1056,128]{1,0:T(8,128)(2,1)S(1)} %get-tuple-element.128), channel_id=1, source_target_pairs={{0,4},{2,6},{4,0},{6,2},{8,12},{10,14},{12,8},{14,10},{16,20},{18,... | collective-permute-start | bytes 811016 | tf_op jit(solution)/shard_map/ppermute | solution.py:33
  61.7 12.2 %collective-permute-start.24 = (bf16[1056,128]{1,0:T(8,128)(2,1)S(1)}, bf16[1056,128]{1,0:T(8,128)(2,1)S(1)}, u32[]{:S(2)}, u32[]{:S(2)}) collective-permute-start(bf16[1056,128]{1,0:T(8,128)(2,1)S(1)} %get-tuple-element.129), channel_id=1, source_target_pairs={{0,6},{2,4},{4,2},{6,0},{8,14},{10,12},{12,10},{14,8},{16,22},{18,... | collective-permute-start | bytes 811016 | tf_op jit(solution)/shard_map/ppermute | solution.py:33
  64.0 11.2 %collective-permute-start.20 = (bf16[512,256]{1,0:T(8,128)(2,1)S(1)}, bf16[512,256]{1,0:T(8,128)(2,1)S(1)}, u32[]{:S(2)}, u32[]{:S(2)}) collective-permute-start(bf16[512,256]{1,0:T(8,128)(2,1)S(1)} %get-tuple-element.122), channel_id=1, source_target_pairs={{0,8},{2,10},{4,12},{6,14},{8,0},{10,2},{12,4},{14,6},{16,24},{18,... | collective-permute-start | bytes 786440 | tf_op jit(solution)/shard_map/ppermute | solution.py:33
  64.7 16.0 %collective-permute-start.21 = (bf16[512,256]{1,0:T(8,128)(2,1)S(1)}, bf16[512,256]{1,0:T(8,128)(2,1)S(1)}, u32[]{:S(2)}, u32[]{:S(2)}) collective-permute-start(bf16[512,256]{1,0:T(8,128)(2,1)S(1)} %get-tuple-element.123), channel_id=1, source_target_pairs={{8,16},{10,18},{12,20},{14,22},{16,8},{18,10},{20,12},{22,14},{9,1... | collective-permute-start | bytes 786440 | tf_op jit(solution)/shard_map/ppermute | solution.py:39
  71.0 19.6 %collective-permute-start.17 = (bf16[784,256]{1,0:T(8,128)(2,1)S(1)}, bf16[784,256]{1,0:T(8,128)(2,1)S(1)}, u32[]{:S(2)}, u32[]{:S(2)}) collective-permute-start(bf16[784,256]{1,0:T(8,128)(2,1)S(1)} %get-tuple-element.117), channel_id=1, source_target_pairs={{0,2},{2,0},{4,6},{6,4},{8,10},{10,8},{12,14},{14,12},{16,18},{18,... | collective-permute-start | bytes 1204232 | tf_op jit(solution)/shard_map/ppermute | solution.py:33
  71.8 18.9 %collective-permute-start.18 = (bf16[784,256]{1,0:T(8,128)(2,1)S(1)}, bf16[784,256]{1,0:T(8,128)(2,1)S(1)}, u32[]{:S(2)}, u32[]{:S(2)}) collective-permute-start(bf16[784,256]{1,0:T(8,128)(2,1)S(1)} %get-tuple-element.118), channel_id=1, source_target_pairs={{0,4},{2,6},{4,0},{6,2},{8,12},{10,14},{12,8},{14,10},{16,20},{18,... | collective-permute-start | bytes 1204232 | tf_op jit(solution)/shard_map/ppermute | solution.py:33
  74.0 16.7 %collective-permute-start.19 = (bf16[784,256]{1,0:T(8,128)(2,1)S(1)}, bf16[784,256]{1,0:T(8,128)(2,1)S(1)}, u32[]{:S(2)}, u32[]{:S(2)}) collective-permute-start(bf16[784,256]{1,0:T(8,128)(2,1)S(1)} %get-tuple-element.119), channel_id=1, source_target_pairs={{0,6},{2,4},{4,2},{6,0},{8,14},{10,12},{12,10},{14,8},{16,22},{18,... | collective-permute-start | bytes 1204232 | tf_op jit(solution)/shard_map/ppermute | solution.py:33
  75.2 10.9 %collective-permute-start.27 = (bf16[512,128]{1,0:T(8,128)(2,1)S(1)}, bf16[512,128]{1,0:T(8,128)(2,1)S(1)}, u32[]{:S(2)}, u32[]{:S(2)}) collective-permute-start(bf16[512,128]{1,0:T(8,128)(2,1)S(1)} %get-tuple-element.137), channel_id=1, source_target_pairs={{0,8},{2,10},{4,12},{6,14},{8,0},{10,2},{12,4},{14,6},{16,24},{18,... | collective-permute-start | bytes 393224 | tf_op jit(solution)/shard_map/ppermute | solution.py:33
  80.6 6.9 %collective-permute-start.28 = (bf16[512,128]{1,0:T(8,128)(2,1)S(1)}, bf16[512,128]{1,0:T(8,128)(2,1)S(1)}, u32[]{:S(2)}, u32[]{:S(2)}) collective-permute-start(bf16[512,128]{1,0:T(8,128)(2,1)S(1)} %get-tuple-element.138), channel_id=1, source_target_pairs={{8,16},{10,18},{12,20},{14,22},{16,8},{18,10},{20,12},{22,14},{9,1... | collective-permute-start | bytes 393224 | tf_op jit(solution)/shard_map/ppermute | solution.py:39
  86.1 6.5 %collective-permute-start.25 = (bf16[528,256]{1,0:T(8,128)(2,1)S(1)}, bf16[528,256]{1,0:T(8,128)(2,1)S(1)}, u32[]{:S(2)}, u32[]{:S(2)}) collective-permute-start(bf16[528,256]{1,0:T(8,128)(2,1)S(1)} %get-tuple-element.135), channel_id=1, source_target_pairs={{0,8},{2,10},{4,12},{6,14},{8,0},{10,2},{12,4},{14,6},{16,24},{18,... | collective-permute-start | bytes 811016 | tf_op jit(solution)/shard_map/ppermute | solution.py:33
  87.5 4.2 %collective-permute-start.26 = (bf16[512,256]{1,0:T(8,128)(2,1)S(1)}, bf16[512,256]{1,0:T(8,128)(2,1)S(1)}, u32[]{:S(2)}, u32[]{:S(2)}) collective-permute-start(bf16[512,256]{1,0:T(8,128)(2,1)S(1)} %get-tuple-element.136), channel_id=1, source_target_pairs={{8,16},{10,18},{12,20},{14,22},{16,8},{18,10},{20,12},{22,14},{9,1... | collective-permute-start | bytes 786440 | tf_op jit(solution)/shard_map/ppermute | solution.py:39
  94.3 21.6 %collective-permute-start.29 = (bf16[784,256]{1,0:T(8,128)(2,1)S(1)}, bf16[784,256]{1,0:T(8,128)(2,1)S(1)}, u32[]{:S(2)}, u32[]{:S(2)}) collective-permute-start(bf16[784,256]{1,0:T(8,128)(2,1)S(1)} %get-tuple-element.141), channel_id=1, source_target_pairs={{0,2},{2,0},{4,6},{6,4},{8,10},{10,8},{12,14},{14,12},{16,18},{18,... | collective-permute-start | bytes 1204232 | tf_op jit(solution)/shard_map/ppermute | solution.py:33
  94.9 22.4 %collective-permute-start.30 = (bf16[784,256]{1,0:T(8,128)(2,1)S(1)}, bf16[784,256]{1,0:T(8,128)(2,1)S(1)}, u32[]{:S(2)}, u32[]{:S(2)}) collective-permute-start(bf16[784,256]{1,0:T(8,128)(2,1)S(1)} %get-tuple-element.142), channel_id=1, source_target_pairs={{0,4},{2,6},{4,0},{6,2},{8,12},{10,14},{12,8},{14,10},{16,20},{18,... | collective-permute-start | bytes 1204232 | tf_op jit(solution)/shard_map/ppermute | solution.py:33
  96.4 20.9 %collective-permute-start.31 = (bf16[784,256]{1,0:T(8,128)(2,1)S(1)}, bf16[784,256]{1,0:T(8,128)(2,1)S(1)}, u32[]{:S(2)}, u32[]{:S(2)}) collective-permute-start(bf16[784,256]{1,0:T(8,128)(2,1)S(1)} %get-tuple-element.143), channel_id=1, source_target_pairs={{0,6},{2,4},{4,2},{6,0},{8,14},{10,12},{12,10},{14,8},{16,22},{18,... | collective-permute-start | bytes 1204232 | tf_op jit(solution)/shard_map/ppermute | solution.py:33
  100.6 6.9 %collective-permute-start.34 = (bf16[16,640]{1,0:T(8,128)(2,1)S(1)}, bf16[16,640]{1,0:T(8,128)(2,1)S(1)}, u32[]{:S(2)}, u32[]{:S(2)}) collective-permute-start(bf16[16,640]{1,0:T(8,128)(2,1)S(1)} %get-tuple-element.154), channel_id=1, source_target_pairs={{0,16},{2,18},{4,20},{6,22},{8,24},{10,26},{12,28},{14,30},{16,0},... | collective-permute-start | bytes 61448 | tf_op jit(solution)/shard_map/ppermute | solution.py:33
  105.2 5.6 %collective-permute-start.35 = (bf16[16,640]{1,0:T(8,128)(2,1)S(1)}, bf16[16,640]{1,0:T(8,128)(2,1)S(1)}, u32[]{:S(2)}, u32[]{:S(2)}) collective-permute-start(bf16[16,640]{1,0:T(8,128)(2,1)S(1)} %get-tuple-element.155), channel_id=1, source_target_pairs={{0,24},{2,26},{4,28},{6,30},{8,16},{10,18},{12,20},{14,22},{16,8},... | collective-permute-start | bytes 61448 | tf_op jit(solution)/shard_map/ppermute | solution.py:33
  107.5 5.3 %collective-permute-start.32 = (bf16[528,128]{1,0:T(8,128)(2,1)S(1)}, bf16[528,128]{1,0:T(8,128)(2,1)S(1)}, u32[]{:S(2)}, u32[]{:S(2)}) collective-permute-start(bf16[528,128]{1,0:T(8,128)(2,1)S(1)} %get-tuple-element.152), channel_id=1, source_target_pairs={{0,8},{2,10},{4,12},{6,14},{8,0},{10,2},{12,4},{14,6},{16,24},{18,... | collective-permute-start | bytes 405512 | tf_op jit(solution)/shard_map/ppermute | solution.py:33
  110.8 0.7 collective-permute-start.33
  113.7 6.0 %collective-permute-start.36 = (bf16[864,128]{1,0:T(8,128)(2,1)S(1)}, bf16[864,128]{1,0:T(8,128)(2,1)S(1)}, u32[]{:S(2)}, u32[]{:S(2)}) collective-permute-start(bf16[864,128]{1,0:T(8,128)(2,1)S(1)} %get-tuple-element.157), channel_id=1, source_target_pairs={{0,2},{2,0},{4,6},{6,4},{8,10},{10,8},{12,14},{14,12},{16,18},{18,... | collective-permute-start | bytes 663560 | tf_op jit(solution)/shard_map/ppermute | solution.py:33
  114.3 7.4 %collective-permute-start.37 = (bf16[864,128]{1,0:T(8,128)(2,1)S(1)}, bf16[864,128]{1,0:T(8,128)(2,1)S(1)}, u32[]{:S(2)}, u32[]{:S(2)}) collective-permute-start(bf16[864,128]{1,0:T(8,128)(2,1)S(1)} %get-tuple-element.158), channel_id=1, source_target_pairs={{0,4},{2,6},{4,0},{6,2},{8,12},{10,14},{12,8},{14,10},{16,20},{18,... | collective-permute-start | bytes 663560 | tf_op jit(solution)/shard_map/ppermute | solution.py:33
  115.9 7.2 %collective-permute-start.38 = (bf16[864,128]{1,0:T(8,128)(2,1)S(1)}, bf16[864,128]{1,0:T(8,128)(2,1)S(1)}, u32[]{:S(2)}, u32[]{:S(2)}) collective-permute-start(bf16[864,128]{1,0:T(8,128)(2,1)S(1)} %get-tuple-element.159), channel_id=1, source_target_pairs={{0,6},{2,4},{4,2},{6,0},{8,14},{10,12},{12,10},{14,8},{16,22},{18,... | collective-permute-start | bytes 663560 | tf_op jit(solution)/shard_map/ppermute | solution.py:33
  124.8 1.4 %collective-permute-start.39 = (f32[256,128]{1,0:T(8,128)S(1)}, f32[256,128]{1,0:T(8,128)S(1)}, u32[]{:S(2)}, u32[]{:S(2)}) collective-permute-start(f32[256,128]{1,0:T(8,128)S(1)} %get-tuple-element.161.dot_ref), channel_id=1, source_target_pairs={{0,1},{1,0},{2,3},{3,2},{4,5},{5,4},{6,7},{7,6},{8,9},{9,8},{10,11... | collective-permute-start | bytes 393224 | tf_op jit(solution)/shard_map/ppermute | solution.py:688
  (3 other events, 3.3 us)

commit v7 on v6

--- a/solution.py
+++ b/solution.py
@@ -503,16 +503,22 @@
             out[(i + 1) * rows : (i + 2) * rows] = total.astype(BF16)
         out[3 * rows : 3 * rows + 16] = part
         if more and head == 0:
+            row = lax.broadcasted_iota(jnp.int32, (32, 16), 0)
+            spot = lax.broadcasted_iota(jnp.int32, (32, 16), 1) - G_DEV * j
+            few = jnp.zeros((32, HEAD_DIM), F32)
             for h in range(rest_g.shape[1] // HEAD_DIM):
-                at = 3 * rows + 16 * (h + 1)
-                out[at : at + 16] = rest_g[:, h * HEAD_DIM : (h + 1) * HEAD_DIM]
+                hot = (spot >= 0) & (spot % 8 < G_DEV) & (row == 4 * h + spot % 8 + spot // 8 * 2)
+                hot = hot.astype(F32).astype(BF16)
+                some = rest_g[:, h * HEAD_DIM : (h + 1) * HEAD_DIM]
+                few = few + contract(hot, some, ((1,), (0,)))
+            out[3 * rows + 16 : 3 * rows + 48] = few.astype(BF16)
 
 
 def settle(place, inner, outer, own_g, near, far, more, after):
     rows, width = inner[0].shape
     rows = rows // 2
     part = (HEAD_DIM, 2 * HEAD_DIM)
-    extra = 16 + 16 * (more[0].shape[1] // HEAD_DIM if more else 0)
+    extra = 48 if more else 16
     home = jax.ShapeDtypeStruct((3 * rows + extra, width), BF16)
     return heads_call(
         settle_kernel,
@@ -548,10 +554,14 @@
             for h in range(count):
                 home = homes[c * GROUP + d]
                 last = homes[(len(chunks) - 1) * GROUP + d]
-                at = 3 * rows + 16 * (first + h + 1)
+                at = 4 * (first + h)
                 part = home[3 * rows : 3 * rows + 16, h * HEAD_DIM : (h + 1) * HEAD_DIM].astype(F32)
-                part = part + last[at : at + 16, :HEAD_DIM].astype(F32)
-                found = [jnp.sum(jnp.where(x, part, 0.0), axis=0, keepdims=True) for x in hot]
+                rest = last[3 * rows + 16 : 3 * rows + 48, :HEAD_DIM].astype(F32)
+                found = [
+                    jnp.sum(jnp.where(x, part, 0.0), axis=0, keepdims=True)
+                    + rest[at + i : at + i + 1]
+                    for i, x in enumerate(hot)
+                ]
                 at = pl.multiple_of(
                     (me ^ d) * (width // GROUP) + (first + h) * HEAD_DIM, HEAD_DIM
                 )

time: 133 us -> 133 us (level)
  no operation moved by 1% of the time
where the time goes in v7:
time: 133 us; the launch traced here: 132 us
  starting transfers between devices  60.9 us (46%)
  Pallas kernels  48.8 us (37%)
  waiting for transfers between devices  18.4 us (14%)
  local copies, waits for them, and re-layouts  2.7 us (2%)
    ppermute x32, starting transfers between devices, swapped(): return lax.ppermute(shard, 'ctx', [(i, i ^ bit) for i in range(count)])  56.8 us
    pallas_call x16, Pallas kernels, heads_call(): pl.pallas_call(run, out_shape=[entry[0] for entry in outputs], in_specs=[...  33.9 us
    ppermute x32, waiting for transfers between devices, swapped(): return lax.ppermute(shard, 'ctx', [(i, i ^ bit) for i in range(count)])  15.8 us
    pallas_call x3, Pallas kernels, pack(): pl.pallas_call(behind(kernel, 11 + len(parts), len(after)), out_shape=[ja...  7 us
    pallas_call x1, Pallas kernels, finish(): pl.pallas_call(functools.partial(finish_kernel, chunks), out_shape=[jax.S...  4.73 us
    ppermute x6, starting transfers between devices, swapped_edges(): return lax.ppermute(shard, 'ctx', pairs)  3.98 us
    unnamed x22, local copies, waits for them, and re-layouts  2.68 us
  transfers between devices with their start and end apart: 40, of which 16 were waited for; matrix products, arithmetic and copies ran while one was open for 0% of the time, Pallas kernels for 30%

profile of v7, /device:TPU:0, one launch (start us, length us, event | category | flops | bytes accessed | tf_op | source)
XLA Modules:
  0.0 131.9 jit_solution(10748905385878571914)
XLA Ops:
  0.7 1.3 copy-done.3
  2.0 1.3 copy-done.5
  4.0 3.0 %collective-permute-start.1 = (bf16[512,256]{1,0:T(8,128)(2,1)S(1)}, bf16[512,256]{1,0:T(8,128)(2,1)S(1)}, u32[]{:S(2)}, u32[]{:S(2)}) collective-permute-start(bf16[512,256]{1,0:T(8,128)(2,1)S(1)} %get-tuple-element.85), channel_id=1, source_target_pairs={{0,2},{2,0},{4,6},{6,4},{8,10},{10,8},{12,14},{14,12},{16,18},{18,... | collective-permute-start | bytes 786440 | tf_op jit(solution)/shard_map/ppermute | solution.py:33
  7.0 1.5 %collective-permute-start.2 = (bf16[512,256]{1,0:T(8,128)(2,1)S(1)}, bf16[512,256]{1,0:T(8,128)(2,1)S(1)}, u32[]{:S(2)}, u32[]{:S(2)}) collective-permute-start(bf16[512,256]{1,0:T(8,128)(2,1)S(1)} %get-tuple-element.86), channel_id=1, source_target_pairs={{0,4},{2,6},{4,0},{6,2},{8,12},{10,14},{12,8},{14,10},{16,20},{18,... | collective-permute-start | bytes 786440 | tf_op jit(solution)/shard_map/ppermute | solution.py:33
  9.3 1.3 collective-permute-done.other_ref.refs_4_
  11.4 4.1 %collective-permute-start.6 = (bf16[16,640]{1,0:T(8,128)(2,1)S(1)}, bf16[16,640]{1,0:T(8,128)(2,1)S(1)}, u32[]{:S(2)}, u32[]{:S(2)}) collective-permute-start(bf16[16,640]{1,0:T(8,128)(2,1)S(1)} %get-tuple-element.92.refs_4_.refs_11_), channel_id=1, source_target_pairs={{0,24},{2,26},{4,28},{6,30},{8,16},{10,18},{12,20},{14,22},{16,8},... | collective-permute-start | bytes 61448 | tf_op jit(solution)/shard_map/ppermute | solution.py:33
  15.5 1.8 %collective-permute-done.6.refs_7_.refs_14_ = bf16[16,640]{1,0:T(8,128)(2,1)S(1)} collective-permute-done((bf16[16,640]{1,0:T(8,128)(2,1)S(1)}, bf16[16,640]{1,0:T(8,128)(2,1)S(1)}, u32[]{:S(2)}, u32[]{:S(2)}) %collective-permute-start.6) | collective-permute-done | bytes 20512 | tf_op jit(solution)/shard_map/ppermute | solution.py:33
  17.5 2.3 %pack.3 = (bf16[544,256]{1,0:T(8,128)(2,1)S(1)}, bf16[544,256]{1,0:T(8,128)(2,1)S(1)}, bf16[544,256]{1,0:T(8,128)(2,1)S(1)}, bf16[544,256]{1,0:T(8,128)(2,1)S(1)}, f32[8,128]{1,0:T(8,128)}) custom-call(s32[2]{0:T(128)S(1)} %pad_add_fusion.place_ref.refs_0_, s32[2,4]{1,0:T(2,128)S(1)} %copy-done.6, s32[1,16]{1,0:T(1,128)S(1)} %copy-done.7, ...), custom_call_target="tpu_custom_call" | custom-call | flops 1 | bytes 1 | tf_op jit(solution)/shard_map/pack/pallas_call | solution.py:253
  21.7 1.8 %collective-permute-start.7 = (bf16[544,256]{1,0:T(8,128)(2,1)S(1)}, bf16[544,256]{1,0:T(8,128)(2,1)S(1)}, u32[]{:S(2)}, u32[]{:S(2)}) collective-permute-start(bf16[544,256]{1,0:T(8,128)(2,1)S(1)} %get-tuple-element.94), channel_id=1, source_target_pairs={{0,2},{2,0},{4,6},{6,4},{8,10},{10,8},{12,14},{14,12},{16,18},{18,... | collective-permute-start | bytes 835592 | tf_op jit(solution)/shard_map/ppermute | solution.py:33
  23.5 1.5 %collective-permute-start.8 = (bf16[544,256]{1,0:T(8,128)(2,1)S(1)}, bf16[544,256]{1,0:T(8,128)(2,1)S(1)}, u32[]{:S(2)}, u32[]{:S(2)}) collective-permute-start(bf16[544,256]{1,0:T(8,128)(2,1)S(1)} %get-tuple-element.95), channel_id=1, source_target_pairs={{0,4},{2,6},{4,0},{6,2},{8,12},{10,14},{12,8},{14,10},{16,20},{18,... | collective-permute-start | bytes 835592 | tf_op jit(solution)/shard_map/ppermute | solution.py:33
  25.3 3.1 %pack.4 = (bf16[1056,256]{1,0:T(8,128)(2,1)S(1)}, bf16[1056,256]{1,0:T(8,128)(2,1)}, bf16[1056,256]{1,0:T(8,128)(2,1)S(1)}, bf16[1056,256]{1,0:T(8,128)(2,1)S(1)}, f32[8,128]{1,0:T(8,128)S(1)}) custom-call(s32[2]{0:T(128)S(1)} %pad_add_fusion.place_ref.refs_0_, s32[2,4]{1,0:T(2,128)S(1)} %copy-done.6, s32[1,16]{1,0:T(1,128)S(1)} %copy-done.7, ...), custom_call_target="tpu_custom_call" | custom-call | flops 1 | bytes 1 | tf_op jit(solution)/shard_map/pack/pallas_call | solution.py:253
  28.4 1.7 %collective-permute-start.14 = (bf16[1056,256]{1,0:T(8,128)(2,1)}, bf16[1056,256]{1,0:T(8,128)(2,1)S(1)}, u32[]{:S(2)}, u32[]{:S(2)}) collective-permute-start(bf16[1056,256]{1,0:T(8,128)(2,1)} %get-tuple-element.111), channel_id=1, source_target_pairs={{0,2},{2,0},{4,6},{6,4},{8,10},{10,8},{12,14},{14,12},{16,18},{18,... | collective-permute-start | bytes 1622024 | tf_op jit(solution)/shard_map/ppermute | solution.py:33
  30.1 1.5 %collective-permute-start.15 = (bf16[1056,256]{1,0:T(8,128)(2,1)S(1)}, bf16[1056,256]{1,0:T(8,128)(2,1)S(1)}, u32[]{:S(2)}, u32[]{:S(2)}) collective-permute-start(bf16[1056,256]{1,0:T(8,128)(2,1)S(1)} %get-tuple-element.112), channel_id=1, source_target_pairs={{0,4},{2,6},{4,0},{6,2},{8,12},{10,14},{12,8},{14,10},{16,20},{18,... | collective-permute-start | bytes 1622024 | tf_op jit(solution)/shard_map/ppermute | solution.py:33
  31.6 2.4 %collective-permute-start.16 = (bf16[1056,256]{1,0:T(8,128)(2,1)S(1)}, bf16[1056,256]{1,0:T(8,128)(2,1)S(1)}, u32[]{:S(2)}, u32[]{:S(2)}) collective-permute-start(bf16[1056,256]{1,0:T(8,128)(2,1)S(1)} %get-tuple-element.113), channel_id=1, source_target_pairs={{0,6},{2,4},{4,2},{6,0},{8,14},{10,12},{12,10},{14,8},{16,22},{18,... | collective-permute-start | bytes 1622024 | tf_op jit(solution)/shard_map/ppermute | solution.py:33
  34.0 1.6 %pack.5 = (bf16[1056,128]{1,0:T(8,128)(2,1)S(1)}, bf16[1056,128]{1,0:T(8,128)(2,1)S(1)}, bf16[1056,128]{1,0:T(8,128)(2,1)S(1)}, bf16[1056,128]{1,0:T(8,128)(2,1)S(1)}, f32[8,128]{1,0:T(8,128)S(1)}) custom-call(s32[2]{0:T(128)S(1)} %pad_add_fusion.place_ref.refs_0_, s32[2,4]{1,0:T(2,128)S(1)} %copy-done.6, s32[1,16]{1,0:T(1,128)S(1)} %copy-done.7, ...), custom_call_target="tpu_custom_call" | custom-call | flops 1 | bytes 1 | tf_op jit(solution)/shard_map/pack/pallas_call | solution.py:253
  35.6 1.2 collective-permute-done.8.refs_6_
  36.8 1.7 %collective-permute-done.9.refs_7_ = bf16[544,256]{1,0:T(8,128)(2,1)S(1)} collective-permute-done((bf16[544,256]{1,0:T(8,128)(2,1)S(1)}, bf16[544,256]{1,0:T(8,128)(2,1)S(1)}, u32[]{:S(2)}, u32[]{:S(2)}) %collective-permute-start.9) | collective-permute-done | bytes 278560 | tf_op jit(solution)/shard_map/ppermute | solution.py:33
  40.6 4.3 %inner.3 = (bf16[512,256]{1,0:T(8,128)(2,1)S(1)}, bf16[1024,512]{1,0:T(8,128)(2,1)S(1)}, f32[32,512]{1,0:T(8,128)S(1)}) custom-call(s32[2]{0:T(128)S(1)} %pad_add_fusion.place_ref.refs_0_, bf16[512,256]{1,0:T(8,128)(2,1)S(1)} %get-tuple-element.84.refs_0_, bf16[512,256]{1,0:T(8,128)(2,1)S(1)} %collective-permute-done.1.refs_8_.refs_1_, ...), custom_call_target="tpu_custom_call" | custom-call | flops 1 | bytes 1 | tf_op jit(solution)/shard_map/inner/pallas_call | solution.py:72
  45.6 4.8 %outer.3 = (bf16[512,256]{1,0:T(8,128)(2,1)S(1)}, bf16[1024,512]{1,0:T(8,128)(2,1)S(1)}, bf16[16,256]{1,0:T(8,128)(2,1)S(1)}, bf16[528,256]{1,0:T(8,128)(2,1)S(1...) custom-call(s32[2]{0:T(128)S(1)} %pad_add_fusion.place_ref.refs_0_, ...), custom_call_target="tpu_custom_call" | custom-call | flops 1 | bytes 1 | tf_op jit(solution)/shard_map/outer/pallas_call | solution.py:72
  50.4 4.7 %collective-permute-start.12 = (bf16[528,256]{1,0:T(8,128)(2,1)S(1)}, bf16[528,256]{1,0:T(8,128)(2,1)S(1)}, u32[]{:S(2)}, u32[]{:S(2)}) collective-permute-start(bf16[528,256]{1,0:T(8,128)(2,1)S(1)} %get-tuple-element.108), channel_id=1, source_target_pairs={{0,8},{2,10},{4,12},{6,14},{8,0},{10,2},{12,4},{14,6},{16,24},{18,... | collective-permute-start | bytes 811016 | tf_op jit(solution)/shard_map/ppermute | solution.py:33
  55.8 1.6 %collective-permute-start.22 = (bf16[1056,128]{1,0:T(8,128)(2,1)S(1)}, bf16[1056,128]{1,0:T(8,128)(2,1)S(1)}, u32[]{:S(2)}, u32[]{:S(2)}) collective-permute-start(bf16[1056,128]{1,0:T(8,128)(2,1)S(1)} %get-tuple-element.127), channel_id=1, source_target_pairs={{0,2},{2,0},{4,6},{6,4},{8,10},{10,8},{12,14},{14,12},{16,18},{18,... | collective-permute-start | bytes 811016 | tf_op jit(solution)/shard_map/ppermute | solution.py:33
  57.3 1.2 collective-permute-done.15.refs_2_
  58.5 3.0 %collective-permute-start.23 = (bf16[1056,128]{1,0:T(8,128)(2,1)S(1)}, bf16[1056,128]{1,0:T(8,128)(2,1)S(1)}, u32[]{:S(2)}, u32[]{:S(2)}) collective-permute-start(bf16[1056,128]{1,0:T(8,128)(2,1)S(1)} %get-tuple-element.128), channel_id=1, source_target_pairs={{0,4},{2,6},{4,0},{6,2},{8,12},{10,14},{12,8},{14,10},{16,20},{18,... | collective-permute-start | bytes 811016 | tf_op jit(solution)/shard_map/ppermute | solution.py:33
  61.7 1.4 %collective-permute-start.24 = (bf16[1056,128]{1,0:T(8,128)(2,1)S(1)}, bf16[1056,128]{1,0:T(8,128)(2,1)S(1)}, u32[]{:S(2)}, u32[]{:S(2)}) collective-permute-start(bf16[1056,128]{1,0:T(8,128)(2,1)S(1)} %get-tuple-element.129), channel_id=1, source_target_pairs={{0,6},{2,4},{4,2},{6,0},{8,14},{10,12},{12,10},{14,8},{16,22},{18,... | collective-permute-start | bytes 811016 | tf_op jit(solution)/shard_map/ppermute | solution.py:33
  65.3 4.3 %inner.4 = (bf16[512,256]{1,0:T(8,128)(2,1)S(1)}, bf16[1024,512]{1,0:T(8,128)(2,1)S(1)}, f32[32,512]{1,0:T(8,128)S(1)}) custom-call(s32[2]{0:T(128)S(1)} %pad_add_fusion.place_ref.refs_0_, bf16[1056,256]{1,0:T(8,128)(2,1)S(1)} %get-tuple-element.110.refs_0_, bf16[1056,256]{1,0:T(8,128)(2,1)S(1)} %collective-permute-done.14.refs_1_, ...), custom_call_target="tpu_custom_call" | custom-call | flops 1 | bytes 1 | tf_op jit(solution)/shard_map/inner/pallas_call | solution.py:72
  69.6 2.1 %settle.3 = (bf16[784,256]{1,0:T(8,128)(2,1)S(1)}, bf16[784,256]{1,0:T(8,128)(2,1)S(1)}, bf16[784,256]{1,0:T(8,128)(2,1)}, bf16[784,256]{1,0:T(8,128)(2,1)S(1)}, f32[8,128]{1,0:T(8,128)S(1)}) custom-call(s32[2]{0:T(128)S(1)} %pad_add_fusion.place_ref.refs_0_, bf16[512,256]{1,0:T(8,128)(2,1)S(1)} %get-tuple-element.100.refs_0_, ...), custom_call_target="tpu_custom_call" | custom-call | flops 1 | bytes 1 | tf_op jit(solution)/shard_map/settle/pallas_call | solution.py:72
  72.4 1.9 %collective-permute-start.18 = (bf16[784,256]{1,0:T(8,128)(2,1)}, bf16[784,256]{1,0:T(8,128)(2,1)S(1)}, u32[]{:S(2)}, u32[]{:S(2)}) collective-permute-start(bf16[784,256]{1,0:T(8,128)(2,1)} %get-tuple-element.118), channel_id=1, source_target_pairs={{0,4},{2,6},{4,0},{6,2},{8,12},{10,14},{12,8},{14,10},{16,20},{18,... | collective-permute-start | bytes 1204232 | tf_op jit(solution)/shard_map/ppermute | solution.py:33
  75.8 5.4 %collective-permute-start.27 = (bf16[512,128]{1,0:T(8,128)(2,1)S(1)}, bf16[512,128]{1,0:T(8,128)(2,1)S(1)}, u32[]{:S(2)}, u32[]{:S(2)}) collective-permute-start(bf16[512,128]{1,0:T(8,128)(2,1)S(1)} %get-tuple-element.137), channel_id=1, source_target_pairs={{0,8},{2,10},{4,12},{6,14},{8,0},{10,2},{12,4},{14,6},{16,24},{18,... | collective-permute-start | bytes 393224 | tf_op jit(solution)/shard_map/ppermute | solution.py:33
  81.9 4.8 %outer.4 = (bf16[512,256]{1,0:T(8,128)(2,1)S(1)}, bf16[1024,512]{1,0:T(8,128)(2,1)S(1)}, bf16[16,256]{1,0:T(8,128)(2,1)S(1)}, bf16[528,256]{1,0:T(8,128)(2,1)S(1...) custom-call(s32[2]{0:T(128)S(1)} %pad_add_fusion.place_ref.refs_0_, ...), custom_call_target="tpu_custom_call", output_to_operand_aliasing={{5}: (8, {}), {6}: (9, {})} | custom-call | flops 1 | bytes 1 | tf_op jit(solution)/shard_map/outer/pallas_call | solution.py:72
  86.7 1.4 %collective-permute-start.25 = (bf16[528,256]{1,0:T(8,128)(2,1)S(1)}, bf16[528,256]{1,0:T(8,128)(2,1)S(1)}, u32[]{:S(2)}, u32[]{:S(2)}) collective-permute-start(bf16[528,256]{1,0:T(8,128)(2,1)S(1)} %get-tuple-element.135), channel_id=1, source_target_pairs={{0,8},{2,10},{4,12},{6,14},{8,0},{10,2},{12,4},{14,6},{16,24},{18,... | collective-permute-start | bytes 811016 | tf_op jit(solution)/shard_map/ppermute | solution.py:33
  88.8 2.5 %inner.5 = (bf16[512,128]{1,0:T(8,128)(2,1)S(1)}, bf16[1024,256]{1,0:T(8,128)(2,1)S(1)}, f32[32,256]{1,0:T(8,128)S(1)}) custom-call(s32[2]{0:T(128)S(1)} %pad_add_fusion.place_ref.refs_0_, bf16[1056,128]{1,0:T(8,128)(2,1)S(1)} %get-tuple-element.126.refs_0_, bf16[1056,128]{1,0:T(8,128)(2,1)S(1)} %collective-permute-done.22.refs_1_, ...), custom_call_target="tpu_custom_call" | custom-call | flops 1 | bytes 1 | tf_op jit(solution)/shard_map/inner/pallas_call | solution.py:72
  93.3 1.6 %settle.4 = (bf16[784,256]{1,0:T(8,128)(2,1)S(1)}, bf16[784,256]{1,0:T(8,128)(2,1)S(1)}, bf16[784,256]{1,0:T(8,128)(2,1)S(1)}, bf16[784,256]{1,0:T(8,128)(2,1)S(1)}, f32[8,128]{1,0:T(8,128)S(1)}) custom-call(s32[2]{0:T(128)S(1)} %pad_add_fusion.place_ref.refs_0_, bf16[512,256]{1,0:T(8,128)(2,1)S(1)} %get-tuple-element.120.refs_0_, ...), custom_call_target="tpu_custom_call" | custom-call | flops 1 | bytes 1 | tf_op jit(solution)/shard_map/settle/pallas_call | solution.py:72
  95.5 1.5 %collective-permute-start.30 = (bf16[784,256]{1,0:T(8,128)(2,1)S(1)}, bf16[784,256]{1,0:T(8,128)(2,1)S(1)}, u32[]{:S(2)}, u32[]{:S(2)}) collective-permute-start(bf16[784,256]{1,0:T(8,128)(2,1)S(1)} %get-tuple-element.142), channel_id=1, source_target_pairs={{0,4},{2,6},{4,0},{6,2},{8,12},{10,14},{12,8},{14,10},{16,20},{18,... | collective-permute-start | bytes 1204232 | tf_op jit(solution)/shard_map/ppermute | solution.py:33
  97.0 1.4 %collective-permute-start.31 = (bf16[784,256]{1,0:T(8,128)(2,1)S(1)}, bf16[784,256]{1,0:T(8,128)(2,1)S(1)}, u32[]{:S(2)}, u32[]{:S(2)}) collective-permute-start(bf16[784,256]{1,0:T(8,128)(2,1)S(1)} %get-tuple-element.143), channel_id=1, source_target_pairs={{0,6},{2,4},{4,2},{6,0},{8,14},{10,12},{12,10},{14,8},{16,22},{18,... | collective-permute-start | bytes 1204232 | tf_op jit(solution)/shard_map/ppermute | solution.py:33
  98.4 2.7 %outer.5 = (bf16[512,128]{1,0:T(8,128)(2,1)S(1)}, bf16[1024,256]{1,0:T(8,128)(2,1)S(1)}, bf16[16,128]{1,0:T(8,128)(2,1)S(1)}, bf16[528,128]{1,0:T(8,128)(2,1)S(1...) custom-call(s32[2]{0:T(128)S(1)} %pad_add_fusion.place_ref.refs_0_, ...), custom_call_target="tpu_custom_call", output_to_operand_aliasing={{5}: (8, {}), {6}: (9, {})} | custom-call | flops 1 | bytes 1 | tf_op jit(solution)/shard_map/outer/pallas_call | solution.py:72
  101.2 4.6 %collective-permute-start.34 = (bf16[16,640]{1,0:T(8,128)(2,1)S(1)}, bf16[16,640]{1,0:T(8,128)(2,1)S(1)}, u32[]{:S(2)}, u32[]{:S(2)}) collective-permute-start(bf16[16,640]{1,0:T(8,128)(2,1)S(1)} %get-tuple-element.154), channel_id=1, source_target_pairs={{0,16},{2,18},{4,20},{6,22},{8,24},{10,26},{12,28},{14,30},{16,0},... | collective-permute-start | bytes 61448 | tf_op jit(solution)/shard_map/ppermute | solution.py:33
  105.8 2.3 %collective-permute-start.35 = (bf16[16,640]{1,0:T(8,128)(2,1)S(1)}, bf16[16,640]{1,0:T(8,128)(2,1)S(1)}, u32[]{:S(2)}, u32[]{:S(2)}) collective-permute-start(bf16[16,640]{1,0:T(8,128)(2,1)S(1)} %get-tuple-element.155), channel_id=1, source_target_pairs={{0,24},{2,26},{4,28},{6,30},{8,16},{10,18},{12,20},{14,22},{16,8},... | collective-permute-start | bytes 61448 | tf_op jit(solution)/shard_map/ppermute | solution.py:33
  108.1 2.3 %collective-permute-start.32 = (bf16[528,128]{1,0:T(8,128)(2,1)S(1)}, bf16[528,128]{1,0:T(8,128)(2,1)S(1)}, u32[]{:S(2)}, u32[]{:S(2)}) collective-permute-start(bf16[528,128]{1,0:T(8,128)(2,1)S(1)} %get-tuple-element.152), channel_id=1, source_target_pairs={{0,8},{2,10},{4,12},{6,14},{8,0},{10,2},{12,4},{14,6},{16,24},{18,... | collective-permute-start | bytes 405512 | tf_op jit(solution)/shard_map/ppermute | solution.py:33
  112.0 1.4 %collective-permute-done.32.refs_5_ = bf16[528,128]{1,0:T(8,128)(2,1)S(1)} collective-permute-done((bf16[528,128]{1,0:T(8,128)(2,1)S(1)}, bf16[528,128]{1,0:T(8,128)(2,1)S(1)}, u32[]{:S(2)}, u32[]{:S(2)}) %collective-permute-start.32) | collective-permute-done | bytes 135200 | tf_op jit(solution)/shard_map/ppermute | solution.py:33
  113.4 1.5 %settle.5 = (bf16[816,128]{1,0:T(8,128)(2,1)S(1)}, bf16[816,128]{1,0:T(8,128)(2,1)S(1)}, bf16[816,128]{1,0:T(8,128)(2,1)S(1)}, bf16[816,128]{1,0:T(8,128)(2,1)S(1)}, f32[8,128]{1,0:T(8,128)S(1)}) custom-call(s32[2]{0:T(128)S(1)} %pad_add_fusion.place_ref.refs_0_, bf16[512,128]{1,0:T(8,128)(2,1)S(1)} %get-tuple-element.144.refs_0_, ...), custom_call_target="tpu_custom_call" | custom-call | flops 1 | bytes 1 | tf_op jit(solution)/shard_map/settle/pallas_call | solution.py:72
  115.5 1.5 %collective-permute-start.37 = (bf16[816,128]{1,0:T(8,128)(2,1)S(1)}, bf16[816,128]{1,0:T(8,128)(2,1)S(1)}, u32[]{:S(2)}, u32[]{:S(2)}) collective-permute-start(bf16[816,128]{1,0:T(8,128)(2,1)S(1)} %get-tuple-element.158), channel_id=1, source_target_pairs={{0,4},{2,6},{4,0},{6,2},{8,12},{10,14},{12,8},{14,10},{16,20},{18,... | collective-permute-start | bytes 626696 | tf_op jit(solution)/shard_map/ppermute | solution.py:33
  117.0 1.4 %collective-permute-start.38 = (bf16[816,128]{1,0:T(8,128)(2,1)S(1)}, bf16[816,128]{1,0:T(8,128)(2,1)S(1)}, u32[]{:S(2)}, u32[]{:S(2)}) collective-permute-start(bf16[816,128]{1,0:T(8,128)(2,1)S(1)} %get-tuple-element.159), channel_id=1, source_target_pairs={{0,6},{2,4},{4,2},{6,0},{8,14},{10,12},{12,10},{14,8},{16,22},{18,... | collective-permute-start | bytes 626696 | tf_op jit(solution)/shard_map/ppermute | solution.py:33
  119.5 1.3 %collective-permute-done.36.refs_9_ = bf16[816,128]{1,0:T(8,128)(2,1)S(1)} collective-permute-done((bf16[816,128]{1,0:T(8,128)(2,1)S(1)}, bf16[816,128]{1,0:T(8,128)(2,1)S(1)}, u32[]{:S(2)}, u32[]{:S(2)}) %collective-permute-start.36) | collective-permute-done | bytes 208928 | tf_op jit(solution)/shard_map/ppermute | solution.py:33
  120.8 1.8 %collective-permute-done.37.refs_10_ = bf16[816,128]{1,0:T(8,128)(2,1)S(1)} collective-permute-done((bf16[816,128]{1,0:T(8,128)(2,1)S(1)}, bf16[816,128]{1,0:T(8,128)(2,1)S(1)}, u32[]{:S(2)}, u32[]{:S(2)}) %collective-permute-start.37) | collective-permute-done | bytes 208928 | tf_op jit(solution)/shard_map/ppermute | solution.py:33
  122.6 1.3 %collective-permute-done.38.refs_11_ = bf16[816,128]{1,0:T(8,128)(2,1)S(1)} collective-permute-done((bf16[816,128]{1,0:T(8,128)(2,1)S(1)}, bf16[816,128]{1,0:T(8,128)(2,1)S(1)}, u32[]{:S(2)}, u32[]{:S(2)}) %collective-permute-start.38) | collective-permute-done | bytes 208928 | tf_op jit(solution)/shard_map/ppermute | solution.py:33
  124.0 1.8 %total_dots.1 = (f32[256,128]{1,0:T(8,128)S(1)}, f32[8,2560]{1,0:T(8,128)S(1)}) custom-call(s32[2]{0:T(128)S(1)} %pad_add_fusion.place_ref.refs_0_, s32[2]{0:T(128)S(1)} %copy-done.8, bf16[16,2560]{1,0:T(8,128)(2,1)S(1)} %get-tuple-element.83.refs_11_.raw_ref, bf16[256,2560]{1,0:T(8,128)(2,1)S(1)} %copy-done.2, bf16[256,2560]{1,0:T(8,128)(2,1)} %refs_14_.1, ...), custom_call_target="tpu_custom_call" | custom-call | flops 1 | bytes 1 | tf_op jit(solution)/shard_map/total_dots/pallas_call | solution.py:590
  125.8 1.3 %collective-permute-done.39.dot_other_ref = f32[256,128]{1,0:T(8,128)S(1)} collective-permute-done((f32[256,128]{1,0:T(8,128)S(1)}, f32[256,128]{1,0:T(8,128)S(1)}, u32[]{:S(2)}, u32[]{:S(2)}) %collective-permute-start.39) | collective-permute-done | bytes 131104 | tf_op jit(solution)/shard_map/ppermute | solution.py:698
  127.1 4.7 %finish.1 = (bf16[256,2560]{1,0:T(8,128)(2,1)}, bf16[256,2560]{1,0:T(8,128)(2,1)}, bf16[256,2560]{1,0:T(8,128)(2,1)}) custom-call(s32[2]{0:T(128)S(1)} %pad_add_fusion.place_ref.refs_0_, s32[2]{0:T(128)S(1)} %copy-done.8, f32[256,128]{1,0:T(8,128)S(1)} %squares.1.own_ref.refs_3_, f32[256,128]{1,0:T(8,128)S(1)} %collective-permute-done.other_ref.refs_4_, ...), custom_call_target="tpu_custom_call" | custom-call | flops 1 | bytes 1 | tf_op jit(solution)/shard_map/finish/pallas_call | solution.py:685
  (80 shorter events, 19.7 us)
Async XLA Ops:
  3.4 5.2 %copy-start = (bf16[256,2560]{1,0:T(8,128)(2,1)S(1)}, bf16[256,2560]{1,0:T(8,128)(2,1)}, u32[]{:S(2)}) copy-start(bf16[256,2560]{1,0:T(8,128)(2,1)} %refs_14_.1) | copy-start | bytes 3932164
  3.4 5.2 %copy-start.1 = (bf16[256,2560]{1,0:T(8,128)(2,1)S(1)}, bf16[256,2560]{1,0:T(8,128)(2,1)}, u32[]{:S(2)}) copy-start(bf16[256,2560]{1,0:T(8,128)(2,1)} %refs_13_.1) | copy-start | bytes 3932164
  4.0 17.0 %collective-permute-start.1 = (bf16[512,256]{1,0:T(8,128)(2,1)S(1)}, bf16[512,256]{1,0:T(8,128)(2,1)S(1)}, u32[]{:S(2)}, u32[]{:S(2)}) collective-permute-start(bf16[512,256]{1,0:T(8,128)(2,1)S(1)} %get-tuple-element.85), channel_id=1, source_target_pairs={{0,2},{2,0},{4,6},{6,4},{8,10},{10,8},{12,14},{14,12},{16,18},{18,... | collective-permute-start | bytes 786440 | tf_op jit(solution)/shard_map/ppermute | solution.py:33
  7.0 14.0 %collective-permute-start.2 = (bf16[512,256]{1,0:T(8,128)(2,1)S(1)}, bf16[512,256]{1,0:T(8,128)(2,1)S(1)}, u32[]{:S(2)}, u32[]{:S(2)}) collective-permute-start(bf16[512,256]{1,0:T(8,128)(2,1)S(1)} %get-tuple-element.86), channel_id=1, source_target_pairs={{0,4},{2,6},{4,0},{6,2},{8,12},{10,14},{12,8},{14,10},{16,20},{18,... | collective-permute-start | bytes 786440 | tf_op jit(solution)/shard_map/ppermute | solution.py:33
  8.5 2.0 %copy-start.4 = (bf16[256,2560]{1,0:T(8,128)(2,1)S(1)}, bf16[256,2560]{1,0:T(8,128)(2,1)}, u32[]{:S(2)}) copy-start(bf16[256,2560]{1,0:T(8,128)(2,1)} %refs_6_.5) | copy-start | bytes 3932164
  8.5 2.0 %copy-start.8 = (s32[2]{0:T(128)S(1)}, s32[2]{0:T(128)}, u32[]{:S(2)}) copy-start(s32[2]{0:T(128)} %ids_ref.5) | copy-start | bytes 28
  8.5 12.5 %collective-permute-start.3 = (bf16[512,256]{1,0:T(8,128)(2,1)S(1)}, bf16[512,256]{1,0:T(8,128)(2,1)S(1)}, u32[]{:S(2)}, u32[]{:S(2)}) collective-permute-start(bf16[512,256]{1,0:T(8,128)(2,1)S(1)} %get-tuple-element.87), channel_id=1, source_target_pairs={{0,6},{2,4},{4,2},{6,0},{8,14},{10,12},{12,10},{14,8},{16,22},{18,... | collective-permute-start | bytes 786440 | tf_op jit(solution)/shard_map/ppermute | solution.py:33
  9.2 1.4 %collective-permute-start = (f32[256,128]{1,0:T(8,128)S(1)}, f32[256,128]{1,0:T(8,128)S(1)}, u32[]{:S(2)}, u32[]{:S(2)}) collective-permute-start(f32[256,128]{1,0:T(8,128)S(1)} %squares.1.own_ref.refs_3_), channel_id=1, source_target_pairs={{0,1},{1,0},{2,3},{3,2},{4,5},{5,4},{6,7},{7,6},{8,9},{9,8},{10,11... | collective-permute-start | bytes 393224 | tf_op jit(solution)/shard_map/ppermute | solution.py:698
  9.2 8.2 %copy-start.10 = (f32[2560]{0:T(1024)S(1)}, f32[2560]{0:T(1024)}, u32[]{:S(2)}) copy-start(f32[2560]{0:T(1024)} %param.13) | copy-start | bytes 30724
  9.2 8.2 %copy-start.6 = (s32[2,4]{1,0:T(2,128)S(1)}, s32[2,4]{1,0:T(2,128)}, u32[]{:S(2)}) copy-start(s32[2,4]{1,0:T(2,128)} %refs_1_.7) | copy-start | bytes 100
  9.3 8.2 %copy-start.7 = (s32[1,16]{1,0:T(1,128)S(1)}, s32[1,16]{1,0:T(1,128)}, u32[]{:S(2)}) copy-start(s32[1,16]{1,0:T(1,128)} %refs_2_.5) | copy-start | bytes 196
  11.4 5.9 %collective-permute-start.6 = (bf16[16,640]{1,0:T(8,128)(2,1)S(1)}, bf16[16,640]{1,0:T(8,128)(2,1)S(1)}, u32[]{:S(2)}, u32[]{:S(2)}) collective-permute-start(bf16[16,640]{1,0:T(8,128)(2,1)S(1)} %get-tuple-element.92.refs_4_.refs_11_), channel_id=1, source_target_pairs={{0,24},{2,26},{4,28},{6,30},{8,16},{10,18},{12,20},{14,22},{16,8},... | collective-permute-start | bytes 61448 | tf_op jit(solution)/shard_map/ppermute | solution.py:33
  15.5 4.7 %collective-permute-start.5 = (bf16[16,640]{1,0:T(8,128)(2,1)S(1)}, bf16[16,640]{1,0:T(8,128)(2,1)S(1)}, u32[]{:S(2)}, u32[]{:S(2)}) collective-permute-start(bf16[16,640]{1,0:T(8,128)(2,1)S(1)} %get-tuple-element.92.refs_4_.refs_11_), channel_id=1, source_target_pairs={{0,16},{2,18},{4,20},{6,22},{8,24},{10,26},{12,28},{14,30},{16,0},... | collective-permute-start | bytes 61448 | tf_op jit(solution)/shard_map/ppermute | solution.py:33
  17.2 3.8 %collective-permute-start.4 = (bf16[16,640]{1,0:T(8,128)(2,1)S(1)}, bf16[16,640]{1,0:T(8,128)(2,1)S(1)}, u32[]{:S(2)}, u32[]{:S(2)}) collective-permute-start(bf16[16,640]{1,0:T(8,128)(2,1)S(1)} %get-tuple-element.92.refs_4_.refs_11_), channel_id=1, source_target_pairs={{0,8},{2,10},{4,12},{6,14},{8,0},{10,2},{12,4},{14,6},{16,24},{18,... | collective-permute-start | bytes 61448 | tf_op jit(solution)/shard_map/ppermute | solution.py:33
  21.7 9.9 %collective-permute-start.7 = (bf16[544,256]{1,0:T(8,128)(2,1)S(1)}, bf16[544,256]{1,0:T(8,128)(2,1)S(1)}, u32[]{:S(2)}, u32[]{:S(2)}) collective-permute-start(bf16[544,256]{1,0:T(8,128)(2,1)S(1)} %get-tuple-element.94), channel_id=1, source_target_pairs={{0,2},{2,0},{4,6},{6,4},{8,10},{10,8},{12,14},{14,12},{16,18},{18,... | collective-permute-start | bytes 835592 | tf_op jit(solution)/shard_map/ppermute | solution.py:33
  23.5 13.4 %collective-permute-start.8 = (bf16[544,256]{1,0:T(8,128)(2,1)S(1)}, bf16[544,256]{1,0:T(8,128)(2,1)S(1)}, u32[]{:S(2)}, u32[]{:S(2)}) collective-permute-start(bf16[544,256]{1,0:T(8,128)(2,1)S(1)} %get-tuple-element.95), channel_id=1, source_target_pairs={{0,4},{2,6},{4,0},{6,2},{8,12},{10,14},{12,8},{14,10},{16,20},{18,... | collective-permute-start | bytes 835592 | tf_op jit(solution)/shard_map/ppermute | solution.py:33
  25.0 13.5 %collective-permute-start.9 = (bf16[544,256]{1,0:T(8,128)(2,1)S(1)}, bf16[544,256]{1,0:T(8,128)(2,1)S(1)}, u32[]{:S(2)}, u32[]{:S(2)}) collective-permute-start(bf16[544,256]{1,0:T(8,128)(2,1)S(1)} %get-tuple-element.96), channel_id=1, source_target_pairs={{0,6},{2,4},{4,2},{6,0},{8,14},{10,12},{12,10},{14,8},{16,22},{18,... | collective-permute-start | bytes 835592 | tf_op jit(solution)/shard_map/ppermute | solution.py:33
  25.3 8.8 %copy-start.2 = (bf16[256,2560]{1,0:T(8,128)(2,1)S(1)}, bf16[256,2560]{1,0:T(8,128)(2,1)}, u32[]{:S(2)}) copy-start(bf16[256,2560]{1,0:T(8,128)(2,1)} %refs_13_.1) | copy-start | bytes 3932164
  28.4 27.4 %collective-permute-start.14 = (bf16[1056,256]{1,0:T(8,128)(2,1)}, bf16[1056,256]{1,0:T(8,128)(2,1)S(1)}, u32[]{:S(2)}, u32[]{:S(2)}) collective-permute-start(bf16[1056,256]{1,0:T(8,128)(2,1)} %get-tuple-element.111), channel_id=1, source_target_pairs={{0,2},{2,0},{4,6},{6,4},{8,10},{10,8},{12,14},{14,12},{16,18},{18,... | collective-permute-start | bytes 1622024 | tf_op jit(solution)/shard_map/ppermute | solution.py:33
  30.1 28.4 %collective-permute-start.15 = (bf16[1056,256]{1,0:T(8,128)(2,1)S(1)}, bf16[1056,256]{1,0:T(8,128)(2,1)S(1)}, u32[]{:S(2)}, u32[]{:S(2)}) collective-permute-start(bf16[1056,256]{1,0:T(8,128)(2,1)S(1)} %get-tuple-element.112), channel_id=1, source_target_pairs={{0,4},{2,6},{4,0},{6,2},{8,12},{10,14},{12,8},{14,10},{16,20},{18,... | collective-permute-start | bytes 1622024 | tf_op jit(solution)/shard_map/ppermute | solution.py:33
  31.6 30.1 %collective-permute-start.16 = (bf16[1056,256]{1,0:T(8,128)(2,1)S(1)}, bf16[1056,256]{1,0:T(8,128)(2,1)S(1)}, u32[]{:S(2)}, u32[]{:S(2)}) collective-permute-start(bf16[1056,256]{1,0:T(8,128)(2,1)S(1)} %get-tuple-element.113), channel_id=1, source_target_pairs={{0,6},{2,4},{4,2},{6,0},{8,14},{10,12},{12,10},{14,8},{16,22},{18,... | collective-permute-start | bytes 1622024 | tf_op jit(solution)/shard_map/ppermute | solution.py:33
  39.1 6.4 %collective-permute-start.10 = (bf16[512,256]{1,0:T(8,128)(2,1)S(1)}, bf16[512,256]{1,0:T(8,128)(2,1)S(1)}, u32[]{:S(2)}, u32[]{:S(2)}) collective-permute-start(bf16[512,256]{1,0:T(8,128)(2,1)S(1)} %get-tuple-element.102), channel_id=1, source_target_pairs={{0,8},{2,10},{4,12},{6,14},{8,0},{10,2},{12,4},{14,6},{16,24},{18,... | collective-permute-start | bytes 786440 | tf_op jit(solution)/shard_map/ppermute | solution.py:33
  40.0 5.6 %collective-permute-start.11 = (bf16[512,256]{1,0:T(8,128)(2,1)S(1)}, bf16[512,256]{1,0:T(8,128)(2,1)S(1)}, u32[]{:S(2)}, u32[]{:S(2)}) collective-permute-start(bf16[512,256]{1,0:T(8,128)(2,1)S(1)} %get-tuple-element.103), channel_id=1, source_target_pairs={{8,16},{10,18},{12,20},{14,22},{16,8},{18,10},{20,12},{22,14},{9,1... | collective-permute-start | bytes 786440 | tf_op jit(solution)/shard_map/ppermute | solution.py:39
  50.4 14.3 %collective-permute-start.12 = (bf16[528,256]{1,0:T(8,128)(2,1)S(1)}, bf16[528,256]{1,0:T(8,128)(2,1)S(1)}, u32[]{:S(2)}, u32[]{:S(2)}) collective-permute-start(bf16[528,256]{1,0:T(8,128)(2,1)S(1)} %get-tuple-element.108), channel_id=1, source_target_pairs={{0,8},{2,10},{4,12},{6,14},{8,0},{10,2},{12,4},{14,6},{16,24},{18,... | collective-permute-start | bytes 811016 | tf_op jit(solution)/shard_map/ppermute | solution.py:33
  55.1 8.9 %collective-permute-start.13 = (bf16[512,256]{1,0:T(8,128)(2,1)S(1)}, bf16[512,256]{1,0:T(8,128)(2,1)S(1)}, u32[]{:S(2)}, u32[]{:S(2)}) collective-permute-start(bf16[512,256]{1,0:T(8,128)(2,1)S(1)} %get-tuple-element.109), channel_id=1, source_target_pairs={{8,16},{10,18},{12,20},{14,22},{16,8},{18,10},{20,12},{22,14},{9,1... | collective-permute-start | bytes 786440 | tf_op jit(solution)/shard_map/ppermute | solution.py:39
  55.8 15.9 %collective-permute-start.22 = (bf16[1056,128]{1,0:T(8,128)(2,1)S(1)}, bf16[1056,128]{1,0:T(8,128)(2,1)S(1)}, u32[]{:S(2)}, u32[]{:S(2)}) collective-permute-start(bf16[1056,128]{1,0:T(8,128)(2,1)S(1)} %get-tuple-element.127), channel_id=1, source_target_pairs={{0,2},{2,0},{4,6},{6,4},{8,10},{10,8},{12,14},{14,12},{16,18},{18,... | collective-permute-start | bytes 811016 | tf_op jit(solution)/shard_map/ppermute | solution.py:33
  58.5 13.9 %collective-permute-start.23 = (bf16[1056,128]{1,0:T(8,128)(2,1)S(1)}, bf16[1056,128]{1,0:T(8,128)(2,1)S(1)}, u32[]{:S(2)}, u32[]{:S(2)}) collective-permute-start(bf16[1056,128]{1,0:T(8,128)(2,1)S(1)} %get-tuple-element.128), channel_id=1, source_target_pairs={{0,4},{2,6},{4,0},{6,2},{8,12},{10,14},{12,8},{14,10},{16,20},{18,... | collective-permute-start | bytes 811016 | tf_op jit(solution)/shard_map/ppermute | solution.py:33
  61.7 12.6 %collective-permute-start.24 = (bf16[1056,128]{1,0:T(8,128)(2,1)S(1)}, bf16[1056,128]{1,0:T(8,128)(2,1)S(1)}, u32[]{:S(2)}, u32[]{:S(2)}) collective-permute-start(bf16[1056,128]{1,0:T(8,128)(2,1)S(1)} %get-tuple-element.129), channel_id=1, source_target_pairs={{0,6},{2,4},{4,2},{6,0},{8,14},{10,12},{12,10},{14,8},{16,22},{18,... | collective-permute-start | bytes 811016 | tf_op jit(solution)/shard_map/ppermute | solution.py:33
  64.0 11.8 %collective-permute-start.20 = (bf16[512,256]{1,0:T(8,128)(2,1)S(1)}, bf16[512,256]{1,0:T(8,128)(2,1)S(1)}, u32[]{:S(2)}, u32[]{:S(2)}) collective-permute-start(bf16[512,256]{1,0:T(8,128)(2,1)S(1)} %get-tuple-element.122), channel_id=1, source_target_pairs={{0,8},{2,10},{4,12},{6,14},{8,0},{10,2},{12,4},{14,6},{16,24},{18,... | collective-permute-start | bytes 786440 | tf_op jit(solution)/shard_map/ppermute | solution.py:33
  64.7 16.6 %collective-permute-start.21 = (bf16[512,256]{1,0:T(8,128)(2,1)S(1)}, bf16[512,256]{1,0:T(8,128)(2,1)S(1)}, u32[]{:S(2)}, u32[]{:S(2)}) collective-permute-start(bf16[512,256]{1,0:T(8,128)(2,1)S(1)} %get-tuple-element.123), channel_id=1, source_target_pairs={{8,16},{10,18},{12,20},{14,22},{16,8},{18,10},{20,12},{22,14},{9,1... | collective-permute-start | bytes 786440 | tf_op jit(solution)/shard_map/ppermute | solution.py:39
  71.7 19.6 %collective-permute-start.17 = (bf16[784,256]{1,0:T(8,128)(2,1)S(1)}, bf16[784,256]{1,0:T(8,128)(2,1)S(1)}, u32[]{:S(2)}, u32[]{:S(2)}) collective-permute-start(bf16[784,256]{1,0:T(8,128)(2,1)S(1)} %get-tuple-element.117), channel_id=1, source_target_pairs={{0,2},{2,0},{4,6},{6,4},{8,10},{10,8},{12,14},{14,12},{16,18},{18,... | collective-permute-start | bytes 1204232 | tf_op jit(solution)/shard_map/ppermute | solution.py:33
  72.4 18.9 %collective-permute-start.18 = (bf16[784,256]{1,0:T(8,128)(2,1)}, bf16[784,256]{1,0:T(8,128)(2,1)S(1)}, u32[]{:S(2)}, u32[]{:S(2)}) collective-permute-start(bf16[784,256]{1,0:T(8,128)(2,1)} %get-tuple-element.118), channel_id=1, source_target_pairs={{0,4},{2,6},{4,0},{6,2},{8,12},{10,14},{12,8},{14,10},{16,20},{18,... | collective-permute-start | bytes 1204232 | tf_op jit(solution)/shard_map/ppermute | solution.py:33
  74.3 17.0 %collective-permute-start.19 = (bf16[784,256]{1,0:T(8,128)(2,1)S(1)}, bf16[784,256]{1,0:T(8,128)(2,1)S(1)}, u32[]{:S(2)}, u32[]{:S(2)}) collective-permute-start(bf16[784,256]{1,0:T(8,128)(2,1)S(1)} %get-tuple-element.119), channel_id=1, source_target_pairs={{0,6},{2,4},{4,2},{6,0},{8,14},{10,12},{12,10},{14,8},{16,22},{18,... | collective-permute-start | bytes 1204232 | tf_op jit(solution)/shard_map/ppermute | solution.py:33
  75.8 10.9 %collective-permute-start.27 = (bf16[512,128]{1,0:T(8,128)(2,1)S(1)}, bf16[512,128]{1,0:T(8,128)(2,1)S(1)}, u32[]{:S(2)}, u32[]{:S(2)}) collective-permute-start(bf16[512,128]{1,0:T(8,128)(2,1)S(1)} %get-tuple-element.137), channel_id=1, source_target_pairs={{0,8},{2,10},{4,12},{6,14},{8,0},{10,2},{12,4},{14,6},{16,24},{18,... | collective-permute-start | bytes 393224 | tf_op jit(solution)/shard_map/ppermute | solution.py:33
  81.2 6.9 %collective-permute-start.28 = (bf16[512,128]{1,0:T(8,128)(2,1)S(1)}, bf16[512,128]{1,0:T(8,128)(2,1)S(1)}, u32[]{:S(2)}, u32[]{:S(2)}) collective-permute-start(bf16[512,128]{1,0:T(8,128)(2,1)S(1)} %get-tuple-element.138), channel_id=1, source_target_pairs={{8,16},{10,18},{12,20},{14,22},{16,8},{18,10},{20,12},{22,14},{9,1... | collective-permute-start | bytes 393224 | tf_op jit(solution)/shard_map/ppermute | solution.py:39
  86.7 6.5 %collective-permute-start.25 = (bf16[528,256]{1,0:T(8,128)(2,1)S(1)}, bf16[528,256]{1,0:T(8,128)(2,1)S(1)}, u32[]{:S(2)}, u32[]{:S(2)}) collective-permute-start(bf16[528,256]{1,0:T(8,128)(2,1)S(1)} %get-tuple-element.135), channel_id=1, source_target_pairs={{0,8},{2,10},{4,12},{6,14},{8,0},{10,2},{12,4},{14,6},{16,24},{18,... | collective-permute-start | bytes 811016 | tf_op jit(solution)/shard_map/ppermute | solution.py:33
  88.1 4.2 %collective-permute-start.26 = (bf16[512,256]{1,0:T(8,128)(2,1)S(1)}, bf16[512,256]{1,0:T(8,128)(2,1)S(1)}, u32[]{:S(2)}, u32[]{:S(2)}) collective-permute-start(bf16[512,256]{1,0:T(8,128)(2,1)S(1)} %get-tuple-element.136), channel_id=1, source_target_pairs={{8,16},{10,18},{12,20},{14,22},{16,8},{18,10},{20,12},{22,14},{9,1... | collective-permute-start | bytes 786440 | tf_op jit(solution)/shard_map/ppermute | solution.py:39
  94.9 22.2 %collective-permute-start.29 = (bf16[784,256]{1,0:T(8,128)(2,1)S(1)}, bf16[784,256]{1,0:T(8,128)(2,1)S(1)}, u32[]{:S(2)}, u32[]{:S(2)}) collective-permute-start(bf16[784,256]{1,0:T(8,128)(2,1)S(1)} %get-tuple-element.141), channel_id=1, source_target_pairs={{0,2},{2,0},{4,6},{6,4},{8,10},{10,8},{12,14},{14,12},{16,18},{18,... | collective-permute-start | bytes 1204232 | tf_op jit(solution)/shard_map/ppermute | solution.py:33
  95.5 23.0 %collective-permute-start.30 = (bf16[784,256]{1,0:T(8,128)(2,1)S(1)}, bf16[784,256]{1,0:T(8,128)(2,1)S(1)}, u32[]{:S(2)}, u32[]{:S(2)}) collective-permute-start(bf16[784,256]{1,0:T(8,128)(2,1)S(1)} %get-tuple-element.142), channel_id=1, source_target_pairs={{0,4},{2,6},{4,0},{6,2},{8,12},{10,14},{12,8},{14,10},{16,20},{18,... | collective-permute-start | bytes 1204232 | tf_op jit(solution)/shard_map/ppermute | solution.py:33
  97.0 21.5 %collective-permute-start.31 = (bf16[784,256]{1,0:T(8,128)(2,1)S(1)}, bf16[784,256]{1,0:T(8,128)(2,1)S(1)}, u32[]{:S(2)}, u32[]{:S(2)}) collective-permute-start(bf16[784,256]{1,0:T(8,128)(2,1)S(1)} %get-tuple-element.143), channel_id=1, source_target_pairs={{0,6},{2,4},{4,2},{6,0},{8,14},{10,12},{12,10},{14,8},{16,22},{18,... | collective-permute-start | bytes 1204232 | tf_op jit(solution)/shard_map/ppermute | solution.py:33
  101.2 7.0 %collective-permute-start.34 = (bf16[16,640]{1,0:T(8,128)(2,1)S(1)}, bf16[16,640]{1,0:T(8,128)(2,1)S(1)}, u32[]{:S(2)}, u32[]{:S(2)}) collective-permute-start(bf16[16,640]{1,0:T(8,128)(2,1)S(1)} %get-tuple-element.154), channel_id=1, source_target_pairs={{0,16},{2,18},{4,20},{6,22},{8,24},{10,26},{12,28},{14,30},{16,0},... | collective-permute-start | bytes 61448 | tf_op jit(solution)/shard_map/ppermute | solution.py:33
  105.8 5.6 %collective-permute-start.35 = (bf16[16,640]{1,0:T(8,128)(2,1)S(1)}, bf16[16,640]{1,0:T(8,128)(2,1)S(1)}, u32[]{:S(2)}, u32[]{:S(2)}) collective-permute-start(bf16[16,640]{1,0:T(8,128)(2,1)S(1)} %get-tuple-element.155), channel_id=1, source_target_pairs={{0,24},{2,26},{4,28},{6,30},{8,16},{10,18},{12,20},{14,22},{16,8},... | collective-permute-start | bytes 61448 | tf_op jit(solution)/shard_map/ppermute | solution.py:33
  108.1 5.3 %collective-permute-start.32 = (bf16[528,128]{1,0:T(8,128)(2,1)S(1)}, bf16[528,128]{1,0:T(8,128)(2,1)S(1)}, u32[]{:S(2)}, u32[]{:S(2)}) collective-permute-start(bf16[528,128]{1,0:T(8,128)(2,1)S(1)} %get-tuple-element.152), channel_id=1, source_target_pairs={{0,8},{2,10},{4,12},{6,14},{8,0},{10,2},{12,4},{14,6},{16,24},{18,... | collective-permute-start | bytes 405512 | tf_op jit(solution)/shard_map/ppermute | solution.py:33
  111.4 0.7 collective-permute-start.33
  115.0 5.8 %collective-permute-start.36 = (bf16[816,128]{1,0:T(8,128)(2,1)S(1)}, bf16[816,128]{1,0:T(8,128)(2,1)S(1)}, u32[]{:S(2)}, u32[]{:S(2)}) collective-permute-start(bf16[816,128]{1,0:T(8,128)(2,1)S(1)} %get-tuple-element.157), channel_id=1, source_target_pairs={{0,2},{2,0},{4,6},{6,4},{8,10},{10,8},{12,14},{14,12},{16,18},{18,... | collective-permute-start | bytes 626696 | tf_op jit(solution)/shard_map/ppermute | solution.py:33
  115.5 7.1 %collective-permute-start.37 = (bf16[816,128]{1,0:T(8,128)(2,1)S(1)}, bf16[816,128]{1,0:T(8,128)(2,1)S(1)}, u32[]{:S(2)}, u32[]{:S(2)}) collective-permute-start(bf16[816,128]{1,0:T(8,128)(2,1)S(1)} %get-tuple-element.158), channel_id=1, source_target_pairs={{0,4},{2,6},{4,0},{6,2},{8,12},{10,14},{12,8},{14,10},{16,20},{18,... | collective-permute-start | bytes 626696 | tf_op jit(solution)/shard_map/ppermute | solution.py:33
  117.0 6.9 %collective-permute-start.38 = (bf16[816,128]{1,0:T(8,128)(2,1)S(1)}, bf16[816,128]{1,0:T(8,128)(2,1)S(1)}, u32[]{:S(2)}, u32[]{:S(2)}) collective-permute-start(bf16[816,128]{1,0:T(8,128)(2,1)S(1)} %get-tuple-element.159), channel_id=1, source_target_pairs={{0,6},{2,4},{4,2},{6,0},{8,14},{10,12},{12,10},{14,8},{16,22},{18,... | collective-permute-start | bytes 626696 | tf_op jit(solution)/shard_map/ppermute | solution.py:33
  125.7 1.4 %collective-permute-start.39 = (f32[256,128]{1,0:T(8,128)S(1)}, f32[256,128]{1,0:T(8,128)S(1)}, u32[]{:S(2)}, u32[]{:S(2)}) collective-permute-start(f32[256,128]{1,0:T(8,128)S(1)} %get-tuple-element.161.dot_ref), channel_id=1, source_target_pairs={{0,1},{1,0},{2,3},{3,2},{4,5},{5,4},{6,7},{7,6},{8,9},{9,8},{10,11... | collective-permute-start | bytes 393224 | tf_op jit(solution)/shard_map/ppermute | solution.py:698
  (3 other events, 3.3 us)
